TPU v7x, 32 devices: a whole 2x2x4 slice. The times are simulated.
32 devices in a mesh: parts: 2 (over x), region: 4 (over y, core), sub: 4 (over z).
Axes of the slice: x: 2, y: 2, z: 4, core: 2. Of those that a mesh axis runs over, the one named last changes fastest.
Arguments:
- node_feats: bfloat16 [16384, 128], P(('parts', 'region', 'sub')), parts along dimension 0, may hold values from -6 to 6
- fine_senders: int32 [98304], P(('parts', 'region', 'sub')), parts along dimension 0, may hold values from 0 to 639
- fine_receivers: int32 [98304], P(('parts', 'region', 'sub')), parts along dimension 0, may hold values from 0 to 511
- fine_edges: bfloat16 [98304, 128], P(('parts', 'region', 'sub')), parts along dimension 0, may hold values from -6 to 6
- halo_rows: int32 [64, 64], P(('parts', 'region', 'sub')), parts along dimension 0, may hold values from 0 to 511
- coarse_senders: int32 [49152], P(('parts', 'region', 'sub')), parts along dimension 0, may hold values from 0 to 319
- coarse_receivers: int32 [49152], P(('parts', 'region', 'sub')), parts along dimension 0, may hold values from 0 to 255
- coarse_edges: bfloat16 [49152, 128], P(('parts', 'region', 'sub')), parts along dimension 0, may hold values from -6 to 6
- coarse_halo_rows: int32 [64, 32], P(('parts', 'region', 'sub')), parts along dimension 0, may hold values from 0 to 255
- pool_dest: int32 [16384, 1], P(('parts', 'region', 'sub')), parts along dimension 0, may hold values from 0 to 3; in each aligned block of 512 rows (0 to 511, 512 to 1023, ...) at most 256 rows name the same one
- pool_target: int32 [16384], P(('parts', 'region', 'sub')), parts along dimension 0, may hold values from 0 to 255
- pool3_target: int32 [8192], P(('parts', 'region', 'sub')), parts along dimension 0, may hold values from 0 to 2047
- top_senders: int32 [16384], P('parts'), parts along dimension 0, may hold values from 0 to 2047
- top_receivers: int32 [16384], P('parts'), parts along dimension 0, may hold values from 0 to 2047
- top_edges: bfloat16 [16384, 128], P('parts'), parts along dimension 0, may hold values from -6 to 6
- edge_in: bfloat16 [5, 384, 128], replicated, may hold values from -0.3125 to 0.3125
- edge_out: bfloat16 [5, 128, 128], replicated, may hold values from -0.5 to 0.5
- node_in: bfloat16 [5, 256, 128], replicated, may hold values from -0.375 to 0.375
- node_out: bfloat16 [5, 128, 128], replicated, may hold values from -0.5 to 0.5
Outputs:
- fine_final: bfloat16 [16384, 128], P(('parts', 'region', 'sub')), parts along dimension 0
There are 2 independent parts, one for each index of `parts`. A program takes and returns all parts, laid end to end along the dimension named above; an argument that names none is the same for every part. Nothing has to cross between parts.
Inputs may be any that keep to these rules, and one draw needn't show every extreme that they name: `pool_dest`: among the rows of one device no region index is named by more than 256 rows; in some devices one index is named by exactly 256.
All inputs are finite; a program needn't handle non-finite values.
Results may differ from a plain program's by a relative error of at most 0.013.
Values may be sent and summed in bfloat16 or wider, within the bound.
No kernel may reach another device: no remote copies, remote signals or barrier semaphores. Data moves between devices by JAX's collectives and lax.ppermute only.
A program may use at most 64 MiB of HBM per device.

v0:
```python
import functools

import jax
import jax.numpy as jnp
from jax import lax
from jax.experimental import pallas as pl
from jax.experimental.pallas import tpu as pltpu
from jax.sharding import PartitionSpec as P

EPSILON = 1e-05
TOP = 2048
LANES = 128
F32, BF16, I32 = jnp.float32, jnp.bfloat16, jnp.int32
TAIL = 16
LIMIT = 40 * 1024 * 1024


def dot(a, b):
    return jnp.dot(a, b, preferred_element_type=F32)


def lane_iota(rows, first=0):
    return lax.broadcasted_iota(I32, (rows, LANES), 1) + first


def column(row):
    return jnp.transpose(jnp.broadcast_to(row, (LANES, row.shape[1])))


def columns(rows):
    return jnp.concatenate([column(rows[i : i + 1]) for i in range(rows.shape[0])], axis=0)


def hot(mask):
    return jnp.where(mask, 1.0, 0.0).astype(BF16)


def hot_rows(col, count):
    return jnp.concatenate(
        [hot(col == lane_iota(col.shape[0], first)) for first in range(0, count, LANES)], axis=1
    )


def hot_cols(rows, count):
    place = lax.broadcasted_iota(I32, (count, LANES), 0)
    return jnp.concatenate([hot(place == rows[i : i + 1]) for i in range(rows.shape[0])], axis=1)


def hot_codes(col, rows):
    return jnp.concatenate([hot(col == rows[i : i + 1]) for i in range(rows.shape[0])], axis=1)


def normalize(values):
    centred = values - jnp.mean(values, axis=-1, keepdims=True)
    variance = jnp.mean(centred * centred, axis=-1, keepdims=True)
    return centred * lax.rsqrt(variance + EPSILON)


def perceptron(features, first, second):
    hidden = jnp.maximum(dot(features, first), 0.0).astype(BF16)
    return normalize(dot(hidden, second))


def node_update(nodes, summed, first, second):
    joined = jnp.concatenate([nodes, summed.astype(BF16)], axis=1)
    return (nodes.astype(F32) + perceptron(joined, first, second)).astype(BF16)


def message_pass(table, own, senders, receivers, edges, weights, new_edges=None, step=1024):
    edge_in, edge_out, node_in, node_out = weights
    first, second = edge_in[...], edge_out[...]
    nodes = table[:own]
    short = -table.shape[0] % LANES
    if short:
        table = jnp.concatenate([table, jnp.zeros((short, LANES), BF16)], axis=0)
    count = edges.shape[0]
    step = min(step, count)
    summed = jnp.zeros((own, LANES), F32)
    for at in range(0, count, step):
        rows = slice(at // LANES, (at + step) // LANES)
        send, recv = senders[rows, :], receivers[rows, :]
        from_send = dot(hot_rows(columns(send), table.shape[0]), table).astype(BF16)
        from_recv = dot(hot_rows(columns(recv), own), nodes).astype(BF16)
        edge = edges[at : at + step, :]
        joined = jnp.concatenate([from_send, from_recv, edge], axis=1)
        new = (edge.astype(F32) + perceptron(joined, first, second)).astype(BF16)
        if new_edges is not None:
            new_edges[at : at + step, :] = new
        summed = summed + dot(hot_cols(recv, own), new)
    return node_update(nodes, summed, node_in[...], node_out[...])


def block_weights(refs, index):
    return [ref.at[index] for ref in refs]


def tail_of(block, count):
    return block[count : count + TAIL, :].astype(F32).astype(I32)


def row_layout(fine, coarse):
    f, c = fine // LANES, coarse // LANES
    return {"dest": 0, "target": f, "high": 2 * f, "low": 2 * f + c, "coarse": 2 * f + 2 * c, "fine_high": 2 * f + 2 * c + 1, "fine_low": 2 * f + 2 * c + 2}


def near_tails(tails, me, count):
    out = []
    for other in (me - 1, me + 1):
        there = jnp.logical_and(other >= 0, other < count)
        near = jnp.where(there, jnp.bitwise_xor(me, other), 0)
        picked = sum(jnp.where(near == j, tail, 0) for j, tail in enumerate(tails))
        out.append((other, there, picked))
    return out


def pick_kernel(nodes, rows, lower, higher):
    for at, out in ((0, lower), (1, higher)):
        col = column(rows[at : at + 1, :])
        out[...] = dot(hot_rows(col, nodes.shape[0]), nodes[...]).astype(BF16)


def fine_kernel(nodes, from_lower, from_higher, senders, receivers, edges, tail, *rest):
    *weights, payload, new_edges = rest
    weights = block_weights(weights, 0)
    own = nodes.shape[0]
    table = jnp.concatenate([nodes[...], from_lower[...], from_higher[...]], axis=0)
    payload[:own, :] = message_pass(table, own, senders, receivers, edges, weights, new_edges)
    payload[own:, :] = tail[...]


def coarse_kernel(regions, halo, coarse, *refs):
    blocks, (senders, receivers, edges, *rest) = refs[:regions], refs[regions:]
    *weights, payload, new_edges = rest
    weights = block_weights(weights, 1)
    me = lax.axis_index("region")
    fine = blocks[0].shape[0] - TAIL
    at = row_layout(fine, coarse)
    tails = [tail_of(block, fine) for block in blocks]
    near = near_tails(tails, me, regions)
    codes = [me * coarse + lax.broadcasted_iota(I32, (coarse, LANES), 0)]
    for side, (other, there, tail) in enumerate(near):
        listed = tail[at["coarse"] : at["coarse"] + 1, :]
        first = halo * (1 - side)
        col = columns(listed)[first : first + halo]
        codes.append(jnp.where(there, other * coarse + col, -1))
    codes = jnp.concatenate(codes, axis=0)
    total = jnp.zeros((codes.shape[0], LANES), F32)
    members = jnp.zeros((codes.shape[0], LANES), F32)
    for block, tail in zip(blocks, tails):
        f = fine // LANES
        parent = tail[at["dest"] : at["dest"] + f] * coarse + tail[at["target"] : at["target"] + f]
        chosen = hot_codes(codes, parent)
        total = total + dot(chosen, block[:fine, :])
        for i in range(f):
            members = members + chosen[:, i * LANES : (i + 1) * LANES].astype(F32)
    members = jnp.sum(members, axis=1, keepdims=True)
    table = (total / jnp.maximum(members, 1.0)).astype(BF16)
    payload[:coarse, :] = message_pass(table, coarse, senders, receivers, edges, weights, new_edges)
    own_tail = tails[0]
    c = coarse // LANES
    payload[coarse:, :] = jnp.concatenate(
        [own_tail[at["high"] : at["high"] + 2 * c], jnp.zeros((TAIL - 2 * c, LANES), I32)], axis=0
    ).astype(F32).astype(BF16)


def compact(first, ranks, codes, edges, size, at_once=8):
    place = lax.broadcasted_iota(I32, (size, LANES), 0) + first

    def body(g, carry):
        latents, found = carry
        rank = ranks[pl.ds(pl.multiple_of(g * at_once, at_once), at_once), :]
        code = codes[pl.ds(pl.multiple_of(g * at_once, at_once), at_once), :]
        hots = []
        for i in range(at_once):
            mask = place == rank[i : i + 1]
            hots.append(hot(mask))
            found = found + jnp.where(mask, code[i : i + 1], 0)
        wide = at_once * LANES
        rows = edges[pl.ds(pl.multiple_of(g * wide, wide), wide), :]
        return latents + dot(jnp.concatenate(hots, axis=1), rows), found

    zero = jnp.zeros((size, LANES), F32), jnp.zeros((size, LANES), I32)
    latents, found = lax.fori_loop(0, ranks.shape[0] // at_once, body, zero)
    found = jnp.sum(found.astype(F32), axis=1, keepdims=True).astype(I32)
    return latents.astype(BF16), jnp.broadcast_to(found, (size, LANES))


def listed_kernel(regions, halo, coarse, wide, size, *refs):
    blocks, refs = refs[:regions], refs[regions:]
    senders, receivers, edges, parents, halo_codes, ranks, codes, latents, found, number = refs
    me = lax.axis_index("region")
    fine = blocks[0].shape[0] - TAIL
    at = row_layout(fine, coarse)
    tails = [tail_of(block, fine) for block in blocks]
    c = coarse // LANES

    def own_parents(tail):
        return tail[at["high"] : at["high"] + c] * LANES + tail[at["low"] : at["low"] + c]

    cols = [columns(own_parents(tails[0]))]
    for side, (other, there, tail) in enumerate(near_tails(tails, me, regions)):
        first = halo * (1 - side)
        col = columns(tail[at["coarse"] : at["coarse"] + 1])[first : first + halo]
        halo_codes[side * halo : (side + 1) * halo, :] = jnp.where(there, other * coarse + col, -1)
        theirs = own_parents(tail).astype(F32)
        value = jnp.zeros((halo, LANES), F32)
        for i in range(c):
            value = value + jnp.where(col == lane_iota(halo, i * LANES), theirs[i : i + 1], 0.0)
        value = jnp.broadcast_to(jnp.sum(value, axis=1, keepdims=True), (halo, LANES)).astype(I32)
        cols.append(jnp.where(there, value, -1))
    cols.append(jnp.full((wide - coarse - 2 * halo, LANES), -1, I32))
    cols = jnp.concatenate(cols, axis=0)
    parents[...] = cols
    count = receivers.shape[0]
    needed = []
    for i in range(count):
        match = jnp.where(cols == receivers[i : i + 1, :], 1.0, 0.0)
        needed.append(jnp.max(match, axis=0, keepdims=True))
    needed = jnp.concatenate(needed, axis=0)
    upto = jnp.where(lax.broadcasted_iota(I32, (LANES, LANES), 0) <= lane_iota(LANES), 1.0, 0.0)
    inside = dot(needed.astype(BF16), upto.astype(BF16))
    sums = jnp.broadcast_to(inside[:, LANES - 1 :], (count, LANES))
    square = (count, count)
    before = lax.broadcasted_iota(I32, square, 1) < lax.broadcasted_iota(I32, square, 0)
    rank = dot(hot(before), sums.astype(BF16)) + inside - 1.0
    ranks[...] = jnp.where(needed > 0.0, rank, -1.0).astype(I32)
    codes[...] = senders[...] * TOP + receivers[...]
    number[0] = jnp.sum(needed).astype(I32)
    latents[...], found[...] = compact(0, ranks, codes, edges, size)


def parent_kernel(regions, halo, coarse, *refs):
    blocks, (table, parents) = refs[:regions], refs[regions:]
    me = lax.axis_index("region")
    fine = blocks[0].shape[0] - TAIL
    at = row_layout(fine, coarse)
    tails = [tail_of(block, fine) for block in blocks]
    f = fine // LANES

    def own_parents(tail):
        return tail[at["dest"] : at["dest"] + f] * coarse + tail[at["target"] : at["target"] + f]

    table[:fine, :] = blocks[0][:fine, :]
    parents[:fine, :] = columns(own_parents(tails[0]))
    for side, (other, there, tail) in enumerate(near_tails(tails, me, regions)):
        rows = slice(fine + side * halo, fine + (side + 1) * halo)
        first = halo * (1 - side)
        listed = tail[at["fine_high"] : at["fine_high"] + 1] * LANES + tail[at["fine_low"] : at["fine_low"] + 1]
        col = columns(listed)[first : first + halo]
        theirs = own_parents(tail).astype(F32)
        value = jnp.zeros((halo, LANES), F32)
        for i in range(f):
            value = value + jnp.where(col == lane_iota(halo, i * LANES), theirs[i : i + 1], 0.0)
        value = jnp.broadcast_to(jnp.sum(value, axis=1, keepdims=True), (halo, LANES)).astype(I32)
        parents[rows, :] = jnp.where(there, value, -1)
        total = jnp.zeros((halo, LANES), F32)
        for j, block in enumerate(blocks):
            here = jnp.logical_and(there, jnp.bitwise_xor(me, j) == other)
            total = total + dot(hot_rows(jnp.where(here, col, -1), fine), block[:fine, :])
        table[rows, :] = total.astype(BF16)


def pooled(col, blocks, coarse):
    c = coarse // LANES

    def add(block, sums):
        total, members = sums
        tail = tail_of(block, coarse)
        chosen = hot_codes(col, tail[:c] * LANES + tail[c : 2 * c])
        total = total + dot(chosen, block[:coarse, :])
        for i in range(c):
            members = members + chosen[:, i * LANES : (i + 1) * LANES].astype(F32)
        return total, members

    sums = (jnp.zeros((col.shape[0], LANES), F32),) * 2
    if isinstance(blocks, tuple):
        for block in blocks:
            sums = add(block, sums)
    else:
        sums = lax.fori_loop(0, blocks.shape[0], lambda n, sums: add(blocks.at[n], sums), sums)
    total, members = sums
    members = jnp.sum(members, axis=1, keepdims=True)
    return (total / jnp.maximum(members, 1.0)).astype(BF16)


def as_rows(col):
    return jnp.concatenate(
        [jnp.transpose(col[i : i + LANES])[:1] for i in range(0, col.shape[0], LANES)], axis=0
    )


def top_kernel(regions, halo, coarse, size, count, *refs):
    blocks, refs = refs[:count] if count > 1 else refs[0], refs[count:]
    parents, halo_codes, ranks, codes, latents, found, number, all_edges = refs[:8]
    senders, receivers, edges = refs[8:11]
    top_weights, weights = block_weights(refs[11:15], 2), block_weights(refs[11:15], 3)
    out, agg = refs[15:]
    me = lax.axis_index("region")
    subs = lax.axis_size("sub")
    own_sub = lambda j: blocks[j * subs] if count > 1 else blocks.at[j * subs]
    wide = parents.shape[0]
    mine = parents[...]
    top_own = pooled(mine, blocks, coarse)
    mine_rows = as_rows(mine)
    row_at = lax.broadcasted_iota(I32, (wide, LANES), 0)
    firsts = []
    for i in range(wide // LANES):
        earlier = jnp.logical_and(mine == mine_rows[i : i + 1], row_at < lane_iota(wide, i * LANES))
        seen = jnp.max(jnp.where(earlier, 1.0, 0.0), axis=0, keepdims=True)
        firsts.append(jnp.where(seen > 0.0, -2, mine_rows[i : i + 1]))
    firsts = jnp.concatenate(firsts, axis=0)
    first, second = top_weights[0][...], top_weights[1][...]
    agg[...] = jnp.zeros_like(agg)
    total = number[0]

    def one(at, edge, code):
        place = lax.broadcasted_iota(I32, (size, LANES), 0) + at
        send = jnp.right_shift(code, TOP.bit_length() - 1)
        recv = jnp.where(place < total, jnp.bitwise_and(code, TOP - 1), -3)
        from_send = pooled(send, blocks, coarse)
        from_recv = dot(hot_codes(recv, firsts), top_own).astype(BF16)
        joined = jnp.concatenate([from_send, from_recv, edge], axis=1)
        new = (edge.astype(F32) + perceptron(joined, first, second)).astype(BF16)
        agg[...] += dot(hot_codes(mine, as_rows(recv)), new)

    one(0, latents[...], found[...])

    def more(b, carry):
        edge, code = compact(b * size, ranks, codes, all_edges, size)
        one(b * size, edge, code)
        return carry

    lax.fori_loop(1, (total + size - 1) // size, more, 0)
    top_final = node_update(top_own, agg[...], top_weights[2][...], top_weights[3][...])
    wanted = halo_codes[...]
    near = jnp.zeros((2 * halo, LANES), F32)
    for j in range(regions):
        col = wanted - jnp.bitwise_xor(me, j) * coarse
        near = near + dot(hot_rows(col, coarse), own_sub(j)[:coarse, :])
    down = jnp.concatenate([own_sub(0)[:coarse, :].astype(F32), near], axis=0)
    table = (down + top_final[: coarse + 2 * halo].astype(F32)).astype(BF16)
    out[...] = message_pass(table, coarse, senders, receivers, edges, weights)


def last_kernel(regions, *refs):
    blocks, refs = refs[:regions], refs[regions:]
    down, parents, senders, receivers, edges, *weights, out = refs
    weights = block_weights(weights, 4)
    me = lax.axis_index("region")
    own, coarse = out.shape[0], blocks[0].shape[0]
    total = down[...].astype(F32)
    wanted = parents[...]
    for j, block in enumerate(blocks):
        col = wanted - jnp.bitwise_xor(me, j) * coarse
        total = total + dot(hot_rows(col, coarse), block[...])
    out[...] = message_pass(total.astype(BF16), own, senders, receivers, edges, weights)


def call(kernel, args, outs, scratch=(), scalars=(), scalar_outs=()):
    specs = [pl.BlockSpec(memory_space=pltpu.SMEM if i in scalars else pltpu.VMEM) for i in range(len(args))]
    out_specs = [pl.BlockSpec(memory_space=pltpu.SMEM if i in scalar_outs else pltpu.VMEM) for i in range(len(outs))]
    return pl.pallas_call(
        kernel,
        out_shape=[jax.ShapeDtypeStruct(shape, dtype) for shape, dtype in outs],
        in_specs=specs,
        out_specs=out_specs,
        scratch_shapes=list(scratch),
        compiler_params=pltpu.CompilerParams(vmem_limit_bytes=LIMIT),
    )(*args)


def over_region(rows):
    count = lax.axis_size("region")
    blocks = {0: rows}
    bit = count // 2
    while bit:
        for j in list(blocks):
            blocks[j + bit] = lax.ppermute(blocks[j], "region", [(i, i ^ bit) for i in range(count)])
        bit //= 2
    return [blocks[j] for j in range(count)]


def over_both(rows):
    regions, subs = lax.axis_size("region"), lax.axis_size("sub")
    turns = [rows] + [
        lax.ppermute(rows, "sub", [(i, (i + k) % subs) for i in range(subs)]) for k in range(1, subs)
    ]
    if regions * subs <= 16:
        spread = [over_region(turn) for turn in turns]
        return [spread[k][j] for j in range(regions) for k in range(subs)]
    blocks, bit = jnp.stack(turns), 1
    while bit < regions:
        there = lax.ppermute(blocks, "region", [(i, i ^ bit) for i in range(regions)])
        blocks, bit = jnp.concatenate([blocks, there]), 2 * bit
    return [blocks]


def on_device(
    node_feats,
    fine_senders,
    fine_receivers,
    fine_edges,
    halo_rows,
    coarse_senders,
    coarse_receivers,
    coarse_edges,
    coarse_halo_rows,
    pool_dest,
    pool_target,
    pool3_target,
    top_senders,
    top_receivers,
    top_edges,
    edge_in,
    edge_out,
    node_in,
    node_out,
):
    weights = (edge_in, edge_out, node_in, node_out)
    regions = lax.axis_size("region")
    fine, coarse = node_feats.shape[0], pool3_target.shape[0]
    halo, halo2 = halo_rows.shape[1], coarse_halo_rows.shape[1]
    rows = lambda a: a.reshape(-1, LANES)
    fine_send, fine_recv = rows(fine_senders), rows(fine_receivers)
    coarse_send, coarse_recv = rows(coarse_senders), rows(coarse_receivers)
    top_send, top_recv = rows(top_senders), rows(top_receivers)

    to_lower, to_higher = call(
        pick_kernel, [node_feats, halo_rows], [((halo, LANES), BF16)] * 2
    )
    up = [(i, i + 1) for i in range(regions - 1)]
    from_lower = lax.ppermute(to_higher, "region", up)
    from_higher = lax.ppermute(to_lower, "region", [(j, i) for i, j in up])

    parent3, listed = rows(pool3_target), halo_rows.reshape(1, -1)
    tail = jnp.concatenate(
        [
            rows(pool_dest),
            rows(pool_target),
            parent3 // LANES,
            parent3 % LANES,
            jnp.pad(coarse_halo_rows.reshape(1, -1), ((0, 0), (0, LANES - 2 * halo2))),
            listed // LANES,
            listed % LANES,
        ],
        axis=0,
    )
    tail = jnp.pad(tail, ((0, TAIL - tail.shape[0]), (0, 0))).astype(BF16)

    payload, fine_edges2 = call(
        fine_kernel,
        [node_feats, from_lower, from_higher, fine_send, fine_recv, fine_edges, tail, *weights],
        [((fine + TAIL, LANES), BF16), (fine_edges.shape, BF16)],
    )
    blocks = over_region(payload)
    payload2, coarse_edges2 = call(
        functools.partial(coarse_kernel, regions, halo2, coarse),
        blocks + [coarse_send, coarse_recv, coarse_edges, *weights],
        [((coarse + TAIL, LANES), BF16), (coarse_edges.shape, BF16)],
    )
    wide = -(-(coarse + 2 * halo2) // LANES) * LANES
    size = min(512, top_edges.shape[0])
    parents, halo_codes, ranks, codes, latents, found, number = call(
        functools.partial(listed_kernel, regions, halo2, coarse, wide, size),
        blocks + [top_send, top_recv, top_edges],
        [
            ((wide, LANES), I32),
            ((2 * halo2, LANES), I32),
            (top_send.shape, I32),
            (top_send.shape, I32),
            ((size, LANES), BF16),
            ((size, LANES), I32),
            ((1,), I32),
        ],
        scalar_outs=(6,),
    )
    fine_table, fine_parents = call(
        functools.partial(parent_kernel, regions, halo, coarse),
        blocks,
        [((fine + 2 * halo, LANES), BF16), ((fine + 2 * halo, LANES), I32)],
    )
    blocks2 = over_both(payload2)
    (coarse_final,) = call(
        functools.partial(top_kernel, regions, halo2, coarse, size, len(blocks2)),
        blocks2
        + [parents, halo_codes, ranks, codes, latents, found, number, top_edges]
        + [coarse_send, coarse_recv, coarse_edges2, *weights],
        [((coarse, LANES), BF16)],
        scratch=[pltpu.VMEM((wide, LANES), F32)],
        scalars=(len(blocks2) + 6,),
    )
    (fine_final,) = call(
        functools.partial(last_kernel, regions),
        over_region(coarse_final) + [fine_table, fine_parents, fine_send, fine_recv, fine_edges2, *weights],
        [((fine, LANES), BF16)],
    )
    return fine_final


def solution(mesh):
    spread = ("parts", "region", "sub")
    rows, flat = P(spread, None), P(spread)
    in_specs = (
        (rows, flat, flat, rows, rows, flat, flat, rows, rows, rows, flat, flat)
        + (P("parts"), P("parts"), P("parts", None))
        + (P(),) * 4
    )
    return jax.shard_map(on_device, mesh=mesh, in_specs=in_specs, out_specs=rows, check_vma=False)
```

profile of v0, /device:TPU:0, one launch (start us, length us, event | category | flops | bytes accessed | tf_op | source)
XLA Modules:
  0.0 81.7 jit_solution(5587908189268586831)
XLA Ops:
  0.0 0.9 %copy-done.13 = bf16[512,128]{1,0:T(8,128)(2,1)S(1)} copy-done((bf16[512,128]{1,0:T(8,128)(2,1)S(1)}, bf16[512,128]{1,0:T(8,128)(2,1)}, u32[]{:S(2)}) %copy-start.13) | copy-done | bytes 131096
  1.9 2.4 %collective-permute-start = (bf16[64,128]{1,0:T(8,128)(2,1)S(1)}, bf16[64,128]{1,0:T(8,128)(2,1)S(1)}, u32[]{:S(2)}, u32[]{:S(2)}) collective-permute-start(bf16[64,128]{1,0:T(8,128)(2,1)S(1)} %get-tuple-element.20), channel_id=1, source_target_pairs={{0,4},{4,8},{8,12},{1,5},{5,9},{9,13},{2,6},{6,10},{10,14},{3,7},{... | collective-permute-start | bytes 49160 | tf_op jit(solution)/shard_map/ppermute | solution.py:432
  4.2 1.3 %collective-permute-start.1 = (bf16[64,128]{1,0:T(8,128)(2,1)S(1)}, bf16[64,128]{1,0:T(8,128)(2,1)S(1)}, u32[]{:S(2)}, u32[]{:S(2)}) collective-permute-start(bf16[64,128]{1,0:T(8,128)(2,1)S(1)} %get-tuple-element.21), channel_id=1, source_target_pairs={{4,0},{8,4},{12,8},{5,1},{9,5},{13,9},{6,2},{10,6},{14,10},{7,3},{... | collective-permute-start | bytes 49160 | tf_op jit(solution)/shard_map/ppermute | solution.py:433
  9.4 1.0 %copy-done.1 = bf16[5,384,128]{2,1,0:T(8,128)(2,1)S(1)} copy-done((bf16[5,384,128]{2,1,0:T(8,128)(2,1)S(1)}, bf16[5,384,128]{2,1,0:T(8,128)(2,1)}, u32[]{:S(2)}) %copy-start.1) | copy-done | bytes 491544
  10.5 1.0 %copy-done.4 = bf16[5,256,128]{2,1,0:T(8,128)(2,1)S(1)} copy-done((bf16[5,256,128]{2,1,0:T(8,128)(2,1)S(1)}, bf16[5,256,128]{2,1,0:T(8,128)(2,1)}, u32[]{:S(2)}) %copy-start.4) | copy-done | bytes 327704
  11.4 0.9 %copy-done.7 = bf16[5,128,128]{2,1,0:T(8,128)(2,1)S(1)} copy-done((bf16[5,128,128]{2,1,0:T(8,128)(2,1)S(1)}, bf16[5,128,128]{2,1,0:T(8,128)(2,1)}, u32[]{:S(2)}) %copy-start.7) | copy-done | bytes 163864
  12.4 0.9 %copy-done.9 = bf16[5,128,128]{2,1,0:T(8,128)(2,1)S(1)} copy-done((bf16[5,128,128]{2,1,0:T(8,128)(2,1)S(1)}, bf16[5,128,128]{2,1,0:T(8,128)(2,1)}, u32[]{:S(2)}) %copy-start.9) | copy-done | bytes 163864
  13.3 1.1 %copy-done.12 = bf16[3072,128]{1,0:T(8,128)(2,1)S(1)} copy-done((bf16[3072,128]{1,0:T(8,128)(2,1)S(1)}, bf16[3072,128]{1,0:T(8,128)(2,1)}, u32[]{:S(2)}) %copy-start.12) | copy-done | bytes 786456
  14.4 0.9 %copy-done.14 = bf16[512,128]{1,0:T(8,128)(2,1)S(1)} copy-done((bf16[512,128]{1,0:T(8,128)(2,1)S(1)}, bf16[512,128]{1,0:T(8,128)(2,1)}, u32[]{:S(2)}) %copy-start.14) | copy-done | bytes 131096
  16.7 5.6 %shard_map.182 = (bf16[528,128]{1,0:T(8,128)(2,1)S(1)}, bf16[3072,128]{1,0:T(8,128)(2,1)S(1)}) custom-call(bf16[512,128]{1,0:T(8,128)(2,1)S(1)} %copy-done.14, bf16[64,128]{1,0:T(8,128)(2,1)S(1)} %collective-permute-done.from_lower, bf16[64,128]{1,0:T(8,128)(2,1)S(1)} %collective-permute-done.1.from_higher, s32[24,128]{1,0:T(8,128)S(1)} %bitcast.29, ...), custom_call_target="tpu_custom_call" | custom-call | tf_op jit(solution)/shard_map/pallas_call | solution.py:362
  22.4 4.1 %collective-permute-start.3 = (bf16[528,128]{1,0:T(8,128)(2,1)S(1)}, bf16[528,128]{1,0:T(8,128)(2,1)S(1)}, u32[]{:S(2)}, u32[]{:S(2)}) collective-permute-start(bf16[528,128]{1,0:T(8,128)(2,1)S(1)} %get-tuple-element.22.refs_0_), channel_id=1, source_target_pairs={{0,8},{4,12},{8,0},{12,4},{1,9},{5,13},{9,1},{13,5},{2,10},{6,14},... | collective-permute-start | bytes 405512 | tf_op jit(solution)/shard_map/ppermute | solution.py:378
  26.4 4.0 %collective-permute-done.3.refs_2_ = bf16[528,128]{1,0:T(8,128)(2,1)S(1)} collective-permute-done((bf16[528,128]{1,0:T(8,128)(2,1)S(1)}, bf16[528,128]{1,0:T(8,128)(2,1)S(1)}, u32[]{:S(2)}, u32[]{:S(2)}) %collective-permute-start.3) | collective-permute-done | bytes 135200 | tf_op jit(solution)/shard_map/ppermute | solution.py:378
  30.4 1.3 %collective-permute-done.4.refs_3_ = bf16[528,128]{1,0:T(8,128)(2,1)S(1)} collective-permute-done((bf16[528,128]{1,0:T(8,128)(2,1)S(1)}, bf16[528,128]{1,0:T(8,128)(2,1)S(1)}, u32[]{:S(2)}, u32[]{:S(2)}) %collective-permute-start.4) | collective-permute-done | bytes 135200 | tf_op jit(solution)/shard_map/ppermute | solution.py:378
  31.8 1.0 %copy-done.2 = bf16[5,384,128]{2,1,0:T(8,128)(2,1)S(1)} copy-done((bf16[5,384,128]{2,1,0:T(8,128)(2,1)S(1)}, bf16[5,384,128]{2,1,0:T(8,128)(2,1)}, u32[]{:S(2)}) %copy-start.2) | copy-done | bytes 491544
  32.8 1.0 %copy-done.5 = bf16[5,256,128]{2,1,0:T(8,128)(2,1)S(1)} copy-done((bf16[5,256,128]{2,1,0:T(8,128)(2,1)S(1)}, bf16[5,256,128]{2,1,0:T(8,128)(2,1)}, u32[]{:S(2)}) %copy-start.5) | copy-done | bytes 327704
  33.8 0.9 %copy-done.10 = bf16[5,128,128]{2,1,0:T(8,128)(2,1)S(1)} copy-done((bf16[5,128,128]{2,1,0:T(8,128)(2,1)S(1)}, bf16[5,128,128]{2,1,0:T(8,128)(2,1)}, u32[]{:S(2)}) %copy-start.10) | copy-done | bytes 163864
  34.7 1.0 %copy-done.15 = bf16[1536,128]{1,0:T(8,128)(2,1)S(1)} copy-done((bf16[1536,128]{1,0:T(8,128)(2,1)S(1)}, bf16[1536,128]{1,0:T(8,128)(2,1)}, u32[]{:S(2)}) %copy-start.15) | copy-done | bytes 393240
  35.7 3.5 %shard_map.183 = (bf16[272,128]{1,0:T(8,128)(2,1)S(1)}, bf16[1536,128]{1,0:T(8,128)(2,1)S(1)}) custom-call(bf16[528,128]{1,0:T(8,128)(2,1)S(1)} %get-tuple-element.22.refs_0_, bf16[528,128]{1,0:T(8,128)(2,1)S(1)} %collective-permute-done.2.refs_1_, bf16[528,128]{1,0:T(8,128)(2,1)S(1)} %collective-permute-done.3.refs_2_, ...), custom_call_target="tpu_custom_call" | custom-call | tf_op jit(solution)/shard_map/pallas_call | solution.py:362
  39.2 1.6 %collective-permute-start.5 = (bf16[272,128]{1,0:T(8,128)(2,1)S(1)}, bf16[272,128]{1,0:T(8,128)(2,1)S(1)}, u32[]{:S(2)}, u32[]{:S(2)}) collective-permute-start(bf16[272,128]{1,0:T(8,128)(2,1)S(1)} %get-tuple-element.23.refs_0_), channel_id=1, source_target_pairs={{0,1},{1,2},{2,3},{3,0},{4,5},{5,6},{6,7},{7,4},{8,9},{9,10},{10,1... | collective-permute-start | bytes 208904 | tf_op jit(solution)/shard_map/ppermute | solution.py:386
  40.8 2.6 %collective-permute-start.6 = (bf16[272,128]{1,0:T(8,128)(2,1)S(1)}, bf16[272,128]{1,0:T(8,128)(2,1)S(1)}, u32[]{:S(2)}, u32[]{:S(2)}) collective-permute-start(bf16[272,128]{1,0:T(8,128)(2,1)S(1)} %get-tuple-element.23.refs_0_), channel_id=1, source_target_pairs={{0,2},{1,3},{2,0},{3,1},{4,6},{5,7},{6,4},{7,5},{8,10},{9,11},{10,... | collective-permute-start | bytes 208904 | tf_op jit(solution)/shard_map/ppermute | solution.py:386
  43.4 1.4 %collective-permute-start.7 = (bf16[272,128]{1,0:T(8,128)(2,1)S(1)}, bf16[272,128]{1,0:T(8,128)(2,1)S(1)}, u32[]{:S(2)}, u32[]{:S(2)}) collective-permute-start(bf16[272,128]{1,0:T(8,128)(2,1)S(1)} %get-tuple-element.23.refs_0_), channel_id=1, source_target_pairs={{0,3},{1,0},{2,1},{3,2},{4,7},{5,4},{6,5},{7,6},{8,11},{9,8},{10,9... | collective-permute-start | bytes 208904 | tf_op jit(solution)/shard_map/ppermute | solution.py:386
  44.8 1.1 %collective-permute-start.12 = (bf16[272,128]{1,0:T(8,128)(2,1)S(1)}, bf16[272,128]{1,0:T(8,128)(2,1)S(1)}, u32[]{:S(2)}, u32[]{:S(2)}) collective-permute-start(bf16[272,128]{1,0:T(8,128)(2,1)S(1)} %get-tuple-element.23.refs_0_), channel_id=1, source_target_pairs={{0,8},{4,12},{8,0},{12,4},{1,9},{5,13},{9,1},{13,5},{2,10},{6,14},... | collective-permute-start | bytes 208904 | tf_op jit(solution)/shard_map/ppermute | solution.py:378
  45.8 1.0 %collective-permute-start.13 = (bf16[272,128]{1,0:T(8,128)(2,1)S(1)}, bf16[272,128]{1,0:T(8,128)(2,1)S(1)}, u32[]{:S(2)}, u32[]{:S(2)}) collective-permute-start(bf16[272,128]{1,0:T(8,128)(2,1)S(1)} %collective-permute-done.5.refs_1_), channel_id=1, source_target_pairs={{0,8},{4,12},{8,0},{12,4},{1,9},{5,13},{9,1},{13,5},{2,10},{6,14},... | collective-permute-start | bytes 208904 | tf_op jit(solution)/shard_map/ppermute | solution.py:378
  46.8 1.6 %collective-permute-done.6.refs_2_ = bf16[272,128]{1,0:T(8,128)(2,1)S(1)} collective-permute-done((bf16[272,128]{1,0:T(8,128)(2,1)S(1)}, bf16[272,128]{1,0:T(8,128)(2,1)S(1)}, u32[]{:S(2)}, u32[]{:S(2)}) %collective-permute-start.6) | collective-permute-done | bytes 69664 | tf_op jit(solution)/shard_map/ppermute | solution.py:386
  48.4 1.1 %collective-permute-start.14 = (bf16[272,128]{1,0:T(8,128)(2,1)S(1)}, bf16[272,128]{1,0:T(8,128)(2,1)S(1)}, u32[]{:S(2)}, u32[]{:S(2)}) collective-permute-start(bf16[272,128]{1,0:T(8,128)(2,1)S(1)} %collective-permute-done.6.refs_2_), channel_id=1, source_target_pairs={{0,8},{4,12},{8,0},{12,4},{1,9},{5,13},{9,1},{13,5},{2,10},{6,14},... | collective-permute-start | bytes 208904 | tf_op jit(solution)/shard_map/ppermute | solution.py:378
  49.5 1.0 %collective-permute-start.15 = (bf16[272,128]{1,0:T(8,128)(2,1)S(1)}, bf16[272,128]{1,0:T(8,128)(2,1)S(1)}, u32[]{:S(2)}, u32[]{:S(2)}) collective-permute-start(bf16[272,128]{1,0:T(8,128)(2,1)S(1)} %collective-permute-done.7.refs_3_), channel_id=1, source_target_pairs={{0,8},{4,12},{8,0},{12,4},{1,9},{5,13},{9,1},{13,5},{2,10},{6,14},... | collective-permute-start | bytes 208904 | tf_op jit(solution)/shard_map/ppermute | solution.py:378
  51.0 2.2 %collective-permute-done.14.refs_10_ = bf16[272,128]{1,0:T(8,128)(2,1)S(1)} collective-permute-done((bf16[272,128]{1,0:T(8,128)(2,1)S(1)}, bf16[272,128]{1,0:T(8,128)(2,1)S(1)}, u32[]{:S(2)}, u32[]{:S(2)}) %collective-permute-start.14) | collective-permute-done | bytes 69664 | tf_op jit(solution)/shard_map/ppermute | solution.py:378
  54.6 7.4 %shard_map.184 = (s32[384,128]{1,0:T(8,128)S(1)}, s32[64,128]{1,0:T(8,128)S(1)}, s32[64,128]{1,0:T(8,128)S(1)}, s32[64,128]{1,0:T(8,128)S(1)}, bf16[512,128]{1,0...) custom-call(bf16[528,128]{1,0:T(8,128)(2,1)S(1)} %get-tuple-element.22.refs_0_, ...), custom_call_target="tpu_custom_call" | custom-call | tf_op jit(solution)/shard_map/pallas_call | solution.py:362
  62.0 7.0 %shard_map.185.refs_0_ = bf16[256,128]{1,0:T(8,128)(2,1)S(1)} custom-call(bf16[272,128]{1,0:T(8,128)(2,1)S(1)} %get-tuple-element.23.refs_0_, bf16[272,128]{1,0:T(8,128)(2,1)S(1)} %collective-permute-done.5.refs_1_, bf16[272,128]{1,0:T(8,128)(2,1)S(1)} %collective-permute-done.6.refs_2_, bf16[272,128]{1,0:T(8,128)(2,1)S(1)} %collective-permute-done.7.refs_3_, ...), custom_call_target="tpu_custom_call" | custom-call | tf_op jit(solution)/shard_map/pallas_call | solution.py:362
  69.1 1.1 %collective-permute-start.21 = (bf16[256,128]{1,0:T(8,128)(2,1)S(1)}, bf16[256,128]{1,0:T(8,128)(2,1)S(1)}, u32[]{:S(2)}, u32[]{:S(2)}) collective-permute-start(bf16[256,128]{1,0:T(8,128)(2,1)S(1)} %shard_map.185.refs_0_), channel_id=1, source_target_pairs={{0,8},{4,12},{8,0},{12,4},{1,9},{5,13},{9,1},{13,5},{2,10},{6,14},... | collective-permute-start | bytes 196616 | tf_op jit(solution)/shard_map/ppermute | solution.py:378
  70.3 3.3 %collective-permute-done.21.refs_2_ = bf16[256,128]{1,0:T(8,128)(2,1)S(1)} collective-permute-done((bf16[256,128]{1,0:T(8,128)(2,1)S(1)}, bf16[256,128]{1,0:T(8,128)(2,1)S(1)}, u32[]{:S(2)}, u32[]{:S(2)}) %collective-permute-start.21) | collective-permute-done | bytes 65568 | tf_op jit(solution)/shard_map/ppermute | solution.py:378
  74.8 6.8 %shard_map.187 = bf16[512,128]{1,0:T(8,128)(2,1)} custom-call(bf16[256,128]{1,0:T(8,128)(2,1)S(1)} %shard_map.185.refs_0_, bf16[256,128]{1,0:T(8,128)(2,1)S(1)} %collective-permute-done.20.refs_1_, bf16[256,128]{1,0:T(8,128)(2,1)S(1)} %collective-permute-done.21.refs_2_, bf16[256,128]{1,0:T(8,128)(2,1)S(1)} %collective-permute-done.22.refs_3_, ...), custom_call_target="tpu_custom_call" | custom-call | tf_op jit(solution)/shard_map/pallas_call | solution.py:362
  (81 shorter events, 9.6 us)
Async XLA Ops:
  0.0 31.7 %copy-start.8 = (bf16[5,128,128]{2,1,0:T(8,128)(2,1)S(1)}, bf16[5,128,128]{2,1,0:T(8,128)(2,1)}, u32[]{:S(2)}) copy-start(bf16[5,128,128]{2,1,0:T(8,128)(2,1)} %refs_10_.3) | copy-start | bytes 491524
  1.6 30.1 %copy-start.22 = (s32[1536]{0:T(1024)S(1)}, s32[1536]{0:T(1024)}, u32[]{:S(2)}) copy-start(s32[1536]{0:T(1024)} %param.24) | copy-start | bytes 18436
  1.6 30.1 %copy-start.23 = (s32[1536]{0:T(1024)S(1)}, s32[1536]{0:T(1024)}, u32[]{:S(2)}) copy-start(s32[1536]{0:T(1024)} %param.25) | copy-start | bytes 18436
  1.9 6.7 %collective-permute-start = (bf16[64,128]{1,0:T(8,128)(2,1)S(1)}, bf16[64,128]{1,0:T(8,128)(2,1)S(1)}, u32[]{:S(2)}, u32[]{:S(2)}) collective-permute-start(bf16[64,128]{1,0:T(8,128)(2,1)S(1)} %get-tuple-element.20), channel_id=1, source_target_pairs={{0,4},{4,8},{8,12},{1,5},{5,9},{9,13},{2,6},{6,10},{10,14},{3,7},{... | collective-permute-start | bytes 49160 | tf_op jit(solution)/shard_map/ppermute | solution.py:432
  4.2 5.2 %collective-permute-start.1 = (bf16[64,128]{1,0:T(8,128)(2,1)S(1)}, bf16[64,128]{1,0:T(8,128)(2,1)S(1)}, u32[]{:S(2)}, u32[]{:S(2)}) collective-permute-start(bf16[64,128]{1,0:T(8,128)(2,1)S(1)} %get-tuple-element.21), channel_id=1, source_target_pairs={{4,0},{8,4},{12,8},{5,1},{9,5},{13,9},{6,2},{10,6},{14,10},{7,3},{... | collective-permute-start | bytes 49160 | tf_op jit(solution)/shard_map/ppermute | solution.py:433
  16.7 37.8 %copy-start = (bf16[8192,128]{1,0:T(8,128)(2,1)S(1)}, bf16[8192,128]{1,0:T(8,128)(2,1)}, u32[]{:S(2)}) copy-start(bf16[8192,128]{1,0:T(8,128)(2,1)} %refs_23_.1) | copy-start | bytes 6291460
  16.7 37.8 %copy-start.20 = (s32[8192]{0:T(1024)S(1)}, s32[8192]{0:T(1024)}, u32[]{:S(2)}) copy-start(s32[8192]{0:T(1024)} %param.31) | copy-start | bytes 98308
  22.4 8.0 %collective-permute-start.3 = (bf16[528,128]{1,0:T(8,128)(2,1)S(1)}, bf16[528,128]{1,0:T(8,128)(2,1)S(1)}, u32[]{:S(2)}, u32[]{:S(2)}) collective-permute-start(bf16[528,128]{1,0:T(8,128)(2,1)S(1)} %get-tuple-element.22.refs_0_), channel_id=1, source_target_pairs={{0,8},{4,12},{8,0},{12,4},{1,9},{5,13},{9,1},{13,5},{2,10},{6,14},... | collective-permute-start | bytes 405512 | tf_op jit(solution)/shard_map/ppermute | solution.py:378
  26.4 4.0 %collective-permute-start.2 = (bf16[528,128]{1,0:T(8,128)(2,1)S(1)}, bf16[528,128]{1,0:T(8,128)(2,1)S(1)}, u32[]{:S(2)}, u32[]{:S(2)}) collective-permute-start(bf16[528,128]{1,0:T(8,128)(2,1)S(1)} %get-tuple-element.22.refs_0_), channel_id=1, source_target_pairs={{0,4},{4,0},{8,12},{12,8},{1,5},{5,1},{9,13},{13,9},{2,6},{6,2},{1... | collective-permute-start | bytes 405512 | tf_op jit(solution)/shard_map/ppermute | solution.py:378
  30.4 1.4 %collective-permute-start.4 = (bf16[528,128]{1,0:T(8,128)(2,1)S(1)}, bf16[528,128]{1,0:T(8,128)(2,1)S(1)}, u32[]{:S(2)}, u32[]{:S(2)}) collective-permute-start(bf16[528,128]{1,0:T(8,128)(2,1)S(1)} %collective-permute-done.3.refs_2_), channel_id=1, source_target_pairs={{0,4},{4,0},{8,12},{12,8},{1,5},{5,1},{9,13},{13,9},{2,6},{6,2},{1... | collective-permute-start | bytes 405512 | tf_op jit(solution)/shard_map/ppermute | solution.py:378
  35.7 18.9 %copy-start.21 = (s32[8192]{0:T(1024)S(1)}, s32[8192]{0:T(1024)}, u32[]{:S(2)}) copy-start(s32[8192]{0:T(1024)} %param.32) | copy-start | bytes 98308
  35.7 26.3 %copy-start.3 = (bf16[5,384,128]{2,1,0:T(8,128)(2,1)S(1)}, bf16[5,384,128]{2,1,0:T(8,128)(2,1)}, u32[]{:S(2)}) copy-start(bf16[5,384,128]{2,1,0:T(8,128)(2,1)} %refs_9_.3) | copy-start | bytes 1474564
  35.7 26.3 %copy-start.11 = (bf16[5,128,128]{2,1,0:T(8,128)(2,1)S(1)}, bf16[5,128,128]{2,1,0:T(8,128)(2,1)}, u32[]{:S(2)}) copy-start(bf16[5,128,128]{2,1,0:T(8,128)(2,1)} %refs_12_.1) | copy-start | bytes 491524
  39.2 6.6 %collective-permute-start.5 = (bf16[272,128]{1,0:T(8,128)(2,1)S(1)}, bf16[272,128]{1,0:T(8,128)(2,1)S(1)}, u32[]{:S(2)}, u32[]{:S(2)}) collective-permute-start(bf16[272,128]{1,0:T(8,128)(2,1)S(1)} %get-tuple-element.23.refs_0_), channel_id=1, source_target_pairs={{0,1},{1,2},{2,3},{3,0},{4,5},{5,6},{6,7},{7,4},{8,9},{9,10},{10,1... | collective-permute-start | bytes 208904 | tf_op jit(solution)/shard_map/ppermute | solution.py:386
  40.8 7.6 %collective-permute-start.6 = (bf16[272,128]{1,0:T(8,128)(2,1)S(1)}, bf16[272,128]{1,0:T(8,128)(2,1)S(1)}, u32[]{:S(2)}, u32[]{:S(2)}) collective-permute-start(bf16[272,128]{1,0:T(8,128)(2,1)S(1)} %get-tuple-element.23.refs_0_), channel_id=1, source_target_pairs={{0,2},{1,3},{2,0},{3,1},{4,6},{5,7},{6,4},{7,5},{8,10},{9,11},{10,... | collective-permute-start | bytes 208904 | tf_op jit(solution)/shard_map/ppermute | solution.py:386
  43.4 6.1 %collective-permute-start.7 = (bf16[272,128]{1,0:T(8,128)(2,1)S(1)}, bf16[272,128]{1,0:T(8,128)(2,1)S(1)}, u32[]{:S(2)}, u32[]{:S(2)}) collective-permute-start(bf16[272,128]{1,0:T(8,128)(2,1)S(1)} %get-tuple-element.23.refs_0_), channel_id=1, source_target_pairs={{0,3},{1,0},{2,1},{3,2},{4,7},{5,4},{6,5},{7,6},{8,11},{9,8},{10,9... | collective-permute-start | bytes 208904 | tf_op jit(solution)/shard_map/ppermute | solution.py:386
  44.8 5.7 %collective-permute-start.12 = (bf16[272,128]{1,0:T(8,128)(2,1)S(1)}, bf16[272,128]{1,0:T(8,128)(2,1)S(1)}, u32[]{:S(2)}, u32[]{:S(2)}) collective-permute-start(bf16[272,128]{1,0:T(8,128)(2,1)S(1)} %get-tuple-element.23.refs_0_), channel_id=1, source_target_pairs={{0,8},{4,12},{8,0},{12,4},{1,9},{5,13},{9,1},{13,5},{2,10},{6,14},... | collective-permute-start | bytes 208904 | tf_op jit(solution)/shard_map/ppermute | solution.py:378
  45.8 4.6 %collective-permute-start.8 = (bf16[272,128]{1,0:T(8,128)(2,1)S(1)}, bf16[272,128]{1,0:T(8,128)(2,1)S(1)}, u32[]{:S(2)}, u32[]{:S(2)}) collective-permute-start(bf16[272,128]{1,0:T(8,128)(2,1)S(1)} %get-tuple-element.23.refs_0_), channel_id=1, source_target_pairs={{0,4},{4,0},{8,12},{12,8},{1,5},{5,1},{9,13},{13,9},{2,6},{6,2},{1... | collective-permute-start | bytes 208904 | tf_op jit(solution)/shard_map/ppermute | solution.py:378
  45.8 5.1 %collective-permute-start.13 = (bf16[272,128]{1,0:T(8,128)(2,1)S(1)}, bf16[272,128]{1,0:T(8,128)(2,1)S(1)}, u32[]{:S(2)}, u32[]{:S(2)}) collective-permute-start(bf16[272,128]{1,0:T(8,128)(2,1)S(1)} %collective-permute-done.5.refs_1_), channel_id=1, source_target_pairs={{0,8},{4,12},{8,0},{12,4},{1,9},{5,13},{9,1},{13,5},{2,10},{6,14},... | collective-permute-start | bytes 208904 | tf_op jit(solution)/shard_map/ppermute | solution.py:378
  48.4 4.8 %collective-permute-start.14 = (bf16[272,128]{1,0:T(8,128)(2,1)S(1)}, bf16[272,128]{1,0:T(8,128)(2,1)S(1)}, u32[]{:S(2)}, u32[]{:S(2)}) collective-permute-start(bf16[272,128]{1,0:T(8,128)(2,1)S(1)} %collective-permute-done.6.refs_2_), channel_id=1, source_target_pairs={{0,8},{4,12},{8,0},{12,4},{1,9},{5,13},{9,1},{13,5},{2,10},{6,14},... | collective-permute-start | bytes 208904 | tf_op jit(solution)/shard_map/ppermute | solution.py:378
  49.5 4.5 %collective-permute-start.15 = (bf16[272,128]{1,0:T(8,128)(2,1)S(1)}, bf16[272,128]{1,0:T(8,128)(2,1)S(1)}, u32[]{:S(2)}, u32[]{:S(2)}) collective-permute-start(bf16[272,128]{1,0:T(8,128)(2,1)S(1)} %collective-permute-done.7.refs_3_), channel_id=1, source_target_pairs={{0,8},{4,12},{8,0},{12,4},{1,9},{5,13},{9,1},{13,5},{2,10},{6,14},... | collective-permute-start | bytes 208904 | tf_op jit(solution)/shard_map/ppermute | solution.py:378
  50.5 3.5 %collective-permute-start.10 = (bf16[272,128]{1,0:T(8,128)(2,1)S(1)}, bf16[272,128]{1,0:T(8,128)(2,1)S(1)}, u32[]{:S(2)}, u32[]{:S(2)}) collective-permute-start(bf16[272,128]{1,0:T(8,128)(2,1)S(1)} %collective-permute-done.6.refs_2_), channel_id=1, source_target_pairs={{0,4},{4,0},{8,12},{12,8},{1,5},{5,1},{9,13},{13,9},{2,6},{6,2},{1... | collective-permute-start | bytes 208904 | tf_op jit(solution)/shard_map/ppermute | solution.py:378
  50.5 4.0 %collective-permute-start.11 = (bf16[272,128]{1,0:T(8,128)(2,1)S(1)}, bf16[272,128]{1,0:T(8,128)(2,1)S(1)}, u32[]{:S(2)}, u32[]{:S(2)}) collective-permute-start(bf16[272,128]{1,0:T(8,128)(2,1)S(1)} %collective-permute-done.7.refs_3_), channel_id=1, source_target_pairs={{0,4},{4,0},{8,12},{12,8},{1,5},{5,1},{9,13},{13,9},{2,6},{6,2},{1... | collective-permute-start | bytes 208904 | tf_op jit(solution)/shard_map/ppermute | solution.py:378
  51.0 11.0 %collective-permute-start.9 = (bf16[272,128]{1,0:T(8,128)(2,1)S(1)}, bf16[272,128]{1,0:T(8,128)(2,1)S(1)}, u32[]{:S(2)}, u32[]{:S(2)}) collective-permute-start(bf16[272,128]{1,0:T(8,128)(2,1)S(1)} %collective-permute-done.5.refs_1_), channel_id=1, source_target_pairs={{0,4},{4,0},{8,12},{12,8},{1,5},{5,1},{9,13},{13,9},{2,6},{6,2},{1... | collective-permute-start | bytes 208904 | tf_op jit(solution)/shard_map/ppermute | solution.py:378
  53.2 8.7 %collective-permute-start.16 = (bf16[272,128]{1,0:T(8,128)(2,1)S(1)}, bf16[272,128]{1,0:T(8,128)(2,1)S(1)}, u32[]{:S(2)}, u32[]{:S(2)}) collective-permute-start(bf16[272,128]{1,0:T(8,128)(2,1)S(1)} %collective-permute-done.12.refs_8_), channel_id=1, source_target_pairs={{0,4},{4,0},{8,12},{12,8},{1,5},{5,1},{9,13},{13,9},{2,6},{6,2},{1... | collective-permute-start | bytes 208904 | tf_op jit(solution)/shard_map/ppermute | solution.py:378
  54.0 8.0 %collective-permute-start.17 = (bf16[272,128]{1,0:T(8,128)(2,1)S(1)}, bf16[272,128]{1,0:T(8,128)(2,1)S(1)}, u32[]{:S(2)}, u32[]{:S(2)}) collective-permute-start(bf16[272,128]{1,0:T(8,128)(2,1)S(1)} %collective-permute-done.13.refs_9_), channel_id=1, source_target_pairs={{0,4},{4,0},{8,12},{12,8},{1,5},{5,1},{9,13},{13,9},{2,6},{6,2},{1... | collective-permute-start | bytes 208904 | tf_op jit(solution)/shard_map/ppermute | solution.py:378
  54.0 8.0 %collective-permute-start.18 = (bf16[272,128]{1,0:T(8,128)(2,1)S(1)}, bf16[272,128]{1,0:T(8,128)(2,1)S(1)}, u32[]{:S(2)}, u32[]{:S(2)}) collective-permute-start(bf16[272,128]{1,0:T(8,128)(2,1)S(1)} %collective-permute-done.14.refs_10_), channel_id=1, source_target_pairs={{0,4},{4,0},{8,12},{12,8},{1,5},{5,1},{9,13},{13,9},{2,6},{6,2},{1... | collective-permute-start | bytes 208904 | tf_op jit(solution)/shard_map/ppermute | solution.py:378
  54.5 7.5 %collective-permute-start.19 = (bf16[272,128]{1,0:T(8,128)(2,1)S(1)}, bf16[272,128]{1,0:T(8,128)(2,1)S(1)}, u32[]{:S(2)}, u32[]{:S(2)}) collective-permute-start(bf16[272,128]{1,0:T(8,128)(2,1)S(1)} %collective-permute-done.15.refs_11_), channel_id=1, source_target_pairs={{0,4},{4,0},{8,12},{12,8},{1,5},{5,1},{9,13},{13,9},{2,6},{6,2},{1... | collective-permute-start | bytes 208904 | tf_op jit(solution)/shard_map/ppermute | solution.py:378
  62.0 12.8 %copy-start.6 = (bf16[5,256,128]{2,1,0:T(8,128)(2,1)S(1)}, bf16[5,256,128]{2,1,0:T(8,128)(2,1)}, u32[]{:S(2)}) copy-start(bf16[5,256,128]{2,1,0:T(8,128)(2,1)} %refs_11_.1) | copy-start | bytes 983044
  69.1 4.5 %collective-permute-start.21 = (bf16[256,128]{1,0:T(8,128)(2,1)S(1)}, bf16[256,128]{1,0:T(8,128)(2,1)S(1)}, u32[]{:S(2)}, u32[]{:S(2)}) collective-permute-start(bf16[256,128]{1,0:T(8,128)(2,1)S(1)} %shard_map.185.refs_0_), channel_id=1, source_target_pairs={{0,8},{4,12},{8,0},{12,4},{1,9},{5,13},{9,1},{13,5},{2,10},{6,14},... | collective-permute-start | bytes 196616 | tf_op jit(solution)/shard_map/ppermute | solution.py:378
  70.1 3.9 %collective-permute-start.20 = (bf16[256,128]{1,0:T(8,128)(2,1)S(1)}, bf16[256,128]{1,0:T(8,128)(2,1)S(1)}, u32[]{:S(2)}, u32[]{:S(2)}) collective-permute-start(bf16[256,128]{1,0:T(8,128)(2,1)S(1)} %shard_map.185.refs_0_), channel_id=1, source_target_pairs={{0,4},{4,0},{8,12},{12,8},{1,5},{5,1},{9,13},{13,9},{2,6},{6,2},{1... | collective-permute-start | bytes 196616 | tf_op jit(solution)/shard_map/ppermute | solution.py:378
  73.6 1.3 %collective-permute-start.22 = (bf16[256,128]{1,0:T(8,128)(2,1)S(1)}, bf16[256,128]{1,0:T(8,128)(2,1)S(1)}, u32[]{:S(2)}, u32[]{:S(2)}) collective-permute-start(bf16[256,128]{1,0:T(8,128)(2,1)S(1)} %collective-permute-done.21.refs_2_), channel_id=1, source_target_pairs={{0,4},{4,0},{8,12},{12,8},{1,5},{5,1},{9,13},{13,9},{2,6},{6,2},{1... | collective-permute-start | bytes 196616 | tf_op jit(solution)/shard_map/ppermute | solution.py:378
  (16 other events, 38.5 us)
where the time goes:
time: 82.4 us; the launch traced here: 81.7 us
  Pallas kernels  31 us (38%)
  starting transfers between devices  19.8 us (24%)
  waiting for transfers between devices  14.8 us (18%)
  local copies, waits for them, and re-layouts  13.1 us (16%)
  other arithmetic  2.77 us (3%)
    pallas_call x7, Pallas kernels, call(): pl.pallas_call(kernel, out_shape=[jax.ShapeDtypeStruct(shape, dtype) for...  31 us
    unnamed x50, local copies, waits for them, and re-layouts  12.9 us
    ppermute x18, waiting for transfers between devices, over_region(): lax.ppermute(blocks[j], 'region', [(i, i ^ bit) for i in range(count)])  12.3 us
    ppermute x18, starting transfers between devices, over_region(): lax.ppermute(blocks[j], 'region', [(i, i ^ bit) for i in range(count)])  10.6 us
    ppermute x3, starting transfers between devices, over_both(): lax.ppermute(rows, 'sub', [(i, (i + k) % subs) for i in range(subs)])  5.56 us
    ppermute x1, starting transfers between devices, on_device(): from_lower = lax.ppermute(to_higher, 'region', up)  2.36 us
    another operation x4, other arithmetic  2.09 us
  transfers between devices with their start and end apart: 23, of which 8 were waited for; matrix products, arithmetic and copies ran while one was open for 4% of the time, Pallas kernels for 10%

commit v1 on v0

--- a/solution.py
+++ b/solution.py
@@ -12,7 +12,7 @@
 LANES = 128
 F32, BF16, I32 = jnp.float32, jnp.bfloat16, jnp.int32
 TAIL = 16
-LIMIT = 40 * 1024 * 1024
+LIMIT = 32 * 1024 * 1024
 
 
 def dot(a, b):
@@ -67,14 +67,14 @@
 
 
 def message_pass(table, own, senders, receivers, edges, weights, new_edges=None, step=1024):
-    edge_in, edge_out, node_in, node_out = weights
-    first, second = edge_in[...], edge_out[...]
     nodes = table[:own]
     short = -table.shape[0] % LANES
     if short:
         table = jnp.concatenate([table, jnp.zeros((short, LANES), BF16)], axis=0)
+    senders, receivers, edges = senders.get(), receivers.get(), edges.get()
     count = edges.shape[0]
     step = min(step, count)
+    first, second = weights[0].get()[...], weights[1].get()[...]
     summed = jnp.zeros((own, LANES), F32)
     for at in range(0, count, step):
         rows = slice(at // LANES, (at + step) // LANES)
@@ -87,11 +87,7 @@
         if new_edges is not None:
             new_edges[at : at + step, :] = new
         summed = summed + dot(hot_cols(recv, own), new)
-    return node_update(nodes, summed, node_in[...], node_out[...])
-
-
-def block_weights(refs, index):
-    return [ref.at[index] for ref in refs]
+    return node_update(nodes, summed, weights[2].get()[...], weights[3].get()[...])
 
 
 def tail_of(block, count):
@@ -113,25 +109,40 @@
     return out
 
 
-def pick_kernel(nodes, rows, lower, higher):
-    for at, out in ((0, lower), (1, higher)):
-        col = column(rows[at : at + 1, :])
-        out[...] = dot(hot_rows(col, nodes.shape[0]), nodes[...]).astype(BF16)
-
-
-def fine_kernel(nodes, from_lower, from_higher, senders, receivers, edges, tail, *rest):
+def pick_kernel(halo, coarse_halo, fine, coarse, nodes, rows, coarse_rows, dest, target, parent, lower, higher, lists):
+    at = row_layout(fine, coarse)
+    lists[...] = jnp.zeros_like(lists)
+    listed, coarse_listed = rows.get()[...], coarse_rows.get()[...]
+    for side in (0, 1):
+        lists[at["coarse"] : at["coarse"] + 1, side * coarse_halo : (side + 1) * coarse_halo] = coarse_listed[side : side + 1]
+        lanes = slice(side * halo, (side + 1) * halo)
+        lists[at["fine_high"] : at["fine_high"] + 1, lanes] = jnp.right_shift(listed[side : side + 1], 7)
+        lists[at["fine_low"] : at["fine_low"] + 1, lanes] = jnp.bitwise_and(listed[side : side + 1], LANES - 1)
+    lists[at["dest"] : at["target"], :] = dest.get()[...]
+    lists[at["target"] : at["high"], :] = target.get()[...]
+    parents = parent.get()[...]
+    lists[at["high"] : at["low"], :] = jnp.right_shift(parents, 7)
+    lists[at["low"] : at["coarse"], :] = jnp.bitwise_and(parents, LANES - 1)
+    tail = lists[...].astype(F32).astype(BF16)
+    nodes = nodes.get()
+    for side, out in ((0, lower), (1, higher)):
+        col = column(listed[side : side + 1])
+        out[:halo, :] = dot(hot_rows(col, fine), nodes[...]).astype(BF16)
+        out[halo:, :] = tail
+
+
+def fine_kernel(halo, from_lower, from_higher, own, nodes, senders, receivers, edges, *rest):
     *weights, payload, new_edges = rest
-    weights = block_weights(weights, 0)
-    own = nodes.shape[0]
-    table = jnp.concatenate([nodes[...], from_lower[...], from_higher[...]], axis=0)
-    payload[:own, :] = message_pass(table, own, senders, receivers, edges, weights, new_edges)
-    payload[own:, :] = tail[...]
+    nodes = nodes.get()
+    fine = nodes.shape[0]
+    table = jnp.concatenate([nodes[...], from_lower[:halo, :], from_higher[:halo, :]], axis=0)
+    payload[:fine, :] = message_pass(table, fine, senders, receivers, edges, weights, new_edges)
+    payload[fine:, :] = own[halo:, :]
 
 
 def coarse_kernel(regions, halo, coarse, *refs):
-    blocks, (senders, receivers, edges, *rest) = refs[:regions], refs[regions:]
+    blocks, (_, _, senders, receivers, edges, *rest) = refs[:regions], refs[regions:]
     *weights, payload, new_edges = rest
-    weights = block_weights(weights, 1)
     me = lax.axis_index("region")
     fine = blocks[0].shape[0] - TAIL
     at = row_layout(fine, coarse)
@@ -185,20 +196,19 @@
     return latents.astype(BF16), jnp.broadcast_to(found, (size, LANES))
 
 
-def listed_kernel(regions, halo, coarse, wide, size, *refs):
-    blocks, refs = refs[:regions], refs[regions:]
-    senders, receivers, edges, parents, halo_codes, ranks, codes, latents, found, number = refs
+def listed_kernel(regions, halo, fine, coarse, wide, *refs):
+    own, lower, higher, senders, receivers, parents, halo_codes, ranks, codes, number = refs
     me = lax.axis_index("region")
-    fine = blocks[0].shape[0] - TAIL
     at = row_layout(fine, coarse)
-    tails = [tail_of(block, fine) for block in blocks]
+    own_tail, lower_tail, higher_tail = (tail_of(ref, ref.shape[0] - TAIL) for ref in (own, lower, higher))
+    near = ((me - 1, me > 0, lower_tail), (me + 1, me < regions - 1, higher_tail))
     c = coarse // LANES
 
     def own_parents(tail):
         return tail[at["high"] : at["high"] + c] * LANES + tail[at["low"] : at["low"] + c]
 
-    cols = [columns(own_parents(tails[0]))]
-    for side, (other, there, tail) in enumerate(near_tails(tails, me, regions)):
+    cols = [columns(own_parents(own_tail))]
+    for side, (other, there, tail) in enumerate(near):
         first = halo * (1 - side)
         col = columns(tail[at["coarse"] : at["coarse"] + 1])[first : first + halo]
         halo_codes[side * halo : (side + 1) * halo, :] = jnp.where(there, other * coarse + col, -1)
@@ -211,6 +221,7 @@
     cols.append(jnp.full((wide - coarse - 2 * halo, LANES), -1, I32))
     cols = jnp.concatenate(cols, axis=0)
     parents[...] = cols
+    receivers = receivers.get()
     count = receivers.shape[0]
     needed = []
     for i in range(count):
@@ -224,9 +235,12 @@
     before = lax.broadcasted_iota(I32, square, 1) < lax.broadcasted_iota(I32, square, 0)
     rank = dot(hot(before), sums.astype(BF16)) + inside - 1.0
     ranks[...] = jnp.where(needed > 0.0, rank, -1.0).astype(I32)
-    codes[...] = senders[...] * TOP + receivers[...]
+    codes[...] = senders.get()[...] * TOP + receivers[...]
     number[0] = jnp.sum(needed).astype(I32)
-    latents[...], found[...] = compact(0, ranks, codes, edges, size)
+
+
+def compact_kernel(size, ranks, codes, edges, latents, found):
+    latents[...], found[...] = compact(0, ranks, codes, edges.get(), size)
 
 
 def parent_kernel(regions, halo, coarse, *refs):
@@ -292,9 +306,9 @@
 def top_kernel(regions, halo, coarse, size, count, *refs):
     blocks, refs = refs[:count] if count > 1 else refs[0], refs[count:]
     parents, halo_codes, ranks, codes, latents, found, number, all_edges = refs[:8]
-    senders, receivers, edges = refs[8:11]
-    top_weights, weights = block_weights(refs[11:15], 2), block_weights(refs[11:15], 3)
-    out, agg = refs[15:]
+    edges, senders, receivers = Here(refs[8]), *refs[9:11]
+    top_weights, weights = refs[11:15], refs[15:19]
+    out, agg, fallback, semaphore = refs[19:]
     me = lax.axis_index("region")
     subs = lax.axis_size("sub")
     own_sub = lambda j: blocks[j * subs] if count > 1 else blocks.at[j * subs]
@@ -309,7 +323,7 @@
         seen = jnp.max(jnp.where(earlier, 1.0, 0.0), axis=0, keepdims=True)
         firsts.append(jnp.where(seen > 0.0, -2, mine_rows[i : i + 1]))
     firsts = jnp.concatenate(firsts, axis=0)
-    first, second = top_weights[0][...], top_weights[1][...]
+    first, second = top_weights[0].get()[...], top_weights[1].get()[...]
     agg[...] = jnp.zeros_like(agg)
     total = number[0]
 
@@ -326,12 +340,15 @@
     one(0, latents[...], found[...])
 
     def more(b, carry):
-        edge, code = compact(b * size, ranks, codes, all_edges, size)
+        copy = pltpu.make_async_copy(all_edges, fallback, semaphore.at[0])
+        copy.start()
+        copy.wait()
+        edge, code = compact(b * size, ranks, codes, fallback, size)
         one(b * size, edge, code)
         return carry
 
     lax.fori_loop(1, (total + size - 1) // size, more, 0)
-    top_final = node_update(top_own, agg[...], top_weights[2][...], top_weights[3][...])
+    top_final = node_update(top_own, agg[...], top_weights[2].get()[...], top_weights[3].get()[...])
     wanted = halo_codes[...]
     near = jnp.zeros((2 * halo, LANES), F32)
     for j in range(regions):
@@ -344,8 +361,8 @@
 
 def last_kernel(regions, *refs):
     blocks, refs = refs[:regions], refs[regions:]
-    down, parents, senders, receivers, edges, *weights, out = refs
-    weights = block_weights(weights, 4)
+    down, parents, edges, senders, receivers, *weights, out = refs
+    edges = Here(edges)
     me = lax.axis_index("region")
     own, coarse = out.shape[0], blocks[0].shape[0]
     total = down[...].astype(F32)
@@ -356,17 +373,56 @@
     out[...] = message_pass(total.astype(BF16), own, senders, receivers, edges, weights)
 
 
-def call(kernel, args, outs, scratch=(), scalars=(), scalar_outs=()):
-    specs = [pl.BlockSpec(memory_space=pltpu.SMEM if i in scalars else pltpu.VMEM) for i in range(len(args))]
+class Here:
+    def __init__(self, place):
+        self.place = place
+
+    def get(self):
+        return self.place
+
+
+class Arriving(Here):
+    def __init__(self, source, place, semaphore):
+        super().__init__(place)
+        self.copy, self.waiting = pltpu.make_async_copy(source, place, semaphore), True
+        self.copy.start()
+
+    def get(self):
+        if self.waiting:
+            self.copy.wait()
+            self.waiting = False
+        return self.place
+
+
+def call(kernel, args, outs, more=(), scratch=(), raw=(), scalars=(), scalar_outs=(), cost=1, far=False, limit=LIMIT):
+    kinds = {i: pltpu.SMEM for i in scalars} | {i: pltpu.HBM for i in raw}
+    specs = [pl.BlockSpec(memory_space=kinds.get(i, pltpu.VMEM)) for i in range(len(args))]
+    specs += [pl.BlockSpec(memory_space=pltpu.HBM if far else pltpu.VMEM)] * len(more)
     out_specs = [pl.BlockSpec(memory_space=pltpu.SMEM if i in scalar_outs else pltpu.VMEM) for i in range(len(outs))]
+    places = []
+    if far:
+        places = [pltpu.VMEM(array.shape, array.dtype) for array, _ in more]
+        places.append(pltpu.SemaphoreType.DMA((len(more),)))
+    n, k, o = len(args), len(more), len(outs)
+
+    def body(*refs):
+        given, sources, results, rest = refs[:n], refs[n : n + k], refs[n + k : n + k + o], refs[n + k + o :]
+        if far:
+            near, semaphores, rest = rest[:k], rest[k], rest[k + 1 :]
+            operands = [Arriving(source, near[i], semaphores.at[i]) for i, source in enumerate(sources)]
+        else:
+            operands = [Here(ref if at is None else ref.at[at]) for ref, (_, at) in zip(sources, more)]
+        kernel(*given, *operands, *results, *rest)
+
     return pl.pallas_call(
-        kernel,
+        body,
         out_shape=[jax.ShapeDtypeStruct(shape, dtype) for shape, dtype in outs],
         in_specs=specs,
         out_specs=out_specs,
-        scratch_shapes=list(scratch),
-        compiler_params=pltpu.CompilerParams(vmem_limit_bytes=LIMIT),
-    )(*args)
+        scratch_shapes=places + list(scratch),
+        compiler_params=pltpu.CompilerParams(vmem_limit_bytes=limit),
+        cost_estimate=pl.CostEstimate(flops=cost * 10**9, bytes_accessed=cost * 10**5, transcendentals=0),
+    )(*args, *[array for array, _ in more])
 
 
 def over_region(rows):
@@ -425,54 +481,59 @@
     coarse_send, coarse_recv = rows(coarse_senders), rows(coarse_receivers)
     top_send, top_recv = rows(top_senders), rows(top_receivers)
 
+    level = lambda index: [(matrix, index) for matrix in weights]
+    plain = lambda *arrays: [(array, None) for array in arrays]
+
     to_lower, to_higher = call(
-        pick_kernel, [node_feats, halo_rows], [((halo, LANES), BF16)] * 2
+        functools.partial(pick_kernel, halo, halo2, fine, coarse),
+        [],
+        [((halo + TAIL, LANES), BF16)] * 2,
+        plain(node_feats, halo_rows, coarse_halo_rows, rows(pool_dest), rows(pool_target), rows(pool3_target)),
+        scratch=[pltpu.VMEM((TAIL, LANES), I32)],
+        far=True,
+        limit=60 * 1024 * 1024,
     )
     up = [(i, i + 1) for i in range(regions - 1)]
     from_lower = lax.ppermute(to_higher, "region", up)
     from_higher = lax.ppermute(to_lower, "region", [(j, i) for i, j in up])
-
-    parent3, listed = rows(pool3_target), halo_rows.reshape(1, -1)
-    tail = jnp.concatenate(
-        [
-            rows(pool_dest),
-            rows(pool_target),
-            parent3 // LANES,
-            parent3 % LANES,
-            jnp.pad(coarse_halo_rows.reshape(1, -1), ((0, 0), (0, LANES - 2 * halo2))),
-            listed // LANES,
-            listed % LANES,
-        ],
-        axis=0,
-    )
-    tail = jnp.pad(tail, ((0, TAIL - tail.shape[0]), (0, 0))).astype(BF16)
-
     payload, fine_edges2 = call(
-        fine_kernel,
-        [node_feats, from_lower, from_higher, fine_send, fine_recv, fine_edges, tail, *weights],
+        functools.partial(fine_kernel, halo),
+        [from_lower, from_higher, to_lower],
         [((fine + TAIL, LANES), BF16), (fine_edges.shape, BF16)],
+        plain(node_feats, fine_send, fine_recv, fine_edges) + level(0),
+        cost=5,
     )
     blocks = over_region(payload)
-    payload2, coarse_edges2 = call(
-        functools.partial(coarse_kernel, regions, halo2, coarse),
-        blocks + [coarse_send, coarse_recv, coarse_edges, *weights],
-        [((coarse + TAIL, LANES), BF16), (coarse_edges.shape, BF16)],
-    )
     wide = -(-(coarse + 2 * halo2) // LANES) * LANES
-    size = min(512, top_edges.shape[0])
-    parents, halo_codes, ranks, codes, latents, found, number = call(
-        functools.partial(listed_kernel, regions, halo2, coarse, wide, size),
-        blocks + [top_send, top_recv, top_edges],
+    size = min(384, top_edges.shape[0])
+    parents, halo_codes, ranks, codes, number = call(
+        functools.partial(listed_kernel, regions, halo2, fine, coarse, wide),
+        [to_lower, from_lower, from_higher],
         [
             ((wide, LANES), I32),
             ((2 * halo2, LANES), I32),
             (top_send.shape, I32),
             (top_send.shape, I32),
-            ((size, LANES), BF16),
-            ((size, LANES), I32),
             ((1,), I32),
         ],
-        scalar_outs=(6,),
+        plain(top_send, top_recv),
+        scalar_outs=(4,),
+        cost=3,
+    )
+    latents, found = call(
+        functools.partial(compact_kernel, size),
+        [ranks, codes],
+        [((size, LANES), BF16), ((size, LANES), I32)],
+        plain(top_edges),
+        cost=3,
+    )
+    payload2, coarse_edges2 = call(
+        functools.partial(coarse_kernel, regions, halo2, coarse),
+        blocks + [number, found],
+        [((coarse + TAIL, LANES), BF16), (coarse_edges.shape, BF16)],
+        plain(coarse_send, coarse_recv, coarse_edges) + level(1),
+        scalars=(regions,),
+        cost=4,
     )
     fine_table, fine_parents = call(
         functools.partial(parent_kernel, regions, halo, coarse),
@@ -480,19 +541,27 @@
         [((fine + 2 * halo, LANES), BF16), ((fine + 2 * halo, LANES), I32)],
     )
     blocks2 = over_both(payload2)
+    many = len(blocks2)
     (coarse_final,) = call(
-        functools.partial(top_kernel, regions, halo2, coarse, size, len(blocks2)),
-        blocks2
-        + [parents, halo_codes, ranks, codes, latents, found, number, top_edges]
-        + [coarse_send, coarse_recv, coarse_edges2, *weights],
+        functools.partial(top_kernel, regions, halo2, coarse, size, many),
+        blocks2 + [parents, halo_codes, ranks, codes, latents, found, number, top_edges, coarse_edges2],
         [((coarse, LANES), BF16)],
-        scratch=[pltpu.VMEM((wide, LANES), F32)],
-        scalars=(len(blocks2) + 6,),
+        plain(coarse_send, coarse_recv) + level(2) + level(3),
+        scratch=[
+            pltpu.VMEM((wide, LANES), F32),
+            pltpu.VMEM(top_edges.shape, BF16),
+            pltpu.SemaphoreType.DMA((1,)),
+        ],
+        scalars=(many + 6,),
+        raw=(many + 7,),
+        cost=6,
     )
     (fine_final,) = call(
         functools.partial(last_kernel, regions),
-        over_region(coarse_final) + [fine_table, fine_parents, fine_send, fine_recv, fine_edges2, *weights],
+        over_region(coarse_final) + [fine_table, fine_parents, fine_edges2],
         [((fine, LANES), BF16)],
+        plain(fine_send, fine_recv) + level(4),
+        cost=6,
     )
     return fine_final
 

time: 82.4 us -> 70 us (0.85)
  local copies, waits for them, and re-layouts: 13.1 us -> 0.78 us
  waiting for transfers between devices: 14.8 us -> 19.2 us
  other arithmetic: 2.77 us -> 0 us
  starting transfers between devices: 19.8 us -> 17.5 us
  Pallas kernels: 31 us -> 32.1 us
    unnamed x50 -> x32, local copies, waits for them, and re-layouts: 12.9 us -> 0.78 us
    ppermute x3, waiting for transfers between devices: 1.62 us -> 5.77 us  [over_both(): lax.ppermute(rows, 'sub', [(i, (i + k) % subs) for i in range(subs)])]
    ppermute x1, waiting for transfers between devices: 0.89 us -> 4.12 us  [on_device(): from_higher = lax.ppermute(to_lower, 'region', [(j, i) for i, j in up])]
    ppermute x18, waiting for transfers between devices: 12.3 us -> 9.34 us  [over_region(): lax.ppermute(blocks[j], 'region', [(i, i ^ bit) for i in range(count)])]
    another operation x4 -> x0, other arithmetic: 2.09 us -> none
    ppermute x18, starting transfers between devices: 10.6 us -> 9.22 us  [over_region(): lax.ppermute(blocks[j], 'region', [(i, i ^ bit) for i in range(count)])]
    pallas_call x7 -> x8, Pallas kernels: 31 us -> 32.1 us  [call(): pl.pallas_call(body, out_shape=[jax.ShapeDtypeStruct(shape, dtype) for sh...]
    ppermute x3, starting transfers between devices: 5.56 us -> 4.61 us  [over_both(): lax.ppermute(rows, 'sub', [(i, (i + k) % subs) for i in range(subs)])]
  transfers between devices with their start and end apart: 23 -> 23, of which waited for: 8 -> 10; matrix products, arithmetic and copies ran while one was open for 4% -> 0% of each run, Pallas kernels for 10% -> 10%
where the time goes in v1:
time: 70 us; the launch traced here: 69.8 us
  Pallas kernels  32.1 us (46%)
  waiting for transfers between devices  19.2 us (27%)
  starting transfers between devices  17.5 us (25%)
  local copies, waits for them, and re-layouts  0.78 us (1%)
    pallas_call x8, Pallas kernels, call(): pl.pallas_call(body, out_shape=[jax.ShapeDtypeStruct(shape, dtype) for sh...  32.1 us
    ppermute x18, waiting for transfers between devices, over_region(): lax.ppermute(blocks[j], 'region', [(i, i ^ bit) for i in range(count)])  9.34 us
    ppermute x18, starting transfers between devices, over_region(): lax.ppermute(blocks[j], 'region', [(i, i ^ bit) for i in range(count)])  9.22 us
    ppermute x3, waiting for transfers between devices, over_both(): lax.ppermute(rows, 'sub', [(i, (i + k) % subs) for i in range(subs)])  5.77 us
    ppermute x3, starting transfers between devices, over_both(): lax.ppermute(rows, 'sub', [(i, (i + k) % subs) for i in range(subs)])  4.61 us
    ppermute x1, waiting for transfers between devices, on_device(): from_higher = lax.ppermute(to_lower, 'region', [(j, i) for i, j in up])  4.12 us
    ppermute x1, starting transfers between devices, on_device(): from_lower = lax.ppermute(to_higher, 'region', up)  2.37 us
  transfers between devices with their start and end apart: 23, of which 10 were waited for; matrix products, arithmetic and copies ran while one was open for 0% of the time, Pallas kernels for 10%

profile of v1, /device:TPU:0, one launch (start us, length us, event | category | flops | bytes accessed | tf_op | source)
XLA Modules:
  0.0 69.8 jit_solution(783053270317776763)
XLA Ops:
  0.0 1.9 %shard_map.181 = (bf16[80,128]{1,0:T(8,128)(2,1)}, bf16[80,128]{1,0:T(8,128)(2,1)}) custom-call(bf16[512,128]{1,0:T(8,128)(2,1)} %refs_3_.1, s32[2,64]{1,0:T(2,128)} %refs_1_.1, s32[2,32]{1,0:T(2,128)} %refs_2_.2, s32[4,128]{1,0:T(4,128)} %bitcast.19, s32[4,128]{1,0:T(4,128)} %bitcast.20, s32[2,128]{1,0:T(2,128)} %bitcast.21), custom_call_target="tpu_custom_call" | custom-call | flops 1000000000 | bytes 100000 | tf_op jit(solution)/shard_map/pallas_call | solution.py:417
  2.0 2.4 %collective-permute-start = (bf16[80,128]{1,0:T(8,128)(2,1)}, bf16[80,128]{1,0:T(8,128)(2,1)S(1)}, u32[]{:S(2)}, u32[]{:S(2)}) collective-permute-start(bf16[80,128]{1,0:T(8,128)(2,1)} %get-tuple-element.20), channel_id=1, source_target_pairs={{0,4},{4,8},{8,12},{1,5},{5,9},{9,13},{2,6},{6,10},{10,14},{3,7},{... | collective-permute-start | bytes 61448 | tf_op jit(solution)/shard_map/ppermute | solution.py:497
  4.4 1.3 %collective-permute-start.1 = (bf16[80,128]{1,0:T(8,128)(2,1)}, bf16[80,128]{1,0:T(8,128)(2,1)S(1)}, u32[]{:S(2)}, u32[]{:S(2)}) collective-permute-start(bf16[80,128]{1,0:T(8,128)(2,1)} %get-tuple-element.21.refs_2_.refs_0_), channel_id=1, source_target_pairs={{4,0},{8,4},{12,8},{5,1},{9,5},{13,9},{6,2},{10,6},{14,10},{7,3},{... | collective-permute-start | bytes 61448 | tf_op jit(solution)/shard_map/ppermute | solution.py:498
  5.7 4.1 %collective-permute-done.1.refs_1_.refs_2_ = bf16[80,128]{1,0:T(8,128)(2,1)S(1)} collective-permute-done((bf16[80,128]{1,0:T(8,128)(2,1)}, bf16[80,128]{1,0:T(8,128)(2,1)S(1)}, u32[]{:S(2)}, u32[]{:S(2)}) %collective-permute-start.1) | collective-permute-done | bytes 20512 | tf_op jit(solution)/shard_map/ppermute | solution.py:498
  9.9 0.7 %copy-done.10 = bf16[80,128]{1,0:T(8,128)(2,1)S(1)} copy-done((bf16[80,128]{1,0:T(8,128)(2,1)S(1)}, bf16[80,128]{1,0:T(8,128)(2,1)}, u32[]{:S(2)}) %copy-start.10) | copy-done | bytes 20504
  10.6 5.6 %shard_map.182 = (bf16[528,128]{1,0:T(8,128)(2,1)S(1)}, bf16[3072,128]{1,0:T(8,128)(2,1)S(1)}) custom-call(bf16[80,128]{1,0:T(8,128)(2,1)S(1)} %collective-permute-done.refs_0_.refs_1_, bf16[80,128]{1,0:T(8,128)(2,1)S(1)} %collective-permute-done.1.refs_1_.refs_2_, bf16[80,128]{1,0:T(8,128)(2,1)S(1)} %copy-done.10, bf16[512,128]{1,0:T(8,128)(2,1)S(1)} %copy-done.7, ...), custom_call_target="tpu_custom_call" | custom-call | flops 5000000000 | bytes 500000 | tf_op jit(solution)/shard_map/pallas_call | solution.py:417
  16.2 2.5 %collective-permute-start.3 = (bf16[528,128]{1,0:T(8,128)(2,1)S(1)}, bf16[528,128]{1,0:T(8,128)(2,1)S(1)}, u32[]{:S(2)}, u32[]{:S(2)}) collective-permute-start(bf16[528,128]{1,0:T(8,128)(2,1)S(1)} %get-tuple-element.22.refs_0_), channel_id=1, source_target_pairs={{0,8},{4,12},{8,0},{12,4},{1,9},{5,13},{9,1},{13,5},{2,10},{6,14},... | collective-permute-start | bytes 405512 | tf_op jit(solution)/shard_map/ppermute | solution.py:434
  18.7 0.2 collective-permute-start.2
  18.9 2.1 %shard_map.183 = (s32[384,128]{1,0:T(8,128)S(1)}, s32[64,128]{1,0:T(8,128)S(1)}, s32[64,128]{1,0:T(8,128)S(1)}, s32[64,128]{1,0:T(8,128)S(1)}, s32[1]{0:T(128)}) custom-call(bf16[80,128]{1,0:T(8,128)(2,1)S(1)} %copy-done.11, bf16[80,128]{1,0:T(8,128)(2,1)S(1)} %collective-permute-done.refs_0_.refs_1_, ...), custom_call_target="tpu_custom_call" | custom-call | flops 3000000000 | bytes 300000 | tf_op jit(solution)/shard_map/pallas_call | solution.py:417
  21.0 1.1 %collective-permute-done.3.refs_2_ = bf16[528,128]{1,0:T(8,128)(2,1)S(1)} collective-permute-done((bf16[528,128]{1,0:T(8,128)(2,1)S(1)}, bf16[528,128]{1,0:T(8,128)(2,1)S(1)}, u32[]{:S(2)}, u32[]{:S(2)}) %collective-permute-start.3) | collective-permute-done | bytes 135200 | tf_op jit(solution)/shard_map/ppermute | solution.py:434
  22.1 0.9 %collective-permute-start.4 = (bf16[528,128]{1,0:T(8,128)(2,1)S(1)}, bf16[528,128]{1,0:T(8,128)(2,1)S(1)}, u32[]{:S(2)}, u32[]{:S(2)}) collective-permute-start(bf16[528,128]{1,0:T(8,128)(2,1)S(1)} %collective-permute-done.3.refs_2_), channel_id=1, source_target_pairs={{0,4},{4,0},{8,12},{12,8},{1,5},{5,1},{9,13},{13,9},{2,6},{6,2},{1... | collective-permute-start | bytes 405512 | tf_op jit(solution)/shard_map/ppermute | solution.py:434
  23.0 4.6 %shard_map.184 = (bf16[384,128]{1,0:T(8,128)(2,1)S(1)}, s32[384,128]{1,0:T(8,128)S(1)}) custom-call(s32[64,128]{1,0:T(8,128)S(1)} %get-tuple-element.24.refs_0_.refs_18_, s32[64,128]{1,0:T(8,128)S(1)} %get-tuple-element.25.refs_1_.refs_19_, bf16[8192,128]{1,0:T(8,128)(2,1)S(1)} %copy-done), custom_call_target="tpu_custom_call" | custom-call | flops 3000000000 | bytes 300000 | tf_op jit(solution)/shard_map/pallas_call | solution.py:417
  27.6 4.2 %shard_map.185 = (bf16[272,128]{1,0:T(8,128)(2,1)S(1)}, bf16[1536,128]{1,0:T(8,128)(2,1)S(1)}) custom-call(bf16[528,128]{1,0:T(8,128)(2,1)S(1)} %get-tuple-element.22.refs_0_, bf16[528,128]{1,0:T(8,128)(2,1)S(1)} %collective-permute-done.2.refs_1_, bf16[528,128]{1,0:T(8,128)(2,1)S(1)} %collective-permute-done.3.refs_2_, ...), custom_call_target="tpu_custom_call" | custom-call | flops 4000000000 | bytes 400000 | tf_op jit(solution)/shard_map/pallas_call | solution.py:417
  31.8 1.7 %collective-permute-start.12 = (bf16[272,128]{1,0:T(8,128)(2,1)S(1)}, bf16[272,128]{1,0:T(8,128)(2,1)S(1)}, u32[]{:S(2)}, u32[]{:S(2)}) collective-permute-start(bf16[272,128]{1,0:T(8,128)(2,1)S(1)} %get-tuple-element.27.refs_0_), channel_id=1, source_target_pairs={{0,8},{4,12},{8,0},{12,4},{1,9},{5,13},{9,1},{13,5},{2,10},{6,14},... | collective-permute-start | bytes 208904 | tf_op jit(solution)/shard_map/ppermute | solution.py:434
  33.5 3.6 %collective-permute-start.7 = (bf16[272,128]{1,0:T(8,128)(2,1)S(1)}, bf16[272,128]{1,0:T(8,128)(2,1)S(1)}, u32[]{:S(2)}, u32[]{:S(2)}) collective-permute-start(bf16[272,128]{1,0:T(8,128)(2,1)S(1)} %get-tuple-element.27.refs_0_), channel_id=1, source_target_pairs={{0,3},{1,0},{2,1},{3,2},{4,7},{5,4},{6,5},{7,6},{8,11},{9,8},{10,9... | collective-permute-start | bytes 208904 | tf_op jit(solution)/shard_map/ppermute | solution.py:442
  37.1 1.0 %collective-permute-start.5 = (bf16[272,128]{1,0:T(8,128)(2,1)S(1)}, bf16[272,128]{1,0:T(8,128)(2,1)S(1)}, u32[]{:S(2)}, u32[]{:S(2)}) collective-permute-start(bf16[272,128]{1,0:T(8,128)(2,1)S(1)} %get-tuple-element.27.refs_0_), channel_id=1, source_target_pairs={{0,1},{1,2},{2,3},{3,0},{4,5},{5,6},{6,7},{7,4},{8,9},{9,10},{10,1... | collective-permute-start | bytes 208904 | tf_op jit(solution)/shard_map/ppermute | solution.py:442
  38.1 1.6 %collective-permute-done.7.refs_3_ = bf16[272,128]{1,0:T(8,128)(2,1)S(1)} collective-permute-done((bf16[272,128]{1,0:T(8,128)(2,1)S(1)}, bf16[272,128]{1,0:T(8,128)(2,1)S(1)}, u32[]{:S(2)}, u32[]{:S(2)}) %collective-permute-start.7) | collective-permute-done | bytes 69664 | tf_op jit(solution)/shard_map/ppermute | solution.py:442
  39.7 0.4 collective-permute-start.15
  40.1 4.2 %collective-permute-done.6.refs_2_ = bf16[272,128]{1,0:T(8,128)(2,1)S(1)} collective-permute-done((bf16[272,128]{1,0:T(8,128)(2,1)S(1)}, bf16[272,128]{1,0:T(8,128)(2,1)S(1)}, u32[]{:S(2)}, u32[]{:S(2)}) %collective-permute-start.6) | collective-permute-done | bytes 69664 | tf_op jit(solution)/shard_map/ppermute | solution.py:442
  44.3 0.3 collective-permute-start.14
  44.6 1.7 %collective-permute-start.13 = (bf16[272,128]{1,0:T(8,128)(2,1)S(1)}, bf16[272,128]{1,0:T(8,128)(2,1)S(1)}, u32[]{:S(2)}, u32[]{:S(2)}) collective-permute-start(bf16[272,128]{1,0:T(8,128)(2,1)S(1)} %collective-permute-done.5.refs_1_), channel_id=1, source_target_pairs={{0,8},{4,12},{8,0},{12,4},{1,9},{5,13},{9,1},{13,5},{2,10},{6,14},... | collective-permute-start | bytes 208904 | tf_op jit(solution)/shard_map/ppermute | solution.py:434
  46.3 0.5 collective-permute-start.9
  46.9 2.1 %collective-permute-done.14.refs_10_ = bf16[272,128]{1,0:T(8,128)(2,1)S(1)} collective-permute-done((bf16[272,128]{1,0:T(8,128)(2,1)S(1)}, bf16[272,128]{1,0:T(8,128)(2,1)S(1)}, u32[]{:S(2)}, u32[]{:S(2)}) %collective-permute-start.14) | collective-permute-done | bytes 69664 | tf_op jit(solution)/shard_map/ppermute | solution.py:434
  49.0 0.7 %collective-permute-done.13.refs_9_ = bf16[272,128]{1,0:T(8,128)(2,1)S(1)} collective-permute-done((bf16[272,128]{1,0:T(8,128)(2,1)S(1)}, bf16[272,128]{1,0:T(8,128)(2,1)S(1)}, u32[]{:S(2)}, u32[]{:S(2)}) %collective-permute-start.13) | collective-permute-done | bytes 69664 | tf_op jit(solution)/shard_map/ppermute | solution.py:434
  49.7 0.5 collective-permute-done.18.refs_14_
  50.2 0.7 %collective-permute-done.17.refs_13_ = bf16[272,128]{1,0:T(8,128)(2,1)S(1)} collective-permute-done((bf16[272,128]{1,0:T(8,128)(2,1)S(1)}, bf16[272,128]{1,0:T(8,128)(2,1)S(1)}, u32[]{:S(2)}, u32[]{:S(2)}) %collective-permute-start.17) | collective-permute-done | bytes 69664 | tf_op jit(solution)/shard_map/ppermute | solution.py:434
  51.0 6.4 %shard_map.186.refs_0_ = bf16[256,128]{1,0:T(8,128)(2,1)S(1)} custom-call(bf16[272,128]{1,0:T(8,128)(2,1)S(1)} %get-tuple-element.27.refs_0_, bf16[272,128]{1,0:T(8,128)(2,1)S(1)} %collective-permute-done.5.refs_1_, bf16[272,128]{1,0:T(8,128)(2,1)S(1)} %collective-permute-done.6.refs_2_, bf16[272,128]{1,0:T(8,128)(2,1)S(1)} %collective-permute-done.7.refs_3_, ...), custom_call_target="tpu_custom_call" | custom-call | flops 6000000000 | bytes 600000 | tf_op jit(solution)/shard_map/pallas_call | solution.py:417
  57.4 1.0 %collective-permute-start.21 = (bf16[256,128]{1,0:T(8,128)(2,1)S(1)}, bf16[256,128]{1,0:T(8,128)(2,1)S(1)}, u32[]{:S(2)}, u32[]{:S(2)}) collective-permute-start(bf16[256,128]{1,0:T(8,128)(2,1)S(1)} %shard_map.186.refs_0_), channel_id=1, source_target_pairs={{0,8},{4,12},{8,0},{12,4},{1,9},{5,13},{9,1},{13,5},{2,10},{6,14},... | collective-permute-start | bytes 196616 | tf_op jit(solution)/shard_map/ppermute | solution.py:434
  58.3 3.4 %collective-permute-done.21.refs_2_ = bf16[256,128]{1,0:T(8,128)(2,1)S(1)} collective-permute-done((bf16[256,128]{1,0:T(8,128)(2,1)S(1)}, bf16[256,128]{1,0:T(8,128)(2,1)S(1)}, u32[]{:S(2)}, u32[]{:S(2)}) %collective-permute-start.21) | collective-permute-done | bytes 65568 | tf_op jit(solution)/shard_map/ppermute | solution.py:434
  61.7 0.4 shard_map.187
  62.1 0.8 %collective-permute-done.22.refs_3_ = bf16[256,128]{1,0:T(8,128)(2,1)S(1)} collective-permute-done((bf16[256,128]{1,0:T(8,128)(2,1)S(1)}, bf16[256,128]{1,0:T(8,128)(2,1)S(1)}, u32[]{:S(2)}, u32[]{:S(2)}) %collective-permute-start.22) | collective-permute-done | bytes 65568 | tf_op jit(solution)/shard_map/ppermute | solution.py:434
  63.0 6.8 %shard_map.188 = bf16[512,128]{1,0:T(8,128)(2,1)} custom-call(bf16[256,128]{1,0:T(8,128)(2,1)S(1)} %shard_map.186.refs_0_, bf16[256,128]{1,0:T(8,128)(2,1)S(1)} %collective-permute-done.20.refs_1_, bf16[256,128]{1,0:T(8,128)(2,1)S(1)} %collective-permute-done.21.refs_2_, bf16[256,128]{1,0:T(8,128)(2,1)S(1)} %collective-permute-done.22.refs_3_, ...), custom_call_target="tpu_custom_call" | custom-call | flops 6000000000 | bytes 600000 | tf_op jit(solution)/shard_map/pallas_call | solution.py:417
  (54 shorter events, 0.2 us)
Async XLA Ops:
  0.0 9.8 %copy-start.7 = (bf16[512,128]{1,0:T(8,128)(2,1)S(1)}, bf16[512,128]{1,0:T(8,128)(2,1)}, u32[]{:S(2)}) copy-start(bf16[512,128]{1,0:T(8,128)(2,1)} %refs_3_.1) | copy-start | bytes 393220
  0.0 9.8 %copy-start.6 = (bf16[5,128,128]{2,1,0:T(8,128)(2,1)S(1)}, bf16[5,128,128]{2,1,0:T(8,128)(2,1)}, u32[]{:S(2)}) copy-start(bf16[5,128,128]{2,1,0:T(8,128)(2,1)} %refs_12_.3) | copy-start | bytes 491524
  0.0 9.8 %copy-start.4 = (bf16[5,256,128]{2,1,0:T(8,128)(2,1)S(1)}, bf16[5,256,128]{2,1,0:T(8,128)(2,1)}, u32[]{:S(2)}) copy-start(bf16[5,256,128]{2,1,0:T(8,128)(2,1)} %refs_11_.3) | copy-start | bytes 983044
  0.0 9.8 %copy-start.5 = (bf16[5,128,128]{2,1,0:T(8,128)(2,1)S(1)}, bf16[5,128,128]{2,1,0:T(8,128)(2,1)}, u32[]{:S(2)}) copy-start(bf16[5,128,128]{2,1,0:T(8,128)(2,1)} %refs_10_.5) | copy-start | bytes 491524
  0.0 9.8 %copy-start.2 = (bf16[5,384,128]{2,1,0:T(8,128)(2,1)S(1)}, bf16[5,384,128]{2,1,0:T(8,128)(2,1)}, u32[]{:S(2)}) copy-start(bf16[5,384,128]{2,1,0:T(8,128)(2,1)} %refs_9_.5) | copy-start | bytes 1474564
  0.0 9.8 %copy-start.1 = (bf16[3072,128]{1,0:T(8,128)(2,1)S(1)}, bf16[3072,128]{1,0:T(8,128)(2,1)}, u32[]{:S(2)}) copy-start(bf16[3072,128]{1,0:T(8,128)(2,1)} %refs_6_.1) | copy-start | bytes 2359300
  0.0 9.8 %copy-start.13 = (s32[3072]{0:T(1024)S(1)}, s32[3072]{0:T(1024)}, u32[]{:S(2)}) copy-start(s32[3072]{0:T(1024)} %param.21) | copy-start | bytes 36868
  0.0 9.8 %copy-start.12 = (s32[3072]{0:T(1024)S(1)}, s32[3072]{0:T(1024)}, u32[]{:S(2)}) copy-start(s32[3072]{0:T(1024)} %param.20) | copy-start | bytes 36868
  2.0 3.7 %collective-permute-start = (bf16[80,128]{1,0:T(8,128)(2,1)}, bf16[80,128]{1,0:T(8,128)(2,1)S(1)}, u32[]{:S(2)}, u32[]{:S(2)}) collective-permute-start(bf16[80,128]{1,0:T(8,128)(2,1)} %get-tuple-element.20), channel_id=1, source_target_pairs={{0,4},{4,8},{8,12},{1,5},{5,9},{9,13},{2,6},{6,10},{10,14},{3,7},{... | collective-permute-start | bytes 61448 | tf_op jit(solution)/shard_map/ppermute | solution.py:497
  4.4 5.4 %collective-permute-start.1 = (bf16[80,128]{1,0:T(8,128)(2,1)}, bf16[80,128]{1,0:T(8,128)(2,1)S(1)}, u32[]{:S(2)}, u32[]{:S(2)}) collective-permute-start(bf16[80,128]{1,0:T(8,128)(2,1)} %get-tuple-element.21.refs_2_.refs_0_), channel_id=1, source_target_pairs={{4,0},{8,4},{12,8},{5,1},{9,5},{13,9},{6,2},{10,6},{14,10},{7,3},{... | collective-permute-start | bytes 61448 | tf_op jit(solution)/shard_map/ppermute | solution.py:498
  10.6 8.3 %copy-start.11 = (bf16[80,128]{1,0:T(8,128)(2,1)S(1)}, bf16[80,128]{1,0:T(8,128)(2,1)}, u32[]{:S(2)}) copy-start(bf16[80,128]{1,0:T(8,128)(2,1)} %get-tuple-element.21.refs_2_.refs_0_) | copy-start | bytes 61444
  16.2 5.9 %collective-permute-start.3 = (bf16[528,128]{1,0:T(8,128)(2,1)S(1)}, bf16[528,128]{1,0:T(8,128)(2,1)S(1)}, u32[]{:S(2)}, u32[]{:S(2)}) collective-permute-start(bf16[528,128]{1,0:T(8,128)(2,1)S(1)} %get-tuple-element.22.refs_0_), channel_id=1, source_target_pairs={{0,8},{4,12},{8,0},{12,4},{1,9},{5,13},{9,1},{13,5},{2,10},{6,14},... | collective-permute-start | bytes 405512 | tf_op jit(solution)/shard_map/ppermute | solution.py:434
  18.7 8.9 %collective-permute-start.2 = (bf16[528,128]{1,0:T(8,128)(2,1)S(1)}, bf16[528,128]{1,0:T(8,128)(2,1)S(1)}, u32[]{:S(2)}, u32[]{:S(2)}) collective-permute-start(bf16[528,128]{1,0:T(8,128)(2,1)S(1)} %get-tuple-element.22.refs_0_), channel_id=1, source_target_pairs={{0,4},{4,0},{8,12},{12,8},{1,5},{5,1},{9,13},{13,9},{2,6},{6,2},{1... | collective-permute-start | bytes 405512 | tf_op jit(solution)/shard_map/ppermute | solution.py:434
  22.1 5.5 %collective-permute-start.4 = (bf16[528,128]{1,0:T(8,128)(2,1)S(1)}, bf16[528,128]{1,0:T(8,128)(2,1)S(1)}, u32[]{:S(2)}, u32[]{:S(2)}) collective-permute-start(bf16[528,128]{1,0:T(8,128)(2,1)S(1)} %collective-permute-done.3.refs_2_), channel_id=1, source_target_pairs={{0,4},{4,0},{8,12},{12,8},{1,5},{5,1},{9,13},{13,9},{2,6},{6,2},{1... | collective-permute-start | bytes 405512 | tf_op jit(solution)/shard_map/ppermute | solution.py:434
  31.8 6.3 %collective-permute-start.12 = (bf16[272,128]{1,0:T(8,128)(2,1)S(1)}, bf16[272,128]{1,0:T(8,128)(2,1)S(1)}, u32[]{:S(2)}, u32[]{:S(2)}) collective-permute-start(bf16[272,128]{1,0:T(8,128)(2,1)S(1)} %get-tuple-element.27.refs_0_), channel_id=1, source_target_pairs={{0,8},{4,12},{8,0},{12,4},{1,9},{5,13},{9,1},{13,5},{2,10},{6,14},... | collective-permute-start | bytes 208904 | tf_op jit(solution)/shard_map/ppermute | solution.py:434
  33.5 6.2 %collective-permute-start.7 = (bf16[272,128]{1,0:T(8,128)(2,1)S(1)}, bf16[272,128]{1,0:T(8,128)(2,1)S(1)}, u32[]{:S(2)}, u32[]{:S(2)}) collective-permute-start(bf16[272,128]{1,0:T(8,128)(2,1)S(1)} %get-tuple-element.27.refs_0_), channel_id=1, source_target_pairs={{0,3},{1,0},{2,1},{3,2},{4,7},{5,4},{6,5},{7,6},{8,11},{9,8},{10,9... | collective-permute-start | bytes 208904 | tf_op jit(solution)/shard_map/ppermute | solution.py:442
  37.1 3.0 %collective-permute-start.8 = (bf16[272,128]{1,0:T(8,128)(2,1)S(1)}, bf16[272,128]{1,0:T(8,128)(2,1)S(1)}, u32[]{:S(2)}, u32[]{:S(2)}) collective-permute-start(bf16[272,128]{1,0:T(8,128)(2,1)S(1)} %get-tuple-element.27.refs_0_), channel_id=1, source_target_pairs={{0,4},{4,0},{8,12},{12,8},{1,5},{5,1},{9,13},{13,9},{2,6},{6,2},{1... | collective-permute-start | bytes 208904 | tf_op jit(solution)/shard_map/ppermute | solution.py:434
  37.1 7.2 %collective-permute-start.6 = (bf16[272,128]{1,0:T(8,128)(2,1)S(1)}, bf16[272,128]{1,0:T(8,128)(2,1)S(1)}, u32[]{:S(2)}, u32[]{:S(2)}) collective-permute-start(bf16[272,128]{1,0:T(8,128)(2,1)S(1)} %get-tuple-element.27.refs_0_), channel_id=1, source_target_pairs={{0,2},{1,3},{2,0},{3,1},{4,6},{5,7},{6,4},{7,5},{8,10},{9,11},{10,... | collective-permute-start | bytes 208904 | tf_op jit(solution)/shard_map/ppermute | solution.py:442
  37.1 7.5 %collective-permute-start.5 = (bf16[272,128]{1,0:T(8,128)(2,1)S(1)}, bf16[272,128]{1,0:T(8,128)(2,1)S(1)}, u32[]{:S(2)}, u32[]{:S(2)}) collective-permute-start(bf16[272,128]{1,0:T(8,128)(2,1)S(1)} %get-tuple-element.27.refs_0_), channel_id=1, source_target_pairs={{0,1},{1,2},{2,3},{3,0},{4,5},{5,6},{6,7},{7,4},{8,9},{9,10},{10,1... | collective-permute-start | bytes 208904 | tf_op jit(solution)/shard_map/ppermute | solution.py:442
  38.1 8.2 %collective-permute-start.16 = (bf16[272,128]{1,0:T(8,128)(2,1)S(1)}, bf16[272,128]{1,0:T(8,128)(2,1)S(1)}, u32[]{:S(2)}, u32[]{:S(2)}) collective-permute-start(bf16[272,128]{1,0:T(8,128)(2,1)S(1)} %collective-permute-done.12.refs_8_), channel_id=1, source_target_pairs={{0,4},{4,0},{8,12},{12,8},{1,5},{5,1},{9,13},{13,9},{2,6},{6,2},{1... | collective-permute-start | bytes 208904 | tf_op jit(solution)/shard_map/ppermute | solution.py:434
  39.7 6.7 %collective-permute-start.15 = (bf16[272,128]{1,0:T(8,128)(2,1)S(1)}, bf16[272,128]{1,0:T(8,128)(2,1)S(1)}, u32[]{:S(2)}, u32[]{:S(2)}) collective-permute-start(bf16[272,128]{1,0:T(8,128)(2,1)S(1)} %collective-permute-done.7.refs_3_), channel_id=1, source_target_pairs={{0,8},{4,12},{8,0},{12,4},{1,9},{5,13},{9,1},{13,5},{2,10},{6,14},... | collective-permute-start | bytes 208904 | tf_op jit(solution)/shard_map/ppermute | solution.py:434
  40.1 6.8 %collective-permute-start.11 = (bf16[272,128]{1,0:T(8,128)(2,1)S(1)}, bf16[272,128]{1,0:T(8,128)(2,1)S(1)}, u32[]{:S(2)}, u32[]{:S(2)}) collective-permute-start(bf16[272,128]{1,0:T(8,128)(2,1)S(1)} %collective-permute-done.7.refs_3_), channel_id=1, source_target_pairs={{0,4},{4,0},{8,12},{12,8},{1,5},{5,1},{9,13},{13,9},{2,6},{6,2},{1... | collective-permute-start | bytes 208904 | tf_op jit(solution)/shard_map/ppermute | solution.py:434
  44.3 4.7 %collective-permute-start.14 = (bf16[272,128]{1,0:T(8,128)(2,1)S(1)}, bf16[272,128]{1,0:T(8,128)(2,1)S(1)}, u32[]{:S(2)}, u32[]{:S(2)}) collective-permute-start(bf16[272,128]{1,0:T(8,128)(2,1)S(1)} %collective-permute-done.6.refs_2_), channel_id=1, source_target_pairs={{0,8},{4,12},{8,0},{12,4},{1,9},{5,13},{9,1},{13,5},{2,10},{6,14},... | collective-permute-start | bytes 208904 | tf_op jit(solution)/shard_map/ppermute | solution.py:434
  44.6 5.1 %collective-permute-start.13 = (bf16[272,128]{1,0:T(8,128)(2,1)S(1)}, bf16[272,128]{1,0:T(8,128)(2,1)S(1)}, u32[]{:S(2)}, u32[]{:S(2)}) collective-permute-start(bf16[272,128]{1,0:T(8,128)(2,1)S(1)} %collective-permute-done.5.refs_1_), channel_id=1, source_target_pairs={{0,8},{4,12},{8,0},{12,4},{1,9},{5,13},{9,1},{13,5},{2,10},{6,14},... | collective-permute-start | bytes 208904 | tf_op jit(solution)/shard_map/ppermute | solution.py:434
  46.3 3.4 %collective-permute-start.10 = (bf16[272,128]{1,0:T(8,128)(2,1)S(1)}, bf16[272,128]{1,0:T(8,128)(2,1)S(1)}, u32[]{:S(2)}, u32[]{:S(2)}) collective-permute-start(bf16[272,128]{1,0:T(8,128)(2,1)S(1)} %collective-permute-done.6.refs_2_), channel_id=1, source_target_pairs={{0,4},{4,0},{8,12},{12,8},{1,5},{5,1},{9,13},{13,9},{2,6},{6,2},{1... | collective-permute-start | bytes 208904 | tf_op jit(solution)/shard_map/ppermute | solution.py:434
  46.3 3.4 %collective-permute-start.9 = (bf16[272,128]{1,0:T(8,128)(2,1)S(1)}, bf16[272,128]{1,0:T(8,128)(2,1)S(1)}, u32[]{:S(2)}, u32[]{:S(2)}) collective-permute-start(bf16[272,128]{1,0:T(8,128)(2,1)S(1)} %collective-permute-done.5.refs_1_), channel_id=1, source_target_pairs={{0,4},{4,0},{8,12},{12,8},{1,5},{5,1},{9,13},{13,9},{2,6},{6,2},{1... | collective-permute-start | bytes 208904 | tf_op jit(solution)/shard_map/ppermute | solution.py:434
  46.8 2.9 %collective-permute-start.19 = (bf16[272,128]{1,0:T(8,128)(2,1)S(1)}, bf16[272,128]{1,0:T(8,128)(2,1)S(1)}, u32[]{:S(2)}, u32[]{:S(2)}) collective-permute-start(bf16[272,128]{1,0:T(8,128)(2,1)S(1)} %collective-permute-done.15.refs_11_), channel_id=1, source_target_pairs={{0,4},{4,0},{8,12},{12,8},{1,5},{5,1},{9,13},{13,9},{2,6},{6,2},{1... | collective-permute-start | bytes 208904 | tf_op jit(solution)/shard_map/ppermute | solution.py:434
  49.0 1.3 %collective-permute-start.18 = (bf16[272,128]{1,0:T(8,128)(2,1)S(1)}, bf16[272,128]{1,0:T(8,128)(2,1)S(1)}, u32[]{:S(2)}, u32[]{:S(2)}) collective-permute-start(bf16[272,128]{1,0:T(8,128)(2,1)S(1)} %collective-permute-done.14.refs_10_), channel_id=1, source_target_pairs={{0,4},{4,0},{8,12},{12,8},{1,5},{5,1},{9,13},{13,9},{2,6},{6,2},{1... | collective-permute-start | bytes 208904 | tf_op jit(solution)/shard_map/ppermute | solution.py:434
  49.7 1.3 %collective-permute-start.17 = (bf16[272,128]{1,0:T(8,128)(2,1)S(1)}, bf16[272,128]{1,0:T(8,128)(2,1)S(1)}, u32[]{:S(2)}, u32[]{:S(2)}) collective-permute-start(bf16[272,128]{1,0:T(8,128)(2,1)S(1)} %collective-permute-done.13.refs_9_), channel_id=1, source_target_pairs={{0,4},{4,0},{8,12},{12,8},{1,5},{5,1},{9,13},{13,9},{2,6},{6,2},{1... | collective-permute-start | bytes 208904 | tf_op jit(solution)/shard_map/ppermute | solution.py:434
  57.4 4.3 %collective-permute-start.21 = (bf16[256,128]{1,0:T(8,128)(2,1)S(1)}, bf16[256,128]{1,0:T(8,128)(2,1)S(1)}, u32[]{:S(2)}, u32[]{:S(2)}) collective-permute-start(bf16[256,128]{1,0:T(8,128)(2,1)S(1)} %shard_map.186.refs_0_), channel_id=1, source_target_pairs={{0,8},{4,12},{8,0},{12,4},{1,9},{5,13},{9,1},{13,5},{2,10},{6,14},... | collective-permute-start | bytes 196616 | tf_op jit(solution)/shard_map/ppermute | solution.py:434
  58.3 3.8 %collective-permute-start.20 = (bf16[256,128]{1,0:T(8,128)(2,1)S(1)}, bf16[256,128]{1,0:T(8,128)(2,1)S(1)}, u32[]{:S(2)}, u32[]{:S(2)}) collective-permute-start(bf16[256,128]{1,0:T(8,128)(2,1)S(1)} %shard_map.186.refs_0_), channel_id=1, source_target_pairs={{0,4},{4,0},{8,12},{12,8},{1,5},{5,1},{9,13},{13,9},{2,6},{6,2},{1... | collective-permute-start | bytes 196616 | tf_op jit(solution)/shard_map/ppermute | solution.py:434
  61.7 1.3 %collective-permute-start.22 = (bf16[256,128]{1,0:T(8,128)(2,1)S(1)}, bf16[256,128]{1,0:T(8,128)(2,1)S(1)}, u32[]{:S(2)}, u32[]{:S(2)}) collective-permute-start(bf16[256,128]{1,0:T(8,128)(2,1)S(1)} %collective-permute-done.21.refs_2_), channel_id=1, source_target_pairs={{0,4},{4,0},{8,12},{12,8},{1,5},{5,1},{9,13},{13,9},{2,6},{6,2},{1... | collective-permute-start | bytes 196616 | tf_op jit(solution)/shard_map/ppermute | solution.py:434
  (7 other events, 35.3 us)

commit v2 on v1

--- a/solution.py
+++ b/solution.py
@@ -11,6 +11,9 @@
 TOP = 2048
 LANES = 128
 F32, BF16, I32 = jnp.float32, jnp.bfloat16, jnp.int32
+GROUP, SLOTS = 8, 64
+CUT_BITS = 8
+CUT = 1 << CUT_BITS
 TAIL = 16
 LIMIT = 32 * 1024 * 1024
 
@@ -44,6 +47,34 @@
 def hot_cols(rows, count):
     place = lax.broadcasted_iota(I32, (count, LANES), 0)
     return jnp.concatenate([hot(place == rows[i : i + 1]) for i in range(rows.shape[0])], axis=1)
+
+
+def gather(row, block, blocks):
+    wide = dot(hot_rows(row, blocks[0].shape[0]), jnp.concatenate(blocks, axis=1))
+    out = jnp.zeros((row.shape[0], LANES), F32)
+    for i in range(len(blocks)):
+        out = jnp.where(block == i, wide[:, i * LANES : (i + 1) * LANES], out)
+    return out
+
+
+def cut(table):
+    short = -table.shape[0] % CUT
+    if short:
+        table = jnp.concatenate([table, jnp.zeros((short, LANES), BF16)], axis=0)
+    return [table[i : i + CUT] for i in range(0, table.shape[0], CUT)]
+
+
+def gather_cut(col, blocks):
+    return gather(jnp.bitwise_and(col, CUT - 1), jnp.right_shift(col, CUT_BITS), blocks).astype(BF16)
+
+
+def segment_sum(rows, col, values, count):
+    block = jnp.right_shift(col, CUT_BITS)
+    wide = [values]
+    if count > CUT:
+        wide = [jnp.where(block == i, values.astype(F32), 0.0).astype(BF16) for i in range(count // CUT)]
+    out = dot(hot_cols(jnp.bitwise_and(rows, CUT - 1), CUT), jnp.concatenate(wide, axis=1))
+    return jnp.concatenate([out[:, i * LANES : (i + 1) * LANES] for i in range(len(wide))], axis=0)
 
 
 def hot_codes(col, rows):
@@ -66,11 +97,9 @@
     return (nodes.astype(F32) + perceptron(joined, first, second)).astype(BF16)
 
 
-def message_pass(table, own, senders, receivers, edges, weights, new_edges=None, step=1024):
+def message_pass(table, own, senders, receivers, edges, weights, new_edges=None, step=1536):
     nodes = table[:own]
-    short = -table.shape[0] % LANES
-    if short:
-        table = jnp.concatenate([table, jnp.zeros((short, LANES), BF16)], axis=0)
+    all_blocks, own_blocks = cut(table), cut(nodes)
     senders, receivers, edges = senders.get(), receivers.get(), edges.get()
     count = edges.shape[0]
     step = min(step, count)
@@ -78,15 +107,16 @@
     summed = jnp.zeros((own, LANES), F32)
     for at in range(0, count, step):
         rows = slice(at // LANES, (at + step) // LANES)
-        send, recv = senders[rows, :], receivers[rows, :]
-        from_send = dot(hot_rows(columns(send), table.shape[0]), table).astype(BF16)
-        from_recv = dot(hot_rows(columns(recv), own), nodes).astype(BF16)
+        recv = receivers[rows, :]
+        send_col, recv_col = columns(senders[rows, :]), columns(recv)
+        from_send = gather_cut(send_col, all_blocks)
+        from_recv = gather_cut(recv_col, own_blocks)
         edge = edges[at : at + step, :]
         joined = jnp.concatenate([from_send, from_recv, edge], axis=1)
         new = (edge.astype(F32) + perceptron(joined, first, second)).astype(BF16)
         if new_edges is not None:
             new_edges[at : at + step, :] = new
-        summed = summed + dot(hot_cols(recv, own), new)
+        summed = summed + segment_sum(recv, recv_col, new, own)
     return node_update(nodes, summed, weights[2].get()[...], weights[3].get()[...])
 
 
@@ -109,7 +139,7 @@
     return out
 
 
-def pick_kernel(halo, coarse_halo, fine, coarse, nodes, rows, coarse_rows, dest, target, parent, lower, higher, lists):
+def pick_kernel(halo, coarse_halo, fine, coarse, nodes, rows, coarse_rows, dest, target, parent, paired, crossed, lists):
     at = row_layout(fine, coarse)
     lists[...] = jnp.zeros_like(lists)
     listed, coarse_listed = rows.get()[...], coarse_rows.get()[...]
@@ -125,23 +155,30 @@
     lists[at["low"] : at["coarse"], :] = jnp.bitwise_and(parents, LANES - 1)
     tail = lists[...].astype(F32).astype(BF16)
     nodes = nodes.get()
-    for side, out in ((0, lower), (1, higher)):
-        col = column(listed[side : side + 1])
+    odd = jnp.bitwise_and(lax.axis_index("region"), 1)
+    for out, up in ((paired, 1 - odd), (crossed, odd)):
+        col = column(jnp.where(up == 1, listed[1:2], listed[0:1]))
         out[:halo, :] = dot(hot_rows(col, fine), nodes[...]).astype(BF16)
         out[halo:, :] = tail
 
 
-def fine_kernel(halo, from_lower, from_higher, own, nodes, senders, receivers, edges, *rest):
+def lower_higher(paired, crossed):
+    odd = jnp.bitwise_and(lax.axis_index("region"), 1) == 1
+    paired, crossed = paired.astype(F32), crossed.astype(F32)
+    return jnp.where(odd, paired, crossed).astype(BF16), jnp.where(odd, crossed, paired).astype(BF16)
+
+
+def fine_kernel(halo, paired, crossed, own, nodes, senders, receivers, edges, *rest):
     *weights, payload, new_edges = rest
     nodes = nodes.get()
     fine = nodes.shape[0]
-    table = jnp.concatenate([nodes[...], from_lower[:halo, :], from_higher[:halo, :]], axis=0)
+    table = jnp.concatenate([nodes[...], *lower_higher(paired[:halo, :], crossed[:halo, :])], axis=0)
     payload[:fine, :] = message_pass(table, fine, senders, receivers, edges, weights, new_edges)
     payload[fine:, :] = own[halo:, :]
 
 
 def coarse_kernel(regions, halo, coarse, *refs):
-    blocks, (_, _, senders, receivers, edges, *rest) = refs[:regions], refs[regions:]
+    blocks, (senders, receivers, edges, *rest) = refs[:regions], refs[regions:]
     *weights, payload, new_edges = rest
     me = lax.axis_index("region")
     fine = blocks[0].shape[0] - TAIL
@@ -160,11 +197,8 @@
     for block, tail in zip(blocks, tails):
         f = fine // LANES
         parent = tail[at["dest"] : at["dest"] + f] * coarse + tail[at["target"] : at["target"] + f]
-        chosen = hot_codes(codes, parent)
-        total = total + dot(chosen, block[:fine, :])
-        for i in range(f):
-            members = members + chosen[:, i * LANES : (i + 1) * LANES].astype(F32)
-    members = jnp.sum(members, axis=1, keepdims=True)
+        more, counted = sums_and_counts(hot_codes(codes, parent), block[:fine, :])
+        total, members = total + more, members + counted
     table = (total / jnp.maximum(members, 1.0)).astype(BF16)
     payload[:coarse, :] = message_pass(table, coarse, senders, receivers, edges, weights, new_edges)
     own_tail = tails[0]
@@ -196,13 +230,27 @@
     return latents.astype(BF16), jnp.broadcast_to(found, (size, LANES))
 
 
-def listed_kernel(regions, halo, fine, coarse, wide, *refs):
-    own, lower, higher, senders, receivers, parents, halo_codes, ranks, codes, number = refs
+def below(rows, same):
+    square = (rows, rows)
+    return hot(same(lax.broadcasted_iota(I32, square, 0), lax.broadcasted_iota(I32, square, 1)))
+
+
+def running(flags):
+    upto = hot(lax.broadcasted_iota(I32, (LANES, LANES), 0) <= lane_iota(LANES))
+    inside = dot(flags.astype(BF16), upto)
+    return inside, jnp.broadcast_to(inside[:, LANES - 1 :], flags.shape)
+
+
+def listed_kernel(regions, halo, fine, coarse, *refs):
+    own, paired, crossed, senders, receivers, edges, parents, halo_rows, halo_blocks, ranks, codes, latents, found, number = refs
     me = lax.axis_index("region")
     at = row_layout(fine, coarse)
-    own_tail, lower_tail, higher_tail = (tail_of(ref, ref.shape[0] - TAIL) for ref in (own, lower, higher))
+    start = own.shape[0] - TAIL
+    lower, higher = lower_higher(paired[start:, :], crossed[start:, :])
+    own_tail, lower_tail, higher_tail = (tail.astype(F32).astype(I32) for tail in (own[start:, :], lower, higher))
     near = ((me - 1, me > 0, lower_tail), (me + 1, me < regions - 1, higher_tail))
     c = coarse // LANES
+    wide, size = parents.shape[0], latents.shape[0]
 
     def own_parents(tail):
         return tail[at["high"] : at["high"] + c] * LANES + tail[at["low"] : at["low"] + c]
@@ -211,7 +259,8 @@
     for side, (other, there, tail) in enumerate(near):
         first = halo * (1 - side)
         col = columns(tail[at["coarse"] : at["coarse"] + 1])[first : first + halo]
-        halo_codes[side * halo : (side + 1) * halo, :] = jnp.where(there, other * coarse + col, -1)
+        halo_rows[side * halo : (side + 1) * halo, :] = col
+        halo_blocks[side * halo : (side + 1) * halo, :] = jnp.full(col.shape, jnp.where(there, jnp.bitwise_xor(me, other), -1))
         theirs = own_parents(tail).astype(F32)
         value = jnp.zeros((halo, LANES), F32)
         for i in range(c):
@@ -221,30 +270,75 @@
     cols.append(jnp.full((wide - coarse - 2 * halo, LANES), -1, I32))
     cols = jnp.concatenate(cols, axis=0)
     parents[...] = cols
+
+    high_count = TOP // LANES
+    rows = as_rows(cols)
+    tops = dot(
+        hot_cols(jnp.right_shift(rows, 7), high_count), hot_rows(jnp.bitwise_and(cols, LANES - 1), LANES)
+    )
+    tops = jnp.minimum(tops, 1.0).astype(BF16)
     receivers = receivers.get()
     count = receivers.shape[0]
+    high = lax.broadcasted_iota(I32, (high_count, LANES), 0)
     needed = []
-    for i in range(count):
-        match = jnp.where(cols == receivers[i : i + 1, :], 1.0, 0.0)
-        needed.append(jnp.max(match, axis=0, keepdims=True))
+    for i in range(0, count, 8):
+        recv = receivers[i : i + 8, :]
+        match = dot(tops, hot_cols(jnp.bitwise_and(recv, LANES - 1), LANES))
+        for k in range(8):
+            mine = jnp.where(high == jnp.right_shift(recv[k : k + 1], 7), match[:, k * LANES : (k + 1) * LANES], 0.0)
+            needed.append(jnp.sum(mine, axis=0, keepdims=True))
     needed = jnp.concatenate(needed, axis=0)
-    upto = jnp.where(lax.broadcasted_iota(I32, (LANES, LANES), 0) <= lane_iota(LANES), 1.0, 0.0)
-    inside = dot(needed.astype(BF16), upto.astype(BF16))
-    sums = jnp.broadcast_to(inside[:, LANES - 1 :], (count, LANES))
-    square = (count, count)
-    before = lax.broadcasted_iota(I32, square, 1) < lax.broadcasted_iota(I32, square, 0)
-    rank = dot(hot(before), sums.astype(BF16)) + inside - 1.0
-    ranks[...] = jnp.where(needed > 0.0, rank, -1.0).astype(I32)
+
+    group_of = lambda i: jnp.right_shift(i, GROUP.bit_length() - 1)
+    inside, sums = running(needed)
+    sums = sums.astype(BF16)
+    local = dot(below(count, lambda i, j: jnp.logical_and(j < i, group_of(i) == group_of(j))), sums) + inside - 1.0
+    in_group = dot(below(count, lambda i, j: group_of(i) == group_of(j)), sums)
+    used = jnp.minimum(in_group, float(SLOTS))
+    before = dot(below(count, lambda i, j: group_of(j) < group_of(i)), (used / GROUP).astype(BF16))
+    placed = jnp.logical_and(local < SLOTS, local + before < size)
+    others = jnp.where(placed, 0.0, needed)
+    inside, sums = running(others)
+    rank = dot(below(count, lambda i, j: j < i), sums.astype(BF16)) + inside - 1.0
+    ranks[...] = jnp.where(others > 0.0, rank, -1.0).astype(I32)
+    number[1] = jnp.sum(others).astype(I32)
+    number[0] = jnp.sum(needed).astype(I32) - number[1]
     codes[...] = senders.get()[...] * TOP + receivers[...]
-    number[0] = jnp.sum(needed).astype(I32)
-
-
-def compact_kernel(size, ranks, codes, edges, latents, found):
-    latents[...], found[...] = compact(0, ranks, codes, edges.get(), size)
+
+    slot = jnp.where(needed > 0.0, local, -1.0).astype(I32)
+    place = lax.broadcasted_iota(I32, (SLOTS, LANES), 0)
+    edges = edges.get()
+    lane = lane_iota(SLOTS)
+    slots, targets = [], []
+    for first in range(0, count, GROUP):
+        hots, code = [], jnp.zeros((SLOTS, LANES), F32)
+        for i in range(first, first + GROUP):
+            mask = place == slot[i : i + 1]
+            hots.append(hot(mask))
+            code = code + jnp.where(mask, codes[i : i + 1, :].astype(F32), 0.0)
+        code = jnp.broadcast_to(jnp.sum(code, axis=1, keepdims=True), (SLOTS, LANES)).astype(I32)
+        parts = jnp.where(
+            lane == 0,
+            jnp.right_shift(code, 16),
+            jnp.where(lane == 1, jnp.bitwise_and(jnp.right_shift(code, 8), 255), jnp.bitwise_and(code, 255)),
+        )
+        parts = jnp.where(lane < 3, parts, 0).astype(F32).astype(BF16)
+        packed = dot(jnp.concatenate(hots, axis=1), edges[first * LANES : (first + GROUP) * LANES, :]).astype(BF16)
+        slots.append(jnp.concatenate([packed, parts], axis=1))
+        target = before[first : first + 1] + lane_iota(1).astype(F32)
+        targets.append(jnp.where(lane_iota(1).astype(F32) < used[first : first + 1], target, -1.0).astype(I32)[:, :SLOTS])
+    per = LANES // SLOTS
+    targets = [jnp.concatenate(targets[i : i + per], axis=1) for i in range(0, len(targets), per)]
+    packed = dot(hot_cols(jnp.concatenate(targets, axis=0), size), jnp.concatenate(slots, axis=0))
+    latents[...] = packed[:, :LANES].astype(BF16)
+    parts = packed[:, LANES:]
+    lane = lane_iota(size)
+    code = jnp.where(lane == 0, parts * 65536.0, jnp.where(lane == 1, parts * 256.0, parts))
+    found[...] = jnp.broadcast_to(jnp.sum(code, axis=1, keepdims=True), (size, LANES)).astype(I32)
 
 
 def parent_kernel(regions, halo, coarse, *refs):
-    blocks, (table, parents) = refs[:regions], refs[regions:]
+    blocks, (table, parent_rows, parent_blocks) = refs[:regions], refs[regions:]
     me = lax.axis_index("region")
     fine = blocks[0].shape[0] - TAIL
     at = row_layout(fine, coarse)
@@ -255,7 +349,9 @@
         return tail[at["dest"] : at["dest"] + f] * coarse + tail[at["target"] : at["target"] + f]
 
     table[:fine, :] = blocks[0][:fine, :]
-    parents[:fine, :] = columns(own_parents(tails[0]))
+    owner = lambda tail: tail[at["dest"] : at["dest"] + f]
+    parent_rows[:fine, :] = columns(tails[0][at["target"] : at["target"] + f])
+    parent_blocks[:fine, :] = jnp.bitwise_xor(columns(owner(tails[0])), me)
     for side, (other, there, tail) in enumerate(near_tails(tails, me, regions)):
         rows = slice(fine + side * halo, fine + (side + 1) * halo)
         first = halo * (1 - side)
@@ -266,7 +362,9 @@
         for i in range(f):
             value = value + jnp.where(col == lane_iota(halo, i * LANES), theirs[i : i + 1], 0.0)
         value = jnp.broadcast_to(jnp.sum(value, axis=1, keepdims=True), (halo, LANES)).astype(I32)
-        parents[rows, :] = jnp.where(there, value, -1)
+        parent_rows[rows, :] = jnp.bitwise_and(value, coarse - 1)
+        block = jnp.bitwise_xor(jnp.right_shift(value, coarse.bit_length() - 1), me)
+        parent_blocks[rows, :] = jnp.where(there, block, -1)
         total = jnp.zeros((halo, LANES), F32)
         for j, block in enumerate(blocks):
             here = jnp.logical_and(there, jnp.bitwise_xor(me, j) == other)
@@ -274,17 +372,18 @@
         table[rows, :] = total.astype(BF16)
 
 
+def sums_and_counts(chosen, rows):
+    both = dot(chosen, jnp.concatenate([rows, jnp.ones(rows.shape, BF16)], axis=1))
+    return both[:, :LANES], both[:, LANES:]
+
+
 def pooled(col, blocks, coarse):
     c = coarse // LANES
 
     def add(block, sums):
-        total, members = sums
         tail = tail_of(block, coarse)
-        chosen = hot_codes(col, tail[:c] * LANES + tail[c : 2 * c])
-        total = total + dot(chosen, block[:coarse, :])
-        for i in range(c):
-            members = members + chosen[:, i * LANES : (i + 1) * LANES].astype(F32)
-        return total, members
+        total, members = sums_and_counts(hot_codes(col, tail[:c] * LANES + tail[c : 2 * c]), block[:coarse, :])
+        return sums[0] + total, sums[1] + members
 
     sums = (jnp.zeros((col.shape[0], LANES), F32),) * 2
     if isinstance(blocks, tuple):
@@ -293,7 +392,6 @@
     else:
         sums = lax.fori_loop(0, blocks.shape[0], lambda n, sums: add(blocks.at[n], sums), sums)
     total, members = sums
-    members = jnp.sum(members, axis=1, keepdims=True)
     return (total / jnp.maximum(members, 1.0)).astype(BF16)
 
 
@@ -304,13 +402,19 @@
 
 
 def top_kernel(regions, halo, coarse, size, count, *refs):
-    blocks, refs = refs[:count] if count > 1 else refs[0], refs[count:]
-    parents, halo_codes, ranks, codes, latents, found, number, all_edges = refs[:8]
-    edges, senders, receivers = Here(refs[8]), *refs[9:11]
-    top_weights, weights = refs[11:15], refs[15:19]
-    out, agg, fallback, semaphore = refs[19:]
+    subs = lax.axis_size("sub")
+    if count > 1:
+        rows = coarse + TAIL
+        there = [refs[count - 1].at[i * rows : (i + 1) * rows] for i in range(count - 1)]
+        blocks = tuple((there if j % 2 else refs)[j // 2 * subs + k] for j in range(regions) for k in range(subs))
+    else:
+        blocks = refs[0]
+    refs = refs[count:]
+    parents, halo_rows, halo_blocks, ranks, codes, latents, found, number, all_edges, edges = refs[:10]
+    senders, receivers = refs[10:12]
+    top_weights, weights = refs[12:16], refs[16:20]
+    out, agg, fallback, semaphore = refs[20:]
     me = lax.axis_index("region")
-    subs = lax.axis_size("sub")
     own_sub = lambda j: blocks[j * subs] if count > 1 else blocks.at[j * subs]
     wide = parents.shape[0]
     mine = parents[...]
@@ -325,10 +429,9 @@
     firsts = jnp.concatenate(firsts, axis=0)
     first, second = top_weights[0].get()[...], top_weights[1].get()[...]
     agg[...] = jnp.zeros_like(agg)
-    total = number[0]
-
-    def one(at, edge, code):
-        place = lax.broadcasted_iota(I32, (size, LANES), 0) + at
+
+    def one(edge, code, first_place, total):
+        place = lax.broadcasted_iota(I32, (size, LANES), 0) + first_place
         send = jnp.right_shift(code, TOP.bit_length() - 1)
         recv = jnp.where(place < total, jnp.bitwise_and(code, TOP - 1), -3)
         from_send = pooled(send, blocks, coarse)
@@ -337,40 +440,30 @@
         new = (edge.astype(F32) + perceptron(joined, first, second)).astype(BF16)
         agg[...] += dot(hot_codes(mine, as_rows(recv)), new)
 
-    one(0, latents[...], found[...])
+    one(latents[...], found[...], 0, number[0])
 
     def more(b, carry):
         copy = pltpu.make_async_copy(all_edges, fallback, semaphore.at[0])
         copy.start()
         copy.wait()
         edge, code = compact(b * size, ranks, codes, fallback, size)
-        one(b * size, edge, code)
+        one(edge, code, b * size, number[1])
         return carry
 
-    lax.fori_loop(1, (total + size - 1) // size, more, 0)
+    lax.fori_loop(0, (number[1] + size - 1) // size, more, 0)
     top_final = node_update(top_own, agg[...], top_weights[2].get()[...], top_weights[3].get()[...])
-    wanted = halo_codes[...]
-    near = jnp.zeros((2 * halo, LANES), F32)
-    for j in range(regions):
-        col = wanted - jnp.bitwise_xor(me, j) * coarse
-        near = near + dot(hot_rows(col, coarse), own_sub(j)[:coarse, :])
+    near = gather(halo_rows[...], halo_blocks[...], [own_sub(j)[:coarse, :] for j in range(regions)])
     down = jnp.concatenate([own_sub(0)[:coarse, :].astype(F32), near], axis=0)
     table = (down + top_final[: coarse + 2 * halo].astype(F32)).astype(BF16)
-    out[...] = message_pass(table, coarse, senders, receivers, edges, weights)
+    out[...] = message_pass(table, coarse, senders, receivers, Here(edges), weights)
 
 
 def last_kernel(regions, *refs):
     blocks, refs = refs[:regions], refs[regions:]
-    down, parents, edges, senders, receivers, *weights, out = refs
-    edges = Here(edges)
-    me = lax.axis_index("region")
-    own, coarse = out.shape[0], blocks[0].shape[0]
-    total = down[...].astype(F32)
-    wanted = parents[...]
-    for j, block in enumerate(blocks):
-        col = wanted - jnp.bitwise_xor(me, j) * coarse
-        total = total + dot(hot_rows(col, coarse), block[...])
-    out[...] = message_pass(total.astype(BF16), own, senders, receivers, edges, weights)
+    down, parent_rows, parent_blocks, edges, senders, receivers, *weights, out = refs
+    parent = gather(parent_rows[...], parent_blocks[...], [block[...] for block in blocks])
+    table = (down[...].astype(F32) + parent).astype(BF16)
+    out[...] = message_pass(table, out.shape[0], senders, receivers, Here(edges), weights)
 
 
 class Here:
@@ -425,29 +518,39 @@
     )(*args, *[array for array, _ in more])
 
 
-def over_region(rows):
+def over_region(rows, beside=None):
     count = lax.axis_size("region")
     blocks = {0: rows}
     bit = count // 2
     while bit:
-        for j in list(blocks):
-            blocks[j + bit] = lax.ppermute(blocks[j], "region", [(i, i ^ bit) for i in range(count)])
+        going = dict(blocks)
+        if beside is not None and len(going) > 1:
+            far = max(going)
+            going[far], beside = lax.optimization_barrier((going[far], beside))
+        for j in blocks:
+            going[j + bit] = lax.ppermute(going[j], "region", [(i, i ^ bit) for i in range(count)])
+        blocks = going
         bit //= 2
-    return [blocks[j] for j in range(count)]
+    blocks = [blocks[j] for j in range(count)]
+    return blocks if beside is None else (blocks, beside)
 
 
 def over_both(rows):
     regions, subs = lax.axis_size("region"), lax.axis_size("sub")
-    turns = [rows] + [
-        lax.ppermute(rows, "sub", [(i, (i + k) % subs) for i in range(subs)]) for k in range(1, subs)
-    ]
+    swap = lambda array, axis, bits: lax.ppermute(array, axis, [(i, i ^ bits) for i in range(lax.axis_size(axis))])
+    turns = [rows] + [swap(rows, "sub", k) for k in range(1, subs)]
     if regions * subs <= 16:
-        spread = [over_region(turn) for turn in turns]
-        return [spread[k][j] for j in range(regions) for k in range(subs)]
+        blocks = {0: turns}
+        bit = regions // 2
+        while bit > 1:
+            for j in list(blocks):
+                blocks[j + bit] = [swap(block, "region", bit) for block in blocks[j]]
+            bit //= 2
+        here = [block for j in range(0, regions, 2) for block in blocks[j]]
+        return here + [swap(jnp.concatenate(here), "region", 1)]
     blocks, bit = jnp.stack(turns), 1
     while bit < regions:
-        there = lax.ppermute(blocks, "region", [(i, i ^ bit) for i in range(regions)])
-        blocks, bit = jnp.concatenate([blocks, there]), 2 * bit
+        blocks, bit = jnp.concatenate([blocks, swap(blocks, "region", bit)]), 2 * bit
     return [blocks]
 
 
@@ -484,7 +587,7 @@
     level = lambda index: [(matrix, index) for matrix in weights]
     plain = lambda *arrays: [(array, None) for array in arrays]
 
-    to_lower, to_higher = call(
+    to_pair, to_other = call(
         functools.partial(pick_kernel, halo, halo2, fine, coarse),
         [],
         [((halo + TAIL, LANES), BF16)] * 2,
@@ -493,58 +596,54 @@
         far=True,
         limit=60 * 1024 * 1024,
     )
-    up = [(i, i + 1) for i in range(regions - 1)]
-    from_lower = lax.ppermute(to_higher, "region", up)
-    from_higher = lax.ppermute(to_lower, "region", [(j, i) for i, j in up])
+    pairs = lambda first: [(i, j) for low in range(first, regions - 1, 2) for i, j in ((low, low + 1), (low + 1, low))]
+    paired = lax.ppermute(to_pair, "region", pairs(0))
+    crossed = lax.ppermute(to_other, "region", pairs(1))
     payload, fine_edges2 = call(
         functools.partial(fine_kernel, halo),
-        [from_lower, from_higher, to_lower],
+        [paired, crossed, to_pair],
         [((fine + TAIL, LANES), BF16), (fine_edges.shape, BF16)],
         plain(node_feats, fine_send, fine_recv, fine_edges) + level(0),
         cost=5,
     )
-    blocks = over_region(payload)
     wide = -(-(coarse + 2 * halo2) // LANES) * LANES
     size = min(384, top_edges.shape[0])
-    parents, halo_codes, ranks, codes, number = call(
-        functools.partial(listed_kernel, regions, halo2, fine, coarse, wide),
-        [to_lower, from_lower, from_higher],
+    selected = call(
+        functools.partial(listed_kernel, regions, halo2, fine, coarse),
+        [to_pair, paired, crossed],
         [
             ((wide, LANES), I32),
             ((2 * halo2, LANES), I32),
+            ((2 * halo2, LANES), I32),
             (top_send.shape, I32),
             (top_send.shape, I32),
-            ((1,), I32),
+            ((size, LANES), BF16),
+            ((size, LANES), I32),
+            ((2,), I32),
         ],
-        plain(top_send, top_recv),
-        scalar_outs=(4,),
+        plain(top_send, top_recv, top_edges),
+        scalar_outs=(7,),
         cost=3,
     )
-    latents, found = call(
-        functools.partial(compact_kernel, size),
-        [ranks, codes],
-        [((size, LANES), BF16), ((size, LANES), I32)],
-        plain(top_edges),
-        cost=3,
-    )
+    blocks, selected = over_region(payload, selected)
     payload2, coarse_edges2 = call(
         functools.partial(coarse_kernel, regions, halo2, coarse),
-        blocks + [number, found],
+        blocks,
         [((coarse + TAIL, LANES), BF16), (coarse_edges.shape, BF16)],
         plain(coarse_send, coarse_recv, coarse_edges) + level(1),
-        scalars=(regions,),
         cost=4,
     )
-    fine_table, fine_parents = call(
+    table_shape = (fine + 2 * halo, LANES)
+    fine_table, parent_rows, parent_blocks = call(
         functools.partial(parent_kernel, regions, halo, coarse),
         blocks,
-        [((fine + 2 * halo, LANES), BF16), ((fine + 2 * halo, LANES), I32)],
+        [(table_shape, BF16), (table_shape, I32), (table_shape, I32)],
     )
     blocks2 = over_both(payload2)
     many = len(blocks2)
     (coarse_final,) = call(
         functools.partial(top_kernel, regions, halo2, coarse, size, many),
-        blocks2 + [parents, halo_codes, ranks, codes, latents, found, number, top_edges, coarse_edges2],
+        blocks2 + [*selected, top_edges, coarse_edges2],
         [((coarse, LANES), BF16)],
         plain(coarse_send, coarse_recv) + level(2) + level(3),
         scratch=[
@@ -552,13 +651,13 @@
             pltpu.VMEM(top_edges.shape, BF16),
             pltpu.SemaphoreType.DMA((1,)),
         ],
-        scalars=(many + 6,),
-        raw=(many + 7,),
+        scalars=(many + 7,),
+        raw=(many + 8,),
         cost=6,
     )
     (fine_final,) = call(
         functools.partial(last_kernel, regions),
-        over_region(coarse_final) + [fine_table, fine_parents, fine_edges2],
+        over_region(coarse_final) + [fine_table, parent_rows, parent_blocks, fine_edges2],
         [((fine, LANES), BF16)],
         plain(fine_send, fine_recv) + level(4),
         cost=6,

time: 70 us -> 58.3 us (0.83)
  Pallas kernels: 32.1 us -> 23.6 us
  waiting for transfers between devices: 19.2 us -> 15.4 us
    pallas_call x8 -> x7, Pallas kernels: 32.1 us -> 23.6 us  [call(): pl.pallas_call(body, out_shape=[jax.ShapeDtypeStruct(shape, dtype) for sh...]
    ppermute x23 -> x16, waiting for transfers between devices: 19.2 us -> 15.4 us  [the longest x8 8.54 us: over_both(): lax.ppermute(array, axis, [(i, i ^ bits) for i in range(lax.axis_size(axi...]
    ppermute x23 -> x16, starting transfers between devices: 17.5 us -> 17.9 us  [the longest x8 8.65 us: over_both(): lax.ppermute(array, axis, [(i, i ^ bits) for i in range(lax.axis_size(axi...]
  transfers between devices with their start and end apart: 23 -> 16, of which waited for: 10 -> 10; matrix products, arithmetic and copies ran while one was open for 0% -> 0% of each run, Pallas kernels for 10% -> 5%
where the time goes in v2:
time: 58.3 us; the launch traced here: 58.1 us
  Pallas kernels  23.6 us (40%)
  starting transfers between devices  17.9 us (31%)
  waiting for transfers between devices  15.4 us (26%)
  local copies, waits for them, and re-layouts  0.88 us (2%)
    pallas_call x7, Pallas kernels, call(): pl.pallas_call(body, out_shape=[jax.ShapeDtypeStruct(shape, dtype) for sh...  23.6 us
    ppermute x8, starting transfers between devices, over_both(): lax.ppermute(array, axis, [(i, i ^ bits) for i in range(lax.axis_size(axi...  8.65 us
    ppermute x8, waiting for transfers between devices, over_both(): lax.ppermute(array, axis, [(i, i ^ bits) for i in range(lax.axis_size(axi...  8.54 us
    ppermute x6, starting transfers between devices, over_region(): lax.ppermute(going[j], 'region', [(i, i ^ bit) for i in range(count)])  8.04 us
    ppermute x6, waiting for transfers between devices, over_region(): lax.ppermute(going[j], 'region', [(i, i ^ bit) for i in range(count)])  6.48 us
  transfers between devices with their start and end apart: 16, of which 10 were waited for; matrix products, arithmetic and copies ran while one was open for 0% of the time, Pallas kernels for 5%

profile of v2, /device:TPU:0, one launch (start us, length us, event | category | flops | bytes accessed | tf_op | source)
XLA Modules:
  0.0 58.1 jit_solution(823239339189909349)
XLA Ops:
  0.0 1.9 %shard_map.181 = (bf16[80,128]{1,0:T(8,128)(2,1)}, bf16[80,128]{1,0:T(8,128)(2,1)}) custom-call(bf16[512,128]{1,0:T(8,128)(2,1)} %refs_3_.1, s32[2,64]{1,0:T(2,128)} %refs_1_.1, s32[2,32]{1,0:T(2,128)} %refs_2_.1, s32[4,128]{1,0:T(4,128)} %bitcast.19, s32[4,128]{1,0:T(4,128)} %bitcast.20, s32[2,128]{1,0:T(2,128)} %bitcast.21), custom_call_target="tpu_custom_call" | custom-call | flops 1000000000 | bytes 100000 | tf_op jit(solution)/shard_map/pallas_call | solution.py:510
  2.0 0.5 collective-permute-start
  2.5 0.7 %collective-permute-start.1 = (bf16[80,128]{1,0:T(8,128)(2,1)}, bf16[80,128]{1,0:T(8,128)(2,1)S(1)}, u32[]{:S(2)}, u32[]{:S(2)}) collective-permute-start(bf16[80,128]{1,0:T(8,128)(2,1)} %get-tuple-element.32), channel_id=1, source_target_pairs={{4,8},{8,4},{5,9},{9,5},{6,10},{10,6},{7,11},{11,7},{20,24},{24,20... | collective-permute-start | bytes 61448 | tf_op jit(solution)/shard_map/ppermute | solution.py:601
  3.2 0.4 collective-permute-done.refs_0_.refs_1_
  3.6 0.0 copy-start.10
  3.7 0.7 %copy-done.10 = bf16[80,128]{1,0:T(8,128)(2,1)S(1)} copy-done((bf16[80,128]{1,0:T(8,128)(2,1)S(1)}, bf16[80,128]{1,0:T(8,128)(2,1)}, u32[]{:S(2)}) %copy-start.10) | copy-done | bytes 20504
  4.4 4.2 %shard_map.182 = (bf16[528,128]{1,0:T(8,128)(2,1)S(1)}, bf16[3072,128]{1,0:T(8,128)(2,1)S(1)}) custom-call(bf16[80,128]{1,0:T(8,128)(2,1)S(1)} %collective-permute-done.refs_0_.refs_1_, bf16[80,128]{1,0:T(8,128)(2,1)S(1)} %collective-permute-done.1.refs_1_.refs_2_, bf16[80,128]{1,0:T(8,128)(2,1)S(1)} %copy-done.10, bf16[512,128]{1,0:T(8,128)(2,1)S(1)} %copy-done.7, ...), custom_call_target="tpu_custom_call" | custom-call | flops 5000000000 | bytes 500000 | tf_op jit(solution)/shard_map/pallas_call | solution.py:510
  8.6 6.8 %collective-permute-start.3 = (bf16[528,128]{1,0:T(8,128)(2,1)S(1)}, bf16[528,128]{1,0:T(8,128)(2,1)S(1)}, u32[]{:S(2)}, u32[]{:S(2)}) collective-permute-start(bf16[528,128]{1,0:T(8,128)(2,1)S(1)} %get-tuple-element.33.refs_0_), channel_id=1, source_target_pairs={{0,8},{4,12},{8,0},{12,4},{1,9},{5,13},{9,1},{13,5},{2,10},{6,14},... | collective-permute-start | bytes 405512 | tf_op jit(solution)/shard_map/ppermute | solution.py:531
  15.5 0.0 copy-start.3
  15.5 0.0 copy-start.13
  15.5 2.6 %shard_map.183 = (s32[384,128]{1,0:T(8,128)S(1)}, s32[64,128]{1,0:T(8,128)S(1)}, s32[64,128]{1,0:T(8,128)S(1)}, s32[64,128]{1,0:T(8,128)S(1)}, s32[64,128]{1,0:T...) custom-call(bf16[80,128]{1,0:T(8,128)(2,1)S(1)} %copy-done.10, ...), custom_call_target="tpu_custom_call" | custom-call | flops 3000000000 | bytes 300000 | tf_op jit(solution)/shard_map/pallas_call | solution.py:510
  18.2 1.2 %collective-permute-done.3.refs_2_ = bf16[528,128]{1,0:T(8,128)(2,1)S(1)} collective-permute-done((bf16[528,128]{1,0:T(8,128)(2,1)S(1)}, bf16[528,128]{1,0:T(8,128)(2,1)S(1)}, u32[]{:S(2)}, u32[]{:S(2)}) %collective-permute-start.3) | collective-permute-done | bytes 135200 | tf_op jit(solution)/shard_map/ppermute | solution.py:531
  19.3 1.3 %collective-permute-done.4.refs_3_ = bf16[528,128]{1,0:T(8,128)(2,1)S(1)} collective-permute-done((bf16[528,128]{1,0:T(8,128)(2,1)S(1)}, bf16[528,128]{1,0:T(8,128)(2,1)S(1)}, u32[]{:S(2)}, u32[]{:S(2)}) %collective-permute-start.4) | collective-permute-done | bytes 135200 | tf_op jit(solution)/shard_map/ppermute | solution.py:531
  20.7 3.2 %shard_map.184 = (bf16[272,128]{1,0:T(8,128)(2,1)S(1)}, bf16[1536,128]{1,0:T(8,128)(2,1)S(1)}) custom-call(bf16[528,128]{1,0:T(8,128)(2,1)S(1)} %get-tuple-element.33.refs_0_, bf16[528,128]{1,0:T(8,128)(2,1)S(1)} %collective-permute-done.2.refs_1_, bf16[528,128]{1,0:T(8,128)(2,1)S(1)} %collective-permute-done.3.refs_2_, ...), custom_call_target="tpu_custom_call" | custom-call | flops 4000000000 | bytes 400000 | tf_op jit(solution)/shard_map/pallas_call | solution.py:510
  23.9 2.2 %collective-permute-start.5 = (bf16[272,128]{1,0:T(8,128)(2,1)S(1)}, bf16[272,128]{1,0:T(8,128)(2,1)S(1)}, u32[]{:S(2)}, u32[]{:S(2)}) collective-permute-start(bf16[272,128]{1,0:T(8,128)(2,1)S(1)} %get-tuple-element.43.refs_0_), channel_id=1, source_target_pairs={{0,1},{1,0},{2,3},{3,2},{4,5},{5,4},{6,7},{7,6},{8,9},{9,8},{10,11... | collective-permute-start | bytes 208904 | tf_op jit(solution)/shard_map/ppermute | solution.py:540
  26.1 2.6 %collective-permute-start.6 = (bf16[272,128]{1,0:T(8,128)(2,1)S(1)}, bf16[272,128]{1,0:T(8,128)(2,1)S(1)}, u32[]{:S(2)}, u32[]{:S(2)}) collective-permute-start(bf16[272,128]{1,0:T(8,128)(2,1)S(1)} %get-tuple-element.43.refs_0_), channel_id=1, source_target_pairs={{0,2},{1,3},{2,0},{3,1},{4,6},{5,7},{6,4},{7,5},{8,10},{9,11},{10,... | collective-permute-start | bytes 208904 | tf_op jit(solution)/shard_map/ppermute | solution.py:540
  28.7 0.8 %collective-permute-start.8 = (bf16[272,128]{1,0:T(8,128)(2,1)S(1)}, bf16[272,128]{1,0:T(8,128)(2,1)S(1)}, u32[]{:S(2)}, u32[]{:S(2)}) collective-permute-start(bf16[272,128]{1,0:T(8,128)(2,1)S(1)} %get-tuple-element.43.refs_0_), channel_id=1, source_target_pairs={{0,8},{4,12},{8,0},{12,4},{1,9},{5,13},{9,1},{13,5},{2,10},{6,14},... | collective-permute-start | bytes 208904 | tf_op jit(solution)/shard_map/ppermute | solution.py:540
  29.5 1.3 %collective-permute-start.9 = (bf16[272,128]{1,0:T(8,128)(2,1)S(1)}, bf16[272,128]{1,0:T(8,128)(2,1)S(1)}, u32[]{:S(2)}, u32[]{:S(2)}) collective-permute-start(bf16[272,128]{1,0:T(8,128)(2,1)S(1)} %collective-permute-done.5.refs_1_), channel_id=1, source_target_pairs={{0,8},{4,12},{8,0},{12,4},{1,9},{5,13},{9,1},{13,5},{2,10},{6,14},... | collective-permute-start | bytes 208904 | tf_op jit(solution)/shard_map/ppermute | solution.py:540
  30.8 3.1 %collective-permute-done.6.refs_2_ = bf16[272,128]{1,0:T(8,128)(2,1)S(1)} collective-permute-done((bf16[272,128]{1,0:T(8,128)(2,1)S(1)}, bf16[272,128]{1,0:T(8,128)(2,1)S(1)}, u32[]{:S(2)}, u32[]{:S(2)}) %collective-permute-start.6) | collective-permute-done | bytes 69664 | tf_op jit(solution)/shard_map/ppermute | solution.py:540
  33.9 0.6 %collective-permute-start.10 = (bf16[272,128]{1,0:T(8,128)(2,1)S(1)}, bf16[272,128]{1,0:T(8,128)(2,1)S(1)}, u32[]{:S(2)}, u32[]{:S(2)}) collective-permute-start(bf16[272,128]{1,0:T(8,128)(2,1)S(1)} %collective-permute-done.6.refs_2_), channel_id=1, source_target_pairs={{0,8},{4,12},{8,0},{12,4},{1,9},{5,13},{9,1},{13,5},{2,10},{6,14},... | collective-permute-start | bytes 208904 | tf_op jit(solution)/shard_map/ppermute | solution.py:540
  34.5 0.4 collective-permute-done.7.refs_3_
  34.9 1.1 %collective-permute-start.11 = (bf16[272,128]{1,0:T(8,128)(2,1)S(1)}, bf16[272,128]{1,0:T(8,128)(2,1)S(1)}, u32[]{:S(2)}, u32[]{:S(2)}) collective-permute-start(bf16[272,128]{1,0:T(8,128)(2,1)S(1)} %collective-permute-done.7.refs_3_), channel_id=1, source_target_pairs={{0,8},{4,12},{8,0},{12,4},{1,9},{5,13},{9,1},{13,5},{2,10},{6,14},... | collective-permute-start | bytes 208904 | tf_op jit(solution)/shard_map/ppermute | solution.py:540
  36.1 2.1 %collective-permute-done.10.refs_6_ = bf16[272,128]{1,0:T(8,128)(2,1)S(1)} collective-permute-done((bf16[272,128]{1,0:T(8,128)(2,1)S(1)}, bf16[272,128]{1,0:T(8,128)(2,1)S(1)}, u32[]{:S(2)}, u32[]{:S(2)}) %collective-permute-start.10) | collective-permute-done | bytes 69664 | tf_op jit(solution)/shard_map/ppermute | solution.py:540
  38.2 1.0 %collective-permute-done.11.refs_7_ = bf16[272,128]{1,0:T(8,128)(2,1)S(1)} collective-permute-done((bf16[272,128]{1,0:T(8,128)(2,1)S(1)}, bf16[272,128]{1,0:T(8,128)(2,1)S(1)}, u32[]{:S(2)}, u32[]{:S(2)}) %collective-permute-start.11) | collective-permute-done | bytes 69664 | tf_op jit(solution)/shard_map/ppermute | solution.py:540
  39.2 0.1 collective-permute-start.12
  39.3 1.9 %collective-permute-done.12.refs_8_ = bf16[2176,128]{1,0:T(8,128)(2,1)S(1)} collective-permute-done((bf16[2176,128]{1,0:T(8,128)(2,1)S(1)}, bf16[2176,128]{1,0:T(8,128)(2,1)S(1)}, u32[]{:S(2)}, u32[]{:S(2)}) %collective-permute-start.12) | collective-permute-done | bytes 557088 | tf_op jit(solution)/shard_map/ppermute | solution.py:540
  41.3 6.0 %shard_map.185.refs_0_ = bf16[256,128]{1,0:T(8,128)(2,1)S(1)} custom-call(bf16[272,128]{1,0:T(8,128)(2,1)S(1)} %get-tuple-element.43.refs_0_, bf16[272,128]{1,0:T(8,128)(2,1)S(1)} %collective-permute-done.5.refs_1_, bf16[272,128]{1,0:T(8,128)(2,1)S(1)} %collective-permute-done.6.refs_2_, bf16[272,128]{1,0:T(8,128)(2,1)S(1)} %collective-permute-done.7.refs_3_, ...), custom_call_target="tpu_custom_call" | custom-call | flops 6000000000 | bytes 600000 | tf_op jit(solution)/shard_map/pallas_call | solution.py:510
  47.3 1.2 %collective-permute-start.14 = (bf16[256,128]{1,0:T(8,128)(2,1)S(1)}, bf16[256,128]{1,0:T(8,128)(2,1)S(1)}, u32[]{:S(2)}, u32[]{:S(2)}) collective-permute-start(bf16[256,128]{1,0:T(8,128)(2,1)S(1)} %shard_map.185.refs_0_), channel_id=1, source_target_pairs={{0,8},{4,12},{8,0},{12,4},{1,9},{5,13},{9,1},{13,5},{2,10},{6,14},... | collective-permute-start | bytes 196616 | tf_op jit(solution)/shard_map/ppermute | solution.py:531
  48.4 3.1 %collective-permute-done.14.refs_2_ = bf16[256,128]{1,0:T(8,128)(2,1)S(1)} collective-permute-done((bf16[256,128]{1,0:T(8,128)(2,1)S(1)}, bf16[256,128]{1,0:T(8,128)(2,1)S(1)}, u32[]{:S(2)}, u32[]{:S(2)}) %collective-permute-start.14) | collective-permute-done | bytes 65568 | tf_op jit(solution)/shard_map/ppermute | solution.py:531
  51.6 0.4 shard_map.186
  52.0 0.8 %collective-permute-done.15.refs_3_ = bf16[256,128]{1,0:T(8,128)(2,1)S(1)} collective-permute-done((bf16[256,128]{1,0:T(8,128)(2,1)S(1)}, bf16[256,128]{1,0:T(8,128)(2,1)S(1)}, u32[]{:S(2)}, u32[]{:S(2)}) %collective-permute-start.15) | collective-permute-done | bytes 65568 | tf_op jit(solution)/shard_map/ppermute | solution.py:531
  52.8 5.2 %shard_map.187 = bf16[512,128]{1,0:T(8,128)(2,1)} custom-call(bf16[256,128]{1,0:T(8,128)(2,1)S(1)} %shard_map.185.refs_0_, bf16[256,128]{1,0:T(8,128)(2,1)S(1)} %collective-permute-done.13.refs_1_, bf16[256,128]{1,0:T(8,128)(2,1)S(1)} %collective-permute-done.14.refs_2_, bf16[256,128]{1,0:T(8,128)(2,1)S(1)} %collective-permute-done.15.refs_3_, ...), custom_call_target="tpu_custom_call" | custom-call | flops 6000000000 | bytes 600000 | tf_op jit(solution)/shard_map/pallas_call | solution.py:510
  (45 shorter events, 0.2 us)
Async XLA Ops:
  0.0 3.6 %copy-start.7 = (bf16[512,128]{1,0:T(8,128)(2,1)S(1)}, bf16[512,128]{1,0:T(8,128)(2,1)}, u32[]{:S(2)}) copy-start(bf16[512,128]{1,0:T(8,128)(2,1)} %refs_3_.1) | copy-start | bytes 393220
  0.0 3.6 %copy-start.11 = (s32[3072]{0:T(1024)S(1)}, s32[3072]{0:T(1024)}, u32[]{:S(2)}) copy-start(s32[3072]{0:T(1024)} %param.20) | copy-start | bytes 36868
  0.0 3.6 %copy-start.12 = (s32[3072]{0:T(1024)S(1)}, s32[3072]{0:T(1024)}, u32[]{:S(2)}) copy-start(s32[3072]{0:T(1024)} %param.21) | copy-start | bytes 36868
  0.0 3.6 %copy-start.1 = (bf16[3072,128]{1,0:T(8,128)(2,1)S(1)}, bf16[3072,128]{1,0:T(8,128)(2,1)}, u32[]{:S(2)}) copy-start(bf16[3072,128]{1,0:T(8,128)(2,1)} %refs_6_.2) | copy-start | bytes 2359300
  0.0 3.6 %copy-start.2 = (bf16[5,384,128]{2,1,0:T(8,128)(2,1)S(1)}, bf16[5,384,128]{2,1,0:T(8,128)(2,1)}, u32[]{:S(2)}) copy-start(bf16[5,384,128]{2,1,0:T(8,128)(2,1)} %refs_10_.5) | copy-start | bytes 1474564
  0.0 3.6 %copy-start.5 = (bf16[5,128,128]{2,1,0:T(8,128)(2,1)S(1)}, bf16[5,128,128]{2,1,0:T(8,128)(2,1)}, u32[]{:S(2)}) copy-start(bf16[5,128,128]{2,1,0:T(8,128)(2,1)} %refs_11_.1) | copy-start | bytes 491524
  0.0 3.6 %copy-start.4 = (bf16[5,256,128]{2,1,0:T(8,128)(2,1)S(1)}, bf16[5,256,128]{2,1,0:T(8,128)(2,1)}, u32[]{:S(2)}) copy-start(bf16[5,256,128]{2,1,0:T(8,128)(2,1)} %refs_12_.1) | copy-start | bytes 983044
  0.0 3.6 %copy-start.6 = (bf16[5,128,128]{2,1,0:T(8,128)(2,1)S(1)}, bf16[5,128,128]{2,1,0:T(8,128)(2,1)}, u32[]{:S(2)}) copy-start(bf16[5,128,128]{2,1,0:T(8,128)(2,1)} %refs_13_.1) | copy-start | bytes 491524
  2.0 1.6 %collective-permute-start = (bf16[80,128]{1,0:T(8,128)(2,1)}, bf16[80,128]{1,0:T(8,128)(2,1)S(1)}, u32[]{:S(2)}, u32[]{:S(2)}) collective-permute-start(bf16[80,128]{1,0:T(8,128)(2,1)} %get-tuple-element.31.refs_2_.refs_0_), channel_id=1, source_target_pairs={{0,4},{4,0},{8,12},{12,8},{1,5},{5,1},{9,13},{13,9},{2,6},{6,2},{1... | collective-permute-start | bytes 61448 | tf_op jit(solution)/shard_map/ppermute | solution.py:600
  2.5 1.1 %collective-permute-start.1 = (bf16[80,128]{1,0:T(8,128)(2,1)}, bf16[80,128]{1,0:T(8,128)(2,1)S(1)}, u32[]{:S(2)}, u32[]{:S(2)}) collective-permute-start(bf16[80,128]{1,0:T(8,128)(2,1)} %get-tuple-element.32), channel_id=1, source_target_pairs={{4,8},{8,4},{5,9},{9,5},{6,10},{10,6},{7,11},{11,7},{20,24},{24,20... | collective-permute-start | bytes 61448 | tf_op jit(solution)/shard_map/ppermute | solution.py:601
  3.6 0.7 %copy-start.10 = (bf16[80,128]{1,0:T(8,128)(2,1)S(1)}, bf16[80,128]{1,0:T(8,128)(2,1)}, u32[]{:S(2)}) copy-start(bf16[80,128]{1,0:T(8,128)(2,1)} %get-tuple-element.31.refs_2_.refs_0_) | copy-start | bytes 61444
  4.4 11.1 %copy-start = (bf16[8192,128]{1,0:T(8,128)(2,1)S(1)}, bf16[8192,128]{1,0:T(8,128)(2,1)}, u32[]{:S(2)}) copy-start(bf16[8192,128]{1,0:T(8,128)(2,1)} %refs_17_.1) | copy-start | bytes 6291460
  4.4 11.1 %copy-start.8 = (s32[8192]{0:T(1024)S(1)}, s32[8192]{0:T(1024)}, u32[]{:S(2)}) copy-start(s32[8192]{0:T(1024)} %param.31) | copy-start | bytes 98308
  4.4 11.1 %copy-start.9 = (s32[8192]{0:T(1024)S(1)}, s32[8192]{0:T(1024)}, u32[]{:S(2)}) copy-start(s32[8192]{0:T(1024)} %param.32) | copy-start | bytes 98308
  8.6 10.7 %collective-permute-start.3 = (bf16[528,128]{1,0:T(8,128)(2,1)S(1)}, bf16[528,128]{1,0:T(8,128)(2,1)S(1)}, u32[]{:S(2)}, u32[]{:S(2)}) collective-permute-start(bf16[528,128]{1,0:T(8,128)(2,1)S(1)} %get-tuple-element.33.refs_0_), channel_id=1, source_target_pairs={{0,8},{4,12},{8,0},{12,4},{1,9},{5,13},{9,1},{13,5},{2,10},{6,14},... | collective-permute-start | bytes 405512 | tf_op jit(solution)/shard_map/ppermute | solution.py:531
  15.4 3.9 %collective-permute-start.2 = (bf16[528,128]{1,0:T(8,128)(2,1)S(1)}, bf16[528,128]{1,0:T(8,128)(2,1)S(1)}, u32[]{:S(2)}, u32[]{:S(2)}) collective-permute-start(bf16[528,128]{1,0:T(8,128)(2,1)S(1)} %get-tuple-element.33.refs_0_), channel_id=1, source_target_pairs={{0,4},{4,0},{8,12},{12,8},{1,5},{5,1},{9,13},{13,9},{2,6},{6,2},{1... | collective-permute-start | bytes 405512 | tf_op jit(solution)/shard_map/ppermute | solution.py:531
  15.5 5.2 %copy-start.3 = (bf16[1536,128]{1,0:T(8,128)(2,1)S(1)}, bf16[1536,128]{1,0:T(8,128)(2,1)}, u32[]{:S(2)}) copy-start(bf16[1536,128]{1,0:T(8,128)(2,1)} %refs_6_.3) | copy-start | bytes 1179652
  15.5 5.2 %copy-start.13 = (s32[1536]{0:T(1024)S(1)}, s32[1536]{0:T(1024)}, u32[]{:S(2)}) copy-start(s32[1536]{0:T(1024)} %param.24) | copy-start | bytes 18436
  15.5 5.2 %copy-start.14 = (s32[1536]{0:T(1024)S(1)}, s32[1536]{0:T(1024)}, u32[]{:S(2)}) copy-start(s32[1536]{0:T(1024)} %param.25) | copy-start | bytes 18436
  19.3 1.4 %collective-permute-start.4 = (bf16[528,128]{1,0:T(8,128)(2,1)S(1)}, bf16[528,128]{1,0:T(8,128)(2,1)S(1)}, u32[]{:S(2)}, u32[]{:S(2)}) collective-permute-start(bf16[528,128]{1,0:T(8,128)(2,1)S(1)} %collective-permute-done.3.refs_2_), channel_id=1, source_target_pairs={{0,4},{4,0},{8,12},{12,8},{1,5},{5,1},{9,13},{13,9},{2,6},{6,2},{1... | collective-permute-start | bytes 405512 | tf_op jit(solution)/shard_map/ppermute | solution.py:531
  23.9 5.6 %collective-permute-start.5 = (bf16[272,128]{1,0:T(8,128)(2,1)S(1)}, bf16[272,128]{1,0:T(8,128)(2,1)S(1)}, u32[]{:S(2)}, u32[]{:S(2)}) collective-permute-start(bf16[272,128]{1,0:T(8,128)(2,1)S(1)} %get-tuple-element.43.refs_0_), channel_id=1, source_target_pairs={{0,1},{1,0},{2,3},{3,2},{4,5},{5,4},{6,7},{7,6},{8,9},{9,8},{10,11... | collective-permute-start | bytes 208904 | tf_op jit(solution)/shard_map/ppermute | solution.py:540
  26.1 7.8 %collective-permute-start.6 = (bf16[272,128]{1,0:T(8,128)(2,1)S(1)}, bf16[272,128]{1,0:T(8,128)(2,1)S(1)}, u32[]{:S(2)}, u32[]{:S(2)}) collective-permute-start(bf16[272,128]{1,0:T(8,128)(2,1)S(1)} %get-tuple-element.43.refs_0_), channel_id=1, source_target_pairs={{0,2},{1,3},{2,0},{3,1},{4,6},{5,7},{6,4},{7,5},{8,10},{9,11},{10,... | collective-permute-start | bytes 208904 | tf_op jit(solution)/shard_map/ppermute | solution.py:540
  28.7 6.2 %collective-permute-start.7 = (bf16[272,128]{1,0:T(8,128)(2,1)S(1)}, bf16[272,128]{1,0:T(8,128)(2,1)S(1)}, u32[]{:S(2)}, u32[]{:S(2)}) collective-permute-start(bf16[272,128]{1,0:T(8,128)(2,1)S(1)} %get-tuple-element.43.refs_0_), channel_id=1, source_target_pairs={{0,3},{1,2},{2,1},{3,0},{4,7},{5,6},{6,5},{7,4},{8,11},{9,10},{10,... | collective-permute-start | bytes 208904 | tf_op jit(solution)/shard_map/ppermute | solution.py:540
  28.7 7.3 %collective-permute-start.8 = (bf16[272,128]{1,0:T(8,128)(2,1)S(1)}, bf16[272,128]{1,0:T(8,128)(2,1)S(1)}, u32[]{:S(2)}, u32[]{:S(2)}) collective-permute-start(bf16[272,128]{1,0:T(8,128)(2,1)S(1)} %get-tuple-element.43.refs_0_), channel_id=1, source_target_pairs={{0,8},{4,12},{8,0},{12,4},{1,9},{5,13},{9,1},{13,5},{2,10},{6,14},... | collective-permute-start | bytes 208904 | tf_op jit(solution)/shard_map/ppermute | solution.py:540
  29.5 6.6 %collective-permute-start.9 = (bf16[272,128]{1,0:T(8,128)(2,1)S(1)}, bf16[272,128]{1,0:T(8,128)(2,1)S(1)}, u32[]{:S(2)}, u32[]{:S(2)}) collective-permute-start(bf16[272,128]{1,0:T(8,128)(2,1)S(1)} %collective-permute-done.5.refs_1_), channel_id=1, source_target_pairs={{0,8},{4,12},{8,0},{12,4},{1,9},{5,13},{9,1},{13,5},{2,10},{6,14},... | collective-permute-start | bytes 208904 | tf_op jit(solution)/shard_map/ppermute | solution.py:540
  33.9 4.3 %collective-permute-start.10 = (bf16[272,128]{1,0:T(8,128)(2,1)S(1)}, bf16[272,128]{1,0:T(8,128)(2,1)S(1)}, u32[]{:S(2)}, u32[]{:S(2)}) collective-permute-start(bf16[272,128]{1,0:T(8,128)(2,1)S(1)} %collective-permute-done.6.refs_2_), channel_id=1, source_target_pairs={{0,8},{4,12},{8,0},{12,4},{1,9},{5,13},{9,1},{13,5},{2,10},{6,14},... | collective-permute-start | bytes 208904 | tf_op jit(solution)/shard_map/ppermute | solution.py:540
  34.9 4.3 %collective-permute-start.11 = (bf16[272,128]{1,0:T(8,128)(2,1)S(1)}, bf16[272,128]{1,0:T(8,128)(2,1)S(1)}, u32[]{:S(2)}, u32[]{:S(2)}) collective-permute-start(bf16[272,128]{1,0:T(8,128)(2,1)S(1)} %collective-permute-done.7.refs_3_), channel_id=1, source_target_pairs={{0,8},{4,12},{8,0},{12,4},{1,9},{5,13},{9,1},{13,5},{2,10},{6,14},... | collective-permute-start | bytes 208904 | tf_op jit(solution)/shard_map/ppermute | solution.py:540
  39.2 2.0 %collective-permute-start.12 = (bf16[2176,128]{1,0:T(8,128)(2,1)S(1)}, bf16[2176,128]{1,0:T(8,128)(2,1)S(1)}, u32[]{:S(2)}, u32[]{:S(2)}) collective-permute-start(bf16[2176,128]{1,0:T(8,128)(2,1)S(1)} %constant_dynamic-update-slice_fusion), channel_id=1, source_target_pairs={{0,4},{4,0},{8,12},{12,8},{1,5},{5,1},{9,13},{13,9},{2,6},{6,2},{1... | collective-permute-start | bytes 1671176 | tf_op jit(solution)/shard_map/ppermute | solution.py:540
  47.3 4.3 %collective-permute-start.14 = (bf16[256,128]{1,0:T(8,128)(2,1)S(1)}, bf16[256,128]{1,0:T(8,128)(2,1)S(1)}, u32[]{:S(2)}, u32[]{:S(2)}) collective-permute-start(bf16[256,128]{1,0:T(8,128)(2,1)S(1)} %shard_map.185.refs_0_), channel_id=1, source_target_pairs={{0,8},{4,12},{8,0},{12,4},{1,9},{5,13},{9,1},{13,5},{2,10},{6,14},... | collective-permute-start | bytes 196616 | tf_op jit(solution)/shard_map/ppermute | solution.py:531
  48.4 3.6 %collective-permute-start.13 = (bf16[256,128]{1,0:T(8,128)(2,1)S(1)}, bf16[256,128]{1,0:T(8,128)(2,1)S(1)}, u32[]{:S(2)}, u32[]{:S(2)}) collective-permute-start(bf16[256,128]{1,0:T(8,128)(2,1)S(1)} %shard_map.185.refs_0_), channel_id=1, source_target_pairs={{0,4},{4,0},{8,12},{12,8},{1,5},{5,1},{9,13},{13,9},{2,6},{6,2},{1... | collective-permute-start | bytes 196616 | tf_op jit(solution)/shard_map/ppermute | solution.py:531
  51.6 1.3 %collective-permute-start.15 = (bf16[256,128]{1,0:T(8,128)(2,1)S(1)}, bf16[256,128]{1,0:T(8,128)(2,1)S(1)}, u32[]{:S(2)}, u32[]{:S(2)}) collective-permute-start(bf16[256,128]{1,0:T(8,128)(2,1)S(1)} %collective-permute-done.14.refs_2_), channel_id=1, source_target_pairs={{0,4},{4,0},{8,12},{12,8},{1,5},{5,1},{9,13},{13,9},{2,6},{6,2},{1... | collective-permute-start | bytes 196616 | tf_op jit(solution)/shard_map/ppermute | solution.py:531

commit v3 on v2

--- a/solution.py
+++ b/solution.py
@@ -10,8 +10,9 @@
 EPSILON = 1e-05
 TOP = 2048
 LANES = 128
-F32, BF16, I32 = jnp.float32, jnp.bfloat16, jnp.int32
+F32, BF16, I32, I16 = jnp.float32, jnp.bfloat16, jnp.int32, jnp.int16
 GROUP, SLOTS = 8, 64
+STEP = 3072
 CUT_BITS = 8
 CUT = 1 << CUT_BITS
 TAIL = 16
@@ -35,24 +36,34 @@
 
 
 def hot(mask):
-    return jnp.where(mask, 1.0, 0.0).astype(BF16)
-
-
-def hot_rows(col, count):
-    return jnp.concatenate(
-        [hot(col == lane_iota(col.shape[0], first)) for first in range(0, count, LANES)], axis=1
-    )
+    return jnp.where(mask, jnp.ones(mask.shape, BF16), jnp.zeros(mask.shape, BF16))
+
+
+def short(row, count):
+    return jnp.concatenate([jnp.broadcast_to(row, (16, LANES)).astype(I16)] * (count // 16), axis=0)
+
+
+def hot_rows(col, count, start=0):
+    col = col.astype(I16)
+    places = [lane_iota(16, first) for first in range(start, start + count, LANES)]
+    return jnp.concatenate([hot(col == short(place[:1], col.shape[0])) for place in places], axis=1)
 
 
 def hot_cols(rows, count):
-    place = lax.broadcasted_iota(I32, (count, LANES), 0)
-    return jnp.concatenate([hot(place == rows[i : i + 1]) for i in range(rows.shape[0])], axis=1)
-
-
-def gather(row, block, blocks):
+    return hot_codes(lax.broadcasted_iota(I32, (count, LANES), 0), rows)
+
+
+def hot_codes(col, rows):
+    col = col.astype(I16)
+    return jnp.concatenate([hot(col == short(rows[i : i + 1], col.shape[0])) for i in range(rows.shape[0])], axis=1)
+
+
+def gather(row, block, blocks, all_there=False):
     wide = dot(hot_rows(row, blocks[0].shape[0]), jnp.concatenate(blocks, axis=1))
-    out = jnp.zeros((row.shape[0], LANES), F32)
-    for i in range(len(blocks)):
+    if block is None:
+        return wide
+    out = wide[:, :LANES] if all_there else jnp.zeros((row.shape[0], LANES), F32)
+    for i in range(1 if all_there else 0, len(blocks)):
         out = jnp.where(block == i, wide[:, i * LANES : (i + 1) * LANES], out)
     return out
 
@@ -64,59 +75,86 @@
     return [table[i : i + CUT] for i in range(0, table.shape[0], CUT)]
 
 
-def gather_cut(col, blocks):
-    return gather(jnp.bitwise_and(col, CUT - 1), jnp.right_shift(col, CUT_BITS), blocks).astype(BF16)
-
-
-def segment_sum(rows, col, values, count):
-    block = jnp.right_shift(col, CUT_BITS)
-    wide = [values]
-    if count > CUT:
-        wide = [jnp.where(block == i, values.astype(F32), 0.0).astype(BF16) for i in range(count // CUT)]
-    out = dot(hot_cols(jnp.bitwise_and(rows, CUT - 1), CUT), jnp.concatenate(wide, axis=1))
-    return jnp.concatenate([out[:, i * LANES : (i + 1) * LANES] for i in range(len(wide))], axis=0)
-
-
-def hot_codes(col, rows):
-    return jnp.concatenate([hot(col == rows[i : i + 1]) for i in range(rows.shape[0])], axis=1)
-
-
-def normalize(values):
-    centred = values - jnp.mean(values, axis=-1, keepdims=True)
-    variance = jnp.mean(centred * centred, axis=-1, keepdims=True)
-    return centred * lax.rsqrt(variance + EPSILON)
-
-
-def perceptron(features, first, second):
-    hidden = jnp.maximum(dot(features, first), 0.0).astype(BF16)
-    return normalize(dot(hidden, second))
+def segment_sum(rows, block, values):
+    chosen = hot_cols(jnp.bitwise_and(rows, CUT - 1), CUT)
+    if block is None:
+        return dot(chosen, values)
+    upper = values * jnp.where(block == 1, 1.0, 0.0).astype(BF16)
+    out = dot(chosen, jnp.concatenate([values - upper, upper], axis=1))
+    return jnp.concatenate([out[:, :LANES], out[:, LANES:]], axis=0)
+
+
+def centre(second):
+    exact = second.astype(F32)
+    return (exact - jnp.mean(exact, axis=1, keepdims=True)).astype(BF16)
+
+
+def perceptron(before, centred_second):
+    out = dot(jnp.maximum(before, 0.0).astype(BF16), centred_second)
+    return out * lax.rsqrt(jnp.mean(out * out, axis=-1, keepdims=True) + EPSILON)
 
 
 def node_update(nodes, summed, first, second):
     joined = jnp.concatenate([nodes, summed.astype(BF16)], axis=1)
-    return (nodes.astype(F32) + perceptron(joined, first, second)).astype(BF16)
-
-
-def message_pass(table, own, senders, receivers, edges, weights, new_edges=None, step=1536):
-    nodes = table[:own]
-    all_blocks, own_blocks = cut(table), cut(nodes)
-    senders, receivers, edges = senders.get(), receivers.get(), edges.get()
-    count = edges.shape[0]
-    step = min(step, count)
-    first, second = weights[0].get()[...], weights[1].get()[...]
-    summed = jnp.zeros((own, LANES), F32)
-    for at in range(0, count, step):
-        rows = slice(at // LANES, (at + step) // LANES)
-        recv = receivers[rows, :]
-        send_col, recv_col = columns(senders[rows, :]), columns(recv)
-        from_send = gather_cut(send_col, all_blocks)
-        from_recv = gather_cut(recv_col, own_blocks)
-        edge = edges[at : at + step, :]
-        joined = jnp.concatenate([from_send, from_recv, edge], axis=1)
-        new = (edge.astype(F32) + perceptron(joined, first, second)).astype(BF16)
+    return (nodes.astype(F32) + perceptron(dot(joined, first), centre(second))).astype(BF16)
+
+
+def project(blocks, matrix):
+    return [dot(block, matrix).astype(BF16) for block in blocks]
+
+
+def edge_columns(own, count):
+    shape = (count, LANES)
+    if own == 2 * CUT:
+        return [(shape, I16), (shape, I16), (shape, I32), (shape, I16), (shape, I32)]
+    return [(shape, I16), (shape, I32), (shape, I16)]
+
+
+def fill_columns(own, senders, receivers, outs):
+    send, recv = columns(senders), columns(receivers)
+    low, high = jnp.bitwise_and(send, CUT - 1), jnp.right_shift(send, CUT_BITS)
+    if own == 2 * CUT:
+        low = jnp.where(send < own, low, -1)
+        values = [send, low, high, jnp.bitwise_and(recv, CUT - 1), jnp.right_shift(recv, CUT_BITS)]
+    else:
+        values = [low, high, recv]
+    for value, out in zip(values, outs):
+        out[...] = value.astype(out.dtype)
+
+
+def from_own(cols, nodes, first):
+    _, low, high, recv_low, recv_high = cols
+    blocks = cut(nodes)
+    sent, received = project(blocks, first[:LANES]), project(blocks, first[LANES : 2 * LANES])
+    return lambda rows: (
+        gather(low[rows, :], high[rows, :], sent, True) + gather(recv_low[rows, :], recv_high[rows, :], received, True)
+    )
+
+
+def from_halo(cols, halo, own, first):
+    sent = dot(halo, first[:LANES]).astype(BF16)
+    return lambda rows: dot(hot_rows(cols[0][rows, :], LANES, own), sent)
+
+
+def from_table(cols, table, first):
+    low, high, recv = cols
+    sent = project(cut(table), first[:LANES])
+    received = project([table[:CUT]], first[LANES : 2 * LANES])
+    return lambda rows: gather(low[rows, :], high[rows, :], sent, True) + gather(recv[rows, :], None, received)
+
+
+def finish(before_at, nodes, receivers, block, edges, weights, new_edges=None, step=STEP):
+    second = centre(weights[1].get()[...])
+    receivers = receivers.get()
+    summed = 0.0
+    for at in range(0, edges.shape[0], step):
+        rows = slice(at, min(at + step, edges.shape[0]))
+        edge = edges[rows, :]
+        new = (edge.astype(F32) + perceptron(before_at(rows), second)).astype(BF16)
         if new_edges is not None:
-            new_edges[at : at + step, :] = new
-        summed = summed + segment_sum(recv, recv_col, new, own)
+            new_edges[rows, :] = new
+        recv = receivers[rows.start // LANES : rows.stop // LANES, :]
+        summed = summed + segment_sum(recv, None if block is None else block[rows, :], new)
     return node_update(nodes, summed, weights[2].get()[...], weights[3].get()[...])
 
 
@@ -139,7 +177,7 @@
     return out
 
 
-def pick_kernel(halo, coarse_halo, fine, coarse, nodes, rows, coarse_rows, dest, target, parent, paired, crossed, lists):
+def pick_kernel(halo, coarse_halo, fine, coarse, nodes, rows, coarse_rows, dest, target, parent, paired, crossed, own_tail, lists):
     at = row_layout(fine, coarse)
     lists[...] = jnp.zeros_like(lists)
     listed, coarse_listed = rows.get()[...], coarse_rows.get()[...]
@@ -160,6 +198,7 @@
         col = column(jnp.where(up == 1, listed[1:2], listed[0:1]))
         out[:halo, :] = dot(hot_rows(col, fine), nodes[...]).astype(BF16)
         out[halo:, :] = tail
+    own_tail[...] = tail
 
 
 def lower_higher(paired, crossed):
@@ -168,18 +207,39 @@
     return jnp.where(odd, paired, crossed).astype(BF16), jnp.where(odd, crossed, paired).astype(BF16)
 
 
-def fine_kernel(halo, paired, crossed, own, nodes, senders, receivers, edges, *rest):
-    *weights, payload, new_edges = rest
-    nodes = nodes.get()
+def ready_kernel(nodes, senders, receivers, edges, first, _1, _2, _3, *outs):
+    *cols, before = outs
+    nodes, first = nodes.get()[...], first.get()[...]
+    fill_columns(nodes.shape[0], senders.get()[...], receivers.get()[...], cols)
+    edges, inner = edges.get(), from_own(cols, nodes, first)
+    for at in range(0, edges.shape[0], STEP):
+        rows = slice(at, min(at + STEP, edges.shape[0]))
+        before[rows, :] = dot(edges[rows, :], first[2 * LANES :]) + inner(rows)
+
+
+def fine_kernel(halo, paired, crossed, tail, before, *refs):
+    cols, (nodes, receivers, edges, *weights), (payload, new_edges) = refs[:5], refs[5:12], refs[12:]
+    nodes = nodes.get()[...]
     fine = nodes.shape[0]
-    table = jnp.concatenate([nodes[...], *lower_higher(paired[:halo, :], crossed[:halo, :])], axis=0)
-    payload[:fine, :] = message_pass(table, fine, senders, receivers, edges, weights, new_edges)
-    payload[fine:, :] = own[halo:, :]
+    outer = jnp.concatenate(lower_higher(paired[:halo, :], crossed[:halo, :]), axis=0)
+    outside = from_halo(cols, outer, fine, weights[0].get()[...])
+    payload[:fine, :] = finish(lambda rows: before[rows, :] + outside(rows), nodes, receivers, cols[-1], edges.get(), weights, new_edges)
+    payload[fine:, :] = tail[...]
+
+
+def columns_kernel(own, senders, receivers, edges, first, *outs):
+    *cols, before = outs
+    fill_columns(own, senders.get()[...], receivers.get()[...], cols)
+    before[...] = dot(edges.get()[...], first.get()[2 * LANES :, :])
+
+
+def edge_kernel(edges, first, before):
+    before[...] = dot(edges[...], first.get()[2 * LANES :, :])
 
 
 def coarse_kernel(regions, halo, coarse, *refs):
-    blocks, (senders, receivers, edges, *rest) = refs[:regions], refs[regions:]
-    *weights, payload, new_edges = rest
+    blocks, (before, *rest) = refs[:regions], refs[regions:]
+    cols, (receivers, edges, *weights), (payload, new_edges) = rest[:3], rest[3:9], rest[9:]
     me = lax.axis_index("region")
     fine = blocks[0].shape[0] - TAIL
     at = row_layout(fine, coarse)
@@ -192,15 +252,19 @@
         col = columns(listed)[first : first + halo]
         codes.append(jnp.where(there, other * coarse + col, -1))
     codes = jnp.concatenate(codes, axis=0)
-    total = jnp.zeros((codes.shape[0], LANES), F32)
-    members = jnp.zeros((codes.shape[0], LANES), F32)
-    for block, tail in zip(blocks, tails):
-        f = fine // LANES
-        parent = tail[at["dest"] : at["dest"] + f] * coarse + tail[at["target"] : at["target"] + f]
-        more, counted = sums_and_counts(hot_codes(codes, parent), block[:fine, :])
-        total, members = total + more, members + counted
-    table = (total / jnp.maximum(members, 1.0)).astype(BF16)
-    payload[:coarse, :] = message_pass(table, coarse, senders, receivers, edges, weights, new_edges)
+    half = codes.shape[0] // 2
+    parts = []
+    for part in (codes[:half], codes[half:]):
+        total, members = 0.0, 0.0
+        for block, tail in zip(blocks, tails):
+            f = fine // LANES
+            parent = tail[at["dest"] : at["dest"] + f] * coarse + tail[at["target"] : at["target"] + f]
+            more, counted = sums_and_counts(hot_codes(part, parent), block[:fine, :])
+            total, members = total + more, members + counted
+        parts.append((total / jnp.maximum(members, 1.0)).astype(BF16))
+    table = jnp.concatenate(parts, axis=0)
+    inner = from_table(cols, table, weights[0].get()[...])
+    payload[:coarse, :] = finish(lambda rows: before[rows, :] + inner(rows), table[:coarse], receivers, None, edges.get(), weights, new_edges)
     own_tail = tails[0]
     c = coarse // LANES
     payload[coarse:, :] = jnp.concatenate(
@@ -215,14 +279,11 @@
         latents, found = carry
         rank = ranks[pl.ds(pl.multiple_of(g * at_once, at_once), at_once), :]
         code = codes[pl.ds(pl.multiple_of(g * at_once, at_once), at_once), :]
-        hots = []
         for i in range(at_once):
-            mask = place == rank[i : i + 1]
-            hots.append(hot(mask))
-            found = found + jnp.where(mask, code[i : i + 1], 0)
+            found = found + jnp.where(place == rank[i : i + 1], code[i : i + 1], 0)
         wide = at_once * LANES
         rows = edges[pl.ds(pl.multiple_of(g * wide, wide), wide), :]
-        return latents + dot(jnp.concatenate(hots, axis=1), rows), found
+        return latents + dot(hot_codes(place, rank), rows), found
 
     zero = jnp.zeros((size, LANES), F32), jnp.zeros((size, LANES), I32)
     latents, found = lax.fori_loop(0, ranks.shape[0] // at_once, body, zero)
@@ -232,22 +293,24 @@
 
 def below(rows, same):
     square = (rows, rows)
-    return hot(same(lax.broadcasted_iota(I32, square, 0), lax.broadcasted_iota(I32, square, 1)))
+    mask = same(lax.broadcasted_iota(I32, square, 0), lax.broadcasted_iota(I32, square, 1))
+    return jnp.where(mask, 1.0, 0.0).astype(BF16)
 
 
 def running(flags):
-    upto = hot(lax.broadcasted_iota(I32, (LANES, LANES), 0) <= lane_iota(LANES))
+    upto = jnp.where(lax.broadcasted_iota(I32, (LANES, LANES), 0) <= lane_iota(LANES), 1.0, 0.0).astype(BF16)
     inside = dot(flags.astype(BF16), upto)
     return inside, jnp.broadcast_to(inside[:, LANES - 1 :], flags.shape)
 
 
 def listed_kernel(regions, halo, fine, coarse, *refs):
-    own, paired, crossed, senders, receivers, edges, parents, halo_rows, halo_blocks, ranks, codes, latents, found, number = refs
+    own, paired, crossed, senders, receivers, edges, parents, firsts, halo_rows, halo_blocks, ranks, codes = refs[:12]
+    latents, send, recv, recv_rows = refs[12:]
     me = lax.axis_index("region")
     at = row_layout(fine, coarse)
-    start = own.shape[0] - TAIL
+    start = paired.shape[0] - TAIL
     lower, higher = lower_higher(paired[start:, :], crossed[start:, :])
-    own_tail, lower_tail, higher_tail = (tail.astype(F32).astype(I32) for tail in (own[start:, :], lower, higher))
+    own_tail, lower_tail, higher_tail = (tail.astype(F32).astype(I32) for tail in (own[...], lower, higher))
     near = ((me - 1, me > 0, lower_tail), (me + 1, me < regions - 1, higher_tail))
     c = coarse // LANES
     wide, size = parents.shape[0], latents.shape[0]
@@ -273,6 +336,11 @@
 
     high_count = TOP // LANES
     rows = as_rows(cols)
+    row_at = lax.broadcasted_iota(I32, (wide, LANES), 0)
+    for i in range(wide // LANES):
+        earlier = jnp.logical_and(cols == rows[i : i + 1], row_at < lane_iota(wide, i * LANES))
+        seen = jnp.max(jnp.where(earlier, 1.0, 0.0), axis=0, keepdims=True)
+        firsts[i : i + 1, :] = jnp.where(seen > 0.0, -2, rows[i : i + 1])
     tops = dot(
         hot_cols(jnp.right_shift(rows, 7), high_count), hot_rows(jnp.bitwise_and(cols, LANES - 1), LANES)
     )
@@ -282,10 +350,10 @@
     high = lax.broadcasted_iota(I32, (high_count, LANES), 0)
     needed = []
     for i in range(0, count, 8):
-        recv = receivers[i : i + 8, :]
-        match = dot(tops, hot_cols(jnp.bitwise_and(recv, LANES - 1), LANES))
+        some = receivers[i : i + 8, :]
+        match = dot(tops, hot_cols(jnp.bitwise_and(some, LANES - 1), LANES))
         for k in range(8):
-            mine = jnp.where(high == jnp.right_shift(recv[k : k + 1], 7), match[:, k * LANES : (k + 1) * LANES], 0.0)
+            mine = jnp.where(high == jnp.right_shift(some[k : k + 1], 7), match[:, k * LANES : (k + 1) * LANES], 0.0)
             needed.append(jnp.sum(mine, axis=0, keepdims=True))
     needed = jnp.concatenate(needed, axis=0)
 
@@ -301,8 +369,7 @@
     inside, sums = running(others)
     rank = dot(below(count, lambda i, j: j < i), sums.astype(BF16)) + inside - 1.0
     ranks[...] = jnp.where(others > 0.0, rank, -1.0).astype(I32)
-    number[1] = jnp.sum(others).astype(I32)
-    number[0] = jnp.sum(needed).astype(I32) - number[1]
+    total = jnp.sum(jnp.sum(needed - others, axis=0, keepdims=True), axis=1, keepdims=True).astype(I32)
     codes[...] = senders.get()[...] * TOP + receivers[...]
 
     slot = jnp.where(needed > 0.0, local, -1.0).astype(I32)
@@ -311,11 +378,9 @@
     lane = lane_iota(SLOTS)
     slots, targets = [], []
     for first in range(0, count, GROUP):
-        hots, code = [], jnp.zeros((SLOTS, LANES), F32)
+        code = jnp.zeros((SLOTS, LANES), F32)
         for i in range(first, first + GROUP):
-            mask = place == slot[i : i + 1]
-            hots.append(hot(mask))
-            code = code + jnp.where(mask, codes[i : i + 1, :].astype(F32), 0.0)
+            code = code + jnp.where(place == slot[i : i + 1], codes[i : i + 1, :].astype(F32), 0.0)
         code = jnp.broadcast_to(jnp.sum(code, axis=1, keepdims=True), (SLOTS, LANES)).astype(I32)
         parts = jnp.where(
             lane == 0,
@@ -323,7 +388,8 @@
             jnp.where(lane == 1, jnp.bitwise_and(jnp.right_shift(code, 8), 255), jnp.bitwise_and(code, 255)),
         )
         parts = jnp.where(lane < 3, parts, 0).astype(F32).astype(BF16)
-        packed = dot(jnp.concatenate(hots, axis=1), edges[first * LANES : (first + GROUP) * LANES, :]).astype(BF16)
+        chosen = hot_cols(slot[first : first + GROUP], SLOTS)
+        packed = dot(chosen, edges[first * LANES : (first + GROUP) * LANES, :]).astype(BF16)
         slots.append(jnp.concatenate([packed, parts], axis=1))
         target = before[first : first + 1] + lane_iota(1).astype(F32)
         targets.append(jnp.where(lane_iota(1).astype(F32) < used[first : first + 1], target, -1.0).astype(I32)[:, :SLOTS])
@@ -334,7 +400,15 @@
     parts = packed[:, LANES:]
     lane = lane_iota(size)
     code = jnp.where(lane == 0, parts * 65536.0, jnp.where(lane == 1, parts * 256.0, parts))
-    found[...] = jnp.broadcast_to(jnp.sum(code, axis=1, keepdims=True), (size, LANES)).astype(I32)
+    code = jnp.broadcast_to(jnp.sum(code, axis=1, keepdims=True), (size, LANES)).astype(I32)
+    send[...], recv[...] = ends(code, 0, total)
+    recv_rows[...] = as_rows(recv[...])
+
+
+def ends(code, first_place, total):
+    place = lax.broadcasted_iota(I32, code.shape, 0) + first_place
+    recv = jnp.where(place < total, jnp.bitwise_and(code, TOP - 1), -3)
+    return jnp.right_shift(code, TOP.bit_length() - 1), recv
 
 
 def parent_kernel(regions, halo, coarse, *refs):
@@ -377,22 +451,22 @@
     return both[:, :LANES], both[:, LANES:]
 
 
-def pooled(col, blocks, coarse):
+def pooled(cols, blocks, coarse):
     c = coarse // LANES
 
     def add(block, sums):
         tail = tail_of(block, coarse)
-        total, members = sums_and_counts(hot_codes(col, tail[:c] * LANES + tail[c : 2 * c]), block[:coarse, :])
-        return sums[0] + total, sums[1] + members
-
-    sums = (jnp.zeros((col.shape[0], LANES), F32),) * 2
+        parent = tail[:c] * LANES + tail[c : 2 * c]
+        more = [sums_and_counts(hot_codes(col, parent), block[:coarse, :]) for col in cols]
+        return tuple((total + a, members + b) for (total, members), (a, b) in zip(sums, more))
+
+    sums = tuple((jnp.zeros(col.shape, F32),) * 2 for col in cols)
     if isinstance(blocks, tuple):
         for block in blocks:
             sums = add(block, sums)
     else:
         sums = lax.fori_loop(0, blocks.shape[0], lambda n, sums: add(blocks.at[n], sums), sums)
-    total, members = sums
-    return (total / jnp.maximum(members, 1.0)).astype(BF16)
+    return [(total / jnp.maximum(members, 1.0)).astype(BF16) for total, members in sums]
 
 
 def as_rows(col):
@@ -410,60 +484,54 @@
     else:
         blocks = refs[0]
     refs = refs[count:]
-    parents, halo_rows, halo_blocks, ranks, codes, latents, found, number, all_edges, edges = refs[:10]
-    senders, receivers = refs[10:12]
-    top_weights, weights = refs[12:16], refs[16:20]
-    out, agg, fallback, semaphore = refs[20:]
+    parents, firsts, halo_rows, halo_blocks, ranks, codes, latents, send, recv, recv_rows, all_edges = refs[:11]
+    edges, before3, *cols = refs[11:16]
+    receivers, top_weights, weights = refs[16], refs[17:21], refs[21:25]
+    out, agg, fallback, semaphore = refs[25:]
     me = lax.axis_index("region")
     own_sub = lambda j: blocks[j * subs] if count > 1 else blocks.at[j * subs]
-    wide = parents.shape[0]
-    mine = parents[...]
-    top_own = pooled(mine, blocks, coarse)
-    mine_rows = as_rows(mine)
-    row_at = lax.broadcasted_iota(I32, (wide, LANES), 0)
-    firsts = []
-    for i in range(wide // LANES):
-        earlier = jnp.logical_and(mine == mine_rows[i : i + 1], row_at < lane_iota(wide, i * LANES))
-        seen = jnp.max(jnp.where(earlier, 1.0, 0.0), axis=0, keepdims=True)
-        firsts.append(jnp.where(seen > 0.0, -2, mine_rows[i : i + 1]))
-    firsts = jnp.concatenate(firsts, axis=0)
-    first, second = top_weights[0].get()[...], top_weights[1].get()[...]
-    agg[...] = jnp.zeros_like(agg)
-
-    def one(edge, code, first_place, total):
-        place = lax.broadcasted_iota(I32, (size, LANES), 0) + first_place
-        send = jnp.right_shift(code, TOP.bit_length() - 1)
-        recv = jnp.where(place < total, jnp.bitwise_and(code, TOP - 1), -3)
-        from_send = pooled(send, blocks, coarse)
-        from_recv = dot(hot_codes(recv, firsts), top_own).astype(BF16)
-        joined = jnp.concatenate([from_send, from_recv, edge], axis=1)
-        new = (edge.astype(F32) + perceptron(joined, first, second)).astype(BF16)
-        agg[...] += dot(hot_codes(mine, as_rows(recv)), new)
-
-    one(latents[...], found[...], 0, number[0])
+    mine, firsts = parents[...], firsts[...]
+    top_own, from_send = pooled([mine, send[...]], blocks, coarse)
+    first, second = top_weights[0].get()[...], centre(top_weights[1].get()[...])
+    received = dot(top_own, first[LANES : 2 * LANES]).astype(BF16)
+    others = jnp.concatenate([first[:LANES], first[2 * LANES :]], axis=0)
+
+    def one(edge, from_send, recv, recv_rows):
+        before = dot(jnp.concatenate([from_send, edge], axis=1), others) + dot(hot_codes(recv, firsts), received)
+        new = (edge.astype(F32) + perceptron(before, second)).astype(BF16)
+        return dot(hot_codes(mine, recv_rows), new)
+
+    agg[...] = one(latents[...], from_send, recv[...], recv_rows[...])
 
     def more(b, carry):
         copy = pltpu.make_async_copy(all_edges, fallback, semaphore.at[0])
         copy.start()
         copy.wait()
         edge, code = compact(b * size, ranks, codes, fallback, size)
-        one(edge, code, b * size, number[1])
+        send, recv = ends(code, b * size, left)
+        (from_send,) = pooled([send], blocks, coarse)
+        agg[...] += one(edge, from_send, recv, as_rows(recv))
         return carry
 
-    lax.fori_loop(0, (number[1] + size - 1) // size, more, 0)
+    left = jnp.max(ranks[...]) + 1
+    lax.fori_loop(0, (left + size - 1) // size, more, 0)
     top_final = node_update(top_own, agg[...], top_weights[2].get()[...], top_weights[3].get()[...])
     near = gather(halo_rows[...], halo_blocks[...], [own_sub(j)[:coarse, :] for j in range(regions)])
     down = jnp.concatenate([own_sub(0)[:coarse, :].astype(F32), near], axis=0)
     table = (down + top_final[: coarse + 2 * halo].astype(F32)).astype(BF16)
-    out[...] = message_pass(table, coarse, senders, receivers, Here(edges), weights)
+    inner = from_table(cols, table, weights[0].get()[...])
+    out[...] = finish(lambda rows: before3[rows, :] + inner(rows), table[:coarse], receivers, None, edges, weights)
 
 
 def last_kernel(regions, *refs):
-    blocks, refs = refs[:regions], refs[regions:]
-    down, parent_rows, parent_blocks, edges, senders, receivers, *weights, out = refs
+    blocks, (down, parent_rows, parent_blocks, edges, before, *rest) = refs[:regions], refs[regions:]
+    cols, receivers, weights, out = rest[:5], rest[5], rest[6:10], rest[10]
+    own = out.shape[0]
     parent = gather(parent_rows[...], parent_blocks[...], [block[...] for block in blocks])
     table = (down[...].astype(F32) + parent).astype(BF16)
-    out[...] = message_pass(table, out.shape[0], senders, receivers, Here(edges), weights)
+    first = weights[0].get()[...]
+    inner, outside = from_own(cols, table[:own], first), from_halo(cols, table[own:], own, first)
+    out[...] = finish(lambda rows: before[rows, :] + inner(rows) + outside(rows), table[:own], receivers, cols[-1], edges, weights)
 
 
 class Here:
@@ -487,11 +555,10 @@
         return self.place
 
 
-def call(kernel, args, outs, more=(), scratch=(), raw=(), scalars=(), scalar_outs=(), cost=1, far=False, limit=LIMIT):
-    kinds = {i: pltpu.SMEM for i in scalars} | {i: pltpu.HBM for i in raw}
-    specs = [pl.BlockSpec(memory_space=kinds.get(i, pltpu.VMEM)) for i in range(len(args))]
+def call(kernel, args, outs, more=(), scratch=(), raw=(), cost=1, far=False, limit=LIMIT):
+    specs = [pl.BlockSpec(memory_space=pltpu.HBM if i in raw else pltpu.VMEM) for i in range(len(args))]
     specs += [pl.BlockSpec(memory_space=pltpu.HBM if far else pltpu.VMEM)] * len(more)
-    out_specs = [pl.BlockSpec(memory_space=pltpu.SMEM if i in scalar_outs else pltpu.VMEM) for i in range(len(outs))]
+    out_specs = [pl.BlockSpec(memory_space=pltpu.VMEM)] * len(outs)
     places = []
     if far:
         places = [pltpu.VMEM(array.shape, array.dtype) for array, _ in more]
@@ -535,11 +602,12 @@
     return blocks if beside is None else (blocks, beside)
 
 
-def over_both(rows):
+def over_both(rows, beside):
     regions, subs = lax.axis_size("region"), lax.axis_size("sub")
     swap = lambda array, axis, bits: lax.ppermute(array, axis, [(i, i ^ bits) for i in range(lax.axis_size(axis))])
     turns = [rows] + [swap(rows, "sub", k) for k in range(1, subs)]
     if regions * subs <= 16:
+        turns[-1], beside = lax.optimization_barrier((turns[-1], beside))
         blocks = {0: turns}
         bit = regions // 2
         while bit > 1:
@@ -547,11 +615,11 @@
                 blocks[j + bit] = [swap(block, "region", bit) for block in blocks[j]]
             bit //= 2
         here = [block for j in range(0, regions, 2) for block in blocks[j]]
-        return here + [swap(jnp.concatenate(here), "region", 1)]
+        return here + [swap(jnp.concatenate(here), "region", 1)], beside
     blocks, bit = jnp.stack(turns), 1
     while bit < regions:
         blocks, bit = jnp.concatenate([blocks, swap(blocks, "region", bit)]), 2 * bit
-    return [blocks]
+    return [blocks], beside
 
 
 def on_device(
@@ -587,10 +655,10 @@
     level = lambda index: [(matrix, index) for matrix in weights]
     plain = lambda *arrays: [(array, None) for array in arrays]
 
-    to_pair, to_other = call(
+    to_pair, to_other, tail = call(
         functools.partial(pick_kernel, halo, halo2, fine, coarse),
         [],
-        [((halo + TAIL, LANES), BF16)] * 2,
+        [((halo + TAIL, LANES), BF16)] * 2 + [((TAIL, LANES), BF16)],
         plain(node_feats, halo_rows, coarse_halo_rows, rows(pool_dest), rows(pool_target), rows(pool3_target)),
         scratch=[pltpu.VMEM((TAIL, LANES), I32)],
         far=True,
@@ -599,68 +667,89 @@
     pairs = lambda first: [(i, j) for low in range(first, regions - 1, 2) for i, j in ((low, low + 1), (low + 1, low))]
     paired = lax.ppermute(to_pair, "region", pairs(0))
     crossed = lax.ppermute(to_other, "region", pairs(1))
+    one = lambda index: [(edge_in, index)]
+    fine_cols, coarse_cols = edge_columns(fine, fine_edges.shape[0]), edge_columns(coarse, coarse_edges.shape[0])
+    late_send, tail = lax.optimization_barrier((fine_send, tail))
+    *fine_cols, before = call(
+        ready_kernel,
+        [],
+        fine_cols + [(fine_edges.shape, F32)],
+        plain(node_feats, late_send, fine_recv, fine_edges) + level(0),
+        cost=2,
+    )
     payload, fine_edges2 = call(
         functools.partial(fine_kernel, halo),
-        [paired, crossed, to_pair],
+        [paired, crossed, tail, before, *fine_cols],
         [((fine + TAIL, LANES), BF16), (fine_edges.shape, BF16)],
-        plain(node_feats, fine_send, fine_recv, fine_edges) + level(0),
-        cost=5,
+        plain(node_feats, fine_recv, fine_edges) + level(0),
+        cost=3,
     )
     wide = -(-(coarse + 2 * halo2) // LANES) * LANES
     size = min(384, top_edges.shape[0])
+    listed_shapes = [
+        ((wide, LANES), I32),
+        ((wide // LANES, LANES), I32),
+        ((2 * halo2, LANES), I32),
+        ((2 * halo2, LANES), I32),
+        (top_send.shape, I32),
+        (top_send.shape, I32),
+        ((size, LANES), BF16),
+        ((size, LANES), I32),
+        ((size, LANES), I32),
+        ((size // LANES, LANES), I32),
+    ]
     selected = call(
         functools.partial(listed_kernel, regions, halo2, fine, coarse),
-        [to_pair, paired, crossed],
-        [
-            ((wide, LANES), I32),
-            ((2 * halo2, LANES), I32),
-            ((2 * halo2, LANES), I32),
-            (top_send.shape, I32),
-            (top_send.shape, I32),
-            ((size, LANES), BF16),
-            ((size, LANES), I32),
-            ((2,), I32),
-        ],
+        [tail, paired, crossed],
+        listed_shapes,
         plain(top_send, top_recv, top_edges),
-        scalar_outs=(7,),
         cost=3,
+    )
+    payload, late_edges = lax.optimization_barrier((payload, coarse_edges))
+    *coarse_cols, before = call(
+        functools.partial(columns_kernel, coarse),
+        [],
+        coarse_cols + [(coarse_edges.shape, F32)],
+        plain(coarse_send, coarse_recv, late_edges) + one(1),
     )
     blocks, selected = over_region(payload, selected)
     payload2, coarse_edges2 = call(
         functools.partial(coarse_kernel, regions, halo2, coarse),
-        blocks,
+        blocks + [before, *coarse_cols],
         [((coarse + TAIL, LANES), BF16), (coarse_edges.shape, BF16)],
-        plain(coarse_send, coarse_recv, coarse_edges) + level(1),
-        cost=4,
+        plain(coarse_recv, coarse_edges) + level(1),
+        cost=3,
     )
     table_shape = (fine + 2 * halo, LANES)
-    fine_table, parent_rows, parent_blocks = call(
+    table = call(
         functools.partial(parent_kernel, regions, halo, coarse),
         blocks,
         [(table_shape, BF16), (table_shape, I32), (table_shape, I32)],
     )
-    blocks2 = over_both(payload2)
+    before = call(edge_kernel, [coarse_edges2], [(coarse_edges.shape, F32)], one(3))
+    blocks2, (table, before) = over_both(payload2, (table, before))
     many = len(blocks2)
     (coarse_final,) = call(
         functools.partial(top_kernel, regions, halo2, coarse, size, many),
-        blocks2 + [*selected, top_edges, coarse_edges2],
+        blocks2 + [*selected, top_edges, coarse_edges2, *before, *coarse_cols],
         [((coarse, LANES), BF16)],
-        plain(coarse_send, coarse_recv) + level(2) + level(3),
+        plain(coarse_recv) + level(2) + level(3),
         scratch=[
             pltpu.VMEM((wide, LANES), F32),
             pltpu.VMEM(top_edges.shape, BF16),
             pltpu.SemaphoreType.DMA((1,)),
         ],
-        scalars=(many + 7,),
-        raw=(many + 8,),
+        raw=(many + len(selected),),
         cost=6,
     )
+    before = call(edge_kernel, [fine_edges2], [(fine_edges.shape, F32)], one(4))
+    blocks3, before = over_region(coarse_final, before)
     (fine_final,) = call(
         functools.partial(last_kernel, regions),
-        over_region(coarse_final) + [fine_table, parent_rows, parent_blocks, fine_edges2],
+        blocks3 + [*table, fine_edges2, *before, *fine_cols],
         [((fine, LANES), BF16)],
-        plain(fine_send, fine_recv) + level(4),
-        cost=6,
+        plain(fine_recv) + level(4),
+        cost=3,
     )
     return fine_final
 

time: 58.3 us -> 54 us (0.926)
  Pallas kernels: 23.6 us -> 20.7 us
  starting transfers between devices: 17.9 us -> 15.2 us
  waiting for transfers between devices: 15.4 us -> 17.4 us
  local copies, waits for them, and re-layouts: 0.88 us -> 0.18 us
    pallas_call x7 -> x11, Pallas kernels: 23.6 us -> 20.7 us  [call(): pl.pallas_call(body, out_shape=[jax.ShapeDtypeStruct(shape, dtype) for sh...]
    ppermute x6, starting transfers between devices: 8.04 us -> 6.02 us  [over_region(): lax.ppermute(going[j], 'region', [(i, i ^ bit) for i in range(count)])]
    ppermute x8, waiting for transfers between devices: 8.54 us -> 10.4 us  [over_both(): lax.ppermute(array, axis, [(i, i ^ bits) for i in range(lax.axis_size(axi...]
    unnamed x37, local copies, waits for them, and re-layouts: 0.87 us -> 0.16 us
    ppermute x8, starting transfers between devices: 8.65 us -> 7.98 us  [over_both(): lax.ppermute(array, axis, [(i, i ^ bits) for i in range(lax.axis_size(axi...]
    ppermute x6, waiting for transfers between devices: 6.48 us -> 7.07 us  [over_region(): lax.ppermute(going[j], 'region', [(i, i ^ bit) for i in range(count)])]
  transfers between devices with their start and end apart: 16 -> 16, of which waited for: 10 -> 8; matrix products, arithmetic and copies ran while one was open for 0% -> 0% of each run, Pallas kernels for 5% -> 11%
where the time goes in v3:
time: 54 us; the launch traced here: 53.8 us
  Pallas kernels  20.7 us (38%)
  waiting for transfers between devices  17.4 us (32%)
  starting transfers between devices  15.2 us (28%)
    pallas_call x11, Pallas kernels, call(): pl.pallas_call(body, out_shape=[jax.ShapeDtypeStruct(shape, dtype) for sh...  20.7 us
    ppermute x8, waiting for transfers between devices, over_both(): lax.ppermute(array, axis, [(i, i ^ bits) for i in range(lax.axis_size(axi...  10.4 us
    ppermute x8, starting transfers between devices, over_both(): lax.ppermute(array, axis, [(i, i ^ bits) for i in range(lax.axis_size(axi...  7.98 us
    ppermute x6, waiting for transfers between devices, over_region(): lax.ppermute(going[j], 'region', [(i, i ^ bit) for i in range(count)])  7.07 us
    ppermute x6, starting transfers between devices, over_region(): lax.ppermute(going[j], 'region', [(i, i ^ bit) for i in range(count)])  6.02 us
  transfers between devices with their start and end apart: 16, of which 8 were waited for; matrix products, arithmetic and copies ran while one was open for 0% of the time, Pallas kernels for 11%

profile of v3, /device:TPU:0, one launch (start us, length us, event | category | flops | bytes accessed | tf_op | source)
XLA Modules:
  0.0 53.8 jit_solution(13082323077237390045)
XLA Ops:
  0.0 1.9 %shard_map.181 = (bf16[80,128]{1,0:T(8,128)(2,1)}, bf16[80,128]{1,0:T(8,128)(2,1)}, bf16[16,128]{1,0:T(8,128)(2,1)}) custom-call(bf16[512,128]{1,0:T(8,128)(2,1)} %refs_9_.2, s32[2,64]{1,0:T(2,128)} %refs_1_.3, s32[2,32]{1,0:T(2,128)} %refs_2_.1, s32[4,128]{1,0:T(4,128)} %bitcast.19, s32[4,128]{1,0:T(4,128)} %bitcast.20, s32[2,128]{1,0:T(2,128)} %bitcast.21), custom_call_target="tpu_custom_call" | custom-call | flops 1000000000 | bytes 100000 | tf_op jit(solution)/shard_map/pallas_call | solution.py:577
  2.0 0.5 collective-permute-start
  2.5 0.7 %collective-permute-start.1 = (bf16[80,128]{1,0:T(8,128)(2,1)}, bf16[80,128]{1,0:T(8,128)(2,1)S(1)}, u32[]{:S(2)}, u32[]{:S(2)}) collective-permute-start(bf16[80,128]{1,0:T(8,128)(2,1)} %get-tuple-element.58), channel_id=1, source_target_pairs={{4,8},{8,4},{5,9},{9,5},{6,10},{10,6},{7,11},{11,7},{20,24},{24,20... | collective-permute-start | bytes 61448 | tf_op jit(solution)/shard_map/ppermute | solution.py:669
  3.3 1.9 %shard_map.182 = (s16[3072,128]{1,0:T(8,128)(2,1)S(1)}, s16[3072,128]{1,0:T(8,128)(2,1)S(1)}, s32[3072,128]{1,0:T(8,128)S(1)}, s16[3072,128]{1,0:T(8,128)(2,1)S(...) custom-call(bf16[512,128]{1,0:T(8,128)(2,1)S(1)} %copy-done.7, s32[24,128]{1,0:T(8,128)S(1)} %bitcast.11, ...), custom_call_target="tpu_custom_call" | custom-call | flops 2000000000 | bytes 200000 | tf_op jit(solution)/shard_map/pallas_call | solution.py:577
  5.2 2.1 %shard_map.183 = (bf16[528,128]{1,0:T(8,128)(2,1)S(1)}, bf16[3072,128]{1,0:T(8,128)(2,1)S(1)}) custom-call(bf16[80,128]{1,0:T(8,128)(2,1)S(1)} %collective-permute-done.refs_0_.refs_1_, bf16[80,128]{1,0:T(8,128)(2,1)S(1)} %collective-permute-done.1.refs_1_.refs_2_, bf16[16,128]{1,0:T(8,128)(2,1)S(1)} %copy-done.14, ...), custom_call_target="tpu_custom_call" | custom-call | flops 3000000000 | bytes 300000 | tf_op jit(solution)/shard_map/pallas_call | solution.py:577
  7.3 5.2 %collective-permute-start.3 = (bf16[528,128]{1,0:T(8,128)(2,1)S(1)}, bf16[528,128]{1,0:T(8,128)(2,1)S(1)}, u32[]{:S(2)}, u32[]{:S(2)}) collective-permute-start(bf16[528,128]{1,0:T(8,128)(2,1)S(1)} %get-tuple-element.69.refs_0_), channel_id=1, source_target_pairs={{0,8},{4,12},{8,0},{12,4},{1,9},{5,13},{9,1},{13,5},{2,10},{6,14},... | collective-permute-start | bytes 405512 | tf_op jit(solution)/shard_map/ppermute | solution.py:598
  12.6 2.4 %shard_map.184 = (s32[384,128]{1,0:T(8,128)S(1)}, s32[3,128]{1,0:T(4,128)S(1)}, s32[64,128]{1,0:T(8,128)S(1)}, s32[64,128]{1,0:T(8,128)S(1)}, s32[64,128]{1,0:T(...) custom-call(bf16[16,128]{1,0:T(8,128)(2,1)S(1)} %copy-done.14, ...), custom_call_target="tpu_custom_call" | custom-call | flops 3000000000 | bytes 300000 | tf_op jit(solution)/shard_map/pallas_call | solution.py:577
  15.0 1.8 %collective-permute-done.3.refs_2_ = bf16[528,128]{1,0:T(8,128)(2,1)S(1)} collective-permute-done((bf16[528,128]{1,0:T(8,128)(2,1)S(1)}, bf16[528,128]{1,0:T(8,128)(2,1)S(1)}, u32[]{:S(2)}, u32[]{:S(2)}) %collective-permute-start.3) | collective-permute-done | bytes 135200 | tf_op jit(solution)/shard_map/ppermute | solution.py:598
  16.8 0.5 shard_map.185
  17.3 0.8 %collective-permute-done.4.refs_3_ = bf16[528,128]{1,0:T(8,128)(2,1)S(1)} collective-permute-done((bf16[528,128]{1,0:T(8,128)(2,1)S(1)}, bf16[528,128]{1,0:T(8,128)(2,1)S(1)}, u32[]{:S(2)}, u32[]{:S(2)}) %collective-permute-start.4) | collective-permute-done | bytes 135200 | tf_op jit(solution)/shard_map/ppermute | solution.py:598
  18.1 2.1 %shard_map.186 = (bf16[272,128]{1,0:T(8,128)(2,1)S(1)}, bf16[1536,128]{1,0:T(8,128)(2,1)S(1)}) custom-call(bf16[528,128]{1,0:T(8,128)(2,1)S(1)} %get-tuple-element.69.refs_0_, bf16[528,128]{1,0:T(8,128)(2,1)S(1)} %collective-permute-done.2.refs_1_, bf16[528,128]{1,0:T(8,128)(2,1)S(1)} %collective-permute-done.3.refs_2_, ...), custom_call_target="tpu_custom_call" | custom-call | flops 3000000000 | bytes 300000 | tf_op jit(solution)/shard_map/pallas_call | solution.py:577
  20.3 1.8 %collective-permute-start.5 = (bf16[272,128]{1,0:T(8,128)(2,1)S(1)}, bf16[272,128]{1,0:T(8,128)(2,1)S(1)}, u32[]{:S(2)}, u32[]{:S(2)}) collective-permute-start(bf16[272,128]{1,0:T(8,128)(2,1)S(1)} %get-tuple-element.86.refs_0_), channel_id=1, source_target_pairs={{0,1},{1,0},{2,3},{3,2},{4,5},{5,4},{6,7},{7,6},{8,9},{9,8},{10,11... | collective-permute-start | bytes 208904 | tf_op jit(solution)/shard_map/ppermute | solution.py:607
  22.1 2.6 %collective-permute-start.6 = (bf16[272,128]{1,0:T(8,128)(2,1)S(1)}, bf16[272,128]{1,0:T(8,128)(2,1)S(1)}, u32[]{:S(2)}, u32[]{:S(2)}) collective-permute-start(bf16[272,128]{1,0:T(8,128)(2,1)S(1)} %get-tuple-element.86.refs_0_), channel_id=1, source_target_pairs={{0,2},{1,3},{2,0},{3,1},{4,6},{5,7},{6,4},{7,5},{8,10},{9,11},{10,... | collective-permute-start | bytes 208904 | tf_op jit(solution)/shard_map/ppermute | solution.py:607
  24.7 0.0 collective-permute-start.7
  24.7 0.8 %collective-permute-start.8 = (bf16[272,128]{1,0:T(8,128)(2,1)S(1)}, bf16[272,128]{1,0:T(8,128)(2,1)S(1)}, u32[]{:S(2)}, u32[]{:S(2)}) collective-permute-start(bf16[272,128]{1,0:T(8,128)(2,1)S(1)} %get-tuple-element.86.refs_0_), channel_id=1, source_target_pairs={{0,8},{4,12},{8,0},{12,4},{1,9},{5,13},{9,1},{13,5},{2,10},{6,14},... | collective-permute-start | bytes 208904 | tf_op jit(solution)/shard_map/ppermute | solution.py:607
  25.5 0.2 shard_map.188.refs_21_
  25.8 0.4 shard_map.187
  26.2 4.8 %collective-permute-done.7.refs_3_ = bf16[272,128]{1,0:T(8,128)(2,1)S(1)} collective-permute-done((bf16[272,128]{1,0:T(8,128)(2,1)S(1)}, bf16[272,128]{1,0:T(8,128)(2,1)S(1)}, u32[]{:S(2)}, u32[]{:S(2)}) %collective-permute-start.7) | collective-permute-done | bytes 69664 | tf_op jit(solution)/shard_map/ppermute | solution.py:607
  30.9 0.6 %collective-permute-start.11 = (bf16[272,128]{1,0:T(8,128)(2,1)S(1)}, bf16[272,128]{1,0:T(8,128)(2,1)S(1)}, u32[]{:S(2)}, u32[]{:S(2)}) collective-permute-start(bf16[272,128]{1,0:T(8,128)(2,1)S(1)} %collective-permute-done.7.refs_3_), channel_id=1, source_target_pairs={{0,8},{4,12},{8,0},{12,4},{1,9},{5,13},{9,1},{13,5},{2,10},{6,14},... | collective-permute-start | bytes 208904 | tf_op jit(solution)/shard_map/ppermute | solution.py:607
  31.5 1.4 %collective-permute-start.9 = (bf16[272,128]{1,0:T(8,128)(2,1)S(1)}, bf16[272,128]{1,0:T(8,128)(2,1)S(1)}, u32[]{:S(2)}, u32[]{:S(2)}) collective-permute-start(bf16[272,128]{1,0:T(8,128)(2,1)S(1)} %collective-permute-done.5.refs_1_), channel_id=1, source_target_pairs={{0,8},{4,12},{8,0},{12,4},{1,9},{5,13},{9,1},{13,5},{2,10},{6,14},... | collective-permute-start | bytes 208904 | tf_op jit(solution)/shard_map/ppermute | solution.py:607
  33.0 0.6 %collective-permute-start.10 = (bf16[272,128]{1,0:T(8,128)(2,1)S(1)}, bf16[272,128]{1,0:T(8,128)(2,1)S(1)}, u32[]{:S(2)}, u32[]{:S(2)}) collective-permute-start(bf16[272,128]{1,0:T(8,128)(2,1)S(1)} %collective-permute-done.6.refs_2_), channel_id=1, source_target_pairs={{0,8},{4,12},{8,0},{12,4},{1,9},{5,13},{9,1},{13,5},{2,10},{6,14},... | collective-permute-start | bytes 208904 | tf_op jit(solution)/shard_map/ppermute | solution.py:607
  33.7 2.3 %collective-permute-done.9.refs_5_ = bf16[272,128]{1,0:T(8,128)(2,1)S(1)} collective-permute-done((bf16[272,128]{1,0:T(8,128)(2,1)S(1)}, bf16[272,128]{1,0:T(8,128)(2,1)S(1)}, u32[]{:S(2)}, u32[]{:S(2)}) %collective-permute-start.9) | collective-permute-done | bytes 69664 | tf_op jit(solution)/shard_map/ppermute | solution.py:607
  36.0 1.4 %collective-permute-done.10.refs_6_ = bf16[272,128]{1,0:T(8,128)(2,1)S(1)} collective-permute-done((bf16[272,128]{1,0:T(8,128)(2,1)S(1)}, bf16[272,128]{1,0:T(8,128)(2,1)S(1)}, u32[]{:S(2)}, u32[]{:S(2)}) %collective-permute-start.10) | collective-permute-done | bytes 69664 | tf_op jit(solution)/shard_map/ppermute | solution.py:607
  37.4 0.1 collective-permute-start.12
  37.5 1.9 %collective-permute-done.12.refs_8_ = bf16[2176,128]{1,0:T(8,128)(2,1)S(1)} collective-permute-done((bf16[2176,128]{1,0:T(8,128)(2,1)S(1)}, bf16[2176,128]{1,0:T(8,128)(2,1)S(1)}, u32[]{:S(2)}, u32[]{:S(2)}) %collective-permute-start.12) | collective-permute-done | bytes 557088 | tf_op jit(solution)/shard_map/ppermute | solution.py:607
  39.4 4.8 %shard_map.189.refs_0_ = bf16[256,128]{1,0:T(8,128)(2,1)S(1)} custom-call(bf16[272,128]{1,0:T(8,128)(2,1)S(1)} %get-tuple-element.86.refs_0_, bf16[272,128]{1,0:T(8,128)(2,1)S(1)} %collective-permute-done.5.refs_1_, bf16[272,128]{1,0:T(8,128)(2,1)S(1)} %collective-permute-done.6.refs_2_, bf16[272,128]{1,0:T(8,128)(2,1)S(1)} %collective-permute-done.7.refs_3_, ...), custom_call_target="tpu_custom_call" | custom-call | flops 6000000000 | bytes 600000 | tf_op jit(solution)/shard_map/pallas_call | solution.py:577
  44.2 0.7 %collective-permute-start.14 = (bf16[256,128]{1,0:T(8,128)(2,1)S(1)}, bf16[256,128]{1,0:T(8,128)(2,1)S(1)}, u32[]{:S(2)}, u32[]{:S(2)}) collective-permute-start(bf16[256,128]{1,0:T(8,128)(2,1)S(1)} %shard_map.189.refs_0_), channel_id=1, source_target_pairs={{0,8},{4,12},{8,0},{12,4},{1,9},{5,13},{9,1},{13,5},{2,10},{6,14},... | collective-permute-start | bytes 196616 | tf_op jit(solution)/shard_map/ppermute | solution.py:598
  45.0 0.3 shard_map.190.refs_8_
  45.3 0.1 collective-permute-start.13
  45.4 3.2 %collective-permute-done.14.refs_2_ = bf16[256,128]{1,0:T(8,128)(2,1)S(1)} collective-permute-done((bf16[256,128]{1,0:T(8,128)(2,1)S(1)}, bf16[256,128]{1,0:T(8,128)(2,1)S(1)}, u32[]{:S(2)}, u32[]{:S(2)}) %collective-permute-start.14) | collective-permute-done | bytes 65568 | tf_op jit(solution)/shard_map/ppermute | solution.py:598
  48.6 1.2 %collective-permute-done.15.refs_3_ = bf16[256,128]{1,0:T(8,128)(2,1)S(1)} collective-permute-done((bf16[256,128]{1,0:T(8,128)(2,1)S(1)}, bf16[256,128]{1,0:T(8,128)(2,1)S(1)}, u32[]{:S(2)}, u32[]{:S(2)}) %collective-permute-start.15) | collective-permute-done | bytes 65568 | tf_op jit(solution)/shard_map/ppermute | solution.py:598
  49.8 4.0 %shard_map.191 = bf16[512,128]{1,0:T(8,128)(2,1)} custom-call(bf16[256,128]{1,0:T(8,128)(2,1)S(1)} %shard_map.189.refs_0_, bf16[256,128]{1,0:T(8,128)(2,1)S(1)} %collective-permute-done.13.refs_1_, bf16[256,128]{1,0:T(8,128)(2,1)S(1)} %collective-permute-done.14.refs_2_, bf16[256,128]{1,0:T(8,128)(2,1)S(1)} %collective-permute-done.15.refs_3_, ...), custom_call_target="tpu_custom_call" | custom-call | flops 3000000000 | bytes 300000 | tf_op jit(solution)/shard_map/pallas_call | solution.py:577
  (49 shorter events, 0.2 us)
Async XLA Ops:
  0.0 3.2 %copy-start.1 = (bf16[3072,128]{1,0:T(8,128)(2,1)S(1)}, bf16[3072,128]{1,0:T(8,128)(2,1)}, u32[]{:S(2)}) copy-start(bf16[3072,128]{1,0:T(8,128)(2,1)} %refs_11_.2) | copy-start | bytes 2359300
  0.0 3.2 %copy-start.2 = (bf16[5,384,128]{2,1,0:T(8,128)(2,1)S(1)}, bf16[5,384,128]{2,1,0:T(8,128)(2,1)}, u32[]{:S(2)}) copy-start(bf16[5,384,128]{2,1,0:T(8,128)(2,1)} %refs_15_.3) | copy-start | bytes 1474564
  0.0 3.2 %copy-start.4 = (bf16[5,256,128]{2,1,0:T(8,128)(2,1)S(1)}, bf16[5,256,128]{2,1,0:T(8,128)(2,1)}, u32[]{:S(2)}) copy-start(bf16[5,256,128]{2,1,0:T(8,128)(2,1)} %refs_17_.1) | copy-start | bytes 983044
  0.0 3.2 %copy-start.5 = (bf16[5,128,128]{2,1,0:T(8,128)(2,1)S(1)}, bf16[5,128,128]{2,1,0:T(8,128)(2,1)}, u32[]{:S(2)}) copy-start(bf16[5,128,128]{2,1,0:T(8,128)(2,1)} %refs_16_.1) | copy-start | bytes 491524
  0.0 3.2 %copy-start.6 = (bf16[5,128,128]{2,1,0:T(8,128)(2,1)S(1)}, bf16[5,128,128]{2,1,0:T(8,128)(2,1)}, u32[]{:S(2)}) copy-start(bf16[5,128,128]{2,1,0:T(8,128)(2,1)} %refs_18_.1) | copy-start | bytes 491524
  0.0 3.2 %copy-start.7 = (bf16[512,128]{1,0:T(8,128)(2,1)S(1)}, bf16[512,128]{1,0:T(8,128)(2,1)}, u32[]{:S(2)}) copy-start(bf16[512,128]{1,0:T(8,128)(2,1)} %refs_9_.2) | copy-start | bytes 393220
  0.0 3.2 %copy-start.10 = (s32[3072]{0:T(1024)S(1)}, s32[3072]{0:T(1024)}, u32[]{:S(2)}) copy-start(s32[3072]{0:T(1024)} %param.20) | copy-start | bytes 36868
  0.0 3.2 %copy-start.11 = (s32[3072]{0:T(1024)S(1)}, s32[3072]{0:T(1024)}, u32[]{:S(2)}) copy-start(s32[3072]{0:T(1024)} %param.21) | copy-start | bytes 36868
  2.0 3.2 %collective-permute-start = (bf16[80,128]{1,0:T(8,128)(2,1)}, bf16[80,128]{1,0:T(8,128)(2,1)S(1)}, u32[]{:S(2)}, u32[]{:S(2)}) collective-permute-start(bf16[80,128]{1,0:T(8,128)(2,1)} %get-tuple-element.57), channel_id=1, source_target_pairs={{0,4},{4,0},{8,12},{12,8},{1,5},{5,1},{9,13},{13,9},{2,6},{6,2},{1... | collective-permute-start | bytes 61448 | tf_op jit(solution)/shard_map/ppermute | solution.py:668
  2.5 2.6 %collective-permute-start.1 = (bf16[80,128]{1,0:T(8,128)(2,1)}, bf16[80,128]{1,0:T(8,128)(2,1)S(1)}, u32[]{:S(2)}, u32[]{:S(2)}) collective-permute-start(bf16[80,128]{1,0:T(8,128)(2,1)} %get-tuple-element.58), channel_id=1, source_target_pairs={{4,8},{8,4},{5,9},{9,5},{6,10},{10,6},{7,11},{11,7},{20,24},{24,20... | collective-permute-start | bytes 61448 | tf_op jit(solution)/shard_map/ppermute | solution.py:669
  3.3 1.9 %copy-start.14 = (bf16[16,128]{1,0:T(8,128)(2,1)S(1)}, bf16[16,128]{1,0:T(8,128)(2,1)}, u32[]{:S(2)}) copy-start(bf16[16,128]{1,0:T(8,128)(2,1)} %get-tuple-element.60.refs_2_.refs_0_) | copy-start | bytes 12292
  5.2 7.4 %copy-start = (bf16[8192,128]{1,0:T(8,128)(2,1)S(1)}, bf16[8192,128]{1,0:T(8,128)(2,1)}, u32[]{:S(2)}) copy-start(bf16[8192,128]{1,0:T(8,128)(2,1)} %refs_19_.1) | copy-start | bytes 6291460
  5.2 7.4 %copy-start.8 = (s32[8192]{0:T(1024)S(1)}, s32[8192]{0:T(1024)}, u32[]{:S(2)}) copy-start(s32[8192]{0:T(1024)} %param.31) | copy-start | bytes 98308
  5.2 7.4 %copy-start.9 = (s32[8192]{0:T(1024)S(1)}, s32[8192]{0:T(1024)}, u32[]{:S(2)}) copy-start(s32[8192]{0:T(1024)} %param.32) | copy-start | bytes 98308
  7.3 9.5 %collective-permute-start.3 = (bf16[528,128]{1,0:T(8,128)(2,1)S(1)}, bf16[528,128]{1,0:T(8,128)(2,1)S(1)}, u32[]{:S(2)}, u32[]{:S(2)}) collective-permute-start(bf16[528,128]{1,0:T(8,128)(2,1)S(1)} %get-tuple-element.69.refs_0_), channel_id=1, source_target_pairs={{0,8},{4,12},{8,0},{12,4},{1,9},{5,13},{9,1},{13,5},{2,10},{6,14},... | collective-permute-start | bytes 405512 | tf_op jit(solution)/shard_map/ppermute | solution.py:598
  12.6 4.8 %collective-permute-start.2 = (bf16[528,128]{1,0:T(8,128)(2,1)S(1)}, bf16[528,128]{1,0:T(8,128)(2,1)S(1)}, u32[]{:S(2)}, u32[]{:S(2)}) collective-permute-start(bf16[528,128]{1,0:T(8,128)(2,1)S(1)} %get-tuple-element.69.refs_0_), channel_id=1, source_target_pairs={{0,4},{4,0},{8,12},{12,8},{1,5},{5,1},{9,13},{13,9},{2,6},{6,2},{1... | collective-permute-start | bytes 405512 | tf_op jit(solution)/shard_map/ppermute | solution.py:598
  12.6 4.2 %copy-start.3 = (bf16[1536,128]{1,0:T(8,128)(2,1)S(1)}, bf16[1536,128]{1,0:T(8,128)(2,1)}, u32[]{:S(2)}) copy-start(bf16[1536,128]{1,0:T(8,128)(2,1)} %refs_9_.3) | copy-start | bytes 1179652
  12.6 4.2 %copy-start.12 = (s32[1536]{0:T(1024)S(1)}, s32[1536]{0:T(1024)}, u32[]{:S(2)}) copy-start(s32[1536]{0:T(1024)} %param.24) | copy-start | bytes 18436
  12.6 4.2 %copy-start.13 = (s32[1536]{0:T(1024)S(1)}, s32[1536]{0:T(1024)}, u32[]{:S(2)}) copy-start(s32[1536]{0:T(1024)} %param.25) | copy-start | bytes 18436
  16.8 1.4 %collective-permute-start.4 = (bf16[528,128]{1,0:T(8,128)(2,1)S(1)}, bf16[528,128]{1,0:T(8,128)(2,1)S(1)}, u32[]{:S(2)}, u32[]{:S(2)}) collective-permute-start(bf16[528,128]{1,0:T(8,128)(2,1)S(1)} %collective-permute-done.3.refs_2_), channel_id=1, source_target_pairs={{0,4},{4,0},{8,12},{12,8},{1,5},{5,1},{9,13},{13,9},{2,6},{6,2},{1... | collective-permute-start | bytes 405512 | tf_op jit(solution)/shard_map/ppermute | solution.py:598
  20.3 11.2 %collective-permute-start.5 = (bf16[272,128]{1,0:T(8,128)(2,1)S(1)}, bf16[272,128]{1,0:T(8,128)(2,1)S(1)}, u32[]{:S(2)}, u32[]{:S(2)}) collective-permute-start(bf16[272,128]{1,0:T(8,128)(2,1)S(1)} %get-tuple-element.86.refs_0_), channel_id=1, source_target_pairs={{0,1},{1,0},{2,3},{3,2},{4,5},{5,4},{6,7},{7,6},{8,9},{9,8},{10,11... | collective-permute-start | bytes 208904 | tf_op jit(solution)/shard_map/ppermute | solution.py:607
  22.1 10.9 %collective-permute-start.6 = (bf16[272,128]{1,0:T(8,128)(2,1)S(1)}, bf16[272,128]{1,0:T(8,128)(2,1)S(1)}, u32[]{:S(2)}, u32[]{:S(2)}) collective-permute-start(bf16[272,128]{1,0:T(8,128)(2,1)S(1)} %get-tuple-element.86.refs_0_), channel_id=1, source_target_pairs={{0,2},{1,3},{2,0},{3,1},{4,6},{5,7},{6,4},{7,5},{8,10},{9,11},{10,... | collective-permute-start | bytes 208904 | tf_op jit(solution)/shard_map/ppermute | solution.py:607
  24.7 6.2 %collective-permute-start.7 = (bf16[272,128]{1,0:T(8,128)(2,1)S(1)}, bf16[272,128]{1,0:T(8,128)(2,1)S(1)}, u32[]{:S(2)}, u32[]{:S(2)}) collective-permute-start(bf16[272,128]{1,0:T(8,128)(2,1)S(1)} %get-tuple-element.86.refs_0_), channel_id=1, source_target_pairs={{0,3},{1,2},{2,1},{3,0},{4,7},{5,6},{6,5},{7,4},{8,11},{9,10},{10,... | collective-permute-start | bytes 208904 | tf_op jit(solution)/shard_map/ppermute | solution.py:607
  24.7 8.9 %collective-permute-start.8 = (bf16[272,128]{1,0:T(8,128)(2,1)S(1)}, bf16[272,128]{1,0:T(8,128)(2,1)S(1)}, u32[]{:S(2)}, u32[]{:S(2)}) collective-permute-start(bf16[272,128]{1,0:T(8,128)(2,1)S(1)} %get-tuple-element.86.refs_0_), channel_id=1, source_target_pairs={{0,8},{4,12},{8,0},{12,4},{1,9},{5,13},{9,1},{13,5},{2,10},{6,14},... | collective-permute-start | bytes 208904 | tf_op jit(solution)/shard_map/ppermute | solution.py:607
  30.9 6.4 %collective-permute-start.11 = (bf16[272,128]{1,0:T(8,128)(2,1)S(1)}, bf16[272,128]{1,0:T(8,128)(2,1)S(1)}, u32[]{:S(2)}, u32[]{:S(2)}) collective-permute-start(bf16[272,128]{1,0:T(8,128)(2,1)S(1)} %collective-permute-done.7.refs_3_), channel_id=1, source_target_pairs={{0,8},{4,12},{8,0},{12,4},{1,9},{5,13},{9,1},{13,5},{2,10},{6,14},... | collective-permute-start | bytes 208904 | tf_op jit(solution)/shard_map/ppermute | solution.py:607
  31.5 4.5 %collective-permute-start.9 = (bf16[272,128]{1,0:T(8,128)(2,1)S(1)}, bf16[272,128]{1,0:T(8,128)(2,1)S(1)}, u32[]{:S(2)}, u32[]{:S(2)}) collective-permute-start(bf16[272,128]{1,0:T(8,128)(2,1)S(1)} %collective-permute-done.5.refs_1_), channel_id=1, source_target_pairs={{0,8},{4,12},{8,0},{12,4},{1,9},{5,13},{9,1},{13,5},{2,10},{6,14},... | collective-permute-start | bytes 208904 | tf_op jit(solution)/shard_map/ppermute | solution.py:607
  33.0 4.4 %collective-permute-start.10 = (bf16[272,128]{1,0:T(8,128)(2,1)S(1)}, bf16[272,128]{1,0:T(8,128)(2,1)S(1)}, u32[]{:S(2)}, u32[]{:S(2)}) collective-permute-start(bf16[272,128]{1,0:T(8,128)(2,1)S(1)} %collective-permute-done.6.refs_2_), channel_id=1, source_target_pairs={{0,8},{4,12},{8,0},{12,4},{1,9},{5,13},{9,1},{13,5},{2,10},{6,14},... | collective-permute-start | bytes 208904 | tf_op jit(solution)/shard_map/ppermute | solution.py:607
  37.4 2.0 %collective-permute-start.12 = (bf16[2176,128]{1,0:T(8,128)(2,1)S(1)}, bf16[2176,128]{1,0:T(8,128)(2,1)S(1)}, u32[]{:S(2)}, u32[]{:S(2)}) collective-permute-start(bf16[2176,128]{1,0:T(8,128)(2,1)S(1)} %constant_dynamic-update-slice_fusion), channel_id=1, source_target_pairs={{0,4},{4,0},{8,12},{12,8},{1,5},{5,1},{9,13},{13,9},{2,6},{6,2},{1... | collective-permute-start | bytes 1671176 | tf_op jit(solution)/shard_map/ppermute | solution.py:607
  44.2 4.3 %collective-permute-start.14 = (bf16[256,128]{1,0:T(8,128)(2,1)S(1)}, bf16[256,128]{1,0:T(8,128)(2,1)S(1)}, u32[]{:S(2)}, u32[]{:S(2)}) collective-permute-start(bf16[256,128]{1,0:T(8,128)(2,1)S(1)} %shard_map.189.refs_0_), channel_id=1, source_target_pairs={{0,8},{4,12},{8,0},{12,4},{1,9},{5,13},{9,1},{13,5},{2,10},{6,14},... | collective-permute-start | bytes 196616 | tf_op jit(solution)/shard_map/ppermute | solution.py:598
  45.3 3.3 %collective-permute-start.13 = (bf16[256,128]{1,0:T(8,128)(2,1)S(1)}, bf16[256,128]{1,0:T(8,128)(2,1)S(1)}, u32[]{:S(2)}, u32[]{:S(2)}) collective-permute-start(bf16[256,128]{1,0:T(8,128)(2,1)S(1)} %shard_map.189.refs_0_), channel_id=1, source_target_pairs={{0,4},{4,0},{8,12},{12,8},{1,5},{5,1},{9,13},{13,9},{2,6},{6,2},{1... | collective-permute-start | bytes 196616 | tf_op jit(solution)/shard_map/ppermute | solution.py:598
  48.6 1.3 %collective-permute-start.15 = (bf16[256,128]{1,0:T(8,128)(2,1)S(1)}, bf16[256,128]{1,0:T(8,128)(2,1)S(1)}, u32[]{:S(2)}, u32[]{:S(2)}) collective-permute-start(bf16[256,128]{1,0:T(8,128)(2,1)S(1)} %collective-permute-done.14.refs_2_), channel_id=1, source_target_pairs={{0,4},{4,0},{8,12},{12,8},{1,5},{5,1},{9,13},{13,9},{2,6},{6,2},{1... | collective-permute-start | bytes 196616 | tf_op jit(solution)/shard_map/ppermute | solution.py:598

commit v4 on v3

--- a/solution.py
+++ b/solution.py
@@ -59,10 +59,14 @@
 
 
 def gather(row, block, blocks, all_there=False):
-    wide = dot(hot_rows(row, blocks[0].shape[0]), jnp.concatenate(blocks, axis=1))
+    return pick(hot_rows(row, blocks[0].shape[0]), block, blocks, all_there)
+
+
+def pick(hots, block, blocks, all_there=False):
+    wide = dot(hots, jnp.concatenate(blocks, axis=1))
     if block is None:
         return wide
-    out = wide[:, :LANES] if all_there else jnp.zeros((row.shape[0], LANES), F32)
+    out = wide[:, :LANES] if all_there else jnp.zeros((hots.shape[0], LANES), F32)
     for i in range(1 if all_there else 0, len(blocks)):
         out = jnp.where(block == i, wide[:, i * LANES : (i + 1) * LANES], out)
     return out
@@ -78,9 +82,10 @@
 def segment_sum(rows, block, values):
     chosen = hot_cols(jnp.bitwise_and(rows, CUT - 1), CUT)
     if block is None:
-        return dot(chosen, values)
-    upper = values * jnp.where(block == 1, 1.0, 0.0).astype(BF16)
-    out = dot(chosen, jnp.concatenate([values - upper, upper], axis=1))
+        return jnp.concatenate([dot(chosen[: CUT // 2], values), dot(chosen[CUT // 2 :], values)], axis=0)
+    upper = values * block
+    wide = jnp.concatenate([values - upper, upper], axis=1)
+    out = jnp.concatenate([dot(chosen[: CUT // 2], wide), dot(chosen[CUT // 2 :], wide)], axis=0)
     return jnp.concatenate([out[:, :LANES], out[:, LANES:]], axis=0)
 
 
@@ -90,7 +95,7 @@
 
 
 def perceptron(before, centred_second):
-    out = dot(jnp.maximum(before, 0.0).astype(BF16), centred_second)
+    out = dot(jnp.maximum(before.astype(BF16), 0.0), centred_second)
     return out * lax.rsqrt(jnp.mean(out * out, axis=-1, keepdims=True) + EPSILON)
 
 
@@ -106,7 +111,7 @@
 def edge_columns(own, count):
     shape = (count, LANES)
     if own == 2 * CUT:
-        return [(shape, I16), (shape, I16), (shape, I32), (shape, I16), (shape, I32)]
+        return [(shape, I16), (shape, I16), (shape, I32), (shape, I16), (shape, I32), (shape, BF16)]
     return [(shape, I16), (shape, I32), (shape, I16)]
 
 
@@ -115,7 +120,8 @@
     low, high = jnp.bitwise_and(send, CUT - 1), jnp.right_shift(send, CUT_BITS)
     if own == 2 * CUT:
         low = jnp.where(send < own, low, -1)
-        values = [send, low, high, jnp.bitwise_and(recv, CUT - 1), jnp.right_shift(recv, CUT_BITS)]
+        recv_high = jnp.right_shift(recv, CUT_BITS)
+        values = [send, low, high, jnp.bitwise_and(recv, CUT - 1), recv_high, recv_high.astype(F32)]
     else:
         values = [low, high, recv]
     for value, out in zip(values, outs):
@@ -123,7 +129,7 @@
 
 
 def from_own(cols, nodes, first):
-    _, low, high, recv_low, recv_high = cols
+    _, low, high, recv_low, recv_high, _ = cols
     blocks = cut(nodes)
     sent, received = project(blocks, first[:LANES]), project(blocks, first[LANES : 2 * LANES])
     return lambda rows: (
@@ -218,7 +224,7 @@
 
 
 def fine_kernel(halo, paired, crossed, tail, before, *refs):
-    cols, (nodes, receivers, edges, *weights), (payload, new_edges) = refs[:5], refs[5:12], refs[12:]
+    cols, (nodes, receivers, edges, *weights), (payload, new_edges) = refs[:6], refs[6:13], refs[13:]
     nodes = nodes.get()[...]
     fine = nodes.shape[0]
     outer = jnp.concatenate(lower_higher(paired[:halo, :], crossed[:halo, :]), axis=0)
@@ -412,7 +418,7 @@
 
 
 def parent_kernel(regions, halo, coarse, *refs):
-    blocks, (table, parent_rows, parent_blocks) = refs[:regions], refs[regions:]
+    blocks, (table, parent_hots, parent_blocks) = refs[:regions], refs[regions:]
     me = lax.axis_index("region")
     fine = blocks[0].shape[0] - TAIL
     at = row_layout(fine, coarse)
@@ -424,7 +430,7 @@
 
     table[:fine, :] = blocks[0][:fine, :]
     owner = lambda tail: tail[at["dest"] : at["dest"] + f]
-    parent_rows[:fine, :] = columns(tails[0][at["target"] : at["target"] + f])
+    parent_hots[:fine, :] = hot_rows(columns(tails[0][at["target"] : at["target"] + f]), coarse)
     parent_blocks[:fine, :] = jnp.bitwise_xor(columns(owner(tails[0])), me)
     for side, (other, there, tail) in enumerate(near_tails(tails, me, regions)):
         rows = slice(fine + side * halo, fine + (side + 1) * halo)
@@ -436,7 +442,7 @@
         for i in range(f):
             value = value + jnp.where(col == lane_iota(halo, i * LANES), theirs[i : i + 1], 0.0)
         value = jnp.broadcast_to(jnp.sum(value, axis=1, keepdims=True), (halo, LANES)).astype(I32)
-        parent_rows[rows, :] = jnp.bitwise_and(value, coarse - 1)
+        parent_hots[rows, :] = hot_rows(jnp.bitwise_and(value, coarse - 1), coarse)
         block = jnp.bitwise_xor(jnp.right_shift(value, coarse.bit_length() - 1), me)
         parent_blocks[rows, :] = jnp.where(there, block, -1)
         total = jnp.zeros((halo, LANES), F32)
@@ -451,7 +457,7 @@
     return both[:, :LANES], both[:, LANES:]
 
 
-def pooled(cols, blocks, coarse):
+def add_blocks(cols, blocks, coarse, sums):
     c = coarse // LANES
 
     def add(block, sums):
@@ -460,13 +466,26 @@
         more = [sums_and_counts(hot_codes(col, parent), block[:coarse, :]) for col in cols]
         return tuple((total + a, members + b) for (total, members), (a, b) in zip(sums, more))
 
-    sums = tuple((jnp.zeros(col.shape, F32),) * 2 for col in cols)
     if isinstance(blocks, tuple):
         for block in blocks:
             sums = add(block, sums)
-    else:
-        sums = lax.fori_loop(0, blocks.shape[0], lambda n, sums: add(blocks.at[n], sums), sums)
+        return sums
+    return lax.fori_loop(0, blocks.shape[0], lambda n, sums: add(blocks.at[n], sums), sums)
+
+
+def nothing(cols):
+    return tuple((jnp.zeros(col.shape, F32),) * 2 for col in cols)
+
+
+def means(sums):
     return [(total / jnp.maximum(members, 1.0)).astype(BF16) for total, members in sums]
+
+
+def half_kernel(coarse, *refs):
+    blocks, (parents, send, *outs) = refs[:-6], refs[-6:]
+    cols = [parents[...], send[...]]
+    for i, value in enumerate(sum(add_blocks(cols, blocks, coarse, nothing(cols)), ())):
+        outs[i][...] = value
 
 
 def as_rows(col):
@@ -479,11 +498,13 @@
     subs = lax.axis_size("sub")
     if count > 1:
         rows = coarse + TAIL
-        there = [refs[count - 1].at[i * rows : (i + 1) * rows] for i in range(count - 1)]
+        there = tuple(refs[count - 1].at[i * rows : (i + 1) * rows] for i in range(count - 1))
         blocks = tuple((there if j % 2 else refs)[j // 2 * subs + k] for j in range(regions) for k in range(subs))
+        begun = [ref[...] for ref in refs[count : count + 4]]
+        begun, refs = ((begun[0], begun[1]), (begun[2], begun[3])), refs[count + 4 :]
     else:
-        blocks = refs[0]
-    refs = refs[count:]
+        there = blocks = refs[0]
+        begun, refs = None, refs[count:]
     parents, firsts, halo_rows, halo_blocks, ranks, codes, latents, send, recv, recv_rows, all_edges = refs[:11]
     edges, before3, *cols = refs[11:16]
     receivers, top_weights, weights = refs[16], refs[17:21], refs[21:25]
@@ -491,7 +512,8 @@
     me = lax.axis_index("region")
     own_sub = lambda j: blocks[j * subs] if count > 1 else blocks.at[j * subs]
     mine, firsts = parents[...], firsts[...]
-    top_own, from_send = pooled([mine, send[...]], blocks, coarse)
+    cols_here = [mine, send[...]]
+    top_own, from_send = means(add_blocks(cols_here, there, coarse, nothing(cols_here) if begun is None else begun))
     first, second = top_weights[0].get()[...], centre(top_weights[1].get()[...])
     received = dot(top_own, first[LANES : 2 * LANES]).astype(BF16)
     others = jnp.concatenate([first[:LANES], first[2 * LANES :]], axis=0)
@@ -509,7 +531,7 @@
         copy.wait()
         edge, code = compact(b * size, ranks, codes, fallback, size)
         send, recv = ends(code, b * size, left)
-        (from_send,) = pooled([send], blocks, coarse)
+        (from_send,) = means(add_blocks([send], blocks, coarse, nothing([send])))
         agg[...] += one(edge, from_send, recv, as_rows(recv))
         return carry
 
@@ -524,10 +546,10 @@
 
 
 def last_kernel(regions, *refs):
-    blocks, (down, parent_rows, parent_blocks, edges, before, *rest) = refs[:regions], refs[regions:]
-    cols, receivers, weights, out = rest[:5], rest[5], rest[6:10], rest[10]
+    blocks, (down, parent_hots, parent_blocks, edges, before, *rest) = refs[:regions], refs[regions:]
+    cols, receivers, weights, out = rest[:6], rest[6], rest[7:11], rest[11]
     own = out.shape[0]
-    parent = gather(parent_rows[...], parent_blocks[...], [block[...] for block in blocks])
+    parent = pick(parent_hots[...], parent_blocks[...], [block[...] for block in blocks])
     table = (down[...].astype(F32) + parent).astype(BF16)
     first = weights[0].get()[...]
     inner, outside = from_own(cols, table[:own], first), from_halo(cols, table[own:], own, first)
@@ -607,7 +629,7 @@
     swap = lambda array, axis, bits: lax.ppermute(array, axis, [(i, i ^ bits) for i in range(lax.axis_size(axis))])
     turns = [rows] + [swap(rows, "sub", k) for k in range(1, subs)]
     if regions * subs <= 16:
-        turns[-1], beside = lax.optimization_barrier((turns[-1], beside))
+        turns[1], beside = lax.optimization_barrier((turns[1], beside))
         blocks = {0: turns}
         bit = regions // 2
         while bit > 1:
@@ -724,14 +746,21 @@
     table = call(
         functools.partial(parent_kernel, regions, halo, coarse),
         blocks,
-        [(table_shape, BF16), (table_shape, I32), (table_shape, I32)],
+        [(table_shape, BF16), ((table_shape[0], coarse), BF16), (table_shape, I32)],
     )
     before = call(edge_kernel, [coarse_edges2], [(coarse_edges.shape, F32)], one(3))
     blocks2, (table, before) = over_both(payload2, (table, before))
     many = len(blocks2)
+    begun = []
+    if many > 1:
+        begun = call(
+            functools.partial(half_kernel, coarse),
+            blocks2[:-1] + [selected[0], selected[7]],
+            [((wide, LANES), F32)] * 2 + [((size, LANES), F32)] * 2,
+        )
     (coarse_final,) = call(
         functools.partial(top_kernel, regions, halo2, coarse, size, many),
-        blocks2 + [*selected, top_edges, coarse_edges2, *before, *coarse_cols],
+        blocks2 + [*begun, *selected, top_edges, coarse_edges2, *before, *coarse_cols],
         [((coarse, LANES), BF16)],
         plain(coarse_recv) + level(2) + level(3),
         scratch=[
@@ -739,7 +768,7 @@
             pltpu.VMEM(top_edges.shape, BF16),
             pltpu.SemaphoreType.DMA((1,)),
         ],
-        raw=(many + len(selected),),
+        raw=(many + len(begun) + len(selected),),
         cost=6,
     )
     before = call(edge_kernel, [fine_edges2], [(fine_edges.shape, F32)], one(4))

time: 54 us -> 51.2 us (0.948)
  waiting for transfers between devices: 17.4 us -> 13.5 us
  starting transfers between devices: 15.2 us -> 16.6 us
    ppermute x8, waiting for transfers between devices: 10.4 us -> 6.68 us  [over_both(): lax.ppermute(array, axis, [(i, i ^ bits) for i in range(lax.axis_size(axi...]
    ppermute x8, starting transfers between devices: 7.98 us -> 9.08 us  [over_both(): lax.ppermute(array, axis, [(i, i ^ bits) for i in range(lax.axis_size(axi...]
    pallas_call x11 -> x12, Pallas kernels: 20.7 us -> 20.4 us  [call(): pl.pallas_call(body, out_shape=[jax.ShapeDtypeStruct(shape, dtype) for sh...]
  transfers between devices with their start and end apart: 16 -> 16, of which waited for: 8 -> 8; matrix products, arithmetic and copies ran while one was open for 0% -> 0% of each run, Pallas kernels for 11% -> 13%
where the time goes in v4:
time: 51.2 us; the launch traced here: 51 us
  Pallas kernels  20.4 us (40%)
  starting transfers between devices  16.6 us (32%)
  waiting for transfers between devices  13.5 us (26%)
    pallas_call x12, Pallas kernels, call(): pl.pallas_call(body, out_shape=[jax.ShapeDtypeStruct(shape, dtype) for sh...  20.4 us
    ppermute x8, starting transfers between devices, over_both(): lax.ppermute(array, axis, [(i, i ^ bits) for i in range(lax.axis_size(axi...  9.08 us
    ppermute x6, waiting for transfers between devices, over_region(): lax.ppermute(going[j], 'region', [(i, i ^ bit) for i in range(count)])  6.85 us
    ppermute x8, waiting for transfers between devices, over_both(): lax.ppermute(array, axis, [(i, i ^ bits) for i in range(lax.axis_size(axi...  6.68 us
    ppermute x6, starting transfers between devices, over_region(): lax.ppermute(going[j], 'region', [(i, i ^ bit) for i in range(count)])  6.33 us
  transfers between devices with their start and end apart: 16, of which 8 were waited for; matrix products, arithmetic and copies ran while one was open for 0% of the time, Pallas kernels for 13%

profile of v4, /device:TPU:0, one launch (start us, length us, event | category | flops | bytes accessed | tf_op | source)
XLA Modules:
  0.0 51.0 jit_solution(2613585363080502180)
XLA Ops:
  0.0 1.9 %shard_map.181 = (bf16[80,128]{1,0:T(8,128)(2,1)}, bf16[80,128]{1,0:T(8,128)(2,1)}, bf16[16,128]{1,0:T(8,128)(2,1)}) custom-call(bf16[512,128]{1,0:T(8,128)(2,1)} %refs_10_.2, s32[2,64]{1,0:T(2,128)} %refs_1_.3, s32[2,32]{1,0:T(2,128)} %refs_2_.1, s32[4,128]{1,0:T(4,128)} %bitcast.19, s32[4,128]{1,0:T(4,128)} %bitcast.20, s32[2,128]{1,0:T(2,128)} %bitcast.21), custom_call_target="tpu_custom_call" | custom-call | flops 1000000000 | bytes 100000 | tf_op jit(solution)/shard_map/pallas_call | solution.py:599
  2.0 0.5 %collective-permute-start = (bf16[80,128]{1,0:T(8,128)(2,1)}, bf16[80,128]{1,0:T(8,128)(2,1)S(1)}, u32[]{:S(2)}, u32[]{:S(2)}) collective-permute-start(bf16[80,128]{1,0:T(8,128)(2,1)} %get-tuple-element.62), channel_id=1, source_target_pairs={{0,4},{4,0},{8,12},{12,8},{1,5},{5,1},{9,13},{13,9},{2,6},{6,2},{1... | collective-permute-start | bytes 61448 | tf_op jit(solution)/shard_map/ppermute | solution.py:690
  2.5 0.7 %collective-permute-start.1 = (bf16[80,128]{1,0:T(8,128)(2,1)}, bf16[80,128]{1,0:T(8,128)(2,1)S(1)}, u32[]{:S(2)}, u32[]{:S(2)}) collective-permute-start(bf16[80,128]{1,0:T(8,128)(2,1)} %get-tuple-element.63), channel_id=1, source_target_pairs={{4,8},{8,4},{5,9},{9,5},{6,10},{10,6},{7,11},{11,7},{20,24},{24,20... | collective-permute-start | bytes 61448 | tf_op jit(solution)/shard_map/ppermute | solution.py:691
  3.3 1.9 %shard_map.182 = (s16[3072,128]{1,0:T(8,128)(2,1)S(1)}, s16[3072,128]{1,0:T(8,128)(2,1)S(1)}, s32[3072,128]{1,0:T(8,128)S(1)}, s16[3072,128]{1,0:T(8,128)(2,1)S(...) custom-call(bf16[512,128]{1,0:T(8,128)(2,1)S(1)} %copy-done.7, ...), custom_call_target="tpu_custom_call" | custom-call | flops 2000000000 | bytes 200000 | tf_op jit(solution)/shard_map/pallas_call | solution.py:599
  5.2 1.8 %shard_map.183 = (bf16[528,128]{1,0:T(8,128)(2,1)S(1)}, bf16[3072,128]{1,0:T(8,128)(2,1)S(1)}) custom-call(bf16[80,128]{1,0:T(8,128)(2,1)S(1)} %collective-permute-done.refs_0_.refs_1_, bf16[80,128]{1,0:T(8,128)(2,1)S(1)} %collective-permute-done.1.refs_1_.refs_2_, bf16[16,128]{1,0:T(8,128)(2,1)S(1)} %copy-done.14, ...), custom_call_target="tpu_custom_call" | custom-call | flops 3000000000 | bytes 300000 | tf_op jit(solution)/shard_map/pallas_call | solution.py:599
  7.0 4.0 %collective-permute-start.2 = (bf16[528,128]{1,0:T(8,128)(2,1)S(1)}, bf16[528,128]{1,0:T(8,128)(2,1)S(1)}, u32[]{:S(2)}, u32[]{:S(2)}) collective-permute-start(bf16[528,128]{1,0:T(8,128)(2,1)S(1)} %get-tuple-element.75.refs_0_), channel_id=1, source_target_pairs={{0,4},{4,0},{8,12},{12,8},{1,5},{5,1},{9,13},{13,9},{2,6},{6,2},{1... | collective-permute-start | bytes 405512 | tf_op jit(solution)/shard_map/ppermute | solution.py:620
  11.0 1.3 %collective-permute-start.3 = (bf16[528,128]{1,0:T(8,128)(2,1)S(1)}, bf16[528,128]{1,0:T(8,128)(2,1)S(1)}, u32[]{:S(2)}, u32[]{:S(2)}) collective-permute-start(bf16[528,128]{1,0:T(8,128)(2,1)S(1)} %get-tuple-element.75.refs_0_), channel_id=1, source_target_pairs={{0,8},{4,12},{8,0},{12,4},{1,9},{5,13},{9,1},{13,5},{2,10},{6,14},... | collective-permute-start | bytes 405512 | tf_op jit(solution)/shard_map/ppermute | solution.py:620
  12.4 2.4 %shard_map.184 = (s32[384,128]{1,0:T(8,128)S(1)}, s32[3,128]{1,0:T(4,128)S(1)}, s32[64,128]{1,0:T(8,128)S(1)}, s32[64,128]{1,0:T(8,128)S(1)}, s32[64,128]{1,0:T(...) custom-call(bf16[16,128]{1,0:T(8,128)(2,1)S(1)} %copy-done.14, ...), custom_call_target="tpu_custom_call" | custom-call | flops 3000000000 | bytes 300000 | tf_op jit(solution)/shard_map/pallas_call | solution.py:599
  14.7 1.8 %collective-permute-done.3.refs_2_ = bf16[528,128]{1,0:T(8,128)(2,1)S(1)} collective-permute-done((bf16[528,128]{1,0:T(8,128)(2,1)S(1)}, bf16[528,128]{1,0:T(8,128)(2,1)S(1)}, u32[]{:S(2)}, u32[]{:S(2)}) %collective-permute-start.3) | collective-permute-done | bytes 135200 | tf_op jit(solution)/shard_map/ppermute | solution.py:620
  16.6 0.5 shard_map.185
  17.1 0.8 %collective-permute-done.4.refs_3_ = bf16[528,128]{1,0:T(8,128)(2,1)S(1)} collective-permute-done((bf16[528,128]{1,0:T(8,128)(2,1)S(1)}, bf16[528,128]{1,0:T(8,128)(2,1)S(1)}, u32[]{:S(2)}, u32[]{:S(2)}) %collective-permute-start.4) | collective-permute-done | bytes 135200 | tf_op jit(solution)/shard_map/ppermute | solution.py:620
  17.9 2.2 %shard_map.186 = (bf16[272,128]{1,0:T(8,128)(2,1)S(1)}, bf16[1536,128]{1,0:T(8,128)(2,1)S(1)}) custom-call(bf16[528,128]{1,0:T(8,128)(2,1)S(1)} %get-tuple-element.75.refs_0_, bf16[528,128]{1,0:T(8,128)(2,1)S(1)} %collective-permute-done.2.refs_1_, bf16[528,128]{1,0:T(8,128)(2,1)S(1)} %collective-permute-done.3.refs_2_, ...), custom_call_target="tpu_custom_call" | custom-call | flops 3000000000 | bytes 300000 | tf_op jit(solution)/shard_map/pallas_call | solution.py:599
  20.1 1.8 %collective-permute-start.5 = (bf16[272,128]{1,0:T(8,128)(2,1)S(1)}, bf16[272,128]{1,0:T(8,128)(2,1)S(1)}, u32[]{:S(2)}, u32[]{:S(2)}) collective-permute-start(bf16[272,128]{1,0:T(8,128)(2,1)S(1)} %get-tuple-element.92.refs_0_), channel_id=1, source_target_pairs={{0,1},{1,0},{2,3},{3,2},{4,5},{5,4},{6,7},{7,6},{8,9},{9,8},{10,11... | collective-permute-start | bytes 208904 | tf_op jit(solution)/shard_map/ppermute | solution.py:629
  21.9 2.6 %collective-permute-start.6 = (bf16[272,128]{1,0:T(8,128)(2,1)S(1)}, bf16[272,128]{1,0:T(8,128)(2,1)S(1)}, u32[]{:S(2)}, u32[]{:S(2)}) collective-permute-start(bf16[272,128]{1,0:T(8,128)(2,1)S(1)} %get-tuple-element.92.refs_0_), channel_id=1, source_target_pairs={{0,2},{1,3},{2,0},{3,1},{4,6},{5,7},{6,4},{7,5},{8,10},{9,11},{10,... | collective-permute-start | bytes 208904 | tf_op jit(solution)/shard_map/ppermute | solution.py:629
  24.5 1.7 %collective-permute-start.8 = (bf16[272,128]{1,0:T(8,128)(2,1)S(1)}, bf16[272,128]{1,0:T(8,128)(2,1)S(1)}, u32[]{:S(2)}, u32[]{:S(2)}) collective-permute-start(bf16[272,128]{1,0:T(8,128)(2,1)S(1)} %get-tuple-element.92.refs_0_), channel_id=1, source_target_pairs={{0,8},{4,12},{8,0},{12,4},{1,9},{5,13},{9,1},{13,5},{2,10},{6,14},... | collective-permute-start | bytes 208904 | tf_op jit(solution)/shard_map/ppermute | solution.py:629
  26.3 0.2 shard_map.188.refs_25_
  26.5 0.4 shard_map.187
  26.9 0.4 collective-permute-start.9
  27.3 2.4 %collective-permute-done.6.refs_2_ = bf16[272,128]{1,0:T(8,128)(2,1)S(1)} collective-permute-done((bf16[272,128]{1,0:T(8,128)(2,1)S(1)}, bf16[272,128]{1,0:T(8,128)(2,1)S(1)}, u32[]{:S(2)}, u32[]{:S(2)}) %collective-permute-start.6) | collective-permute-done | bytes 69664 | tf_op jit(solution)/shard_map/ppermute | solution.py:629
  29.7 1.5 %collective-permute-start.10 = (bf16[272,128]{1,0:T(8,128)(2,1)S(1)}, bf16[272,128]{1,0:T(8,128)(2,1)S(1)}, u32[]{:S(2)}, u32[]{:S(2)}) collective-permute-start(bf16[272,128]{1,0:T(8,128)(2,1)S(1)} %collective-permute-done.6.refs_2_), channel_id=1, source_target_pairs={{0,8},{4,12},{8,0},{12,4},{1,9},{5,13},{9,1},{13,5},{2,10},{6,14},... | collective-permute-start | bytes 208904 | tf_op jit(solution)/shard_map/ppermute | solution.py:629
  31.3 1.0 %collective-permute-start.11 = (bf16[272,128]{1,0:T(8,128)(2,1)S(1)}, bf16[272,128]{1,0:T(8,128)(2,1)S(1)}, u32[]{:S(2)}, u32[]{:S(2)}) collective-permute-start(bf16[272,128]{1,0:T(8,128)(2,1)S(1)} %collective-permute-done.7.refs_3_), channel_id=1, source_target_pairs={{0,8},{4,12},{8,0},{12,4},{1,9},{5,13},{9,1},{13,5},{2,10},{6,14},... | collective-permute-start | bytes 208904 | tf_op jit(solution)/shard_map/ppermute | solution.py:629
  32.3 1.7 %collective-permute-done.10.refs_6_ = bf16[272,128]{1,0:T(8,128)(2,1)S(1)} collective-permute-done((bf16[272,128]{1,0:T(8,128)(2,1)S(1)}, bf16[272,128]{1,0:T(8,128)(2,1)S(1)}, u32[]{:S(2)}, u32[]{:S(2)}) %collective-permute-start.10) | collective-permute-done | bytes 69664 | tf_op jit(solution)/shard_map/ppermute | solution.py:629
  34.1 1.6 %collective-permute-done.11.refs_7_ = bf16[272,128]{1,0:T(8,128)(2,1)S(1)} collective-permute-done((bf16[272,128]{1,0:T(8,128)(2,1)S(1)}, bf16[272,128]{1,0:T(8,128)(2,1)S(1)}, u32[]{:S(2)}, u32[]{:S(2)}) %collective-permute-start.11) | collective-permute-done | bytes 69664 | tf_op jit(solution)/shard_map/ppermute | solution.py:629
  35.6 0.1 collective-permute-start.12
  35.7 1.0 %shard_map.189 = (f32[384,128]{1,0:T(8,128)S(1)}, f32[384,128]{1,0:T(8,128)S(1)}, f32[384,128]{1,0:T(8,128)S(1)}, f32[384,128]{1,0:T(8,128)S(1)}) custom-call(bf16[272,128]{1,0:T(8,128)(2,1)S(1)} %get-tuple-element.92.refs_0_, bf16[272,128]{1,0:T(8,128)(2,1)S(1)} %collective-permute-done.5.refs_1_, bf16[272,128]{1,0:T(8,128)(2,1)S(1)} %collective-permute-done.6.refs_2_, ...), custom_call_target="tpu_custom_call" | custom-call | flops 1000000000 | bytes 100000 | tf_op jit(solution)/shard_map/pallas_call | solution.py:599
  36.7 1.0 %collective-permute-done.12.refs_8_ = bf16[2176,128]{1,0:T(8,128)(2,1)S(1)} collective-permute-done((bf16[2176,128]{1,0:T(8,128)(2,1)S(1)}, bf16[2176,128]{1,0:T(8,128)(2,1)S(1)}, u32[]{:S(2)}, u32[]{:S(2)}) %collective-permute-start.12) | collective-permute-done | bytes 557088 | tf_op jit(solution)/shard_map/ppermute | solution.py:629
  37.7 4.0 %shard_map.190.refs_0_ = bf16[256,128]{1,0:T(8,128)(2,1)S(1)} custom-call(bf16[272,128]{1,0:T(8,128)(2,1)S(1)} %get-tuple-element.92.refs_0_, bf16[272,128]{1,0:T(8,128)(2,1)S(1)} %collective-permute-done.5.refs_1_, bf16[272,128]{1,0:T(8,128)(2,1)S(1)} %collective-permute-done.6.refs_2_, bf16[272,128]{1,0:T(8,128)(2,1)S(1)} %collective-permute-done.7.refs_3_, ...), custom_call_target="tpu_custom_call" | custom-call | flops 6000000000 | bytes 600000 | tf_op jit(solution)/shard_map/pallas_call | solution.py:599
  41.7 1.0 %collective-permute-start.14 = (bf16[256,128]{1,0:T(8,128)(2,1)S(1)}, bf16[256,128]{1,0:T(8,128)(2,1)S(1)}, u32[]{:S(2)}, u32[]{:S(2)}) collective-permute-start(bf16[256,128]{1,0:T(8,128)(2,1)S(1)} %shard_map.190.refs_0_), channel_id=1, source_target_pairs={{0,8},{4,12},{8,0},{12,4},{1,9},{5,13},{9,1},{13,5},{2,10},{6,14},... | collective-permute-start | bytes 196616 | tf_op jit(solution)/shard_map/ppermute | solution.py:620
  42.7 0.3 shard_map.191.refs_8_
  43.1 2.9 %collective-permute-done.14.refs_2_ = bf16[256,128]{1,0:T(8,128)(2,1)S(1)} collective-permute-done((bf16[256,128]{1,0:T(8,128)(2,1)S(1)}, bf16[256,128]{1,0:T(8,128)(2,1)S(1)}, u32[]{:S(2)}, u32[]{:S(2)}) %collective-permute-start.14) | collective-permute-done | bytes 65568 | tf_op jit(solution)/shard_map/ppermute | solution.py:620
  46.0 1.2 %collective-permute-done.15.refs_3_ = bf16[256,128]{1,0:T(8,128)(2,1)S(1)} collective-permute-done((bf16[256,128]{1,0:T(8,128)(2,1)S(1)}, bf16[256,128]{1,0:T(8,128)(2,1)S(1)}, u32[]{:S(2)}, u32[]{:S(2)}) %collective-permute-start.15) | collective-permute-done | bytes 65568 | tf_op jit(solution)/shard_map/ppermute | solution.py:620
  47.3 3.7 %shard_map.192 = bf16[512,128]{1,0:T(8,128)(2,1)} custom-call(bf16[256,128]{1,0:T(8,128)(2,1)S(1)} %shard_map.190.refs_0_, bf16[256,128]{1,0:T(8,128)(2,1)S(1)} %collective-permute-done.13.refs_1_, bf16[256,128]{1,0:T(8,128)(2,1)S(1)} %collective-permute-done.14.refs_2_, bf16[256,128]{1,0:T(8,128)(2,1)S(1)} %collective-permute-done.15.refs_3_, ...), custom_call_target="tpu_custom_call" | custom-call | flops 3000000000 | bytes 300000 | tf_op jit(solution)/shard_map/pallas_call | solution.py:599
  (50 shorter events, 0.3 us)
Async XLA Ops:
  0.0 3.2 %copy-start.1 = (bf16[3072,128]{1,0:T(8,128)(2,1)S(1)}, bf16[3072,128]{1,0:T(8,128)(2,1)}, u32[]{:S(2)}) copy-start(bf16[3072,128]{1,0:T(8,128)(2,1)} %refs_12_.2) | copy-start | bytes 2359300
  0.0 3.2 %copy-start.2 = (bf16[5,384,128]{2,1,0:T(8,128)(2,1)S(1)}, bf16[5,384,128]{2,1,0:T(8,128)(2,1)}, u32[]{:S(2)}) copy-start(bf16[5,384,128]{2,1,0:T(8,128)(2,1)} %refs_16_.3) | copy-start | bytes 1474564
  0.0 3.2 %copy-start.4 = (bf16[5,256,128]{2,1,0:T(8,128)(2,1)S(1)}, bf16[5,256,128]{2,1,0:T(8,128)(2,1)}, u32[]{:S(2)}) copy-start(bf16[5,256,128]{2,1,0:T(8,128)(2,1)} %refs_18_.1) | copy-start | bytes 983044
  0.0 3.2 %copy-start.5 = (bf16[5,128,128]{2,1,0:T(8,128)(2,1)S(1)}, bf16[5,128,128]{2,1,0:T(8,128)(2,1)}, u32[]{:S(2)}) copy-start(bf16[5,128,128]{2,1,0:T(8,128)(2,1)} %refs_17_.1) | copy-start | bytes 491524
  0.0 3.2 %copy-start.6 = (bf16[5,128,128]{2,1,0:T(8,128)(2,1)S(1)}, bf16[5,128,128]{2,1,0:T(8,128)(2,1)}, u32[]{:S(2)}) copy-start(bf16[5,128,128]{2,1,0:T(8,128)(2,1)} %refs_19_.1) | copy-start | bytes 491524
  0.0 3.2 %copy-start.7 = (bf16[512,128]{1,0:T(8,128)(2,1)S(1)}, bf16[512,128]{1,0:T(8,128)(2,1)}, u32[]{:S(2)}) copy-start(bf16[512,128]{1,0:T(8,128)(2,1)} %refs_10_.2) | copy-start | bytes 393220
  0.0 3.2 %copy-start.10 = (s32[3072]{0:T(1024)S(1)}, s32[3072]{0:T(1024)}, u32[]{:S(2)}) copy-start(s32[3072]{0:T(1024)} %param.20) | copy-start | bytes 36868
  0.0 3.2 %copy-start.11 = (s32[3072]{0:T(1024)S(1)}, s32[3072]{0:T(1024)}, u32[]{:S(2)}) copy-start(s32[3072]{0:T(1024)} %param.21) | copy-start | bytes 36868
  2.0 3.2 %collective-permute-start = (bf16[80,128]{1,0:T(8,128)(2,1)}, bf16[80,128]{1,0:T(8,128)(2,1)S(1)}, u32[]{:S(2)}, u32[]{:S(2)}) collective-permute-start(bf16[80,128]{1,0:T(8,128)(2,1)} %get-tuple-element.62), channel_id=1, source_target_pairs={{0,4},{4,0},{8,12},{12,8},{1,5},{5,1},{9,13},{13,9},{2,6},{6,2},{1... | collective-permute-start | bytes 61448 | tf_op jit(solution)/shard_map/ppermute | solution.py:690
  2.5 2.7 %collective-permute-start.1 = (bf16[80,128]{1,0:T(8,128)(2,1)}, bf16[80,128]{1,0:T(8,128)(2,1)S(1)}, u32[]{:S(2)}, u32[]{:S(2)}) collective-permute-start(bf16[80,128]{1,0:T(8,128)(2,1)} %get-tuple-element.63), channel_id=1, source_target_pairs={{4,8},{8,4},{5,9},{9,5},{6,10},{10,6},{7,11},{11,7},{20,24},{24,20... | collective-permute-start | bytes 61448 | tf_op jit(solution)/shard_map/ppermute | solution.py:691
  3.3 1.9 %copy-start.14 = (bf16[16,128]{1,0:T(8,128)(2,1)S(1)}, bf16[16,128]{1,0:T(8,128)(2,1)}, u32[]{:S(2)}) copy-start(bf16[16,128]{1,0:T(8,128)(2,1)} %get-tuple-element.65.refs_2_.refs_0_) | copy-start | bytes 12292
  5.2 7.1 %copy-start = (bf16[8192,128]{1,0:T(8,128)(2,1)S(1)}, bf16[8192,128]{1,0:T(8,128)(2,1)}, u32[]{:S(2)}) copy-start(bf16[8192,128]{1,0:T(8,128)(2,1)} %refs_23_.1) | copy-start | bytes 6291460
  5.2 7.1 %copy-start.8 = (s32[8192]{0:T(1024)S(1)}, s32[8192]{0:T(1024)}, u32[]{:S(2)}) copy-start(s32[8192]{0:T(1024)} %param.31) | copy-start | bytes 98308
  5.2 7.1 %copy-start.9 = (s32[8192]{0:T(1024)S(1)}, s32[8192]{0:T(1024)}, u32[]{:S(2)}) copy-start(s32[8192]{0:T(1024)} %param.32) | copy-start | bytes 98308
  7.0 10.1 %collective-permute-start.2 = (bf16[528,128]{1,0:T(8,128)(2,1)S(1)}, bf16[528,128]{1,0:T(8,128)(2,1)S(1)}, u32[]{:S(2)}, u32[]{:S(2)}) collective-permute-start(bf16[528,128]{1,0:T(8,128)(2,1)S(1)} %get-tuple-element.75.refs_0_), channel_id=1, source_target_pairs={{0,4},{4,0},{8,12},{12,8},{1,5},{5,1},{9,13},{13,9},{2,6},{6,2},{1... | collective-permute-start | bytes 405512 | tf_op jit(solution)/shard_map/ppermute | solution.py:620
  11.0 5.6 %collective-permute-start.3 = (bf16[528,128]{1,0:T(8,128)(2,1)S(1)}, bf16[528,128]{1,0:T(8,128)(2,1)S(1)}, u32[]{:S(2)}, u32[]{:S(2)}) collective-permute-start(bf16[528,128]{1,0:T(8,128)(2,1)S(1)} %get-tuple-element.75.refs_0_), channel_id=1, source_target_pairs={{0,8},{4,12},{8,0},{12,4},{1,9},{5,13},{9,1},{13,5},{2,10},{6,14},... | collective-permute-start | bytes 405512 | tf_op jit(solution)/shard_map/ppermute | solution.py:620
  12.3 4.3 %copy-start.3 = (bf16[1536,128]{1,0:T(8,128)(2,1)S(1)}, bf16[1536,128]{1,0:T(8,128)(2,1)}, u32[]{:S(2)}) copy-start(bf16[1536,128]{1,0:T(8,128)(2,1)} %refs_9_.1) | copy-start | bytes 1179652
  12.3 4.2 %copy-start.12 = (s32[1536]{0:T(1024)S(1)}, s32[1536]{0:T(1024)}, u32[]{:S(2)}) copy-start(s32[1536]{0:T(1024)} %param.24) | copy-start | bytes 18436
  12.3 4.2 %copy-start.13 = (s32[1536]{0:T(1024)S(1)}, s32[1536]{0:T(1024)}, u32[]{:S(2)}) copy-start(s32[1536]{0:T(1024)} %param.25) | copy-start | bytes 18436
  16.6 1.4 %collective-permute-start.4 = (bf16[528,128]{1,0:T(8,128)(2,1)S(1)}, bf16[528,128]{1,0:T(8,128)(2,1)S(1)}, u32[]{:S(2)}, u32[]{:S(2)}) collective-permute-start(bf16[528,128]{1,0:T(8,128)(2,1)S(1)} %collective-permute-done.3.refs_2_), channel_id=1, source_target_pairs={{0,4},{4,0},{8,12},{12,8},{1,5},{5,1},{9,13},{13,9},{2,6},{6,2},{1... | collective-permute-start | bytes 405512 | tf_op jit(solution)/shard_map/ppermute | solution.py:620
  20.1 6.8 %collective-permute-start.5 = (bf16[272,128]{1,0:T(8,128)(2,1)S(1)}, bf16[272,128]{1,0:T(8,128)(2,1)S(1)}, u32[]{:S(2)}, u32[]{:S(2)}) collective-permute-start(bf16[272,128]{1,0:T(8,128)(2,1)S(1)} %get-tuple-element.92.refs_0_), channel_id=1, source_target_pairs={{0,1},{1,0},{2,3},{3,2},{4,5},{5,4},{6,7},{7,6},{8,9},{9,8},{10,11... | collective-permute-start | bytes 208904 | tf_op jit(solution)/shard_map/ppermute | solution.py:629
  21.9 7.8 %collective-permute-start.6 = (bf16[272,128]{1,0:T(8,128)(2,1)S(1)}, bf16[272,128]{1,0:T(8,128)(2,1)S(1)}, u32[]{:S(2)}, u32[]{:S(2)}) collective-permute-start(bf16[272,128]{1,0:T(8,128)(2,1)S(1)} %get-tuple-element.92.refs_0_), channel_id=1, source_target_pairs={{0,2},{1,3},{2,0},{3,1},{4,6},{5,7},{6,4},{7,5},{8,10},{9,11},{10,... | collective-permute-start | bytes 208904 | tf_op jit(solution)/shard_map/ppermute | solution.py:629
  24.5 6.7 %collective-permute-start.7 = (bf16[272,128]{1,0:T(8,128)(2,1)S(1)}, bf16[272,128]{1,0:T(8,128)(2,1)S(1)}, u32[]{:S(2)}, u32[]{:S(2)}) collective-permute-start(bf16[272,128]{1,0:T(8,128)(2,1)S(1)} %get-tuple-element.92.refs_0_), channel_id=1, source_target_pairs={{0,3},{1,2},{2,1},{3,0},{4,7},{5,6},{6,5},{7,4},{8,11},{9,10},{10,... | collective-permute-start | bytes 208904 | tf_op jit(solution)/shard_map/ppermute | solution.py:629
  24.5 7.7 %collective-permute-start.8 = (bf16[272,128]{1,0:T(8,128)(2,1)S(1)}, bf16[272,128]{1,0:T(8,128)(2,1)S(1)}, u32[]{:S(2)}, u32[]{:S(2)}) collective-permute-start(bf16[272,128]{1,0:T(8,128)(2,1)S(1)} %get-tuple-element.92.refs_0_), channel_id=1, source_target_pairs={{0,8},{4,12},{8,0},{12,4},{1,9},{5,13},{9,1},{13,5},{2,10},{6,14},... | collective-permute-start | bytes 208904 | tf_op jit(solution)/shard_map/ppermute | solution.py:629
  26.9 5.4 %collective-permute-start.9 = (bf16[272,128]{1,0:T(8,128)(2,1)S(1)}, bf16[272,128]{1,0:T(8,128)(2,1)S(1)}, u32[]{:S(2)}, u32[]{:S(2)}) collective-permute-start(bf16[272,128]{1,0:T(8,128)(2,1)S(1)} %collective-permute-done.5.refs_1_), channel_id=1, source_target_pairs={{0,8},{4,12},{8,0},{12,4},{1,9},{5,13},{9,1},{13,5},{2,10},{6,14},... | collective-permute-start | bytes 208904 | tf_op jit(solution)/shard_map/ppermute | solution.py:629
  29.7 4.3 %collective-permute-start.10 = (bf16[272,128]{1,0:T(8,128)(2,1)S(1)}, bf16[272,128]{1,0:T(8,128)(2,1)S(1)}, u32[]{:S(2)}, u32[]{:S(2)}) collective-permute-start(bf16[272,128]{1,0:T(8,128)(2,1)S(1)} %collective-permute-done.6.refs_2_), channel_id=1, source_target_pairs={{0,8},{4,12},{8,0},{12,4},{1,9},{5,13},{9,1},{13,5},{2,10},{6,14},... | collective-permute-start | bytes 208904 | tf_op jit(solution)/shard_map/ppermute | solution.py:629
  31.3 4.4 %collective-permute-start.11 = (bf16[272,128]{1,0:T(8,128)(2,1)S(1)}, bf16[272,128]{1,0:T(8,128)(2,1)S(1)}, u32[]{:S(2)}, u32[]{:S(2)}) collective-permute-start(bf16[272,128]{1,0:T(8,128)(2,1)S(1)} %collective-permute-done.7.refs_3_), channel_id=1, source_target_pairs={{0,8},{4,12},{8,0},{12,4},{1,9},{5,13},{9,1},{13,5},{2,10},{6,14},... | collective-permute-start | bytes 208904 | tf_op jit(solution)/shard_map/ppermute | solution.py:629
  35.6 2.0 %collective-permute-start.12 = (bf16[2176,128]{1,0:T(8,128)(2,1)S(1)}, bf16[2176,128]{1,0:T(8,128)(2,1)S(1)}, u32[]{:S(2)}, u32[]{:S(2)}) collective-permute-start(bf16[2176,128]{1,0:T(8,128)(2,1)S(1)} %constant_dynamic-update-slice_fusion), channel_id=1, source_target_pairs={{0,4},{4,0},{8,12},{12,8},{1,5},{5,1},{9,13},{13,9},{2,6},{6,2},{1... | collective-permute-start | bytes 1671176 | tf_op jit(solution)/shard_map/ppermute | solution.py:629
  41.7 4.3 %collective-permute-start.14 = (bf16[256,128]{1,0:T(8,128)(2,1)S(1)}, bf16[256,128]{1,0:T(8,128)(2,1)S(1)}, u32[]{:S(2)}, u32[]{:S(2)}) collective-permute-start(bf16[256,128]{1,0:T(8,128)(2,1)S(1)} %shard_map.190.refs_0_), channel_id=1, source_target_pairs={{0,8},{4,12},{8,0},{12,4},{1,9},{5,13},{9,1},{13,5},{2,10},{6,14},... | collective-permute-start | bytes 196616 | tf_op jit(solution)/shard_map/ppermute | solution.py:620
  43.0 3.0 %collective-permute-start.13 = (bf16[256,128]{1,0:T(8,128)(2,1)S(1)}, bf16[256,128]{1,0:T(8,128)(2,1)S(1)}, u32[]{:S(2)}, u32[]{:S(2)}) collective-permute-start(bf16[256,128]{1,0:T(8,128)(2,1)S(1)} %shard_map.190.refs_0_), channel_id=1, source_target_pairs={{0,4},{4,0},{8,12},{12,8},{1,5},{5,1},{9,13},{13,9},{2,6},{6,2},{1... | collective-permute-start | bytes 196616 | tf_op jit(solution)/shard_map/ppermute | solution.py:620
  46.0 1.3 %collective-permute-start.15 = (bf16[256,128]{1,0:T(8,128)(2,1)S(1)}, bf16[256,128]{1,0:T(8,128)(2,1)S(1)}, u32[]{:S(2)}, u32[]{:S(2)}) collective-permute-start(bf16[256,128]{1,0:T(8,128)(2,1)S(1)} %collective-permute-done.14.refs_2_), channel_id=1, source_target_pairs={{0,4},{4,0},{8,12},{12,8},{1,5},{5,1},{9,13},{13,9},{2,6},{6,2},{1... | collective-permute-start | bytes 196616 | tf_op jit(solution)/shard_map/ppermute | solution.py:620

commit v5 on v4

--- a/solution.py
+++ b/solution.py
@@ -100,8 +100,8 @@
 
 
 def node_update(nodes, summed, first, second):
-    joined = jnp.concatenate([nodes, summed.astype(BF16)], axis=1)
-    return (nodes.astype(F32) + perceptron(dot(joined, first), centre(second))).astype(BF16)
+    before = dot(nodes, first[:LANES]) + dot(summed.astype(BF16), first[LANES:])
+    return (nodes.astype(F32) + perceptron(before, centre(second))).astype(BF16)
 
 
 def project(blocks, matrix):
@@ -514,6 +514,8 @@
     mine, firsts = parents[...], firsts[...]
     cols_here = [mine, send[...]]
     top_own, from_send = means(add_blocks(cols_here, there, coarse, nothing(cols_here) if begun is None else begun))
+    near = gather(halo_rows[...], halo_blocks[...], [own_sub(j)[:coarse, :] for j in range(regions)])
+    down = jnp.concatenate([own_sub(0)[:coarse, :].astype(F32), near], axis=0)
     first, second = top_weights[0].get()[...], centre(top_weights[1].get()[...])
     received = dot(top_own, first[LANES : 2 * LANES]).astype(BF16)
     others = jnp.concatenate([first[:LANES], first[2 * LANES :]], axis=0)
@@ -529,17 +531,15 @@
         copy = pltpu.make_async_copy(all_edges, fallback, semaphore.at[0])
         copy.start()
         copy.wait()
-        edge, code = compact(b * size, ranks, codes, fallback, size)
-        send, recv = ends(code, b * size, left)
+        edge, code = compact(b * LANES, ranks, codes, fallback, LANES)
+        send, recv = ends(code, b * LANES, left)
         (from_send,) = means(add_blocks([send], blocks, coarse, nothing([send])))
         agg[...] += one(edge, from_send, recv, as_rows(recv))
         return carry
 
     left = jnp.max(ranks[...]) + 1
-    lax.fori_loop(0, (left + size - 1) // size, more, 0)
+    lax.fori_loop(0, (left + LANES - 1) // LANES, more, 0)
     top_final = node_update(top_own, agg[...], top_weights[2].get()[...], top_weights[3].get()[...])
-    near = gather(halo_rows[...], halo_blocks[...], [own_sub(j)[:coarse, :] for j in range(regions)])
-    down = jnp.concatenate([own_sub(0)[:coarse, :].astype(F32), near], axis=0)
     table = (down + top_final[: coarse + 2 * halo].astype(F32)).astype(BF16)
     inner = from_table(cols, table, weights[0].get()[...])
     out[...] = finish(lambda rows: before3[rows, :] + inner(rows), table[:coarse], receivers, None, edges, weights)
@@ -614,8 +614,8 @@
     while bit:
         going = dict(blocks)
         if beside is not None and len(going) > 1:
-            far = max(going)
-            going[far], beside = lax.optimization_barrier((going[far], beside))
+            for j in (0, max(going)):
+                going[j], beside = lax.optimization_barrier((going[j], beside))
         for j in blocks:
             going[j + bit] = lax.ppermute(going[j], "region", [(i, i ^ bit) for i in range(count)])
         blocks = going

time: 51.2 us -> 50.6 us (0.988)
  starting transfers between devices: 16.6 us -> 16 us
    ppermute x8, starting transfers between devices: 9.08 us -> 8.32 us  [over_both(): lax.ppermute(array, axis, [(i, i ^ bits) for i in range(lax.axis_size(axi...]
  transfers between devices with their start and end apart: 16 -> 16, of which waited for: 8 -> 9; matrix products, arithmetic and copies ran while one was open for 0% -> 0% of each run, Pallas kernels for 13% -> 13%
where the time goes in v5:
time: 50.6 us; the launch traced here: 50.5 us
  Pallas kernels  20.5 us (41%)
  starting transfers between devices  16 us (32%)
  waiting for transfers between devices  13.4 us (26%)
    pallas_call x12, Pallas kernels, call(): pl.pallas_call(body, out_shape=[jax.ShapeDtypeStruct(shape, dtype) for sh...  20.5 us
    ppermute x8, starting transfers between devices, over_both(): lax.ppermute(array, axis, [(i, i ^ bits) for i in range(lax.axis_size(axi...  8.32 us
    ppermute x8, waiting for transfers between devices, over_both(): lax.ppermute(array, axis, [(i, i ^ bits) for i in range(lax.axis_size(axi...  6.85 us
    ppermute x6, waiting for transfers between devices, over_region(): lax.ppermute(going[j], 'region', [(i, i ^ bit) for i in range(count)])  6.56 us
    ppermute x6, starting transfers between devices, over_region(): lax.ppermute(going[j], 'region', [(i, i ^ bit) for i in range(count)])  6.54 us
  transfers between devices with their start and end apart: 16, of which 9 were waited for; matrix products, arithmetic and copies ran while one was open for 0% of the time, Pallas kernels for 13%

profile of v5, /device:TPU:0, one launch (start us, length us, event | category | flops | bytes accessed | tf_op | source)
XLA Modules:
  0.0 50.5 jit_solution(712691848634761369)
XLA Ops:
  0.0 1.9 %shard_map.181 = (bf16[80,128]{1,0:T(8,128)(2,1)}, bf16[80,128]{1,0:T(8,128)(2,1)}, bf16[16,128]{1,0:T(8,128)(2,1)}) custom-call(bf16[512,128]{1,0:T(8,128)(2,1)} %refs_10_.2, s32[2,64]{1,0:T(2,128)} %refs_1_.3, s32[2,32]{1,0:T(2,128)} %refs_2_.1, s32[4,128]{1,0:T(4,128)} %bitcast.19, s32[4,128]{1,0:T(4,128)} %bitcast.20, s32[2,128]{1,0:T(2,128)} %bitcast.21), custom_call_target="tpu_custom_call" | custom-call | flops 1000000000 | bytes 100000 | tf_op jit(solution)/shard_map/pallas_call | solution.py:599
  2.0 0.5 %collective-permute-start = (bf16[80,128]{1,0:T(8,128)(2,1)}, bf16[80,128]{1,0:T(8,128)(2,1)S(1)}, u32[]{:S(2)}, u32[]{:S(2)}) collective-permute-start(bf16[80,128]{1,0:T(8,128)(2,1)} %get-tuple-element.75), channel_id=1, source_target_pairs={{0,4},{4,0},{8,12},{12,8},{1,5},{5,1},{9,13},{13,9},{2,6},{6,2},{1... | collective-permute-start | bytes 61448 | tf_op jit(solution)/shard_map/ppermute | solution.py:690
  2.5 0.7 %collective-permute-start.1 = (bf16[80,128]{1,0:T(8,128)(2,1)}, bf16[80,128]{1,0:T(8,128)(2,1)S(1)}, u32[]{:S(2)}, u32[]{:S(2)}) collective-permute-start(bf16[80,128]{1,0:T(8,128)(2,1)} %get-tuple-element.76), channel_id=1, source_target_pairs={{4,8},{8,4},{5,9},{9,5},{6,10},{10,6},{7,11},{11,7},{20,24},{24,20... | collective-permute-start | bytes 61448 | tf_op jit(solution)/shard_map/ppermute | solution.py:691
  3.3 1.9 %shard_map.182 = (s16[3072,128]{1,0:T(8,128)(2,1)S(1)}, s16[3072,128]{1,0:T(8,128)(2,1)S(1)}, s32[3072,128]{1,0:T(8,128)S(1)}, s16[3072,128]{1,0:T(8,128)(2,1)S(...) custom-call(bf16[512,128]{1,0:T(8,128)(2,1)S(1)} %copy-done.7, ...), custom_call_target="tpu_custom_call" | custom-call | flops 2000000000 | bytes 200000 | tf_op jit(solution)/shard_map/pallas_call | solution.py:599
  5.2 1.8 %shard_map.183 = (bf16[528,128]{1,0:T(8,128)(2,1)S(1)}, bf16[3072,128]{1,0:T(8,128)(2,1)S(1)}) custom-call(bf16[80,128]{1,0:T(8,128)(2,1)S(1)} %collective-permute-done.refs_0_.refs_1_, bf16[80,128]{1,0:T(8,128)(2,1)S(1)} %collective-permute-done.1.refs_1_.refs_2_, bf16[16,128]{1,0:T(8,128)(2,1)S(1)} %copy-done.14, ...), custom_call_target="tpu_custom_call" | custom-call | flops 3000000000 | bytes 300000 | tf_op jit(solution)/shard_map/pallas_call | solution.py:599
  7.1 5.2 %collective-permute-start.3 = (bf16[528,128]{1,0:T(8,128)(2,1)S(1)}, bf16[528,128]{1,0:T(8,128)(2,1)S(1)}, u32[]{:S(2)}, u32[]{:S(2)}) collective-permute-start(bf16[528,128]{1,0:T(8,128)(2,1)S(1)} %get-tuple-element.99.refs_0_), channel_id=1, source_target_pairs={{0,8},{4,12},{8,0},{12,4},{1,9},{5,13},{9,1},{13,5},{2,10},{6,14},... | collective-permute-start | bytes 405512 | tf_op jit(solution)/shard_map/ppermute | solution.py:620
  12.3 2.4 %shard_map.184 = (s32[384,128]{1,0:T(8,128)S(1)}, s32[3,128]{1,0:T(4,128)S(1)}, s32[64,128]{1,0:T(8,128)S(1)}, s32[64,128]{1,0:T(8,128)S(1)}, s32[64,128]{1,0:T(...) custom-call(bf16[16,128]{1,0:T(8,128)(2,1)S(1)} %copy-done.14, ...), custom_call_target="tpu_custom_call" | custom-call | flops 3000000000 | bytes 300000 | tf_op jit(solution)/shard_map/pallas_call | solution.py:599
  14.7 1.8 %collective-permute-done.3.refs_2_ = bf16[528,128]{1,0:T(8,128)(2,1)S(1)} collective-permute-done((bf16[528,128]{1,0:T(8,128)(2,1)S(1)}, bf16[528,128]{1,0:T(8,128)(2,1)S(1)}, u32[]{:S(2)}, u32[]{:S(2)}) %collective-permute-start.3) | collective-permute-done | bytes 135200 | tf_op jit(solution)/shard_map/ppermute | solution.py:620
  16.5 0.5 %shard_map.185 = (s16[1536,128]{1,0:T(8,128)(2,1)S(1)}, s32[1536,128]{1,0:T(8,128)S(1)}, s16[1536,128]{1,0:T(8,128)(2,1)S(1)}, f32[1536,128]{1,0:T(8,128)S(1)}) custom-call(s32[12,128]{1,0:T(8,128)S(1)} %bitcast.15, s32[12,128]{1,0:T(8,128)S(1)} %bitcast.16, bf16[1536,128]{1,0:T(8,128)(2,1)S(1)} %copy-done.3, bf16[5,384,128]{2,1,0:T(8,128)(2,1)S(1)} %copy-done.2), custom_call_target="tpu_custom_call" | custom-call | flops 1000000000 | bytes 100000 | tf_op jit(solution)/shard_map/pallas_call | solution.py:599
  17.1 0.8 %collective-permute-done.4.refs_3_ = bf16[528,128]{1,0:T(8,128)(2,1)S(1)} collective-permute-done((bf16[528,128]{1,0:T(8,128)(2,1)S(1)}, bf16[528,128]{1,0:T(8,128)(2,1)S(1)}, u32[]{:S(2)}, u32[]{:S(2)}) %collective-permute-start.4) | collective-permute-done | bytes 135200 | tf_op jit(solution)/shard_map/ppermute | solution.py:620
  17.9 2.2 %shard_map.186 = (bf16[272,128]{1,0:T(8,128)(2,1)S(1)}, bf16[1536,128]{1,0:T(8,128)(2,1)S(1)}) custom-call(bf16[528,128]{1,0:T(8,128)(2,1)S(1)} %get-tuple-element.99.refs_0_, bf16[528,128]{1,0:T(8,128)(2,1)S(1)} %collective-permute-done.2.refs_1_, bf16[528,128]{1,0:T(8,128)(2,1)S(1)} %collective-permute-done.3.refs_2_, ...), custom_call_target="tpu_custom_call" | custom-call | flops 3000000000 | bytes 300000 | tf_op jit(solution)/shard_map/pallas_call | solution.py:599
  20.1 1.8 %collective-permute-start.5 = (bf16[272,128]{1,0:T(8,128)(2,1)S(1)}, bf16[272,128]{1,0:T(8,128)(2,1)S(1)}, u32[]{:S(2)}, u32[]{:S(2)}) collective-permute-start(bf16[272,128]{1,0:T(8,128)(2,1)S(1)} %get-tuple-element.116.refs_0_), channel_id=1, source_target_pairs={{0,1},{1,0},{2,3},{3,2},{4,5},{5,4},{6,7},{7,6},{8,9},{9,8},{10,11... | collective-permute-start | bytes 208904 | tf_op jit(solution)/shard_map/ppermute | solution.py:629
  21.9 2.6 %collective-permute-start.6 = (bf16[272,128]{1,0:T(8,128)(2,1)S(1)}, bf16[272,128]{1,0:T(8,128)(2,1)S(1)}, u32[]{:S(2)}, u32[]{:S(2)}) collective-permute-start(bf16[272,128]{1,0:T(8,128)(2,1)S(1)} %get-tuple-element.116.refs_0_), channel_id=1, source_target_pairs={{0,2},{1,3},{2,0},{3,1},{4,6},{5,7},{6,4},{7,5},{8,10},{9,11},{10,... | collective-permute-start | bytes 208904 | tf_op jit(solution)/shard_map/ppermute | solution.py:629
  24.5 0.8 %collective-permute-start.8 = (bf16[272,128]{1,0:T(8,128)(2,1)S(1)}, bf16[272,128]{1,0:T(8,128)(2,1)S(1)}, u32[]{:S(2)}, u32[]{:S(2)}) collective-permute-start(bf16[272,128]{1,0:T(8,128)(2,1)S(1)} %get-tuple-element.116.refs_0_), channel_id=1, source_target_pairs={{0,8},{4,12},{8,0},{12,4},{1,9},{5,13},{9,1},{13,5},{2,10},{6,14},... | collective-permute-start | bytes 208904 | tf_op jit(solution)/shard_map/ppermute | solution.py:629
  25.3 0.2 shard_map.188.refs_25_
  25.5 0.4 shard_map.187
  25.9 1.3 %collective-permute-start.9 = (bf16[272,128]{1,0:T(8,128)(2,1)S(1)}, bf16[272,128]{1,0:T(8,128)(2,1)S(1)}, u32[]{:S(2)}, u32[]{:S(2)}) collective-permute-start(bf16[272,128]{1,0:T(8,128)(2,1)S(1)} %collective-permute-done.5.refs_1_), channel_id=1, source_target_pairs={{0,8},{4,12},{8,0},{12,4},{1,9},{5,13},{9,1},{13,5},{2,10},{6,14},... | collective-permute-start | bytes 208904 | tf_op jit(solution)/shard_map/ppermute | solution.py:629
  27.3 2.4 %collective-permute-done.6.refs_2_ = bf16[272,128]{1,0:T(8,128)(2,1)S(1)} collective-permute-done((bf16[272,128]{1,0:T(8,128)(2,1)S(1)}, bf16[272,128]{1,0:T(8,128)(2,1)S(1)}, u32[]{:S(2)}, u32[]{:S(2)}) %collective-permute-start.6) | collective-permute-done | bytes 69664 | tf_op jit(solution)/shard_map/ppermute | solution.py:629
  29.7 0.6 %collective-permute-start.10 = (bf16[272,128]{1,0:T(8,128)(2,1)S(1)}, bf16[272,128]{1,0:T(8,128)(2,1)S(1)}, u32[]{:S(2)}, u32[]{:S(2)}) collective-permute-start(bf16[272,128]{1,0:T(8,128)(2,1)S(1)} %collective-permute-done.6.refs_2_), channel_id=1, source_target_pairs={{0,8},{4,12},{8,0},{12,4},{1,9},{5,13},{9,1},{13,5},{2,10},{6,14},... | collective-permute-start | bytes 208904 | tf_op jit(solution)/shard_map/ppermute | solution.py:629
  30.3 0.4 collective-permute-done.7.refs_3_
  30.7 1.1 %collective-permute-start.11 = (bf16[272,128]{1,0:T(8,128)(2,1)S(1)}, bf16[272,128]{1,0:T(8,128)(2,1)S(1)}, u32[]{:S(2)}, u32[]{:S(2)}) collective-permute-start(bf16[272,128]{1,0:T(8,128)(2,1)S(1)} %collective-permute-done.7.refs_3_), channel_id=1, source_target_pairs={{0,8},{4,12},{8,0},{12,4},{1,9},{5,13},{9,1},{13,5},{2,10},{6,14},... | collective-permute-start | bytes 208904 | tf_op jit(solution)/shard_map/ppermute | solution.py:629
  31.9 2.1 %collective-permute-done.10.refs_6_ = bf16[272,128]{1,0:T(8,128)(2,1)S(1)} collective-permute-done((bf16[272,128]{1,0:T(8,128)(2,1)S(1)}, bf16[272,128]{1,0:T(8,128)(2,1)S(1)}, u32[]{:S(2)}, u32[]{:S(2)}) %collective-permute-start.10) | collective-permute-done | bytes 69664 | tf_op jit(solution)/shard_map/ppermute | solution.py:629
  34.0 1.0 %collective-permute-done.11.refs_7_ = bf16[272,128]{1,0:T(8,128)(2,1)S(1)} collective-permute-done((bf16[272,128]{1,0:T(8,128)(2,1)S(1)}, bf16[272,128]{1,0:T(8,128)(2,1)S(1)}, u32[]{:S(2)}, u32[]{:S(2)}) %collective-permute-start.11) | collective-permute-done | bytes 69664 | tf_op jit(solution)/shard_map/ppermute | solution.py:629
  35.0 0.1 collective-permute-start.12
  35.1 1.0 %shard_map.189 = (f32[384,128]{1,0:T(8,128)S(1)}, f32[384,128]{1,0:T(8,128)S(1)}, f32[384,128]{1,0:T(8,128)S(1)}, f32[384,128]{1,0:T(8,128)S(1)}) custom-call(bf16[272,128]{1,0:T(8,128)(2,1)S(1)} %get-tuple-element.116.refs_0_, bf16[272,128]{1,0:T(8,128)(2,1)S(1)} %collective-permute-done.5.refs_1_, bf16[272,128]{1,0:T(8,128)(2,1)S(1)} %collective-permute-done.6.refs_2_, ...), custom_call_target="tpu_custom_call" | custom-call | flops 1000000000 | bytes 100000 | tf_op jit(solution)/shard_map/pallas_call | solution.py:599
  36.1 1.0 %collective-permute-done.12.refs_8_ = bf16[2176,128]{1,0:T(8,128)(2,1)S(1)} collective-permute-done((bf16[2176,128]{1,0:T(8,128)(2,1)S(1)}, bf16[2176,128]{1,0:T(8,128)(2,1)S(1)}, u32[]{:S(2)}, u32[]{:S(2)}) %collective-permute-start.12) | collective-permute-done | bytes 557088 | tf_op jit(solution)/shard_map/ppermute | solution.py:629
  37.0 4.0 %shard_map.190.refs_0_ = bf16[256,128]{1,0:T(8,128)(2,1)S(1)} custom-call(bf16[272,128]{1,0:T(8,128)(2,1)S(1)} %get-tuple-element.116.refs_0_, bf16[272,128]{1,0:T(8,128)(2,1)S(1)} %collective-permute-done.5.refs_1_, bf16[272,128]{1,0:T(8,128)(2,1)S(1)} %collective-permute-done.6.refs_2_, bf16[272,128]{1,0:T(8,128)(2,1)S(1)} %collective-permute-done.7.refs_3_, ...), custom_call_target="tpu_custom_call" | custom-call | flops 6000000000 | bytes 600000 | tf_op jit(solution)/shard_map/pallas_call | solution.py:599
  41.1 1.2 %collective-permute-start.14 = (bf16[256,128]{1,0:T(8,128)(2,1)S(1)}, bf16[256,128]{1,0:T(8,128)(2,1)S(1)}, u32[]{:S(2)}, u32[]{:S(2)}) collective-permute-start(bf16[256,128]{1,0:T(8,128)(2,1)S(1)} %shard_map.190.refs_0_), channel_id=1, source_target_pairs={{0,8},{4,12},{8,0},{12,4},{1,9},{5,13},{9,1},{13,5},{2,10},{6,14},... | collective-permute-start | bytes 196616 | tf_op jit(solution)/shard_map/ppermute | solution.py:620
  42.3 0.3 shard_map.191.refs_8_
  42.7 2.7 %collective-permute-done.14.refs_2_ = bf16[256,128]{1,0:T(8,128)(2,1)S(1)} collective-permute-done((bf16[256,128]{1,0:T(8,128)(2,1)S(1)}, bf16[256,128]{1,0:T(8,128)(2,1)S(1)}, u32[]{:S(2)}, u32[]{:S(2)}) %collective-permute-start.14) | collective-permute-done | bytes 65568 | tf_op jit(solution)/shard_map/ppermute | solution.py:620
  45.4 1.2 %collective-permute-done.15.refs_3_ = bf16[256,128]{1,0:T(8,128)(2,1)S(1)} collective-permute-done((bf16[256,128]{1,0:T(8,128)(2,1)S(1)}, bf16[256,128]{1,0:T(8,128)(2,1)S(1)}, u32[]{:S(2)}, u32[]{:S(2)}) %collective-permute-start.15) | collective-permute-done | bytes 65568 | tf_op jit(solution)/shard_map/ppermute | solution.py:620
  46.7 3.8 %shard_map.192 = bf16[512,128]{1,0:T(8,128)(2,1)} custom-call(bf16[256,128]{1,0:T(8,128)(2,1)S(1)} %shard_map.190.refs_0_, bf16[256,128]{1,0:T(8,128)(2,1)S(1)} %collective-permute-done.13.refs_1_, bf16[256,128]{1,0:T(8,128)(2,1)S(1)} %collective-permute-done.14.refs_2_, bf16[256,128]{1,0:T(8,128)(2,1)S(1)} %collective-permute-done.15.refs_3_, ...), custom_call_target="tpu_custom_call" | custom-call | flops 3000000000 | bytes 300000 | tf_op jit(solution)/shard_map/pallas_call | solution.py:599
  (50 shorter events, 0.4 us)
Async XLA Ops:
  0.0 3.2 %copy-start.1 = (bf16[3072,128]{1,0:T(8,128)(2,1)S(1)}, bf16[3072,128]{1,0:T(8,128)(2,1)}, u32[]{:S(2)}) copy-start(bf16[3072,128]{1,0:T(8,128)(2,1)} %refs_12_.2) | copy-start | bytes 2359300
  0.0 3.2 %copy-start.2 = (bf16[5,384,128]{2,1,0:T(8,128)(2,1)S(1)}, bf16[5,384,128]{2,1,0:T(8,128)(2,1)}, u32[]{:S(2)}) copy-start(bf16[5,384,128]{2,1,0:T(8,128)(2,1)} %refs_16_.3) | copy-start | bytes 1474564
  0.0 3.2 %copy-start.4 = (bf16[5,256,128]{2,1,0:T(8,128)(2,1)S(1)}, bf16[5,256,128]{2,1,0:T(8,128)(2,1)}, u32[]{:S(2)}) copy-start(bf16[5,256,128]{2,1,0:T(8,128)(2,1)} %refs_18_.1) | copy-start | bytes 983044
  0.0 3.2 %copy-start.5 = (bf16[5,128,128]{2,1,0:T(8,128)(2,1)S(1)}, bf16[5,128,128]{2,1,0:T(8,128)(2,1)}, u32[]{:S(2)}) copy-start(bf16[5,128,128]{2,1,0:T(8,128)(2,1)} %refs_17_.1) | copy-start | bytes 491524
  0.0 3.2 %copy-start.6 = (bf16[5,128,128]{2,1,0:T(8,128)(2,1)S(1)}, bf16[5,128,128]{2,1,0:T(8,128)(2,1)}, u32[]{:S(2)}) copy-start(bf16[5,128,128]{2,1,0:T(8,128)(2,1)} %refs_19_.1) | copy-start | bytes 491524
  0.0 3.2 %copy-start.7 = (bf16[512,128]{1,0:T(8,128)(2,1)S(1)}, bf16[512,128]{1,0:T(8,128)(2,1)}, u32[]{:S(2)}) copy-start(bf16[512,128]{1,0:T(8,128)(2,1)} %refs_10_.2) | copy-start | bytes 393220
  0.0 3.2 %copy-start.10 = (s32[3072]{0:T(1024)S(1)}, s32[3072]{0:T(1024)}, u32[]{:S(2)}) copy-start(s32[3072]{0:T(1024)} %param.20) | copy-start | bytes 36868
  0.0 3.2 %copy-start.11 = (s32[3072]{0:T(1024)S(1)}, s32[3072]{0:T(1024)}, u32[]{:S(2)}) copy-start(s32[3072]{0:T(1024)} %param.21) | copy-start | bytes 36868
  2.0 3.2 %collective-permute-start = (bf16[80,128]{1,0:T(8,128)(2,1)}, bf16[80,128]{1,0:T(8,128)(2,1)S(1)}, u32[]{:S(2)}, u32[]{:S(2)}) collective-permute-start(bf16[80,128]{1,0:T(8,128)(2,1)} %get-tuple-element.75), channel_id=1, source_target_pairs={{0,4},{4,0},{8,12},{12,8},{1,5},{5,1},{9,13},{13,9},{2,6},{6,2},{1... | collective-permute-start | bytes 61448 | tf_op jit(solution)/shard_map/ppermute | solution.py:690
  2.5 2.7 %collective-permute-start.1 = (bf16[80,128]{1,0:T(8,128)(2,1)}, bf16[80,128]{1,0:T(8,128)(2,1)S(1)}, u32[]{:S(2)}, u32[]{:S(2)}) collective-permute-start(bf16[80,128]{1,0:T(8,128)(2,1)} %get-tuple-element.76), channel_id=1, source_target_pairs={{4,8},{8,4},{5,9},{9,5},{6,10},{10,6},{7,11},{11,7},{20,24},{24,20... | collective-permute-start | bytes 61448 | tf_op jit(solution)/shard_map/ppermute | solution.py:691
  3.3 1.9 %copy-start.14 = (bf16[16,128]{1,0:T(8,128)(2,1)S(1)}, bf16[16,128]{1,0:T(8,128)(2,1)}, u32[]{:S(2)}) copy-start(bf16[16,128]{1,0:T(8,128)(2,1)} %get-tuple-element.78.refs_2_.refs_0_) | copy-start | bytes 12292
  5.2 7.1 %copy-start = (bf16[8192,128]{1,0:T(8,128)(2,1)S(1)}, bf16[8192,128]{1,0:T(8,128)(2,1)}, u32[]{:S(2)}) copy-start(bf16[8192,128]{1,0:T(8,128)(2,1)} %refs_23_.1) | copy-start | bytes 6291460
  5.2 7.1 %copy-start.8 = (s32[8192]{0:T(1024)S(1)}, s32[8192]{0:T(1024)}, u32[]{:S(2)}) copy-start(s32[8192]{0:T(1024)} %param.31) | copy-start | bytes 98308
  5.2 7.0 %copy-start.9 = (s32[8192]{0:T(1024)S(1)}, s32[8192]{0:T(1024)}, u32[]{:S(2)}) copy-start(s32[8192]{0:T(1024)} %param.32) | copy-start | bytes 98308
  7.1 9.5 %collective-permute-start.3 = (bf16[528,128]{1,0:T(8,128)(2,1)S(1)}, bf16[528,128]{1,0:T(8,128)(2,1)S(1)}, u32[]{:S(2)}, u32[]{:S(2)}) collective-permute-start(bf16[528,128]{1,0:T(8,128)(2,1)S(1)} %get-tuple-element.99.refs_0_), channel_id=1, source_target_pairs={{0,8},{4,12},{8,0},{12,4},{1,9},{5,13},{9,1},{13,5},{2,10},{6,14},... | collective-permute-start | bytes 405512 | tf_op jit(solution)/shard_map/ppermute | solution.py:620
  12.3 4.2 %copy-start.3 = (bf16[1536,128]{1,0:T(8,128)(2,1)S(1)}, bf16[1536,128]{1,0:T(8,128)(2,1)}, u32[]{:S(2)}) copy-start(bf16[1536,128]{1,0:T(8,128)(2,1)} %refs_9_.1) | copy-start | bytes 1179652
  12.3 4.2 %copy-start.12 = (s32[1536]{0:T(1024)S(1)}, s32[1536]{0:T(1024)}, u32[]{:S(2)}) copy-start(s32[1536]{0:T(1024)} %param.24) | copy-start | bytes 18436
  12.3 4.2 %copy-start.13 = (s32[1536]{0:T(1024)S(1)}, s32[1536]{0:T(1024)}, u32[]{:S(2)}) copy-start(s32[1536]{0:T(1024)} %param.25) | copy-start | bytes 18436
  14.7 2.4 %collective-permute-start.2 = (bf16[528,128]{1,0:T(8,128)(2,1)S(1)}, bf16[528,128]{1,0:T(8,128)(2,1)S(1)}, u32[]{:S(2)}, u32[]{:S(2)}) collective-permute-start(bf16[528,128]{1,0:T(8,128)(2,1)S(1)} %get-tuple-element.99.refs_0_), channel_id=1, source_target_pairs={{0,4},{4,0},{8,12},{12,8},{1,5},{5,1},{9,13},{13,9},{2,6},{6,2},{1... | collective-permute-start | bytes 405512 | tf_op jit(solution)/shard_map/ppermute | solution.py:620
  16.5 1.4 %collective-permute-start.4 = (bf16[528,128]{1,0:T(8,128)(2,1)S(1)}, bf16[528,128]{1,0:T(8,128)(2,1)S(1)}, u32[]{:S(2)}, u32[]{:S(2)}) collective-permute-start(bf16[528,128]{1,0:T(8,128)(2,1)S(1)} %collective-permute-done.3.refs_2_), channel_id=1, source_target_pairs={{0,4},{4,0},{8,12},{12,8},{1,5},{5,1},{9,13},{13,9},{2,6},{6,2},{1... | collective-permute-start | bytes 405512 | tf_op jit(solution)/shard_map/ppermute | solution.py:620
  20.1 5.9 %collective-permute-start.5 = (bf16[272,128]{1,0:T(8,128)(2,1)S(1)}, bf16[272,128]{1,0:T(8,128)(2,1)S(1)}, u32[]{:S(2)}, u32[]{:S(2)}) collective-permute-start(bf16[272,128]{1,0:T(8,128)(2,1)S(1)} %get-tuple-element.116.refs_0_), channel_id=1, source_target_pairs={{0,1},{1,0},{2,3},{3,2},{4,5},{5,4},{6,7},{7,6},{8,9},{9,8},{10,11... | collective-permute-start | bytes 208904 | tf_op jit(solution)/shard_map/ppermute | solution.py:629
  21.9 7.8 %collective-permute-start.6 = (bf16[272,128]{1,0:T(8,128)(2,1)S(1)}, bf16[272,128]{1,0:T(8,128)(2,1)S(1)}, u32[]{:S(2)}, u32[]{:S(2)}) collective-permute-start(bf16[272,128]{1,0:T(8,128)(2,1)S(1)} %get-tuple-element.116.refs_0_), channel_id=1, source_target_pairs={{0,2},{1,3},{2,0},{3,1},{4,6},{5,7},{6,4},{7,5},{8,10},{9,11},{10,... | collective-permute-start | bytes 208904 | tf_op jit(solution)/shard_map/ppermute | solution.py:629
  24.5 6.2 %collective-permute-start.7 = (bf16[272,128]{1,0:T(8,128)(2,1)S(1)}, bf16[272,128]{1,0:T(8,128)(2,1)S(1)}, u32[]{:S(2)}, u32[]{:S(2)}) collective-permute-start(bf16[272,128]{1,0:T(8,128)(2,1)S(1)} %get-tuple-element.116.refs_0_), channel_id=1, source_target_pairs={{0,3},{1,2},{2,1},{3,0},{4,7},{5,6},{6,5},{7,4},{8,11},{9,10},{10,... | collective-permute-start | bytes 208904 | tf_op jit(solution)/shard_map/ppermute | solution.py:629
  24.5 7.3 %collective-permute-start.8 = (bf16[272,128]{1,0:T(8,128)(2,1)S(1)}, bf16[272,128]{1,0:T(8,128)(2,1)S(1)}, u32[]{:S(2)}, u32[]{:S(2)}) collective-permute-start(bf16[272,128]{1,0:T(8,128)(2,1)S(1)} %get-tuple-element.116.refs_0_), channel_id=1, source_target_pairs={{0,8},{4,12},{8,0},{12,4},{1,9},{5,13},{9,1},{13,5},{2,10},{6,14},... | collective-permute-start | bytes 208904 | tf_op jit(solution)/shard_map/ppermute | solution.py:629
  25.9 5.9 %collective-permute-start.9 = (bf16[272,128]{1,0:T(8,128)(2,1)S(1)}, bf16[272,128]{1,0:T(8,128)(2,1)S(1)}, u32[]{:S(2)}, u32[]{:S(2)}) collective-permute-start(bf16[272,128]{1,0:T(8,128)(2,1)S(1)} %collective-permute-done.5.refs_1_), channel_id=1, source_target_pairs={{0,8},{4,12},{8,0},{12,4},{1,9},{5,13},{9,1},{13,5},{2,10},{6,14},... | collective-permute-start | bytes 208904 | tf_op jit(solution)/shard_map/ppermute | solution.py:629
  29.7 4.3 %collective-permute-start.10 = (bf16[272,128]{1,0:T(8,128)(2,1)S(1)}, bf16[272,128]{1,0:T(8,128)(2,1)S(1)}, u32[]{:S(2)}, u32[]{:S(2)}) collective-permute-start(bf16[272,128]{1,0:T(8,128)(2,1)S(1)} %collective-permute-done.6.refs_2_), channel_id=1, source_target_pairs={{0,8},{4,12},{8,0},{12,4},{1,9},{5,13},{9,1},{13,5},{2,10},{6,14},... | collective-permute-start | bytes 208904 | tf_op jit(solution)/shard_map/ppermute | solution.py:629
  30.7 4.3 %collective-permute-start.11 = (bf16[272,128]{1,0:T(8,128)(2,1)S(1)}, bf16[272,128]{1,0:T(8,128)(2,1)S(1)}, u32[]{:S(2)}, u32[]{:S(2)}) collective-permute-start(bf16[272,128]{1,0:T(8,128)(2,1)S(1)} %collective-permute-done.7.refs_3_), channel_id=1, source_target_pairs={{0,8},{4,12},{8,0},{12,4},{1,9},{5,13},{9,1},{13,5},{2,10},{6,14},... | collective-permute-start | bytes 208904 | tf_op jit(solution)/shard_map/ppermute | solution.py:629
  35.0 2.0 %collective-permute-start.12 = (bf16[2176,128]{1,0:T(8,128)(2,1)S(1)}, bf16[2176,128]{1,0:T(8,128)(2,1)S(1)}, u32[]{:S(2)}, u32[]{:S(2)}) collective-permute-start(bf16[2176,128]{1,0:T(8,128)(2,1)S(1)} %constant_dynamic-update-slice_fusion), channel_id=1, source_target_pairs={{0,4},{4,0},{8,12},{12,8},{1,5},{5,1},{9,13},{13,9},{2,6},{6,2},{1... | collective-permute-start | bytes 1671176 | tf_op jit(solution)/shard_map/ppermute | solution.py:629
  41.1 4.3 %collective-permute-start.14 = (bf16[256,128]{1,0:T(8,128)(2,1)S(1)}, bf16[256,128]{1,0:T(8,128)(2,1)S(1)}, u32[]{:S(2)}, u32[]{:S(2)}) collective-permute-start(bf16[256,128]{1,0:T(8,128)(2,1)S(1)} %shard_map.190.refs_0_), channel_id=1, source_target_pairs={{0,8},{4,12},{8,0},{12,4},{1,9},{5,13},{9,1},{13,5},{2,10},{6,14},... | collective-permute-start | bytes 196616 | tf_op jit(solution)/shard_map/ppermute | solution.py:620
  42.6 2.8 %collective-permute-start.13 = (bf16[256,128]{1,0:T(8,128)(2,1)S(1)}, bf16[256,128]{1,0:T(8,128)(2,1)S(1)}, u32[]{:S(2)}, u32[]{:S(2)}) collective-permute-start(bf16[256,128]{1,0:T(8,128)(2,1)S(1)} %shard_map.190.refs_0_), channel_id=1, source_target_pairs={{0,4},{4,0},{8,12},{12,8},{1,5},{5,1},{9,13},{13,9},{2,6},{6,2},{1... | collective-permute-start | bytes 196616 | tf_op jit(solution)/shard_map/ppermute | solution.py:620
  45.4 1.3 %collective-permute-start.15 = (bf16[256,128]{1,0:T(8,128)(2,1)S(1)}, bf16[256,128]{1,0:T(8,128)(2,1)S(1)}, u32[]{:S(2)}, u32[]{:S(2)}) collective-permute-start(bf16[256,128]{1,0:T(8,128)(2,1)S(1)} %collective-permute-done.14.refs_2_), channel_id=1, source_target_pairs={{0,4},{4,0},{8,12},{12,8},{1,5},{5,1},{9,13},{13,9},{2,6},{6,2},{1... | collective-permute-start | bytes 196616 | tf_op jit(solution)/shard_map/ppermute | solution.py:620

commit v6 on v5

--- a/solution.py
+++ b/solution.py
@@ -111,8 +111,8 @@
 def edge_columns(own, count):
     shape = (count, LANES)
     if own == 2 * CUT:
-        return [(shape, I16), (shape, I16), (shape, I32), (shape, I16), (shape, I32), (shape, BF16)]
-    return [(shape, I16), (shape, I32), (shape, I16)]
+        return [(shape, I32), (shape, I32), (shape, I32), (shape, I32), (shape, I32), (shape, BF16)]
+    return [(shape, I32), (shape, I32), (shape, I32)]
 
 
 def fill_columns(own, senders, receivers, outs):
@@ -498,7 +498,8 @@
     subs = lax.axis_size("sub")
     if count > 1:
         rows = coarse + TAIL
-        there = tuple(refs[count - 1].at[i * rows : (i + 1) * rows] for i in range(count - 1))
+        stacks = refs[count - regions // 2 : count]
+        there = tuple(stack.at[i * rows : (i + 1) * rows] for stack in stacks for i in range(subs))
         blocks = tuple((there if j % 2 else refs)[j // 2 * subs + k] for j in range(regions) for k in range(subs))
         begun = [ref[...] for ref in refs[count : count + 4]]
         begun, refs = ((begun[0], begun[1]), (begun[2], begun[3])), refs[count + 4 :]
@@ -637,7 +638,7 @@
                 blocks[j + bit] = [swap(block, "region", bit) for block in blocks[j]]
             bit //= 2
         here = [block for j in range(0, regions, 2) for block in blocks[j]]
-        return here + [swap(jnp.concatenate(here), "region", 1)], beside
+        return here + [swap(jnp.concatenate(blocks[j]), "region", 1) for j in range(0, regions, 2)], beside
     blocks, bit = jnp.stack(turns), 1
     while bit < regions:
         blocks, bit = jnp.concatenate([blocks, swap(blocks, "region", bit)]), 2 * bit
@@ -755,7 +756,7 @@
     if many > 1:
         begun = call(
             functools.partial(half_kernel, coarse),
-            blocks2[:-1] + [selected[0], selected[7]],
+            blocks2[: -(regions // 2)] + [selected[0], selected[7]],
             [((wide, LANES), F32)] * 2 + [((size, LANES), F32)] * 2,
         )
     (coarse_final,) = call(

time: 50.6 us -> 50.2 us (level)
  starting transfers between devices: 16 us -> 16.8 us
  Pallas kernels: 20.5 us -> 19.9 us
    pallas_call x12, Pallas kernels: 20.5 us -> 19.9 us  [call(): pl.pallas_call(body, out_shape=[jax.ShapeDtypeStruct(shape, dtype) for sh...]
    ppermute x8 -> x9, starting transfers between devices: 8.32 us -> 8.64 us  [over_both(): lax.ppermute(array, axis, [(i, i ^ bits) for i in range(lax.axis_size(axi...]
    ppermute x8 -> x9, waiting for transfers between devices: 6.85 us -> 6.58 us  [over_both(): lax.ppermute(array, axis, [(i, i ^ bits) for i in range(lax.axis_size(axi...]
  transfers between devices with their start and end apart: 16 -> 17, of which waited for: 9 -> 9; matrix products, arithmetic and copies ran while one was open for 0% -> 0% of each run, Pallas kernels for 13% -> 12%
where the time goes in v6:
time: 50.2 us; the launch traced here: 50 us
  Pallas kernels  19.9 us (40%)
  starting transfers between devices  16.8 us (33%)
  waiting for transfers between devices  12.9 us (26%)
    pallas_call x12, Pallas kernels, call(): pl.pallas_call(body, out_shape=[jax.ShapeDtypeStruct(shape, dtype) for sh...  19.9 us
    ppermute x9, starting transfers between devices, over_both(): lax.ppermute(array, axis, [(i, i ^ bits) for i in range(lax.axis_size(axi...  8.64 us
    ppermute x6, starting transfers between devices, over_region(): lax.ppermute(going[j], 'region', [(i, i ^ bit) for i in range(count)])  6.93 us
    ppermute x9, waiting for transfers between devices, over_both(): lax.ppermute(array, axis, [(i, i ^ bits) for i in range(lax.axis_size(axi...  6.58 us
    ppermute x6, waiting for transfers between devices, over_region(): lax.ppermute(going[j], 'region', [(i, i ^ bit) for i in range(count)])  6.29 us
  transfers between devices with their start and end apart: 17, of which 9 were waited for; matrix products, arithmetic and copies ran while one was open for 0% of the time, Pallas kernels for 12%

profile of v6, /device:TPU:0, one launch (start us, length us, event | category | flops | bytes accessed | tf_op | source)
XLA Modules:
  0.0 50.0 jit_solution(17141922562828991772)
XLA Ops:
  0.0 1.9 %shard_map.181 = (bf16[80,128]{1,0:T(8,128)(2,1)}, bf16[80,128]{1,0:T(8,128)(2,1)}, bf16[16,128]{1,0:T(8,128)(2,1)}) custom-call(bf16[512,128]{1,0:T(8,128)(2,1)} %refs_10_.2, s32[2,64]{1,0:T(2,128)} %refs_1_.3, s32[2,32]{1,0:T(2,128)} %refs_2_.1, s32[4,128]{1,0:T(4,128)} %bitcast.19, s32[4,128]{1,0:T(4,128)} %bitcast.20, s32[2,128]{1,0:T(2,128)} %bitcast.21), custom_call_target="tpu_custom_call" | custom-call | flops 1000000000 | bytes 100000 | tf_op jit(solution)/shard_map/pallas_call | solution.py:600
  2.0 0.5 %collective-permute-start = (bf16[80,128]{1,0:T(8,128)(2,1)}, bf16[80,128]{1,0:T(8,128)(2,1)S(1)}, u32[]{:S(2)}, u32[]{:S(2)}) collective-permute-start(bf16[80,128]{1,0:T(8,128)(2,1)} %get-tuple-element.75), channel_id=1, source_target_pairs={{0,4},{4,0},{8,12},{12,8},{1,5},{5,1},{9,13},{13,9},{2,6},{6,2},{1... | collective-permute-start | bytes 61448 | tf_op jit(solution)/shard_map/ppermute | solution.py:691
  2.5 0.7 %collective-permute-start.1 = (bf16[80,128]{1,0:T(8,128)(2,1)}, bf16[80,128]{1,0:T(8,128)(2,1)S(1)}, u32[]{:S(2)}, u32[]{:S(2)}) collective-permute-start(bf16[80,128]{1,0:T(8,128)(2,1)} %get-tuple-element.76), channel_id=1, source_target_pairs={{4,8},{8,4},{5,9},{9,5},{6,10},{10,6},{7,11},{11,7},{20,24},{24,20... | collective-permute-start | bytes 61448 | tf_op jit(solution)/shard_map/ppermute | solution.py:692
  3.3 1.4 %shard_map.182 = (s32[3072,128]{1,0:T(8,128)S(1)}, s32[3072,128]{1,0:T(8,128)S(1)}, s32[3072,128]{1,0:T(8,128)S(1)}, s32[3072,128]{1,0:T(8,128)S(1)}, s32[3072,1...) custom-call(bf16[512,128]{1,0:T(8,128)(2,1)S(1)} %copy-done.5, s32[24,128]{1,0:T(8,128)S(1)} %bitcast.14, ...), custom_call_target="tpu_custom_call" | custom-call | flops 2000000000 | bytes 200000 | tf_op jit(solution)/shard_map/pallas_call | solution.py:600
  4.7 1.8 %shard_map.183 = (bf16[528,128]{1,0:T(8,128)(2,1)S(1)}, bf16[3072,128]{1,0:T(8,128)(2,1)S(1)}) custom-call(bf16[80,128]{1,0:T(8,128)(2,1)S(1)} %collective-permute-done.refs_0_.refs_1_, bf16[80,128]{1,0:T(8,128)(2,1)S(1)} %collective-permute-done.1.refs_1_.refs_2_, bf16[16,128]{1,0:T(8,128)(2,1)S(1)} %copy-done.7, ...), custom_call_target="tpu_custom_call" | custom-call | flops 3000000000 | bytes 300000 | tf_op jit(solution)/shard_map/pallas_call | solution.py:600
  6.5 5.7 %collective-permute-start.3 = (bf16[528,128]{1,0:T(8,128)(2,1)S(1)}, bf16[528,128]{1,0:T(8,128)(2,1)S(1)}, u32[]{:S(2)}, u32[]{:S(2)}) collective-permute-start(bf16[528,128]{1,0:T(8,128)(2,1)S(1)} %get-tuple-element.99.refs_0_), channel_id=1, source_target_pairs={{0,8},{4,12},{8,0},{12,4},{1,9},{5,13},{9,1},{13,5},{2,10},{6,14},... | collective-permute-start | bytes 405512 | tf_op jit(solution)/shard_map/ppermute | solution.py:621
  12.3 2.4 %shard_map.184 = (s32[384,128]{1,0:T(8,128)S(1)}, s32[3,128]{1,0:T(4,128)S(1)}, s32[64,128]{1,0:T(8,128)S(1)}, s32[64,128]{1,0:T(8,128)S(1)}, s32[64,128]{1,0:T(...) custom-call(bf16[16,128]{1,0:T(8,128)(2,1)S(1)} %copy-done.7, ...), custom_call_target="tpu_custom_call" | custom-call | flops 3000000000 | bytes 300000 | tf_op jit(solution)/shard_map/pallas_call | solution.py:600
  14.7 1.4 %collective-permute-done.3.refs_2_ = bf16[528,128]{1,0:T(8,128)(2,1)S(1)} collective-permute-done((bf16[528,128]{1,0:T(8,128)(2,1)S(1)}, bf16[528,128]{1,0:T(8,128)(2,1)S(1)}, u32[]{:S(2)}, u32[]{:S(2)}) %collective-permute-start.3) | collective-permute-done | bytes 135200 | tf_op jit(solution)/shard_map/ppermute | solution.py:621
  16.1 0.5 shard_map.185
  16.6 0.8 %collective-permute-done.4.refs_3_ = bf16[528,128]{1,0:T(8,128)(2,1)S(1)} collective-permute-done((bf16[528,128]{1,0:T(8,128)(2,1)S(1)}, bf16[528,128]{1,0:T(8,128)(2,1)S(1)}, u32[]{:S(2)}, u32[]{:S(2)}) %collective-permute-start.4) | collective-permute-done | bytes 135200 | tf_op jit(solution)/shard_map/ppermute | solution.py:621
  17.5 2.2 %shard_map.186 = (bf16[272,128]{1,0:T(8,128)(2,1)S(1)}, bf16[1536,128]{1,0:T(8,128)(2,1)S(1)}) custom-call(bf16[528,128]{1,0:T(8,128)(2,1)S(1)} %get-tuple-element.99.refs_0_, bf16[528,128]{1,0:T(8,128)(2,1)S(1)} %collective-permute-done.2.refs_1_, bf16[528,128]{1,0:T(8,128)(2,1)S(1)} %collective-permute-done.3.refs_2_, ...), custom_call_target="tpu_custom_call" | custom-call | flops 3000000000 | bytes 300000 | tf_op jit(solution)/shard_map/pallas_call | solution.py:600
  19.6 2.2 %collective-permute-start.5 = (bf16[272,128]{1,0:T(8,128)(2,1)S(1)}, bf16[272,128]{1,0:T(8,128)(2,1)S(1)}, u32[]{:S(2)}, u32[]{:S(2)}) collective-permute-start(bf16[272,128]{1,0:T(8,128)(2,1)S(1)} %get-tuple-element.116.refs_0_), channel_id=1, source_target_pairs={{0,1},{1,0},{2,3},{3,2},{4,5},{5,4},{6,7},{7,6},{8,9},{9,8},{10,11... | collective-permute-start | bytes 208904 | tf_op jit(solution)/shard_map/ppermute | solution.py:630
  21.8 2.6 %collective-permute-start.6 = (bf16[272,128]{1,0:T(8,128)(2,1)S(1)}, bf16[272,128]{1,0:T(8,128)(2,1)S(1)}, u32[]{:S(2)}, u32[]{:S(2)}) collective-permute-start(bf16[272,128]{1,0:T(8,128)(2,1)S(1)} %get-tuple-element.116.refs_0_), channel_id=1, source_target_pairs={{0,2},{1,3},{2,0},{3,1},{4,6},{5,7},{6,4},{7,5},{8,10},{9,11},{10,... | collective-permute-start | bytes 208904 | tf_op jit(solution)/shard_map/ppermute | solution.py:630
  24.4 0.8 %collective-permute-start.8 = (bf16[272,128]{1,0:T(8,128)(2,1)S(1)}, bf16[272,128]{1,0:T(8,128)(2,1)S(1)}, u32[]{:S(2)}, u32[]{:S(2)}) collective-permute-start(bf16[272,128]{1,0:T(8,128)(2,1)S(1)} %get-tuple-element.116.refs_0_), channel_id=1, source_target_pairs={{0,8},{4,12},{8,0},{12,4},{1,9},{5,13},{9,1},{13,5},{2,10},{6,14},... | collective-permute-start | bytes 208904 | tf_op jit(solution)/shard_map/ppermute | solution.py:630
  25.2 0.2 shard_map.188.refs_26_
  25.5 0.4 shard_map.187
  25.9 1.3 %collective-permute-start.9 = (bf16[272,128]{1,0:T(8,128)(2,1)S(1)}, bf16[272,128]{1,0:T(8,128)(2,1)S(1)}, u32[]{:S(2)}, u32[]{:S(2)}) collective-permute-start(bf16[272,128]{1,0:T(8,128)(2,1)S(1)} %collective-permute-done.5.refs_1_), channel_id=1, source_target_pairs={{0,8},{4,12},{8,0},{12,4},{1,9},{5,13},{9,1},{13,5},{2,10},{6,14},... | collective-permute-start | bytes 208904 | tf_op jit(solution)/shard_map/ppermute | solution.py:630
  27.2 2.5 %collective-permute-done.6.refs_2_ = bf16[272,128]{1,0:T(8,128)(2,1)S(1)} collective-permute-done((bf16[272,128]{1,0:T(8,128)(2,1)S(1)}, bf16[272,128]{1,0:T(8,128)(2,1)S(1)}, u32[]{:S(2)}, u32[]{:S(2)}) %collective-permute-start.6) | collective-permute-done | bytes 69664 | tf_op jit(solution)/shard_map/ppermute | solution.py:630
  29.6 0.6 %collective-permute-start.10 = (bf16[272,128]{1,0:T(8,128)(2,1)S(1)}, bf16[272,128]{1,0:T(8,128)(2,1)S(1)}, u32[]{:S(2)}, u32[]{:S(2)}) collective-permute-start(bf16[272,128]{1,0:T(8,128)(2,1)S(1)} %collective-permute-done.6.refs_2_), channel_id=1, source_target_pairs={{0,8},{4,12},{8,0},{12,4},{1,9},{5,13},{9,1},{13,5},{2,10},{6,14},... | collective-permute-start | bytes 208904 | tf_op jit(solution)/shard_map/ppermute | solution.py:630
  30.2 0.4 collective-permute-done.7.refs_3_
  30.6 1.0 %collective-permute-start.11 = (bf16[272,128]{1,0:T(8,128)(2,1)S(1)}, bf16[272,128]{1,0:T(8,128)(2,1)S(1)}, u32[]{:S(2)}, u32[]{:S(2)}) collective-permute-start(bf16[272,128]{1,0:T(8,128)(2,1)S(1)} %collective-permute-done.7.refs_3_), channel_id=1, source_target_pairs={{0,8},{4,12},{8,0},{12,4},{1,9},{5,13},{9,1},{13,5},{2,10},{6,14},... | collective-permute-start | bytes 208904 | tf_op jit(solution)/shard_map/ppermute | solution.py:630
  31.8 2.2 %collective-permute-done.10.refs_6_ = bf16[272,128]{1,0:T(8,128)(2,1)S(1)} collective-permute-done((bf16[272,128]{1,0:T(8,128)(2,1)S(1)}, bf16[272,128]{1,0:T(8,128)(2,1)S(1)}, u32[]{:S(2)}, u32[]{:S(2)}) %collective-permute-start.10) | collective-permute-done | bytes 69664 | tf_op jit(solution)/shard_map/ppermute | solution.py:630
  34.0 1.0 %collective-permute-done.11.refs_7_ = bf16[272,128]{1,0:T(8,128)(2,1)S(1)} collective-permute-done((bf16[272,128]{1,0:T(8,128)(2,1)S(1)}, bf16[272,128]{1,0:T(8,128)(2,1)S(1)}, u32[]{:S(2)}, u32[]{:S(2)}) %collective-permute-start.11) | collective-permute-done | bytes 69664 | tf_op jit(solution)/shard_map/ppermute | solution.py:630
  35.0 0.1 collective-permute-start.13
  35.1 1.0 %shard_map.189 = (f32[384,128]{1,0:T(8,128)S(1)}, f32[384,128]{1,0:T(8,128)S(1)}, f32[384,128]{1,0:T(8,128)S(1)}, f32[384,128]{1,0:T(8,128)S(1)}) custom-call(bf16[272,128]{1,0:T(8,128)(2,1)S(1)} %get-tuple-element.116.refs_0_, bf16[272,128]{1,0:T(8,128)(2,1)S(1)} %collective-permute-done.5.refs_1_, bf16[272,128]{1,0:T(8,128)(2,1)S(1)} %collective-permute-done.6.refs_2_, ...), custom_call_target="tpu_custom_call" | custom-call | flops 1000000000 | bytes 100000 | tf_op jit(solution)/shard_map/pallas_call | solution.py:600
  36.1 0.6 %collective-permute-done.13.refs_9_ = bf16[1088,128]{1,0:T(8,128)(2,1)S(1)} collective-permute-done((bf16[1088,128]{1,0:T(8,128)(2,1)S(1)}, bf16[1088,128]{1,0:T(8,128)(2,1)S(1)}, u32[]{:S(2)}, u32[]{:S(2)}) %collective-permute-start.13) | collective-permute-done | bytes 278560 | tf_op jit(solution)/shard_map/ppermute | solution.py:630
  36.6 4.1 %shard_map.190.refs_0_ = bf16[256,128]{1,0:T(8,128)(2,1)S(1)} custom-call(bf16[272,128]{1,0:T(8,128)(2,1)S(1)} %get-tuple-element.116.refs_0_, bf16[272,128]{1,0:T(8,128)(2,1)S(1)} %collective-permute-done.5.refs_1_, bf16[272,128]{1,0:T(8,128)(2,1)S(1)} %collective-permute-done.6.refs_2_, bf16[272,128]{1,0:T(8,128)(2,1)S(1)} %collective-permute-done.7.refs_3_, ...), custom_call_target="tpu_custom_call" | custom-call | flops 6000000000 | bytes 600000 | tf_op jit(solution)/shard_map/pallas_call | solution.py:600
  40.7 1.1 %collective-permute-start.15 = (bf16[256,128]{1,0:T(8,128)(2,1)S(1)}, bf16[256,128]{1,0:T(8,128)(2,1)S(1)}, u32[]{:S(2)}, u32[]{:S(2)}) collective-permute-start(bf16[256,128]{1,0:T(8,128)(2,1)S(1)} %shard_map.190.refs_0_), channel_id=1, source_target_pairs={{0,8},{4,12},{8,0},{12,4},{1,9},{5,13},{9,1},{13,5},{2,10},{6,14},... | collective-permute-start | bytes 196616 | tf_op jit(solution)/shard_map/ppermute | solution.py:621
  41.8 0.3 shard_map.191.refs_8_
  42.2 2.8 %collective-permute-done.15.refs_2_ = bf16[256,128]{1,0:T(8,128)(2,1)S(1)} collective-permute-done((bf16[256,128]{1,0:T(8,128)(2,1)S(1)}, bf16[256,128]{1,0:T(8,128)(2,1)S(1)}, u32[]{:S(2)}, u32[]{:S(2)}) %collective-permute-start.15) | collective-permute-done | bytes 65568 | tf_op jit(solution)/shard_map/ppermute | solution.py:621
  45.0 1.2 %collective-permute-done.16.refs_3_ = bf16[256,128]{1,0:T(8,128)(2,1)S(1)} collective-permute-done((bf16[256,128]{1,0:T(8,128)(2,1)S(1)}, bf16[256,128]{1,0:T(8,128)(2,1)S(1)}, u32[]{:S(2)}, u32[]{:S(2)}) %collective-permute-start.16) | collective-permute-done | bytes 65568 | tf_op jit(solution)/shard_map/ppermute | solution.py:621
  46.3 3.7 %shard_map.192 = bf16[512,128]{1,0:T(8,128)(2,1)} custom-call(bf16[256,128]{1,0:T(8,128)(2,1)S(1)} %shard_map.190.refs_0_, bf16[256,128]{1,0:T(8,128)(2,1)S(1)} %collective-permute-done.14.refs_1_, bf16[256,128]{1,0:T(8,128)(2,1)S(1)} %collective-permute-done.15.refs_2_, bf16[256,128]{1,0:T(8,128)(2,1)S(1)} %collective-permute-done.16.refs_3_, ...), custom_call_target="tpu_custom_call" | custom-call | flops 3000000000 | bytes 300000 | tf_op jit(solution)/shard_map/pallas_call | solution.py:600
  (46 shorter events, 0.3 us)
Async XLA Ops:
  0.0 3.2 %copy-start = (bf16[5,384,128]{2,1,0:T(8,128)(2,1)S(1)}, bf16[5,384,128]{2,1,0:T(8,128)(2,1)}, u32[]{:S(2)}) copy-start(bf16[5,384,128]{2,1,0:T(8,128)(2,1)} %refs_16_.3) | copy-start | bytes 1474564
  0.0 3.2 %copy-start.1 = (bf16[5,256,128]{2,1,0:T(8,128)(2,1)S(1)}, bf16[5,256,128]{2,1,0:T(8,128)(2,1)}, u32[]{:S(2)}) copy-start(bf16[5,256,128]{2,1,0:T(8,128)(2,1)} %refs_18_.1) | copy-start | bytes 983044
  0.0 3.2 %copy-start.2 = (bf16[3072,128]{1,0:T(8,128)(2,1)S(1)}, bf16[3072,128]{1,0:T(8,128)(2,1)}, u32[]{:S(2)}) copy-start(bf16[3072,128]{1,0:T(8,128)(2,1)} %refs_12_.2) | copy-start | bytes 2359300
  0.0 3.2 %copy-start.3 = (bf16[5,128,128]{2,1,0:T(8,128)(2,1)S(1)}, bf16[5,128,128]{2,1,0:T(8,128)(2,1)}, u32[]{:S(2)}) copy-start(bf16[5,128,128]{2,1,0:T(8,128)(2,1)} %refs_17_.1) | copy-start | bytes 491524
  0.0 3.2 %copy-start.4 = (bf16[5,128,128]{2,1,0:T(8,128)(2,1)S(1)}, bf16[5,128,128]{2,1,0:T(8,128)(2,1)}, u32[]{:S(2)}) copy-start(bf16[5,128,128]{2,1,0:T(8,128)(2,1)} %refs_19_.1) | copy-start | bytes 491524
  0.0 3.2 %copy-start.5 = (bf16[512,128]{1,0:T(8,128)(2,1)S(1)}, bf16[512,128]{1,0:T(8,128)(2,1)}, u32[]{:S(2)}) copy-start(bf16[512,128]{1,0:T(8,128)(2,1)} %refs_10_.2) | copy-start | bytes 393220
  0.0 3.2 %copy-start.6 = (s32[3072]{0:T(1024)S(1)}, s32[3072]{0:T(1024)}, u32[]{:S(2)}) copy-start(s32[3072]{0:T(1024)} %param.21) | copy-start | bytes 36868
  0.0 3.2 %copy-start.12 = (s32[3072]{0:T(1024)S(1)}, s32[3072]{0:T(1024)}, u32[]{:S(2)}) copy-start(s32[3072]{0:T(1024)} %param.20) | copy-start | bytes 36868
  2.0 2.7 %collective-permute-start = (bf16[80,128]{1,0:T(8,128)(2,1)}, bf16[80,128]{1,0:T(8,128)(2,1)S(1)}, u32[]{:S(2)}, u32[]{:S(2)}) collective-permute-start(bf16[80,128]{1,0:T(8,128)(2,1)} %get-tuple-element.75), channel_id=1, source_target_pairs={{0,4},{4,0},{8,12},{12,8},{1,5},{5,1},{9,13},{13,9},{2,6},{6,2},{1... | collective-permute-start | bytes 61448 | tf_op jit(solution)/shard_map/ppermute | solution.py:691
  2.5 2.2 %collective-permute-start.1 = (bf16[80,128]{1,0:T(8,128)(2,1)}, bf16[80,128]{1,0:T(8,128)(2,1)S(1)}, u32[]{:S(2)}, u32[]{:S(2)}) collective-permute-start(bf16[80,128]{1,0:T(8,128)(2,1)} %get-tuple-element.76), channel_id=1, source_target_pairs={{4,8},{8,4},{5,9},{9,5},{6,10},{10,6},{7,11},{11,7},{20,24},{24,20... | collective-permute-start | bytes 61448 | tf_op jit(solution)/shard_map/ppermute | solution.py:692
  3.3 1.4 %copy-start.7 = (bf16[16,128]{1,0:T(8,128)(2,1)S(1)}, bf16[16,128]{1,0:T(8,128)(2,1)}, u32[]{:S(2)}) copy-start(bf16[16,128]{1,0:T(8,128)(2,1)} %get-tuple-element.78.refs_2_.refs_0_) | copy-start | bytes 12292
  4.7 7.5 %copy-start.8 = (bf16[8192,128]{1,0:T(8,128)(2,1)S(1)}, bf16[8192,128]{1,0:T(8,128)(2,1)}, u32[]{:S(2)}) copy-start(bf16[8192,128]{1,0:T(8,128)(2,1)} %refs_24_.1) | copy-start | bytes 6291460
  4.7 7.5 %copy-start.10 = (s32[8192]{0:T(1024)S(1)}, s32[8192]{0:T(1024)}, u32[]{:S(2)}) copy-start(s32[8192]{0:T(1024)} %param.31) | copy-start | bytes 98308
  4.7 7.5 %copy-start.11 = (s32[8192]{0:T(1024)S(1)}, s32[8192]{0:T(1024)}, u32[]{:S(2)}) copy-start(s32[8192]{0:T(1024)} %param.32) | copy-start | bytes 98308
  6.5 9.6 %collective-permute-start.3 = (bf16[528,128]{1,0:T(8,128)(2,1)S(1)}, bf16[528,128]{1,0:T(8,128)(2,1)S(1)}, u32[]{:S(2)}, u32[]{:S(2)}) collective-permute-start(bf16[528,128]{1,0:T(8,128)(2,1)S(1)} %get-tuple-element.99.refs_0_), channel_id=1, source_target_pairs={{0,8},{4,12},{8,0},{12,4},{1,9},{5,13},{9,1},{13,5},{2,10},{6,14},... | collective-permute-start | bytes 405512 | tf_op jit(solution)/shard_map/ppermute | solution.py:621
  12.3 3.9 %copy-start.9 = (bf16[1536,128]{1,0:T(8,128)(2,1)S(1)}, bf16[1536,128]{1,0:T(8,128)(2,1)}, u32[]{:S(2)}) copy-start(bf16[1536,128]{1,0:T(8,128)(2,1)} %refs_9_.1) | copy-start | bytes 1179652
  12.3 3.9 %copy-start.13 = (s32[1536]{0:T(1024)S(1)}, s32[1536]{0:T(1024)}, u32[]{:S(2)}) copy-start(s32[1536]{0:T(1024)} %param.24) | copy-start | bytes 18436
  12.3 3.9 %copy-start.14 = (s32[1536]{0:T(1024)S(1)}, s32[1536]{0:T(1024)}, u32[]{:S(2)}) copy-start(s32[1536]{0:T(1024)} %param.25) | copy-start | bytes 18436
  14.7 2.0 %collective-permute-start.2 = (bf16[528,128]{1,0:T(8,128)(2,1)S(1)}, bf16[528,128]{1,0:T(8,128)(2,1)S(1)}, u32[]{:S(2)}, u32[]{:S(2)}) collective-permute-start(bf16[528,128]{1,0:T(8,128)(2,1)S(1)} %get-tuple-element.99.refs_0_), channel_id=1, source_target_pairs={{0,4},{4,0},{8,12},{12,8},{1,5},{5,1},{9,13},{13,9},{2,6},{6,2},{1... | collective-permute-start | bytes 405512 | tf_op jit(solution)/shard_map/ppermute | solution.py:621
  16.1 1.4 %collective-permute-start.4 = (bf16[528,128]{1,0:T(8,128)(2,1)S(1)}, bf16[528,128]{1,0:T(8,128)(2,1)S(1)}, u32[]{:S(2)}, u32[]{:S(2)}) collective-permute-start(bf16[528,128]{1,0:T(8,128)(2,1)S(1)} %collective-permute-done.3.refs_2_), channel_id=1, source_target_pairs={{0,4},{4,0},{8,12},{12,8},{1,5},{5,1},{9,13},{13,9},{2,6},{6,2},{1... | collective-permute-start | bytes 405512 | tf_op jit(solution)/shard_map/ppermute | solution.py:621
  19.6 6.3 %collective-permute-start.5 = (bf16[272,128]{1,0:T(8,128)(2,1)S(1)}, bf16[272,128]{1,0:T(8,128)(2,1)S(1)}, u32[]{:S(2)}, u32[]{:S(2)}) collective-permute-start(bf16[272,128]{1,0:T(8,128)(2,1)S(1)} %get-tuple-element.116.refs_0_), channel_id=1, source_target_pairs={{0,1},{1,0},{2,3},{3,2},{4,5},{5,4},{6,7},{7,6},{8,9},{9,8},{10,11... | collective-permute-start | bytes 208904 | tf_op jit(solution)/shard_map/ppermute | solution.py:630
  21.8 7.8 %collective-permute-start.6 = (bf16[272,128]{1,0:T(8,128)(2,1)S(1)}, bf16[272,128]{1,0:T(8,128)(2,1)S(1)}, u32[]{:S(2)}, u32[]{:S(2)}) collective-permute-start(bf16[272,128]{1,0:T(8,128)(2,1)S(1)} %get-tuple-element.116.refs_0_), channel_id=1, source_target_pairs={{0,2},{1,3},{2,0},{3,1},{4,6},{5,7},{6,4},{7,5},{8,10},{9,11},{10,... | collective-permute-start | bytes 208904 | tf_op jit(solution)/shard_map/ppermute | solution.py:630
  24.4 6.2 %collective-permute-start.7 = (bf16[272,128]{1,0:T(8,128)(2,1)S(1)}, bf16[272,128]{1,0:T(8,128)(2,1)S(1)}, u32[]{:S(2)}, u32[]{:S(2)}) collective-permute-start(bf16[272,128]{1,0:T(8,128)(2,1)S(1)} %get-tuple-element.116.refs_0_), channel_id=1, source_target_pairs={{0,3},{1,2},{2,1},{3,0},{4,7},{5,6},{6,5},{7,4},{8,11},{9,10},{10,... | collective-permute-start | bytes 208904 | tf_op jit(solution)/shard_map/ppermute | solution.py:630
  24.4 7.3 %collective-permute-start.8 = (bf16[272,128]{1,0:T(8,128)(2,1)S(1)}, bf16[272,128]{1,0:T(8,128)(2,1)S(1)}, u32[]{:S(2)}, u32[]{:S(2)}) collective-permute-start(bf16[272,128]{1,0:T(8,128)(2,1)S(1)} %get-tuple-element.116.refs_0_), channel_id=1, source_target_pairs={{0,8},{4,12},{8,0},{12,4},{1,9},{5,13},{9,1},{13,5},{2,10},{6,14},... | collective-permute-start | bytes 208904 | tf_op jit(solution)/shard_map/ppermute | solution.py:630
  25.9 5.9 %collective-permute-start.9 = (bf16[272,128]{1,0:T(8,128)(2,1)S(1)}, bf16[272,128]{1,0:T(8,128)(2,1)S(1)}, u32[]{:S(2)}, u32[]{:S(2)}) collective-permute-start(bf16[272,128]{1,0:T(8,128)(2,1)S(1)} %collective-permute-done.5.refs_1_), channel_id=1, source_target_pairs={{0,8},{4,12},{8,0},{12,4},{1,9},{5,13},{9,1},{13,5},{2,10},{6,14},... | collective-permute-start | bytes 208904 | tf_op jit(solution)/shard_map/ppermute | solution.py:630
  29.6 4.3 %collective-permute-start.10 = (bf16[272,128]{1,0:T(8,128)(2,1)S(1)}, bf16[272,128]{1,0:T(8,128)(2,1)S(1)}, u32[]{:S(2)}, u32[]{:S(2)}) collective-permute-start(bf16[272,128]{1,0:T(8,128)(2,1)S(1)} %collective-permute-done.6.refs_2_), channel_id=1, source_target_pairs={{0,8},{4,12},{8,0},{12,4},{1,9},{5,13},{9,1},{13,5},{2,10},{6,14},... | collective-permute-start | bytes 208904 | tf_op jit(solution)/shard_map/ppermute | solution.py:630
  30.6 4.3 %collective-permute-start.11 = (bf16[272,128]{1,0:T(8,128)(2,1)S(1)}, bf16[272,128]{1,0:T(8,128)(2,1)S(1)}, u32[]{:S(2)}, u32[]{:S(2)}) collective-permute-start(bf16[272,128]{1,0:T(8,128)(2,1)S(1)} %collective-permute-done.7.refs_3_), channel_id=1, source_target_pairs={{0,8},{4,12},{8,0},{12,4},{1,9},{5,13},{9,1},{13,5},{2,10},{6,14},... | collective-permute-start | bytes 208904 | tf_op jit(solution)/shard_map/ppermute | solution.py:630
  31.7 4.3 %collective-permute-start.12 = (bf16[1088,128]{1,0:T(8,128)(2,1)S(1)}, bf16[1088,128]{1,0:T(8,128)(2,1)S(1)}, u32[]{:S(2)}, u32[]{:S(2)}) collective-permute-start(bf16[1088,128]{1,0:T(8,128)(2,1)S(1)} %pad_maximum_fusion), channel_id=1, source_target_pairs={{0,4},{4,0},{8,12},{12,8},{1,5},{5,1},{9,13},{13,9},{2,6},{6,2},{1... | collective-permute-start | bytes 835592 | tf_op jit(solution)/shard_map/ppermute | solution.py:630
  35.0 1.6 %collective-permute-start.13 = (bf16[1088,128]{1,0:T(8,128)(2,1)S(1)}, bf16[1088,128]{1,0:T(8,128)(2,1)S(1)}, u32[]{:S(2)}, u32[]{:S(2)}) collective-permute-start(bf16[1088,128]{1,0:T(8,128)(2,1)S(1)} %pad_maximum_fusion.1), channel_id=1, source_target_pairs={{0,4},{4,0},{8,12},{12,8},{1,5},{5,1},{9,13},{13,9},{2,6},{6,2},{1... | collective-permute-start | bytes 835592 | tf_op jit(solution)/shard_map/ppermute | solution.py:630
  40.7 4.3 %collective-permute-start.15 = (bf16[256,128]{1,0:T(8,128)(2,1)S(1)}, bf16[256,128]{1,0:T(8,128)(2,1)S(1)}, u32[]{:S(2)}, u32[]{:S(2)}) collective-permute-start(bf16[256,128]{1,0:T(8,128)(2,1)S(1)} %shard_map.190.refs_0_), channel_id=1, source_target_pairs={{0,8},{4,12},{8,0},{12,4},{1,9},{5,13},{9,1},{13,5},{2,10},{6,14},... | collective-permute-start | bytes 196616 | tf_op jit(solution)/shard_map/ppermute | solution.py:621
  42.1 2.9 %collective-permute-start.14 = (bf16[256,128]{1,0:T(8,128)(2,1)S(1)}, bf16[256,128]{1,0:T(8,128)(2,1)S(1)}, u32[]{:S(2)}, u32[]{:S(2)}) collective-permute-start(bf16[256,128]{1,0:T(8,128)(2,1)S(1)} %shard_map.190.refs_0_), channel_id=1, source_target_pairs={{0,4},{4,0},{8,12},{12,8},{1,5},{5,1},{9,13},{13,9},{2,6},{6,2},{1... | collective-permute-start | bytes 196616 | tf_op jit(solution)/shard_map/ppermute | solution.py:621
  45.0 1.3 %collective-permute-start.16 = (bf16[256,128]{1,0:T(8,128)(2,1)S(1)}, bf16[256,128]{1,0:T(8,128)(2,1)S(1)}, u32[]{:S(2)}, u32[]{:S(2)}) collective-permute-start(bf16[256,128]{1,0:T(8,128)(2,1)S(1)} %collective-permute-done.15.refs_2_), channel_id=1, source_target_pairs={{0,4},{4,0},{8,12},{12,8},{1,5},{5,1},{9,13},{13,9},{2,6},{6,2},{1... | collective-permute-start | bytes 196616 | tf_op jit(solution)/shard_map/ppermute | solution.py:621

commit v7 on v6

--- a/solution.py
+++ b/solution.py
@@ -243,38 +243,38 @@
     before[...] = dot(edges[...], first.get()[2 * LANES :, :])
 
 
-def coarse_kernel(regions, halo, coarse, *refs):
-    blocks, (before, *rest) = refs[:regions], refs[regions:]
+def add_fine(codes, blocks, coarse, sums):
+    half = codes.shape[0] // 2
+    for block in blocks:
+        fine = block.shape[0] - TAIL
+        at, tail, f = row_layout(fine, coarse), tail_of(block, fine), fine // LANES
+        parent = tail[at["dest"] : at["dest"] + f] * coarse + tail[at["target"] : at["target"] + f]
+        more = [sums_and_counts(hot_codes(part, parent), block[:fine, :]) for part in (codes[:half], codes[half:])]
+        sums = [(total + a, members + b) for (total, members), (a, b) in zip(sums, more)]
+    return sums
+
+
+def begin_kernel(coarse, *refs):
+    *blocks, codes, totals, members = refs
+    half = codes.shape[0] // 2
+    zero = jnp.zeros((half, LANES), F32)
+    for i, (total, count) in enumerate(add_fine(codes[...], blocks, coarse, [(zero, zero)] * 2)):
+        totals[i * half : (i + 1) * half, :] = total
+        members[i * half : (i + 1) * half, :] = count
+
+
+def coarse_kernel(coarse, own, last, codes, totals, members, before, *rest):
     cols, (receivers, edges, *weights), (payload, new_edges) = rest[:3], rest[3:9], rest[9:]
-    me = lax.axis_index("region")
-    fine = blocks[0].shape[0] - TAIL
-    at = row_layout(fine, coarse)
-    tails = [tail_of(block, fine) for block in blocks]
-    near = near_tails(tails, me, regions)
-    codes = [me * coarse + lax.broadcasted_iota(I32, (coarse, LANES), 0)]
-    for side, (other, there, tail) in enumerate(near):
-        listed = tail[at["coarse"] : at["coarse"] + 1, :]
-        first = halo * (1 - side)
-        col = columns(listed)[first : first + halo]
-        codes.append(jnp.where(there, other * coarse + col, -1))
-    codes = jnp.concatenate(codes, axis=0)
     half = codes.shape[0] // 2
-    parts = []
-    for part in (codes[:half], codes[half:]):
-        total, members = 0.0, 0.0
-        for block, tail in zip(blocks, tails):
-            f = fine // LANES
-            parent = tail[at["dest"] : at["dest"] + f] * coarse + tail[at["target"] : at["target"] + f]
-            more, counted = sums_and_counts(hot_codes(part, parent), block[:fine, :])
-            total, members = total + more, members + counted
-        parts.append((total / jnp.maximum(members, 1.0)).astype(BF16))
-    table = jnp.concatenate(parts, axis=0)
+    halves = (slice(0, half), slice(half, 2 * half))
+    sums = [(totals[rows, :], members[rows, :]) for rows in halves]
+    table = jnp.concatenate(means(add_fine(codes[...], [last], coarse, sums)), axis=0)
     inner = from_table(cols, table, weights[0].get()[...])
     payload[:coarse, :] = finish(lambda rows: before[rows, :] + inner(rows), table[:coarse], receivers, None, edges.get(), weights, new_edges)
-    own_tail = tails[0]
-    c = coarse // LANES
+    fine, c = own.shape[0] - TAIL, coarse // LANES
+    high = row_layout(fine, coarse)["high"]
     payload[coarse:, :] = jnp.concatenate(
-        [own_tail[at["high"] : at["high"] + 2 * c], jnp.zeros((TAIL - 2 * c, LANES), I32)], axis=0
+        [tail_of(own, fine)[high : high + 2 * c], jnp.zeros((TAIL - 2 * c, LANES), I32)], axis=0
     ).astype(F32).astype(BF16)
 
 
@@ -311,7 +311,7 @@
 
 def listed_kernel(regions, halo, fine, coarse, *refs):
     own, paired, crossed, senders, receivers, edges, parents, firsts, halo_rows, halo_blocks, ranks, codes = refs[:12]
-    latents, send, recv, recv_rows = refs[12:]
+    latents, send, recv, recv_rows, pool_codes = refs[12:]
     me = lax.axis_index("region")
     at = row_layout(fine, coarse)
     start = paired.shape[0] - TAIL
@@ -325,10 +325,12 @@
         return tail[at["high"] : at["high"] + c] * LANES + tail[at["low"] : at["low"] + c]
 
     cols = [columns(own_parents(own_tail))]
+    pool_codes[:coarse, :] = me * coarse + lax.broadcasted_iota(I32, (coarse, LANES), 0)
     for side, (other, there, tail) in enumerate(near):
         first = halo * (1 - side)
         col = columns(tail[at["coarse"] : at["coarse"] + 1])[first : first + halo]
         halo_rows[side * halo : (side + 1) * halo, :] = col
+        pool_codes[coarse + side * halo : coarse + (side + 1) * halo, :] = jnp.where(there, other * coarse + col, -1)
         halo_blocks[side * halo : (side + 1) * halo, :] = jnp.full(col.shape, jnp.where(there, jnp.bitwise_xor(me, other), -1))
         theirs = own_parents(tail).astype(F32)
         value = jnp.zeros((halo, LANES), F32)
@@ -482,7 +484,10 @@
 
 
 def half_kernel(coarse, *refs):
-    blocks, (parents, send, *outs) = refs[:-6], refs[-6:]
+    *blocks, stack = refs[:-6]
+    rows = coarse + TAIL
+    blocks = tuple(blocks) + tuple(stack.at[i : i + rows] for i in range(0, stack.shape[0], rows))
+    parents, send, *outs = refs[-6:]
     cols = [parents[...], send[...]]
     for i, value in enumerate(sum(add_blocks(cols, blocks, coarse, nothing(cols)), ())):
         outs[i][...] = value
@@ -514,7 +519,7 @@
     own_sub = lambda j: blocks[j * subs] if count > 1 else blocks.at[j * subs]
     mine, firsts = parents[...], firsts[...]
     cols_here = [mine, send[...]]
-    top_own, from_send = means(add_blocks(cols_here, there, coarse, nothing(cols_here) if begun is None else begun))
+    top_own, from_send = means(add_blocks(cols_here, there[subs:] if count > 1 else there, coarse, nothing(cols_here) if begun is None else begun))
     near = gather(halo_rows[...], halo_blocks[...], [own_sub(j)[:coarse, :] for j in range(regions)])
     down = jnp.concatenate([own_sub(0)[:coarse, :].astype(F32), near], axis=0)
     first, second = top_weights[0].get()[...], centre(top_weights[1].get()[...])
@@ -720,6 +725,7 @@
         ((size, LANES), I32),
         ((size, LANES), I32),
         ((size // LANES, LANES), I32),
+        ((coarse + 2 * halo2, LANES), I32),
     ]
     selected = call(
         functools.partial(listed_kernel, regions, halo2, fine, coarse),
@@ -736,9 +742,15 @@
         plain(coarse_send, coarse_recv, late_edges) + one(1),
     )
     blocks, selected = over_region(payload, selected)
+    *selected, pool_codes = selected
+    totals, members = call(
+        functools.partial(begin_kernel, coarse),
+        blocks[:-1] + [pool_codes],
+        [(pool_codes.shape, F32)] * 2,
+    )
     payload2, coarse_edges2 = call(
-        functools.partial(coarse_kernel, regions, halo2, coarse),
-        blocks + [before, *coarse_cols],
+        functools.partial(coarse_kernel, coarse),
+        [blocks[0], blocks[-1], pool_codes, totals, members, before, *coarse_cols],
         [((coarse + TAIL, LANES), BF16), (coarse_edges.shape, BF16)],
         plain(coarse_recv, coarse_edges) + level(1),
         cost=3,
@@ -756,7 +768,7 @@
     if many > 1:
         begun = call(
             functools.partial(half_kernel, coarse),
-            blocks2[: -(regions // 2)] + [selected[0], selected[7]],
+            blocks2[: 1 - regions // 2] + [selected[0], selected[7]],
             [((wide, LANES), F32)] * 2 + [((size, LANES), F32)] * 2,
         )
     (coarse_final,) = call(

time: 50.2 us -> 49.6 us (0.988)
  waiting for transfers between devices: 12.9 us -> 12.1 us
    pallas_call x12 -> x13, Pallas kernels: 19.9 us -> 20.1 us  [call(): pl.pallas_call(body, out_shape=[jax.ShapeDtypeStruct(shape, dtype) for sh...]
  transfers between devices with their start and end apart: 17 -> 17, of which waited for: 9 -> 9; matrix products, arithmetic and copies ran while one was open for 0% -> 0% of each run, Pallas kernels for 12% -> 14%
where the time goes in v7:
time: 49.6 us; the launch traced here: 49.4 us
  Pallas kernels  20.1 us (41%)
  starting transfers between devices  16.8 us (34%)
  waiting for transfers between devices  12.1 us (24%)
    pallas_call x13, Pallas kernels, call(): pl.pallas_call(body, out_shape=[jax.ShapeDtypeStruct(shape, dtype) for sh...  20.1 us
    ppermute x9, starting transfers between devices, over_both(): lax.ppermute(array, axis, [(i, i ^ bits) for i in range(lax.axis_size(axi...  8.64 us
    ppermute x6, starting transfers between devices, over_region(): lax.ppermute(going[j], 'region', [(i, i ^ bit) for i in range(count)])  7.03 us
    ppermute x9, waiting for transfers between devices, over_both(): lax.ppermute(array, axis, [(i, i ^ bits) for i in range(lax.axis_size(axi...  6.17 us
    ppermute x6, waiting for transfers between devices, over_region(): lax.ppermute(going[j], 'region', [(i, i ^ bit) for i in range(count)])  5.89 us
  transfers between devices with their start and end apart: 17, of which 9 were waited for; matrix products, arithmetic and copies ran while one was open for 0% of the time, Pallas kernels for 14%

profile of v7, /device:TPU:0, one launch (start us, length us, event | category | flops | bytes accessed | tf_op | source)
XLA Modules:
  0.0 49.4 jit_solution(9300387660539146430)
XLA Ops:
  0.0 1.9 %shard_map.181 = (bf16[80,128]{1,0:T(8,128)(2,1)}, bf16[80,128]{1,0:T(8,128)(2,1)}, bf16[16,128]{1,0:T(8,128)(2,1)}) custom-call(bf16[512,128]{1,0:T(8,128)(2,1)} %refs_10_.2, s32[2,64]{1,0:T(2,128)} %refs_1_.3, s32[2,32]{1,0:T(2,128)} %refs_2_.1, s32[4,128]{1,0:T(4,128)} %bitcast.19, s32[4,128]{1,0:T(4,128)} %bitcast.20, s32[2,128]{1,0:T(2,128)} %bitcast.21), custom_call_target="tpu_custom_call" | custom-call | flops 1000000000 | bytes 100000 | tf_op jit(solution)/shard_map/pallas_call | solution.py:605
  2.0 0.5 %collective-permute-start = (bf16[80,128]{1,0:T(8,128)(2,1)}, bf16[80,128]{1,0:T(8,128)(2,1)S(1)}, u32[]{:S(2)}, u32[]{:S(2)}) collective-permute-start(bf16[80,128]{1,0:T(8,128)(2,1)} %get-tuple-element.80), channel_id=1, source_target_pairs={{0,4},{4,0},{8,12},{12,8},{1,5},{5,1},{9,13},{13,9},{2,6},{6,2},{1... | collective-permute-start | bytes 61448 | tf_op jit(solution)/shard_map/ppermute | solution.py:696
  2.5 0.7 %collective-permute-start.1 = (bf16[80,128]{1,0:T(8,128)(2,1)}, bf16[80,128]{1,0:T(8,128)(2,1)S(1)}, u32[]{:S(2)}, u32[]{:S(2)}) collective-permute-start(bf16[80,128]{1,0:T(8,128)(2,1)} %get-tuple-element.81), channel_id=1, source_target_pairs={{4,8},{8,4},{5,9},{9,5},{6,10},{10,6},{7,11},{11,7},{20,24},{24,20... | collective-permute-start | bytes 61448 | tf_op jit(solution)/shard_map/ppermute | solution.py:697
  3.3 1.4 %shard_map.182 = (s32[3072,128]{1,0:T(8,128)S(1)}, s32[3072,128]{1,0:T(8,128)S(1)}, s32[3072,128]{1,0:T(8,128)S(1)}, s32[3072,128]{1,0:T(8,128)S(1)}, s32[3072,1...) custom-call(bf16[512,128]{1,0:T(8,128)(2,1)S(1)} %copy-done.5, s32[24,128]{1,0:T(8,128)S(1)} %bitcast.14, ...), custom_call_target="tpu_custom_call" | custom-call | flops 2000000000 | bytes 200000 | tf_op jit(solution)/shard_map/pallas_call | solution.py:605
  4.7 1.8 %shard_map.183 = (bf16[528,128]{1,0:T(8,128)(2,1)S(1)}, bf16[3072,128]{1,0:T(8,128)(2,1)S(1)}) custom-call(bf16[80,128]{1,0:T(8,128)(2,1)S(1)} %collective-permute-done.refs_0_.refs_1_, bf16[80,128]{1,0:T(8,128)(2,1)S(1)} %collective-permute-done.1.refs_1_.refs_2_, bf16[16,128]{1,0:T(8,128)(2,1)S(1)} %copy-done.7, ...), custom_call_target="tpu_custom_call" | custom-call | flops 3000000000 | bytes 300000 | tf_op jit(solution)/shard_map/pallas_call | solution.py:605
  6.5 5.7 %collective-permute-start.2 = (bf16[528,128]{1,0:T(8,128)(2,1)S(1)}, bf16[528,128]{1,0:T(8,128)(2,1)S(1)}, u32[]{:S(2)}, u32[]{:S(2)}) collective-permute-start(bf16[528,128]{1,0:T(8,128)(2,1)S(1)} %get-tuple-element.105.refs_0_), channel_id=1, source_target_pairs={{0,8},{4,12},{8,0},{12,4},{1,9},{5,13},{9,1},{13,5},{2,10},{6,14},... | collective-permute-start | bytes 405512 | tf_op jit(solution)/shard_map/ppermute | solution.py:626
  12.3 2.4 %shard_map.184 = (s32[384,128]{1,0:T(8,128)S(1)}, s32[3,128]{1,0:T(4,128)S(1)}, s32[64,128]{1,0:T(8,128)S(1)}, s32[64,128]{1,0:T(8,128)S(1)}, s32[64,128]{1,0:T(...) custom-call(bf16[16,128]{1,0:T(8,128)(2,1)S(1)} %copy-done.7, ...), custom_call_target="tpu_custom_call" | custom-call | flops 3000000000 | bytes 300000 | tf_op jit(solution)/shard_map/pallas_call | solution.py:605
  14.7 1.4 %collective-permute-done.2.refs_2_ = bf16[528,128]{1,0:T(8,128)(2,1)S(1)} collective-permute-done((bf16[528,128]{1,0:T(8,128)(2,1)S(1)}, bf16[528,128]{1,0:T(8,128)(2,1)S(1)}, u32[]{:S(2)}, u32[]{:S(2)}) %collective-permute-start.2) | collective-permute-done | bytes 135200 | tf_op jit(solution)/shard_map/ppermute | solution.py:626
  16.1 0.5 shard_map.186
  16.6 0.4 shard_map.185
  17.1 0.4 collective-permute-done.3.refs_1_.refs_3_
  17.5 1.9 %shard_map.187 = (bf16[272,128]{1,0:T(8,128)(2,1)S(1)}, bf16[1536,128]{1,0:T(8,128)(2,1)S(1)}) custom-call(bf16[528,128]{1,0:T(8,128)(2,1)S(1)} %get-tuple-element.105.refs_0_, bf16[528,128]{1,0:T(8,128)(2,1)S(1)} %collective-permute-done.3.refs_1_.refs_3_, s32[320,128]{1,0:T(8,128)S(1)} %get-tuple-element.118.refs_3_.refs_2_, ...), custom_call_target="tpu_custom_call" | custom-call | flops 3000000000 | bytes 300000 | tf_op jit(solution)/shard_map/pallas_call | solution.py:605
  19.4 2.2 %collective-permute-start.5 = (bf16[272,128]{1,0:T(8,128)(2,1)S(1)}, bf16[272,128]{1,0:T(8,128)(2,1)S(1)}, u32[]{:S(2)}, u32[]{:S(2)}) collective-permute-start(bf16[272,128]{1,0:T(8,128)(2,1)S(1)} %get-tuple-element.126.refs_0_), channel_id=1, source_target_pairs={{0,1},{1,0},{2,3},{3,2},{4,5},{5,4},{6,7},{7,6},{8,9},{9,8},{10,11... | collective-permute-start | bytes 208904 | tf_op jit(solution)/shard_map/ppermute | solution.py:635
  21.6 2.6 %collective-permute-start.6 = (bf16[272,128]{1,0:T(8,128)(2,1)S(1)}, bf16[272,128]{1,0:T(8,128)(2,1)S(1)}, u32[]{:S(2)}, u32[]{:S(2)}) collective-permute-start(bf16[272,128]{1,0:T(8,128)(2,1)S(1)} %get-tuple-element.126.refs_0_), channel_id=1, source_target_pairs={{0,2},{1,3},{2,0},{3,1},{4,6},{5,7},{6,4},{7,5},{8,10},{9,11},{10,... | collective-permute-start | bytes 208904 | tf_op jit(solution)/shard_map/ppermute | solution.py:635
  24.2 0.8 %collective-permute-start.8 = (bf16[272,128]{1,0:T(8,128)(2,1)S(1)}, bf16[272,128]{1,0:T(8,128)(2,1)S(1)}, u32[]{:S(2)}, u32[]{:S(2)}) collective-permute-start(bf16[272,128]{1,0:T(8,128)(2,1)S(1)} %get-tuple-element.126.refs_0_), channel_id=1, source_target_pairs={{0,8},{4,12},{8,0},{12,4},{1,9},{5,13},{9,1},{13,5},{2,10},{6,14},... | collective-permute-start | bytes 208904 | tf_op jit(solution)/shard_map/ppermute | solution.py:635
  25.0 0.2 shard_map.189.refs_26_
  25.2 0.4 shard_map.188
  25.6 1.3 %collective-permute-start.9 = (bf16[272,128]{1,0:T(8,128)(2,1)S(1)}, bf16[272,128]{1,0:T(8,128)(2,1)S(1)}, u32[]{:S(2)}, u32[]{:S(2)}) collective-permute-start(bf16[272,128]{1,0:T(8,128)(2,1)S(1)} %collective-permute-done.5.refs_1_), channel_id=1, source_target_pairs={{0,8},{4,12},{8,0},{12,4},{1,9},{5,13},{9,1},{13,5},{2,10},{6,14},... | collective-permute-start | bytes 208904 | tf_op jit(solution)/shard_map/ppermute | solution.py:635
  26.9 2.4 %collective-permute-done.6.refs_2_ = bf16[272,128]{1,0:T(8,128)(2,1)S(1)} collective-permute-done((bf16[272,128]{1,0:T(8,128)(2,1)S(1)}, bf16[272,128]{1,0:T(8,128)(2,1)S(1)}, u32[]{:S(2)}, u32[]{:S(2)}) %collective-permute-start.6) | collective-permute-done | bytes 69664 | tf_op jit(solution)/shard_map/ppermute | solution.py:635
  29.4 0.6 %collective-permute-start.10 = (bf16[272,128]{1,0:T(8,128)(2,1)S(1)}, bf16[272,128]{1,0:T(8,128)(2,1)S(1)}, u32[]{:S(2)}, u32[]{:S(2)}) collective-permute-start(bf16[272,128]{1,0:T(8,128)(2,1)S(1)} %collective-permute-done.6.refs_2_), channel_id=1, source_target_pairs={{0,8},{4,12},{8,0},{12,4},{1,9},{5,13},{9,1},{13,5},{2,10},{6,14},... | collective-permute-start | bytes 208904 | tf_op jit(solution)/shard_map/ppermute | solution.py:635
  30.0 0.4 collective-permute-done.7.refs_3_
  30.4 1.0 %collective-permute-start.11 = (bf16[272,128]{1,0:T(8,128)(2,1)S(1)}, bf16[272,128]{1,0:T(8,128)(2,1)S(1)}, u32[]{:S(2)}, u32[]{:S(2)}) collective-permute-start(bf16[272,128]{1,0:T(8,128)(2,1)S(1)} %collective-permute-done.7.refs_3_), channel_id=1, source_target_pairs={{0,8},{4,12},{8,0},{12,4},{1,9},{5,13},{9,1},{13,5},{2,10},{6,14},... | collective-permute-start | bytes 208904 | tf_op jit(solution)/shard_map/ppermute | solution.py:635
  31.5 2.2 %collective-permute-done.10.refs_6_ = bf16[272,128]{1,0:T(8,128)(2,1)S(1)} collective-permute-done((bf16[272,128]{1,0:T(8,128)(2,1)S(1)}, bf16[272,128]{1,0:T(8,128)(2,1)S(1)}, u32[]{:S(2)}, u32[]{:S(2)}) %collective-permute-start.10) | collective-permute-done | bytes 69664 | tf_op jit(solution)/shard_map/ppermute | solution.py:635
  33.7 1.0 %collective-permute-done.11.refs_7_ = bf16[272,128]{1,0:T(8,128)(2,1)S(1)} collective-permute-done((bf16[272,128]{1,0:T(8,128)(2,1)S(1)}, bf16[272,128]{1,0:T(8,128)(2,1)S(1)}, u32[]{:S(2)}, u32[]{:S(2)}) %collective-permute-start.11) | collective-permute-done | bytes 69664 | tf_op jit(solution)/shard_map/ppermute | solution.py:635
  34.8 1.4 %shard_map.190 = (f32[384,128]{1,0:T(8,128)S(1)}, f32[384,128]{1,0:T(8,128)S(1)}, f32[384,128]{1,0:T(8,128)S(1)}, f32[384,128]{1,0:T(8,128)S(1)}) custom-call(bf16[272,128]{1,0:T(8,128)(2,1)S(1)} %get-tuple-element.126.refs_0_, bf16[272,128]{1,0:T(8,128)(2,1)S(1)} %collective-permute-done.5.refs_1_, bf16[272,128]{1,0:T(8,128)(2,1)S(1)} %collective-permute-done.6.refs_2_, ...), custom_call_target="tpu_custom_call" | custom-call | flops 1000000000 | bytes 100000 | tf_op jit(solution)/shard_map/pallas_call | solution.py:605
  36.3 3.7 %shard_map.191.refs_0_ = bf16[256,128]{1,0:T(8,128)(2,1)S(1)} custom-call(bf16[272,128]{1,0:T(8,128)(2,1)S(1)} %get-tuple-element.126.refs_0_, bf16[272,128]{1,0:T(8,128)(2,1)S(1)} %collective-permute-done.5.refs_1_, bf16[272,128]{1,0:T(8,128)(2,1)S(1)} %collective-permute-done.6.refs_2_, bf16[272,128]{1,0:T(8,128)(2,1)S(1)} %collective-permute-done.7.refs_3_, ...), custom_call_target="tpu_custom_call" | custom-call | flops 6000000000 | bytes 600000 | tf_op jit(solution)/shard_map/pallas_call | solution.py:605
  40.0 1.1 %collective-permute-start.15 = (bf16[256,128]{1,0:T(8,128)(2,1)S(1)}, bf16[256,128]{1,0:T(8,128)(2,1)S(1)}, u32[]{:S(2)}, u32[]{:S(2)}) collective-permute-start(bf16[256,128]{1,0:T(8,128)(2,1)S(1)} %shard_map.191.refs_0_), channel_id=1, source_target_pairs={{0,8},{4,12},{8,0},{12,4},{1,9},{5,13},{9,1},{13,5},{2,10},{6,14},... | collective-permute-start | bytes 196616 | tf_op jit(solution)/shard_map/ppermute | solution.py:626
  41.1 0.3 shard_map.192.refs_8_
  41.5 0.2 collective-permute-start.14
  41.6 2.8 %collective-permute-done.15.refs_2_ = bf16[256,128]{1,0:T(8,128)(2,1)S(1)} collective-permute-done((bf16[256,128]{1,0:T(8,128)(2,1)S(1)}, bf16[256,128]{1,0:T(8,128)(2,1)S(1)}, u32[]{:S(2)}, u32[]{:S(2)}) %collective-permute-start.15) | collective-permute-done | bytes 65568 | tf_op jit(solution)/shard_map/ppermute | solution.py:626
  44.4 1.2 %collective-permute-done.16.refs_3_ = bf16[256,128]{1,0:T(8,128)(2,1)S(1)} collective-permute-done((bf16[256,128]{1,0:T(8,128)(2,1)S(1)}, bf16[256,128]{1,0:T(8,128)(2,1)S(1)}, u32[]{:S(2)}, u32[]{:S(2)}) %collective-permute-start.16) | collective-permute-done | bytes 65568 | tf_op jit(solution)/shard_map/ppermute | solution.py:626
  45.7 3.7 %shard_map.193 = bf16[512,128]{1,0:T(8,128)(2,1)} custom-call(bf16[256,128]{1,0:T(8,128)(2,1)S(1)} %shard_map.191.refs_0_, bf16[256,128]{1,0:T(8,128)(2,1)S(1)} %collective-permute-done.14.refs_1_, bf16[256,128]{1,0:T(8,128)(2,1)S(1)} %collective-permute-done.15.refs_2_, bf16[256,128]{1,0:T(8,128)(2,1)S(1)} %collective-permute-done.16.refs_3_, ...), custom_call_target="tpu_custom_call" | custom-call | flops 3000000000 | bytes 300000 | tf_op jit(solution)/shard_map/pallas_call | solution.py:605
  (47 shorter events, 0.5 us)
Async XLA Ops:
  0.0 3.2 %copy-start = (bf16[5,384,128]{2,1,0:T(8,128)(2,1)S(1)}, bf16[5,384,128]{2,1,0:T(8,128)(2,1)}, u32[]{:S(2)}) copy-start(bf16[5,384,128]{2,1,0:T(8,128)(2,1)} %refs_16_.3) | copy-start | bytes 1474564
  0.0 3.2 %copy-start.1 = (bf16[5,256,128]{2,1,0:T(8,128)(2,1)S(1)}, bf16[5,256,128]{2,1,0:T(8,128)(2,1)}, u32[]{:S(2)}) copy-start(bf16[5,256,128]{2,1,0:T(8,128)(2,1)} %refs_18_.1) | copy-start | bytes 983044
  0.0 3.2 %copy-start.2 = (bf16[3072,128]{1,0:T(8,128)(2,1)S(1)}, bf16[3072,128]{1,0:T(8,128)(2,1)}, u32[]{:S(2)}) copy-start(bf16[3072,128]{1,0:T(8,128)(2,1)} %refs_12_.2) | copy-start | bytes 2359300
  0.0 3.2 %copy-start.3 = (bf16[5,128,128]{2,1,0:T(8,128)(2,1)S(1)}, bf16[5,128,128]{2,1,0:T(8,128)(2,1)}, u32[]{:S(2)}) copy-start(bf16[5,128,128]{2,1,0:T(8,128)(2,1)} %refs_17_.1) | copy-start | bytes 491524
  0.0 3.2 %copy-start.4 = (bf16[5,128,128]{2,1,0:T(8,128)(2,1)S(1)}, bf16[5,128,128]{2,1,0:T(8,128)(2,1)}, u32[]{:S(2)}) copy-start(bf16[5,128,128]{2,1,0:T(8,128)(2,1)} %refs_19_.1) | copy-start | bytes 491524
  0.0 3.2 %copy-start.5 = (bf16[512,128]{1,0:T(8,128)(2,1)S(1)}, bf16[512,128]{1,0:T(8,128)(2,1)}, u32[]{:S(2)}) copy-start(bf16[512,128]{1,0:T(8,128)(2,1)} %refs_10_.2) | copy-start | bytes 393220
  0.0 3.2 %copy-start.6 = (s32[3072]{0:T(1024)S(1)}, s32[3072]{0:T(1024)}, u32[]{:S(2)}) copy-start(s32[3072]{0:T(1024)} %param.21) | copy-start | bytes 36868
  0.0 3.2 %copy-start.12 = (s32[3072]{0:T(1024)S(1)}, s32[3072]{0:T(1024)}, u32[]{:S(2)}) copy-start(s32[3072]{0:T(1024)} %param.20) | copy-start | bytes 36868
  2.0 2.7 %collective-permute-start = (bf16[80,128]{1,0:T(8,128)(2,1)}, bf16[80,128]{1,0:T(8,128)(2,1)S(1)}, u32[]{:S(2)}, u32[]{:S(2)}) collective-permute-start(bf16[80,128]{1,0:T(8,128)(2,1)} %get-tuple-element.80), channel_id=1, source_target_pairs={{0,4},{4,0},{8,12},{12,8},{1,5},{5,1},{9,13},{13,9},{2,6},{6,2},{1... | collective-permute-start | bytes 61448 | tf_op jit(solution)/shard_map/ppermute | solution.py:696
  2.5 2.2 %collective-permute-start.1 = (bf16[80,128]{1,0:T(8,128)(2,1)}, bf16[80,128]{1,0:T(8,128)(2,1)S(1)}, u32[]{:S(2)}, u32[]{:S(2)}) collective-permute-start(bf16[80,128]{1,0:T(8,128)(2,1)} %get-tuple-element.81), channel_id=1, source_target_pairs={{4,8},{8,4},{5,9},{9,5},{6,10},{10,6},{7,11},{11,7},{20,24},{24,20... | collective-permute-start | bytes 61448 | tf_op jit(solution)/shard_map/ppermute | solution.py:697
  3.3 1.4 %copy-start.7 = (bf16[16,128]{1,0:T(8,128)(2,1)S(1)}, bf16[16,128]{1,0:T(8,128)(2,1)}, u32[]{:S(2)}) copy-start(bf16[16,128]{1,0:T(8,128)(2,1)} %get-tuple-element.83.refs_2_.refs_0_) | copy-start | bytes 12292
  4.7 7.5 %copy-start.8 = (bf16[8192,128]{1,0:T(8,128)(2,1)S(1)}, bf16[8192,128]{1,0:T(8,128)(2,1)}, u32[]{:S(2)}) copy-start(bf16[8192,128]{1,0:T(8,128)(2,1)} %refs_24_.1) | copy-start | bytes 6291460
  4.7 7.5 %copy-start.10 = (s32[8192]{0:T(1024)S(1)}, s32[8192]{0:T(1024)}, u32[]{:S(2)}) copy-start(s32[8192]{0:T(1024)} %param.31) | copy-start | bytes 98308
  4.7 7.5 %copy-start.11 = (s32[8192]{0:T(1024)S(1)}, s32[8192]{0:T(1024)}, u32[]{:S(2)}) copy-start(s32[8192]{0:T(1024)} %param.32) | copy-start | bytes 98308
  6.5 9.6 %collective-permute-start.2 = (bf16[528,128]{1,0:T(8,128)(2,1)S(1)}, bf16[528,128]{1,0:T(8,128)(2,1)S(1)}, u32[]{:S(2)}, u32[]{:S(2)}) collective-permute-start(bf16[528,128]{1,0:T(8,128)(2,1)S(1)} %get-tuple-element.105.refs_0_), channel_id=1, source_target_pairs={{0,8},{4,12},{8,0},{12,4},{1,9},{5,13},{9,1},{13,5},{2,10},{6,14},... | collective-permute-start | bytes 405512 | tf_op jit(solution)/shard_map/ppermute | solution.py:626
  12.3 3.9 %copy-start.9 = (bf16[1536,128]{1,0:T(8,128)(2,1)S(1)}, bf16[1536,128]{1,0:T(8,128)(2,1)}, u32[]{:S(2)}) copy-start(bf16[1536,128]{1,0:T(8,128)(2,1)} %refs_10_.3) | copy-start | bytes 1179652
  12.3 3.9 %copy-start.13 = (s32[1536]{0:T(1024)S(1)}, s32[1536]{0:T(1024)}, u32[]{:S(2)}) copy-start(s32[1536]{0:T(1024)} %param.24) | copy-start | bytes 18436
  12.3 3.9 %copy-start.14 = (s32[1536]{0:T(1024)S(1)}, s32[1536]{0:T(1024)}, u32[]{:S(2)}) copy-start(s32[1536]{0:T(1024)} %param.25) | copy-start | bytes 18436
  14.7 2.0 %collective-permute-start.4 = (bf16[528,128]{1,0:T(8,128)(2,1)S(1)}, bf16[528,128]{1,0:T(8,128)(2,1)S(1)}, u32[]{:S(2)}, u32[]{:S(2)}) collective-permute-start(bf16[528,128]{1,0:T(8,128)(2,1)S(1)} %get-tuple-element.105.refs_0_), channel_id=1, source_target_pairs={{0,4},{4,0},{8,12},{12,8},{1,5},{5,1},{9,13},{13,9},{2,6},{6,2},{1... | collective-permute-start | bytes 405512 | tf_op jit(solution)/shard_map/ppermute | solution.py:626
  16.1 1.4 %collective-permute-start.3 = (bf16[528,128]{1,0:T(8,128)(2,1)S(1)}, bf16[528,128]{1,0:T(8,128)(2,1)S(1)}, u32[]{:S(2)}, u32[]{:S(2)}) collective-permute-start(bf16[528,128]{1,0:T(8,128)(2,1)S(1)} %collective-permute-done.2.refs_2_), channel_id=1, source_target_pairs={{0,4},{4,0},{8,12},{12,8},{1,5},{5,1},{9,13},{13,9},{2,6},{6,2},{1... | collective-permute-start | bytes 405512 | tf_op jit(solution)/shard_map/ppermute | solution.py:626
  19.4 6.3 %collective-permute-start.5 = (bf16[272,128]{1,0:T(8,128)(2,1)S(1)}, bf16[272,128]{1,0:T(8,128)(2,1)S(1)}, u32[]{:S(2)}, u32[]{:S(2)}) collective-permute-start(bf16[272,128]{1,0:T(8,128)(2,1)S(1)} %get-tuple-element.126.refs_0_), channel_id=1, source_target_pairs={{0,1},{1,0},{2,3},{3,2},{4,5},{5,4},{6,7},{7,6},{8,9},{9,8},{10,11... | collective-permute-start | bytes 208904 | tf_op jit(solution)/shard_map/ppermute | solution.py:635
  21.6 7.8 %collective-permute-start.6 = (bf16[272,128]{1,0:T(8,128)(2,1)S(1)}, bf16[272,128]{1,0:T(8,128)(2,1)S(1)}, u32[]{:S(2)}, u32[]{:S(2)}) collective-permute-start(bf16[272,128]{1,0:T(8,128)(2,1)S(1)} %get-tuple-element.126.refs_0_), channel_id=1, source_target_pairs={{0,2},{1,3},{2,0},{3,1},{4,6},{5,7},{6,4},{7,5},{8,10},{9,11},{10,... | collective-permute-start | bytes 208904 | tf_op jit(solution)/shard_map/ppermute | solution.py:635
  24.2 6.2 %collective-permute-start.7 = (bf16[272,128]{1,0:T(8,128)(2,1)S(1)}, bf16[272,128]{1,0:T(8,128)(2,1)S(1)}, u32[]{:S(2)}, u32[]{:S(2)}) collective-permute-start(bf16[272,128]{1,0:T(8,128)(2,1)S(1)} %get-tuple-element.126.refs_0_), channel_id=1, source_target_pairs={{0,3},{1,2},{2,1},{3,0},{4,7},{5,6},{6,5},{7,4},{8,11},{9,10},{10,... | collective-permute-start | bytes 208904 | tf_op jit(solution)/shard_map/ppermute | solution.py:635
  24.2 7.3 %collective-permute-start.8 = (bf16[272,128]{1,0:T(8,128)(2,1)S(1)}, bf16[272,128]{1,0:T(8,128)(2,1)S(1)}, u32[]{:S(2)}, u32[]{:S(2)}) collective-permute-start(bf16[272,128]{1,0:T(8,128)(2,1)S(1)} %get-tuple-element.126.refs_0_), channel_id=1, source_target_pairs={{0,8},{4,12},{8,0},{12,4},{1,9},{5,13},{9,1},{13,5},{2,10},{6,14},... | collective-permute-start | bytes 208904 | tf_op jit(solution)/shard_map/ppermute | solution.py:635
  25.6 5.9 %collective-permute-start.9 = (bf16[272,128]{1,0:T(8,128)(2,1)S(1)}, bf16[272,128]{1,0:T(8,128)(2,1)S(1)}, u32[]{:S(2)}, u32[]{:S(2)}) collective-permute-start(bf16[272,128]{1,0:T(8,128)(2,1)S(1)} %collective-permute-done.5.refs_1_), channel_id=1, source_target_pairs={{0,8},{4,12},{8,0},{12,4},{1,9},{5,13},{9,1},{13,5},{2,10},{6,14},... | collective-permute-start | bytes 208904 | tf_op jit(solution)/shard_map/ppermute | solution.py:635
  29.4 4.3 %collective-permute-start.10 = (bf16[272,128]{1,0:T(8,128)(2,1)S(1)}, bf16[272,128]{1,0:T(8,128)(2,1)S(1)}, u32[]{:S(2)}, u32[]{:S(2)}) collective-permute-start(bf16[272,128]{1,0:T(8,128)(2,1)S(1)} %collective-permute-done.6.refs_2_), channel_id=1, source_target_pairs={{0,8},{4,12},{8,0},{12,4},{1,9},{5,13},{9,1},{13,5},{2,10},{6,14},... | collective-permute-start | bytes 208904 | tf_op jit(solution)/shard_map/ppermute | solution.py:635
  30.4 4.3 %collective-permute-start.11 = (bf16[272,128]{1,0:T(8,128)(2,1)S(1)}, bf16[272,128]{1,0:T(8,128)(2,1)S(1)}, u32[]{:S(2)}, u32[]{:S(2)}) collective-permute-start(bf16[272,128]{1,0:T(8,128)(2,1)S(1)} %collective-permute-done.7.refs_3_), channel_id=1, source_target_pairs={{0,8},{4,12},{8,0},{12,4},{1,9},{5,13},{9,1},{13,5},{2,10},{6,14},... | collective-permute-start | bytes 208904 | tf_op jit(solution)/shard_map/ppermute | solution.py:635
  31.4 3.4 %collective-permute-start.12 = (bf16[1088,128]{1,0:T(8,128)(2,1)S(1)}, bf16[1088,128]{1,0:T(8,128)(2,1)S(1)}, u32[]{:S(2)}, u32[]{:S(2)}) collective-permute-start(bf16[1088,128]{1,0:T(8,128)(2,1)S(1)} %pad_maximum_fusion), channel_id=1, source_target_pairs={{0,4},{4,0},{8,12},{12,8},{1,5},{5,1},{9,13},{13,9},{2,6},{6,2},{1... | collective-permute-start | bytes 835592 | tf_op jit(solution)/shard_map/ppermute | solution.py:635
  34.7 1.6 %collective-permute-start.13 = (bf16[1088,128]{1,0:T(8,128)(2,1)S(1)}, bf16[1088,128]{1,0:T(8,128)(2,1)S(1)}, u32[]{:S(2)}, u32[]{:S(2)}) collective-permute-start(bf16[1088,128]{1,0:T(8,128)(2,1)S(1)} %pad_maximum_fusion.1), channel_id=1, source_target_pairs={{0,4},{4,0},{8,12},{12,8},{1,5},{5,1},{9,13},{13,9},{2,6},{6,2},{1... | collective-permute-start | bytes 835592 | tf_op jit(solution)/shard_map/ppermute | solution.py:635
  40.0 4.4 %collective-permute-start.15 = (bf16[256,128]{1,0:T(8,128)(2,1)S(1)}, bf16[256,128]{1,0:T(8,128)(2,1)S(1)}, u32[]{:S(2)}, u32[]{:S(2)}) collective-permute-start(bf16[256,128]{1,0:T(8,128)(2,1)S(1)} %shard_map.191.refs_0_), channel_id=1, source_target_pairs={{0,8},{4,12},{8,0},{12,4},{1,9},{5,13},{9,1},{13,5},{2,10},{6,14},... | collective-permute-start | bytes 196616 | tf_op jit(solution)/shard_map/ppermute | solution.py:626
  41.5 3.0 %collective-permute-start.14 = (bf16[256,128]{1,0:T(8,128)(2,1)S(1)}, bf16[256,128]{1,0:T(8,128)(2,1)S(1)}, u32[]{:S(2)}, u32[]{:S(2)}) collective-permute-start(bf16[256,128]{1,0:T(8,128)(2,1)S(1)} %shard_map.191.refs_0_), channel_id=1, source_target_pairs={{0,4},{4,0},{8,12},{12,8},{1,5},{5,1},{9,13},{13,9},{2,6},{6,2},{1... | collective-permute-start | bytes 196616 | tf_op jit(solution)/shard_map/ppermute | solution.py:626
  44.4 1.3 %collective-permute-start.16 = (bf16[256,128]{1,0:T(8,128)(2,1)S(1)}, bf16[256,128]{1,0:T(8,128)(2,1)S(1)}, u32[]{:S(2)}, u32[]{:S(2)}) collective-permute-start(bf16[256,128]{1,0:T(8,128)(2,1)S(1)} %collective-permute-done.15.refs_2_), channel_id=1, source_target_pairs={{0,4},{4,0},{8,12},{12,8},{1,5},{5,1},{9,13},{13,9},{2,6},{6,2},{1... | collective-permute-start | bytes 196616 | tf_op jit(solution)/shard_map/ppermute | solution.py:626

commit v8 on v7

--- a/solution.py
+++ b/solution.py
@@ -551,12 +551,15 @@
     out[...] = finish(lambda rows: before3[rows, :] + inner(rows), table[:coarse], receivers, None, edges, weights)
 
 
-def last_kernel(regions, *refs):
-    blocks, (down, parent_hots, parent_blocks, edges, before, *rest) = refs[:regions], refs[regions:]
+def raise_kernel(*refs):
+    *blocks, down, hots, which, out = refs
+    out[...] = down[...].astype(F32) + pick(hots[...], which[...], [block[...] for block in blocks])
+
+
+def last_kernel(place, last, raised, hots, which, edges, before, *rest):
     cols, receivers, weights, out = rest[:6], rest[6], rest[7:11], rest[11]
     own = out.shape[0]
-    parent = pick(parent_hots[...], parent_blocks[...], [block[...] for block in blocks])
-    table = (down[...].astype(F32) + parent).astype(BF16)
+    table = (raised[...] + jnp.where(which[...] == place, dot(hots[...], last[...]), 0.0)).astype(BF16)
     first = weights[0].get()[...]
     inner, outside = from_own(cols, table[:own], first), from_halo(cols, table[own:], own, first)
     out[...] = finish(lambda rows: before[rows, :] + inner(rows) + outside(rows), table[:own], receivers, cols[-1], edges, weights)
@@ -786,9 +789,11 @@
     )
     before = call(edge_kernel, [fine_edges2], [(fine_edges.shape, F32)], one(4))
     blocks3, before = over_region(coarse_final, before)
+    table, hots, which = table
+    (raised,) = call(raise_kernel, blocks3[:-1] + [table, hots, which], [(table_shape, F32)])
     (fine_final,) = call(
-        functools.partial(last_kernel, regions),
-        blocks3 + [*table, fine_edges2, *before, *fine_cols],
+        functools.partial(last_kernel, regions - 1),
+        [blocks3[-1], raised, hots, which, fine_edges2, *before, *fine_cols],
         [((fine, LANES), BF16)],
         plain(fine_recv) + level(4),
         cost=3,

time: 49.6 us -> 49.5 us (level)
    pallas_call x13 -> x14, Pallas kernels: 20.1 us -> 20.3 us  [call(): pl.pallas_call(body, out_shape=[jax.ShapeDtypeStruct(shape, dtype) for sh...]
  transfers between devices with their start and end apart: 17 -> 17, of which waited for: 9 -> 9; matrix products, arithmetic and copies ran while one was open for 0% -> 0% of each run, Pallas kernels for 14% -> 15%
where the time goes in v8:
time: 49.5 us; the launch traced here: 49.4 us
  Pallas kernels  20.3 us (41%)
  starting transfers between devices  16.8 us (34%)
  waiting for transfers between devices  11.7 us (24%)
    pallas_call x14, Pallas kernels, call(): pl.pallas_call(body, out_shape=[jax.ShapeDtypeStruct(shape, dtype) for sh...  20.3 us
    ppermute x9, starting transfers between devices, over_both(): lax.ppermute(array, axis, [(i, i ^ bits) for i in range(lax.axis_size(axi...  8.63 us
    ppermute x6, starting transfers between devices, over_region(): lax.ppermute(going[j], 'region', [(i, i ^ bit) for i in range(count)])  7.03 us
    ppermute x9, waiting for transfers between devices, over_both(): lax.ppermute(array, axis, [(i, i ^ bits) for i in range(lax.axis_size(axi...  6.17 us
    ppermute x6, waiting for transfers between devices, over_region(): lax.ppermute(going[j], 'region', [(i, i ^ bit) for i in range(count)])  5.57 us
  transfers between devices with their start and end apart: 17, of which 9 were waited for; matrix products, arithmetic and copies ran while one was open for 0% of the time, Pallas kernels for 15%

profile of v8, /device:TPU:0, one launch (start us, length us, event | category | flops | bytes accessed | tf_op | source)
XLA Modules:
  0.0 49.4 jit_solution(9299504260814457562)
XLA Ops:
  0.0 1.9 %shard_map.181 = (bf16[80,128]{1,0:T(8,128)(2,1)}, bf16[80,128]{1,0:T(8,128)(2,1)}, bf16[16,128]{1,0:T(8,128)(2,1)}) custom-call(bf16[512,128]{1,0:T(8,128)(2,1)} %refs_10_.2, s32[2,64]{1,0:T(2,128)} %refs_1_.3, s32[2,32]{1,0:T(2,128)} %refs_2_.1, s32[4,128]{1,0:T(4,128)} %bitcast.19, s32[4,128]{1,0:T(4,128)} %bitcast.20, s32[2,128]{1,0:T(2,128)} %bitcast.21), custom_call_target="tpu_custom_call" | custom-call | flops 1000000000 | bytes 100000 | tf_op jit(solution)/shard_map/pallas_call | solution.py:608
  2.0 0.5 %collective-permute-start = (bf16[80,128]{1,0:T(8,128)(2,1)}, bf16[80,128]{1,0:T(8,128)(2,1)S(1)}, u32[]{:S(2)}, u32[]{:S(2)}) collective-permute-start(bf16[80,128]{1,0:T(8,128)(2,1)} %get-tuple-element.80), channel_id=1, source_target_pairs={{0,4},{4,0},{8,12},{12,8},{1,5},{5,1},{9,13},{13,9},{2,6},{6,2},{1... | collective-permute-start | bytes 61448 | tf_op jit(solution)/shard_map/ppermute | solution.py:699
  2.5 0.7 %collective-permute-start.1 = (bf16[80,128]{1,0:T(8,128)(2,1)}, bf16[80,128]{1,0:T(8,128)(2,1)S(1)}, u32[]{:S(2)}, u32[]{:S(2)}) collective-permute-start(bf16[80,128]{1,0:T(8,128)(2,1)} %get-tuple-element.81), channel_id=1, source_target_pairs={{4,8},{8,4},{5,9},{9,5},{6,10},{10,6},{7,11},{11,7},{20,24},{24,20... | collective-permute-start | bytes 61448 | tf_op jit(solution)/shard_map/ppermute | solution.py:700
  3.3 1.4 %shard_map.182 = (s32[3072,128]{1,0:T(8,128)S(1)}, s32[3072,128]{1,0:T(8,128)S(1)}, s32[3072,128]{1,0:T(8,128)S(1)}, s32[3072,128]{1,0:T(8,128)S(1)}, s32[3072,1...) custom-call(bf16[512,128]{1,0:T(8,128)(2,1)S(1)} %copy-done.5, s32[24,128]{1,0:T(8,128)S(1)} %bitcast.14, ...), custom_call_target="tpu_custom_call" | custom-call | flops 2000000000 | bytes 200000 | tf_op jit(solution)/shard_map/pallas_call | solution.py:608
  4.7 1.8 %shard_map.183 = (bf16[528,128]{1,0:T(8,128)(2,1)S(1)}, bf16[3072,128]{1,0:T(8,128)(2,1)S(1)}) custom-call(bf16[80,128]{1,0:T(8,128)(2,1)S(1)} %collective-permute-done.refs_0_.refs_1_, bf16[80,128]{1,0:T(8,128)(2,1)S(1)} %collective-permute-done.1.refs_1_.refs_2_, bf16[16,128]{1,0:T(8,128)(2,1)S(1)} %copy-done.7, ...), custom_call_target="tpu_custom_call" | custom-call | flops 3000000000 | bytes 300000 | tf_op jit(solution)/shard_map/pallas_call | solution.py:608
  6.5 5.7 %collective-permute-start.2 = (bf16[528,128]{1,0:T(8,128)(2,1)S(1)}, bf16[528,128]{1,0:T(8,128)(2,1)S(1)}, u32[]{:S(2)}, u32[]{:S(2)}) collective-permute-start(bf16[528,128]{1,0:T(8,128)(2,1)S(1)} %get-tuple-element.105.refs_0_), channel_id=1, source_target_pairs={{0,8},{4,12},{8,0},{12,4},{1,9},{5,13},{9,1},{13,5},{2,10},{6,14},... | collective-permute-start | bytes 405512 | tf_op jit(solution)/shard_map/ppermute | solution.py:629
  12.3 2.3 %shard_map.184 = (s32[384,128]{1,0:T(8,128)S(1)}, s32[3,128]{1,0:T(4,128)S(1)}, s32[64,128]{1,0:T(8,128)S(1)}, s32[64,128]{1,0:T(8,128)S(1)}, s32[64,128]{1,0:T(...) custom-call(bf16[16,128]{1,0:T(8,128)(2,1)S(1)} %copy-done.7, ...), custom_call_target="tpu_custom_call" | custom-call | flops 3000000000 | bytes 300000 | tf_op jit(solution)/shard_map/pallas_call | solution.py:608
  14.7 1.4 %collective-permute-done.2.refs_2_ = bf16[528,128]{1,0:T(8,128)(2,1)S(1)} collective-permute-done((bf16[528,128]{1,0:T(8,128)(2,1)S(1)}, bf16[528,128]{1,0:T(8,128)(2,1)S(1)}, u32[]{:S(2)}, u32[]{:S(2)}) %collective-permute-start.2) | collective-permute-done | bytes 135200 | tf_op jit(solution)/shard_map/ppermute | solution.py:629
  16.1 0.5 shard_map.186
  16.6 0.4 shard_map.185
  17.1 0.4 collective-permute-done.3.refs_1_.refs_3_
  17.5 1.9 %shard_map.187 = (bf16[272,128]{1,0:T(8,128)(2,1)S(1)}, bf16[1536,128]{1,0:T(8,128)(2,1)S(1)}) custom-call(bf16[528,128]{1,0:T(8,128)(2,1)S(1)} %get-tuple-element.105.refs_0_, bf16[528,128]{1,0:T(8,128)(2,1)S(1)} %collective-permute-done.3.refs_1_.refs_3_, s32[320,128]{1,0:T(8,128)S(1)} %get-tuple-element.118.refs_3_.refs_2_, ...), custom_call_target="tpu_custom_call" | custom-call | flops 3000000000 | bytes 300000 | tf_op jit(solution)/shard_map/pallas_call | solution.py:608
  19.4 2.2 %collective-permute-start.5 = (bf16[272,128]{1,0:T(8,128)(2,1)S(1)}, bf16[272,128]{1,0:T(8,128)(2,1)S(1)}, u32[]{:S(2)}, u32[]{:S(2)}) collective-permute-start(bf16[272,128]{1,0:T(8,128)(2,1)S(1)} %get-tuple-element.126.refs_0_), channel_id=1, source_target_pairs={{0,1},{1,0},{2,3},{3,2},{4,5},{5,4},{6,7},{7,6},{8,9},{9,8},{10,11... | collective-permute-start | bytes 208904 | tf_op jit(solution)/shard_map/ppermute | solution.py:638
  21.6 2.6 %collective-permute-start.6 = (bf16[272,128]{1,0:T(8,128)(2,1)S(1)}, bf16[272,128]{1,0:T(8,128)(2,1)S(1)}, u32[]{:S(2)}, u32[]{:S(2)}) collective-permute-start(bf16[272,128]{1,0:T(8,128)(2,1)S(1)} %get-tuple-element.126.refs_0_), channel_id=1, source_target_pairs={{0,2},{1,3},{2,0},{3,1},{4,6},{5,7},{6,4},{7,5},{8,10},{9,11},{10,... | collective-permute-start | bytes 208904 | tf_op jit(solution)/shard_map/ppermute | solution.py:638
  24.2 0.8 %collective-permute-start.8 = (bf16[272,128]{1,0:T(8,128)(2,1)S(1)}, bf16[272,128]{1,0:T(8,128)(2,1)S(1)}, u32[]{:S(2)}, u32[]{:S(2)}) collective-permute-start(bf16[272,128]{1,0:T(8,128)(2,1)S(1)} %get-tuple-element.126.refs_0_), channel_id=1, source_target_pairs={{0,8},{4,12},{8,0},{12,4},{1,9},{5,13},{9,1},{13,5},{2,10},{6,14},... | collective-permute-start | bytes 208904 | tf_op jit(solution)/shard_map/ppermute | solution.py:638
  25.0 0.2 shard_map.189.refs_26_
  25.2 0.4 shard_map.188
  25.6 1.3 %collective-permute-start.9 = (bf16[272,128]{1,0:T(8,128)(2,1)S(1)}, bf16[272,128]{1,0:T(8,128)(2,1)S(1)}, u32[]{:S(2)}, u32[]{:S(2)}) collective-permute-start(bf16[272,128]{1,0:T(8,128)(2,1)S(1)} %collective-permute-done.5.refs_1_), channel_id=1, source_target_pairs={{0,8},{4,12},{8,0},{12,4},{1,9},{5,13},{9,1},{13,5},{2,10},{6,14},... | collective-permute-start | bytes 208904 | tf_op jit(solution)/shard_map/ppermute | solution.py:638
  26.9 2.5 %collective-permute-done.6.refs_2_ = bf16[272,128]{1,0:T(8,128)(2,1)S(1)} collective-permute-done((bf16[272,128]{1,0:T(8,128)(2,1)S(1)}, bf16[272,128]{1,0:T(8,128)(2,1)S(1)}, u32[]{:S(2)}, u32[]{:S(2)}) %collective-permute-start.6) | collective-permute-done | bytes 69664 | tf_op jit(solution)/shard_map/ppermute | solution.py:638
  29.4 0.6 %collective-permute-start.10 = (bf16[272,128]{1,0:T(8,128)(2,1)S(1)}, bf16[272,128]{1,0:T(8,128)(2,1)S(1)}, u32[]{:S(2)}, u32[]{:S(2)}) collective-permute-start(bf16[272,128]{1,0:T(8,128)(2,1)S(1)} %collective-permute-done.6.refs_2_), channel_id=1, source_target_pairs={{0,8},{4,12},{8,0},{12,4},{1,9},{5,13},{9,1},{13,5},{2,10},{6,14},... | collective-permute-start | bytes 208904 | tf_op jit(solution)/shard_map/ppermute | solution.py:638
  30.0 0.4 collective-permute-done.7.refs_3_
  30.4 1.0 %collective-permute-start.11 = (bf16[272,128]{1,0:T(8,128)(2,1)S(1)}, bf16[272,128]{1,0:T(8,128)(2,1)S(1)}, u32[]{:S(2)}, u32[]{:S(2)}) collective-permute-start(bf16[272,128]{1,0:T(8,128)(2,1)S(1)} %collective-permute-done.7.refs_3_), channel_id=1, source_target_pairs={{0,8},{4,12},{8,0},{12,4},{1,9},{5,13},{9,1},{13,5},{2,10},{6,14},... | collective-permute-start | bytes 208904 | tf_op jit(solution)/shard_map/ppermute | solution.py:638
  31.5 2.2 %collective-permute-done.10.refs_6_ = bf16[272,128]{1,0:T(8,128)(2,1)S(1)} collective-permute-done((bf16[272,128]{1,0:T(8,128)(2,1)S(1)}, bf16[272,128]{1,0:T(8,128)(2,1)S(1)}, u32[]{:S(2)}, u32[]{:S(2)}) %collective-permute-start.10) | collective-permute-done | bytes 69664 | tf_op jit(solution)/shard_map/ppermute | solution.py:638
  33.7 1.0 %collective-permute-done.11.refs_7_ = bf16[272,128]{1,0:T(8,128)(2,1)S(1)} collective-permute-done((bf16[272,128]{1,0:T(8,128)(2,1)S(1)}, bf16[272,128]{1,0:T(8,128)(2,1)S(1)}, u32[]{:S(2)}, u32[]{:S(2)}) %collective-permute-start.11) | collective-permute-done | bytes 69664 | tf_op jit(solution)/shard_map/ppermute | solution.py:638
  34.8 1.4 %shard_map.190 = (f32[384,128]{1,0:T(8,128)S(1)}, f32[384,128]{1,0:T(8,128)S(1)}, f32[384,128]{1,0:T(8,128)S(1)}, f32[384,128]{1,0:T(8,128)S(1)}) custom-call(bf16[272,128]{1,0:T(8,128)(2,1)S(1)} %get-tuple-element.126.refs_0_, bf16[272,128]{1,0:T(8,128)(2,1)S(1)} %collective-permute-done.5.refs_1_, bf16[272,128]{1,0:T(8,128)(2,1)S(1)} %collective-permute-done.6.refs_2_, ...), custom_call_target="tpu_custom_call" | custom-call | flops 1000000000 | bytes 100000 | tf_op jit(solution)/shard_map/pallas_call | solution.py:608
  36.3 3.7 %shard_map.191.refs_0_ = bf16[256,128]{1,0:T(8,128)(2,1)S(1)} custom-call(bf16[272,128]{1,0:T(8,128)(2,1)S(1)} %get-tuple-element.126.refs_0_, bf16[272,128]{1,0:T(8,128)(2,1)S(1)} %collective-permute-done.5.refs_1_, bf16[272,128]{1,0:T(8,128)(2,1)S(1)} %collective-permute-done.6.refs_2_, bf16[272,128]{1,0:T(8,128)(2,1)S(1)} %collective-permute-done.7.refs_3_, ...), custom_call_target="tpu_custom_call" | custom-call | flops 6000000000 | bytes 600000 | tf_op jit(solution)/shard_map/pallas_call | solution.py:608
  40.0 1.1 %collective-permute-start.14 = (bf16[256,128]{1,0:T(8,128)(2,1)S(1)}, bf16[256,128]{1,0:T(8,128)(2,1)S(1)}, u32[]{:S(2)}, u32[]{:S(2)}) collective-permute-start(bf16[256,128]{1,0:T(8,128)(2,1)S(1)} %shard_map.191.refs_0_), channel_id=1, source_target_pairs={{0,8},{4,12},{8,0},{12,4},{1,9},{5,13},{9,1},{13,5},{2,10},{6,14},... | collective-permute-start | bytes 196616 | tf_op jit(solution)/shard_map/ppermute | solution.py:629
  41.1 0.3 shard_map.192.refs_5_
  41.6 2.8 %collective-permute-done.14.refs_2_ = bf16[256,128]{1,0:T(8,128)(2,1)S(1)} collective-permute-done((bf16[256,128]{1,0:T(8,128)(2,1)S(1)}, bf16[256,128]{1,0:T(8,128)(2,1)S(1)}, u32[]{:S(2)}, u32[]{:S(2)}) %collective-permute-start.14) | collective-permute-done | bytes 65568 | tf_op jit(solution)/shard_map/ppermute | solution.py:629
  44.4 0.3 shard_map.193.refs_1_
  44.8 0.9 %collective-permute-done.15.refs_0_ = bf16[256,128]{1,0:T(8,128)(2,1)S(1)} collective-permute-done((bf16[256,128]{1,0:T(8,128)(2,1)S(1)}, bf16[256,128]{1,0:T(8,128)(2,1)S(1)}, u32[]{:S(2)}, u32[]{:S(2)}) %collective-permute-start.15) | collective-permute-done | bytes 65568 | tf_op jit(solution)/shard_map/ppermute | solution.py:629
  45.7 3.7 %shard_map.194 = bf16[512,128]{1,0:T(8,128)(2,1)} custom-call(bf16[256,128]{1,0:T(8,128)(2,1)S(1)} %collective-permute-done.15.refs_0_, f32[640,128]{1,0:T(8,128)S(1)} %shard_map.193.refs_1_, bf16[640,256]{1,0:T(8,128)(2,1)S(1)} %get-tuple-element.152.refs_4_.refs_2_, s32[640,128]{1,0:T(8,128)S(1)} %get-tuple-element.153.refs_5_.refs_3_, ...), custom_call_target="tpu_custom_call" | custom-call | flops 3000000000 | bytes 300000 | tf_op jit(solution)/shard_map/pallas_call | solution.py:608
  (48 shorter events, 0.6 us)
Async XLA Ops:
  0.0 3.2 %copy-start = (bf16[5,384,128]{2,1,0:T(8,128)(2,1)S(1)}, bf16[5,384,128]{2,1,0:T(8,128)(2,1)}, u32[]{:S(2)}) copy-start(bf16[5,384,128]{2,1,0:T(8,128)(2,1)} %refs_13_.5) | copy-start | bytes 1474564
  0.0 3.2 %copy-start.1 = (bf16[5,256,128]{2,1,0:T(8,128)(2,1)S(1)}, bf16[5,256,128]{2,1,0:T(8,128)(2,1)}, u32[]{:S(2)}) copy-start(bf16[5,256,128]{2,1,0:T(8,128)(2,1)} %refs_15_.3) | copy-start | bytes 983044
  0.0 3.2 %copy-start.2 = (bf16[3072,128]{1,0:T(8,128)(2,1)S(1)}, bf16[3072,128]{1,0:T(8,128)(2,1)}, u32[]{:S(2)}) copy-start(bf16[3072,128]{1,0:T(8,128)(2,1)} %refs_12_.2) | copy-start | bytes 2359300
  0.0 3.2 %copy-start.3 = (bf16[5,128,128]{2,1,0:T(8,128)(2,1)S(1)}, bf16[5,128,128]{2,1,0:T(8,128)(2,1)}, u32[]{:S(2)}) copy-start(bf16[5,128,128]{2,1,0:T(8,128)(2,1)} %refs_14_.5) | copy-start | bytes 491524
  0.0 3.2 %copy-start.4 = (bf16[5,128,128]{2,1,0:T(8,128)(2,1)S(1)}, bf16[5,128,128]{2,1,0:T(8,128)(2,1)}, u32[]{:S(2)}) copy-start(bf16[5,128,128]{2,1,0:T(8,128)(2,1)} %refs_16_.3) | copy-start | bytes 491524
  0.0 3.2 %copy-start.5 = (bf16[512,128]{1,0:T(8,128)(2,1)S(1)}, bf16[512,128]{1,0:T(8,128)(2,1)}, u32[]{:S(2)}) copy-start(bf16[512,128]{1,0:T(8,128)(2,1)} %refs_10_.2) | copy-start | bytes 393220
  0.0 3.2 %copy-start.6 = (s32[3072]{0:T(1024)S(1)}, s32[3072]{0:T(1024)}, u32[]{:S(2)}) copy-start(s32[3072]{0:T(1024)} %param.21) | copy-start | bytes 36868
  0.0 3.2 %copy-start.12 = (s32[3072]{0:T(1024)S(1)}, s32[3072]{0:T(1024)}, u32[]{:S(2)}) copy-start(s32[3072]{0:T(1024)} %param.20) | copy-start | bytes 36868
  2.0 2.7 %collective-permute-start = (bf16[80,128]{1,0:T(8,128)(2,1)}, bf16[80,128]{1,0:T(8,128)(2,1)S(1)}, u32[]{:S(2)}, u32[]{:S(2)}) collective-permute-start(bf16[80,128]{1,0:T(8,128)(2,1)} %get-tuple-element.80), channel_id=1, source_target_pairs={{0,4},{4,0},{8,12},{12,8},{1,5},{5,1},{9,13},{13,9},{2,6},{6,2},{1... | collective-permute-start | bytes 61448 | tf_op jit(solution)/shard_map/ppermute | solution.py:699
  2.5 2.2 %collective-permute-start.1 = (bf16[80,128]{1,0:T(8,128)(2,1)}, bf16[80,128]{1,0:T(8,128)(2,1)S(1)}, u32[]{:S(2)}, u32[]{:S(2)}) collective-permute-start(bf16[80,128]{1,0:T(8,128)(2,1)} %get-tuple-element.81), channel_id=1, source_target_pairs={{4,8},{8,4},{5,9},{9,5},{6,10},{10,6},{7,11},{11,7},{20,24},{24,20... | collective-permute-start | bytes 61448 | tf_op jit(solution)/shard_map/ppermute | solution.py:700
  3.3 1.4 %copy-start.7 = (bf16[16,128]{1,0:T(8,128)(2,1)S(1)}, bf16[16,128]{1,0:T(8,128)(2,1)}, u32[]{:S(2)}) copy-start(bf16[16,128]{1,0:T(8,128)(2,1)} %get-tuple-element.83.refs_2_.refs_0_) | copy-start | bytes 12292
  4.7 7.5 %copy-start.8 = (bf16[8192,128]{1,0:T(8,128)(2,1)S(1)}, bf16[8192,128]{1,0:T(8,128)(2,1)}, u32[]{:S(2)}) copy-start(bf16[8192,128]{1,0:T(8,128)(2,1)} %refs_24_.1) | copy-start | bytes 6291460
  4.7 7.5 %copy-start.10 = (s32[8192]{0:T(1024)S(1)}, s32[8192]{0:T(1024)}, u32[]{:S(2)}) copy-start(s32[8192]{0:T(1024)} %param.31) | copy-start | bytes 98308
  4.7 7.5 %copy-start.11 = (s32[8192]{0:T(1024)S(1)}, s32[8192]{0:T(1024)}, u32[]{:S(2)}) copy-start(s32[8192]{0:T(1024)} %param.32) | copy-start | bytes 98308
  6.5 9.6 %collective-permute-start.2 = (bf16[528,128]{1,0:T(8,128)(2,1)S(1)}, bf16[528,128]{1,0:T(8,128)(2,1)S(1)}, u32[]{:S(2)}, u32[]{:S(2)}) collective-permute-start(bf16[528,128]{1,0:T(8,128)(2,1)S(1)} %get-tuple-element.105.refs_0_), channel_id=1, source_target_pairs={{0,8},{4,12},{8,0},{12,4},{1,9},{5,13},{9,1},{13,5},{2,10},{6,14},... | collective-permute-start | bytes 405512 | tf_op jit(solution)/shard_map/ppermute | solution.py:629
  12.3 3.9 %copy-start.9 = (bf16[1536,128]{1,0:T(8,128)(2,1)S(1)}, bf16[1536,128]{1,0:T(8,128)(2,1)}, u32[]{:S(2)}) copy-start(bf16[1536,128]{1,0:T(8,128)(2,1)} %refs_10_.3) | copy-start | bytes 1179652
  12.3 3.9 %copy-start.13 = (s32[1536]{0:T(1024)S(1)}, s32[1536]{0:T(1024)}, u32[]{:S(2)}) copy-start(s32[1536]{0:T(1024)} %param.24) | copy-start | bytes 18436
  12.3 3.9 %copy-start.14 = (s32[1536]{0:T(1024)S(1)}, s32[1536]{0:T(1024)}, u32[]{:S(2)}) copy-start(s32[1536]{0:T(1024)} %param.25) | copy-start | bytes 18436
  14.6 2.0 %collective-permute-start.4 = (bf16[528,128]{1,0:T(8,128)(2,1)S(1)}, bf16[528,128]{1,0:T(8,128)(2,1)S(1)}, u32[]{:S(2)}, u32[]{:S(2)}) collective-permute-start(bf16[528,128]{1,0:T(8,128)(2,1)S(1)} %get-tuple-element.105.refs_0_), channel_id=1, source_target_pairs={{0,4},{4,0},{8,12},{12,8},{1,5},{5,1},{9,13},{13,9},{2,6},{6,2},{1... | collective-permute-start | bytes 405512 | tf_op jit(solution)/shard_map/ppermute | solution.py:629
  16.1 1.4 %collective-permute-start.3 = (bf16[528,128]{1,0:T(8,128)(2,1)S(1)}, bf16[528,128]{1,0:T(8,128)(2,1)S(1)}, u32[]{:S(2)}, u32[]{:S(2)}) collective-permute-start(bf16[528,128]{1,0:T(8,128)(2,1)S(1)} %collective-permute-done.2.refs_2_), channel_id=1, source_target_pairs={{0,4},{4,0},{8,12},{12,8},{1,5},{5,1},{9,13},{13,9},{2,6},{6,2},{1... | collective-permute-start | bytes 405512 | tf_op jit(solution)/shard_map/ppermute | solution.py:629
  19.4 6.3 %collective-permute-start.5 = (bf16[272,128]{1,0:T(8,128)(2,1)S(1)}, bf16[272,128]{1,0:T(8,128)(2,1)S(1)}, u32[]{:S(2)}, u32[]{:S(2)}) collective-permute-start(bf16[272,128]{1,0:T(8,128)(2,1)S(1)} %get-tuple-element.126.refs_0_), channel_id=1, source_target_pairs={{0,1},{1,0},{2,3},{3,2},{4,5},{5,4},{6,7},{7,6},{8,9},{9,8},{10,11... | collective-permute-start | bytes 208904 | tf_op jit(solution)/shard_map/ppermute | solution.py:638
  21.6 7.8 %collective-permute-start.6 = (bf16[272,128]{1,0:T(8,128)(2,1)S(1)}, bf16[272,128]{1,0:T(8,128)(2,1)S(1)}, u32[]{:S(2)}, u32[]{:S(2)}) collective-permute-start(bf16[272,128]{1,0:T(8,128)(2,1)S(1)} %get-tuple-element.126.refs_0_), channel_id=1, source_target_pairs={{0,2},{1,3},{2,0},{3,1},{4,6},{5,7},{6,4},{7,5},{8,10},{9,11},{10,... | collective-permute-start | bytes 208904 | tf_op jit(solution)/shard_map/ppermute | solution.py:638
  24.2 6.2 %collective-permute-start.7 = (bf16[272,128]{1,0:T(8,128)(2,1)S(1)}, bf16[272,128]{1,0:T(8,128)(2,1)S(1)}, u32[]{:S(2)}, u32[]{:S(2)}) collective-permute-start(bf16[272,128]{1,0:T(8,128)(2,1)S(1)} %get-tuple-element.126.refs_0_), channel_id=1, source_target_pairs={{0,3},{1,2},{2,1},{3,0},{4,7},{5,6},{6,5},{7,4},{8,11},{9,10},{10,... | collective-permute-start | bytes 208904 | tf_op jit(solution)/shard_map/ppermute | solution.py:638
  24.2 7.3 %collective-permute-start.8 = (bf16[272,128]{1,0:T(8,128)(2,1)S(1)}, bf16[272,128]{1,0:T(8,128)(2,1)S(1)}, u32[]{:S(2)}, u32[]{:S(2)}) collective-permute-start(bf16[272,128]{1,0:T(8,128)(2,1)S(1)} %get-tuple-element.126.refs_0_), channel_id=1, source_target_pairs={{0,8},{4,12},{8,0},{12,4},{1,9},{5,13},{9,1},{13,5},{2,10},{6,14},... | collective-permute-start | bytes 208904 | tf_op jit(solution)/shard_map/ppermute | solution.py:638
  25.6 5.9 %collective-permute-start.9 = (bf16[272,128]{1,0:T(8,128)(2,1)S(1)}, bf16[272,128]{1,0:T(8,128)(2,1)S(1)}, u32[]{:S(2)}, u32[]{:S(2)}) collective-permute-start(bf16[272,128]{1,0:T(8,128)(2,1)S(1)} %collective-permute-done.5.refs_1_), channel_id=1, source_target_pairs={{0,8},{4,12},{8,0},{12,4},{1,9},{5,13},{9,1},{13,5},{2,10},{6,14},... | collective-permute-start | bytes 208904 | tf_op jit(solution)/shard_map/ppermute | solution.py:638
  29.4 4.3 %collective-permute-start.10 = (bf16[272,128]{1,0:T(8,128)(2,1)S(1)}, bf16[272,128]{1,0:T(8,128)(2,1)S(1)}, u32[]{:S(2)}, u32[]{:S(2)}) collective-permute-start(bf16[272,128]{1,0:T(8,128)(2,1)S(1)} %collective-permute-done.6.refs_2_), channel_id=1, source_target_pairs={{0,8},{4,12},{8,0},{12,4},{1,9},{5,13},{9,1},{13,5},{2,10},{6,14},... | collective-permute-start | bytes 208904 | tf_op jit(solution)/shard_map/ppermute | solution.py:638
  30.4 4.3 %collective-permute-start.11 = (bf16[272,128]{1,0:T(8,128)(2,1)S(1)}, bf16[272,128]{1,0:T(8,128)(2,1)S(1)}, u32[]{:S(2)}, u32[]{:S(2)}) collective-permute-start(bf16[272,128]{1,0:T(8,128)(2,1)S(1)} %collective-permute-done.7.refs_3_), channel_id=1, source_target_pairs={{0,8},{4,12},{8,0},{12,4},{1,9},{5,13},{9,1},{13,5},{2,10},{6,14},... | collective-permute-start | bytes 208904 | tf_op jit(solution)/shard_map/ppermute | solution.py:638
  31.4 3.4 %collective-permute-start.12 = (bf16[1088,128]{1,0:T(8,128)(2,1)S(1)}, bf16[1088,128]{1,0:T(8,128)(2,1)S(1)}, u32[]{:S(2)}, u32[]{:S(2)}) collective-permute-start(bf16[1088,128]{1,0:T(8,128)(2,1)S(1)} %pad_maximum_fusion), channel_id=1, source_target_pairs={{0,4},{4,0},{8,12},{12,8},{1,5},{5,1},{9,13},{13,9},{2,6},{6,2},{1... | collective-permute-start | bytes 835592 | tf_op jit(solution)/shard_map/ppermute | solution.py:638
  34.7 1.6 %collective-permute-start.13 = (bf16[1088,128]{1,0:T(8,128)(2,1)S(1)}, bf16[1088,128]{1,0:T(8,128)(2,1)S(1)}, u32[]{:S(2)}, u32[]{:S(2)}) collective-permute-start(bf16[1088,128]{1,0:T(8,128)(2,1)S(1)} %pad_maximum_fusion.1), channel_id=1, source_target_pairs={{0,4},{4,0},{8,12},{12,8},{1,5},{5,1},{9,13},{13,9},{2,6},{6,2},{1... | collective-permute-start | bytes 835592 | tf_op jit(solution)/shard_map/ppermute | solution.py:638
  40.0 4.4 %collective-permute-start.14 = (bf16[256,128]{1,0:T(8,128)(2,1)S(1)}, bf16[256,128]{1,0:T(8,128)(2,1)S(1)}, u32[]{:S(2)}, u32[]{:S(2)}) collective-permute-start(bf16[256,128]{1,0:T(8,128)(2,1)S(1)} %shard_map.191.refs_0_), channel_id=1, source_target_pairs={{0,8},{4,12},{8,0},{12,4},{1,9},{5,13},{9,1},{13,5},{2,10},{6,14},... | collective-permute-start | bytes 196616 | tf_op jit(solution)/shard_map/ppermute | solution.py:629
  41.5 3.0 %collective-permute-start.16 = (bf16[256,128]{1,0:T(8,128)(2,1)S(1)}, bf16[256,128]{1,0:T(8,128)(2,1)S(1)}, u32[]{:S(2)}, u32[]{:S(2)}) collective-permute-start(bf16[256,128]{1,0:T(8,128)(2,1)S(1)} %shard_map.191.refs_0_), channel_id=1, source_target_pairs={{0,4},{4,0},{8,12},{12,8},{1,5},{5,1},{9,13},{13,9},{2,6},{6,2},{1... | collective-permute-start | bytes 196616 | tf_op jit(solution)/shard_map/ppermute | solution.py:629
  44.4 1.3 %collective-permute-start.15 = (bf16[256,128]{1,0:T(8,128)(2,1)S(1)}, bf16[256,128]{1,0:T(8,128)(2,1)S(1)}, u32[]{:S(2)}, u32[]{:S(2)}) collective-permute-start(bf16[256,128]{1,0:T(8,128)(2,1)S(1)} %collective-permute-done.14.refs_2_), channel_id=1, source_target_pairs={{0,4},{4,0},{8,12},{12,8},{1,5},{5,1},{9,13},{13,9},{2,6},{6,2},{1... | collective-permute-start | bytes 196616 | tf_op jit(solution)/shard_map/ppermute | solution.py:629

commit v9 on v7

--- a/solution.py
+++ b/solution.py
@@ -762,7 +762,7 @@
         [(table_shape, BF16), ((table_shape[0], coarse), BF16), (table_shape, I32)],
     )
     before = call(edge_kernel, [coarse_edges2], [(coarse_edges.shape, F32)], one(3))
-    blocks2, (table, before) = over_both(payload2, (table, before))
+    blocks2, before = over_both(payload2, before)
     many = len(blocks2)
     begun = []
     if many > 1:
@@ -785,7 +785,7 @@
         cost=6,
     )
     before = call(edge_kernel, [fine_edges2], [(fine_edges.shape, F32)], one(4))
-    blocks3, before = over_region(coarse_final, before)
+    blocks3, (before, table) = over_region(coarse_final, (before, table))
     (fine_final,) = call(
         functools.partial(last_kernel, regions),
         blocks3 + [*table, fine_edges2, *before, *fine_cols],

time: 49.6 us -> 49.9 us (level)
  transfers between devices with their start and end apart: 17 -> 17, of which waited for: 9 -> 8; matrix products, arithmetic and copies ran while one was open for 0% -> 0% of each run, Pallas kernels for 14% -> 14%
where the time goes in v9:
time: 49.9 us; the launch traced here: 49.8 us
  Pallas kernels  20.1 us (40%)
  starting transfers between devices  17 us (34%)
  waiting for transfers between devices  12.3 us (25%)
    pallas_call x13, Pallas kernels, call(): pl.pallas_call(body, out_shape=[jax.ShapeDtypeStruct(shape, dtype) for sh...  20.1 us
    ppermute x9, starting transfers between devices, over_both(): lax.ppermute(array, axis, [(i, i ^ bits) for i in range(lax.axis_size(axi...  8.63 us
    ppermute x6, starting transfers between devices, over_region(): lax.ppermute(going[j], 'region', [(i, i ^ bit) for i in range(count)])  7.15 us
    ppermute x9, waiting for transfers between devices, over_both(): lax.ppermute(array, axis, [(i, i ^ bits) for i in range(lax.axis_size(axi...  6.44 us
    ppermute x6, waiting for transfers between devices, over_region(): lax.ppermute(going[j], 'region', [(i, i ^ bit) for i in range(count)])  5.82 us
  transfers between devices with their start and end apart: 17, of which 8 were waited for; matrix products, arithmetic and copies ran while one was open for 0% of the time, Pallas kernels for 14%

profile of v9, /device:TPU:0, one launch (start us, length us, event | category | flops | bytes accessed | tf_op | source)
XLA Modules:
  0.0 49.8 jit_solution(3698972698609439577)
XLA Ops:
  0.0 1.9 %shard_map.181 = (bf16[80,128]{1,0:T(8,128)(2,1)}, bf16[80,128]{1,0:T(8,128)(2,1)}, bf16[16,128]{1,0:T(8,128)(2,1)}) custom-call(bf16[512,128]{1,0:T(8,128)(2,1)} %refs_10_.2, s32[2,64]{1,0:T(2,128)} %refs_1_.3, s32[2,32]{1,0:T(2,128)} %refs_2_.1, s32[4,128]{1,0:T(4,128)} %bitcast.19, s32[4,128]{1,0:T(4,128)} %bitcast.20, s32[2,128]{1,0:T(2,128)} %bitcast.21), custom_call_target="tpu_custom_call" | custom-call | flops 1000000000 | bytes 100000 | tf_op jit(solution)/shard_map/pallas_call | solution.py:605
  2.0 0.5 %collective-permute-start = (bf16[80,128]{1,0:T(8,128)(2,1)}, bf16[80,128]{1,0:T(8,128)(2,1)S(1)}, u32[]{:S(2)}, u32[]{:S(2)}) collective-permute-start(bf16[80,128]{1,0:T(8,128)(2,1)} %get-tuple-element.83), channel_id=1, source_target_pairs={{0,4},{4,0},{8,12},{12,8},{1,5},{5,1},{9,13},{13,9},{2,6},{6,2},{1... | collective-permute-start | bytes 61448 | tf_op jit(solution)/shard_map/ppermute | solution.py:696
  2.5 0.7 %collective-permute-start.1 = (bf16[80,128]{1,0:T(8,128)(2,1)}, bf16[80,128]{1,0:T(8,128)(2,1)S(1)}, u32[]{:S(2)}, u32[]{:S(2)}) collective-permute-start(bf16[80,128]{1,0:T(8,128)(2,1)} %get-tuple-element.84), channel_id=1, source_target_pairs={{4,8},{8,4},{5,9},{9,5},{6,10},{10,6},{7,11},{11,7},{20,24},{24,20... | collective-permute-start | bytes 61448 | tf_op jit(solution)/shard_map/ppermute | solution.py:697
  3.3 1.4 %shard_map.182 = (s32[3072,128]{1,0:T(8,128)S(1)}, s32[3072,128]{1,0:T(8,128)S(1)}, s32[3072,128]{1,0:T(8,128)S(1)}, s32[3072,128]{1,0:T(8,128)S(1)}, s32[3072,1...) custom-call(bf16[512,128]{1,0:T(8,128)(2,1)S(1)} %copy-done.5, s32[24,128]{1,0:T(8,128)S(1)} %bitcast.14, ...), custom_call_target="tpu_custom_call" | custom-call | flops 2000000000 | bytes 200000 | tf_op jit(solution)/shard_map/pallas_call | solution.py:605
  4.7 1.8 %shard_map.183 = (bf16[528,128]{1,0:T(8,128)(2,1)S(1)}, bf16[3072,128]{1,0:T(8,128)(2,1)S(1)}) custom-call(bf16[80,128]{1,0:T(8,128)(2,1)S(1)} %collective-permute-done.refs_0_.refs_1_, bf16[80,128]{1,0:T(8,128)(2,1)S(1)} %collective-permute-done.1.refs_1_.refs_2_, bf16[16,128]{1,0:T(8,128)(2,1)S(1)} %copy-done.7, ...), custom_call_target="tpu_custom_call" | custom-call | flops 3000000000 | bytes 300000 | tf_op jit(solution)/shard_map/pallas_call | solution.py:605
  6.5 5.7 %collective-permute-start.2 = (bf16[528,128]{1,0:T(8,128)(2,1)S(1)}, bf16[528,128]{1,0:T(8,128)(2,1)S(1)}, u32[]{:S(2)}, u32[]{:S(2)}) collective-permute-start(bf16[528,128]{1,0:T(8,128)(2,1)S(1)} %get-tuple-element.108.refs_0_), channel_id=1, source_target_pairs={{0,8},{4,12},{8,0},{12,4},{1,9},{5,13},{9,1},{13,5},{2,10},{6,14},... | collective-permute-start | bytes 405512 | tf_op jit(solution)/shard_map/ppermute | solution.py:626
  12.3 2.4 %shard_map.184 = (s32[384,128]{1,0:T(8,128)S(1)}, s32[3,128]{1,0:T(4,128)S(1)}, s32[64,128]{1,0:T(8,128)S(1)}, s32[64,128]{1,0:T(8,128)S(1)}, s32[64,128]{1,0:T(...) custom-call(bf16[16,128]{1,0:T(8,128)(2,1)S(1)} %copy-done.7, ...), custom_call_target="tpu_custom_call" | custom-call | flops 3000000000 | bytes 300000 | tf_op jit(solution)/shard_map/pallas_call | solution.py:605
  14.7 1.4 %collective-permute-done.2.refs_2_ = bf16[528,128]{1,0:T(8,128)(2,1)S(1)} collective-permute-done((bf16[528,128]{1,0:T(8,128)(2,1)S(1)}, bf16[528,128]{1,0:T(8,128)(2,1)S(1)}, u32[]{:S(2)}, u32[]{:S(2)}) %collective-permute-start.2) | collective-permute-done | bytes 135200 | tf_op jit(solution)/shard_map/ppermute | solution.py:626
  16.1 0.5 shard_map.186
  16.6 0.4 shard_map.185
  17.1 0.4 collective-permute-done.3.refs_1_.refs_3_
  17.5 1.9 %shard_map.187 = (bf16[272,128]{1,0:T(8,128)(2,1)S(1)}, bf16[1536,128]{1,0:T(8,128)(2,1)S(1)}) custom-call(bf16[528,128]{1,0:T(8,128)(2,1)S(1)} %get-tuple-element.108.refs_0_, bf16[528,128]{1,0:T(8,128)(2,1)S(1)} %collective-permute-done.3.refs_1_.refs_3_, s32[320,128]{1,0:T(8,128)S(1)} %get-tuple-element.121.refs_3_.refs_2_, ...), custom_call_target="tpu_custom_call" | custom-call | flops 3000000000 | bytes 300000 | tf_op jit(solution)/shard_map/pallas_call | solution.py:605
  19.4 2.2 %collective-permute-start.5 = (bf16[272,128]{1,0:T(8,128)(2,1)S(1)}, bf16[272,128]{1,0:T(8,128)(2,1)S(1)}, u32[]{:S(2)}, u32[]{:S(2)}) collective-permute-start(bf16[272,128]{1,0:T(8,128)(2,1)S(1)} %get-tuple-element.129.refs_0_), channel_id=1, source_target_pairs={{0,1},{1,0},{2,3},{3,2},{4,5},{5,4},{6,7},{7,6},{8,9},{9,8},{10,11... | collective-permute-start | bytes 208904 | tf_op jit(solution)/shard_map/ppermute | solution.py:635
  21.6 2.6 %collective-permute-start.6 = (bf16[272,128]{1,0:T(8,128)(2,1)S(1)}, bf16[272,128]{1,0:T(8,128)(2,1)S(1)}, u32[]{:S(2)}, u32[]{:S(2)}) collective-permute-start(bf16[272,128]{1,0:T(8,128)(2,1)S(1)} %get-tuple-element.129.refs_0_), channel_id=1, source_target_pairs={{0,2},{1,3},{2,0},{3,1},{4,6},{5,7},{6,4},{7,5},{8,10},{9,11},{10,... | collective-permute-start | bytes 208904 | tf_op jit(solution)/shard_map/ppermute | solution.py:635
  24.2 0.8 %collective-permute-start.8 = (bf16[272,128]{1,0:T(8,128)(2,1)S(1)}, bf16[272,128]{1,0:T(8,128)(2,1)S(1)}, u32[]{:S(2)}, u32[]{:S(2)}) collective-permute-start(bf16[272,128]{1,0:T(8,128)(2,1)S(1)} %get-tuple-element.129.refs_0_), channel_id=1, source_target_pairs={{0,8},{4,12},{8,0},{12,4},{1,9},{5,13},{9,1},{13,5},{2,10},{6,14},... | collective-permute-start | bytes 208904 | tf_op jit(solution)/shard_map/ppermute | solution.py:635
  25.0 0.2 shard_map.188.refs_26_
  25.2 1.3 %collective-permute-start.9 = (bf16[272,128]{1,0:T(8,128)(2,1)S(1)}, bf16[272,128]{1,0:T(8,128)(2,1)S(1)}, u32[]{:S(2)}, u32[]{:S(2)}) collective-permute-start(bf16[272,128]{1,0:T(8,128)(2,1)S(1)} %collective-permute-done.5.refs_1_), channel_id=1, source_target_pairs={{0,8},{4,12},{8,0},{12,4},{1,9},{5,13},{9,1},{13,5},{2,10},{6,14},... | collective-permute-start | bytes 208904 | tf_op jit(solution)/shard_map/ppermute | solution.py:635
  26.5 2.9 %collective-permute-done.6.refs_2_ = bf16[272,128]{1,0:T(8,128)(2,1)S(1)} collective-permute-done((bf16[272,128]{1,0:T(8,128)(2,1)S(1)}, bf16[272,128]{1,0:T(8,128)(2,1)S(1)}, u32[]{:S(2)}, u32[]{:S(2)}) %collective-permute-start.6) | collective-permute-done | bytes 69664 | tf_op jit(solution)/shard_map/ppermute | solution.py:635
  29.4 0.6 %collective-permute-start.10 = (bf16[272,128]{1,0:T(8,128)(2,1)S(1)}, bf16[272,128]{1,0:T(8,128)(2,1)S(1)}, u32[]{:S(2)}, u32[]{:S(2)}) collective-permute-start(bf16[272,128]{1,0:T(8,128)(2,1)S(1)} %collective-permute-done.6.refs_2_), channel_id=1, source_target_pairs={{0,8},{4,12},{8,0},{12,4},{1,9},{5,13},{9,1},{13,5},{2,10},{6,14},... | collective-permute-start | bytes 208904 | tf_op jit(solution)/shard_map/ppermute | solution.py:635
  30.0 0.4 collective-permute-done.7.refs_3_
  30.4 1.0 %collective-permute-start.11 = (bf16[272,128]{1,0:T(8,128)(2,1)S(1)}, bf16[272,128]{1,0:T(8,128)(2,1)S(1)}, u32[]{:S(2)}, u32[]{:S(2)}) collective-permute-start(bf16[272,128]{1,0:T(8,128)(2,1)S(1)} %collective-permute-done.7.refs_3_), channel_id=1, source_target_pairs={{0,8},{4,12},{8,0},{12,4},{1,9},{5,13},{9,1},{13,5},{2,10},{6,14},... | collective-permute-start | bytes 208904 | tf_op jit(solution)/shard_map/ppermute | solution.py:635
  31.5 2.2 %collective-permute-done.10.refs_6_ = bf16[272,128]{1,0:T(8,128)(2,1)S(1)} collective-permute-done((bf16[272,128]{1,0:T(8,128)(2,1)S(1)}, bf16[272,128]{1,0:T(8,128)(2,1)S(1)}, u32[]{:S(2)}, u32[]{:S(2)}) %collective-permute-start.10) | collective-permute-done | bytes 69664 | tf_op jit(solution)/shard_map/ppermute | solution.py:635
  33.7 1.0 %collective-permute-done.11.refs_7_ = bf16[272,128]{1,0:T(8,128)(2,1)S(1)} collective-permute-done((bf16[272,128]{1,0:T(8,128)(2,1)S(1)}, bf16[272,128]{1,0:T(8,128)(2,1)S(1)}, u32[]{:S(2)}, u32[]{:S(2)}) %collective-permute-start.11) | collective-permute-done | bytes 69664 | tf_op jit(solution)/shard_map/ppermute | solution.py:635
  34.8 0.4 shard_map.191.refs_8_
  35.1 1.4 %shard_map.189 = (f32[384,128]{1,0:T(8,128)S(1)}, f32[384,128]{1,0:T(8,128)S(1)}, f32[384,128]{1,0:T(8,128)S(1)}, f32[384,128]{1,0:T(8,128)S(1)}) custom-call(bf16[272,128]{1,0:T(8,128)(2,1)S(1)} %get-tuple-element.129.refs_0_, bf16[272,128]{1,0:T(8,128)(2,1)S(1)} %collective-permute-done.5.refs_1_, bf16[272,128]{1,0:T(8,128)(2,1)S(1)} %collective-permute-done.6.refs_2_, ...), custom_call_target="tpu_custom_call" | custom-call | flops 1000000000 | bytes 100000 | tf_op jit(solution)/shard_map/pallas_call | solution.py:605
  36.5 3.7 %shard_map.190.refs_0_ = bf16[256,128]{1,0:T(8,128)(2,1)S(1)} custom-call(bf16[272,128]{1,0:T(8,128)(2,1)S(1)} %get-tuple-element.129.refs_0_, bf16[272,128]{1,0:T(8,128)(2,1)S(1)} %collective-permute-done.5.refs_1_, bf16[272,128]{1,0:T(8,128)(2,1)S(1)} %collective-permute-done.6.refs_2_, bf16[272,128]{1,0:T(8,128)(2,1)S(1)} %collective-permute-done.7.refs_3_, ...), custom_call_target="tpu_custom_call" | custom-call | flops 6000000000 | bytes 600000 | tf_op jit(solution)/shard_map/pallas_call | solution.py:605
  40.2 1.1 %collective-permute-start.15 = (bf16[256,128]{1,0:T(8,128)(2,1)S(1)}, bf16[256,128]{1,0:T(8,128)(2,1)S(1)}, u32[]{:S(2)}, u32[]{:S(2)}) collective-permute-start(bf16[256,128]{1,0:T(8,128)(2,1)S(1)} %shard_map.190.refs_0_), channel_id=1, source_target_pairs={{0,8},{4,12},{8,0},{12,4},{1,9},{5,13},{9,1},{13,5},{2,10},{6,14},... | collective-permute-start | bytes 196616 | tf_op jit(solution)/shard_map/ppermute | solution.py:626
  41.3 0.4 shard_map.192
  41.7 0.3 collective-permute-start.14
  42.0 2.8 %collective-permute-done.15.refs_2_ = bf16[256,128]{1,0:T(8,128)(2,1)S(1)} collective-permute-done((bf16[256,128]{1,0:T(8,128)(2,1)S(1)}, bf16[256,128]{1,0:T(8,128)(2,1)S(1)}, u32[]{:S(2)}, u32[]{:S(2)}) %collective-permute-start.15) | collective-permute-done | bytes 65568 | tf_op jit(solution)/shard_map/ppermute | solution.py:626
  44.8 1.2 %collective-permute-done.16.refs_3_ = bf16[256,128]{1,0:T(8,128)(2,1)S(1)} collective-permute-done((bf16[256,128]{1,0:T(8,128)(2,1)S(1)}, bf16[256,128]{1,0:T(8,128)(2,1)S(1)}, u32[]{:S(2)}, u32[]{:S(2)}) %collective-permute-start.16) | collective-permute-done | bytes 65568 | tf_op jit(solution)/shard_map/ppermute | solution.py:626
  46.1 3.7 %shard_map.193 = bf16[512,128]{1,0:T(8,128)(2,1)} custom-call(bf16[256,128]{1,0:T(8,128)(2,1)S(1)} %shard_map.190.refs_0_, bf16[256,128]{1,0:T(8,128)(2,1)S(1)} %collective-permute-done.14.refs_1_, bf16[256,128]{1,0:T(8,128)(2,1)S(1)} %collective-permute-done.15.refs_2_, bf16[256,128]{1,0:T(8,128)(2,1)S(1)} %collective-permute-done.16.refs_3_, ...), custom_call_target="tpu_custom_call" | custom-call | flops 3000000000 | bytes 300000 | tf_op jit(solution)/shard_map/pallas_call | solution.py:605
  (47 shorter events, 0.3 us)
Async XLA Ops:
  0.0 3.2 %copy-start = (bf16[5,384,128]{2,1,0:T(8,128)(2,1)S(1)}, bf16[5,384,128]{2,1,0:T(8,128)(2,1)}, u32[]{:S(2)}) copy-start(bf16[5,384,128]{2,1,0:T(8,128)(2,1)} %refs_16_.3) | copy-start | bytes 1474564
  0.0 3.2 %copy-start.1 = (bf16[5,256,128]{2,1,0:T(8,128)(2,1)S(1)}, bf16[5,256,128]{2,1,0:T(8,128)(2,1)}, u32[]{:S(2)}) copy-start(bf16[5,256,128]{2,1,0:T(8,128)(2,1)} %refs_18_.1) | copy-start | bytes 983044
  0.0 3.2 %copy-start.2 = (bf16[3072,128]{1,0:T(8,128)(2,1)S(1)}, bf16[3072,128]{1,0:T(8,128)(2,1)}, u32[]{:S(2)}) copy-start(bf16[3072,128]{1,0:T(8,128)(2,1)} %refs_12_.2) | copy-start | bytes 2359300
  0.0 3.2 %copy-start.3 = (bf16[5,128,128]{2,1,0:T(8,128)(2,1)S(1)}, bf16[5,128,128]{2,1,0:T(8,128)(2,1)}, u32[]{:S(2)}) copy-start(bf16[5,128,128]{2,1,0:T(8,128)(2,1)} %refs_17_.1) | copy-start | bytes 491524
  0.0 3.2 %copy-start.4 = (bf16[5,128,128]{2,1,0:T(8,128)(2,1)S(1)}, bf16[5,128,128]{2,1,0:T(8,128)(2,1)}, u32[]{:S(2)}) copy-start(bf16[5,128,128]{2,1,0:T(8,128)(2,1)} %refs_19_.1) | copy-start | bytes 491524
  0.0 3.2 %copy-start.5 = (bf16[512,128]{1,0:T(8,128)(2,1)S(1)}, bf16[512,128]{1,0:T(8,128)(2,1)}, u32[]{:S(2)}) copy-start(bf16[512,128]{1,0:T(8,128)(2,1)} %refs_10_.2) | copy-start | bytes 393220
  0.0 3.2 %copy-start.6 = (s32[3072]{0:T(1024)S(1)}, s32[3072]{0:T(1024)}, u32[]{:S(2)}) copy-start(s32[3072]{0:T(1024)} %param.21) | copy-start | bytes 36868
  0.0 3.2 %copy-start.12 = (s32[3072]{0:T(1024)S(1)}, s32[3072]{0:T(1024)}, u32[]{:S(2)}) copy-start(s32[3072]{0:T(1024)} %param.20) | copy-start | bytes 36868
  2.0 2.7 %collective-permute-start = (bf16[80,128]{1,0:T(8,128)(2,1)}, bf16[80,128]{1,0:T(8,128)(2,1)S(1)}, u32[]{:S(2)}, u32[]{:S(2)}) collective-permute-start(bf16[80,128]{1,0:T(8,128)(2,1)} %get-tuple-element.83), channel_id=1, source_target_pairs={{0,4},{4,0},{8,12},{12,8},{1,5},{5,1},{9,13},{13,9},{2,6},{6,2},{1... | collective-permute-start | bytes 61448 | tf_op jit(solution)/shard_map/ppermute | solution.py:696
  2.5 2.2 %collective-permute-start.1 = (bf16[80,128]{1,0:T(8,128)(2,1)}, bf16[80,128]{1,0:T(8,128)(2,1)S(1)}, u32[]{:S(2)}, u32[]{:S(2)}) collective-permute-start(bf16[80,128]{1,0:T(8,128)(2,1)} %get-tuple-element.84), channel_id=1, source_target_pairs={{4,8},{8,4},{5,9},{9,5},{6,10},{10,6},{7,11},{11,7},{20,24},{24,20... | collective-permute-start | bytes 61448 | tf_op jit(solution)/shard_map/ppermute | solution.py:697
  3.3 1.4 %copy-start.7 = (bf16[16,128]{1,0:T(8,128)(2,1)S(1)}, bf16[16,128]{1,0:T(8,128)(2,1)}, u32[]{:S(2)}) copy-start(bf16[16,128]{1,0:T(8,128)(2,1)} %get-tuple-element.86.refs_2_.refs_0_) | copy-start | bytes 12292
  4.7 7.5 %copy-start.8 = (bf16[8192,128]{1,0:T(8,128)(2,1)S(1)}, bf16[8192,128]{1,0:T(8,128)(2,1)}, u32[]{:S(2)}) copy-start(bf16[8192,128]{1,0:T(8,128)(2,1)} %refs_24_.1) | copy-start | bytes 6291460
  4.7 7.5 %copy-start.10 = (s32[8192]{0:T(1024)S(1)}, s32[8192]{0:T(1024)}, u32[]{:S(2)}) copy-start(s32[8192]{0:T(1024)} %param.31) | copy-start | bytes 98308
  4.7 7.5 %copy-start.11 = (s32[8192]{0:T(1024)S(1)}, s32[8192]{0:T(1024)}, u32[]{:S(2)}) copy-start(s32[8192]{0:T(1024)} %param.32) | copy-start | bytes 98308
  6.5 9.6 %collective-permute-start.2 = (bf16[528,128]{1,0:T(8,128)(2,1)S(1)}, bf16[528,128]{1,0:T(8,128)(2,1)S(1)}, u32[]{:S(2)}, u32[]{:S(2)}) collective-permute-start(bf16[528,128]{1,0:T(8,128)(2,1)S(1)} %get-tuple-element.108.refs_0_), channel_id=1, source_target_pairs={{0,8},{4,12},{8,0},{12,4},{1,9},{5,13},{9,1},{13,5},{2,10},{6,14},... | collective-permute-start | bytes 405512 | tf_op jit(solution)/shard_map/ppermute | solution.py:626
  12.3 3.9 %copy-start.9 = (bf16[1536,128]{1,0:T(8,128)(2,1)S(1)}, bf16[1536,128]{1,0:T(8,128)(2,1)}, u32[]{:S(2)}) copy-start(bf16[1536,128]{1,0:T(8,128)(2,1)} %refs_10_.3) | copy-start | bytes 1179652
  12.3 3.9 %copy-start.13 = (s32[1536]{0:T(1024)S(1)}, s32[1536]{0:T(1024)}, u32[]{:S(2)}) copy-start(s32[1536]{0:T(1024)} %param.24) | copy-start | bytes 18436
  12.3 3.9 %copy-start.14 = (s32[1536]{0:T(1024)S(1)}, s32[1536]{0:T(1024)}, u32[]{:S(2)}) copy-start(s32[1536]{0:T(1024)} %param.25) | copy-start | bytes 18436
  14.7 2.0 %collective-permute-start.4 = (bf16[528,128]{1,0:T(8,128)(2,1)S(1)}, bf16[528,128]{1,0:T(8,128)(2,1)S(1)}, u32[]{:S(2)}, u32[]{:S(2)}) collective-permute-start(bf16[528,128]{1,0:T(8,128)(2,1)S(1)} %get-tuple-element.108.refs_0_), channel_id=1, source_target_pairs={{0,4},{4,0},{8,12},{12,8},{1,5},{5,1},{9,13},{13,9},{2,6},{6,2},{1... | collective-permute-start | bytes 405512 | tf_op jit(solution)/shard_map/ppermute | solution.py:626
  16.1 1.4 %collective-permute-start.3 = (bf16[528,128]{1,0:T(8,128)(2,1)S(1)}, bf16[528,128]{1,0:T(8,128)(2,1)S(1)}, u32[]{:S(2)}, u32[]{:S(2)}) collective-permute-start(bf16[528,128]{1,0:T(8,128)(2,1)S(1)} %collective-permute-done.2.refs_2_), channel_id=1, source_target_pairs={{0,4},{4,0},{8,12},{12,8},{1,5},{5,1},{9,13},{13,9},{2,6},{6,2},{1... | collective-permute-start | bytes 405512 | tf_op jit(solution)/shard_map/ppermute | solution.py:626
  19.4 5.8 %collective-permute-start.5 = (bf16[272,128]{1,0:T(8,128)(2,1)S(1)}, bf16[272,128]{1,0:T(8,128)(2,1)S(1)}, u32[]{:S(2)}, u32[]{:S(2)}) collective-permute-start(bf16[272,128]{1,0:T(8,128)(2,1)S(1)} %get-tuple-element.129.refs_0_), channel_id=1, source_target_pairs={{0,1},{1,0},{2,3},{3,2},{4,5},{5,4},{6,7},{7,6},{8,9},{9,8},{10,11... | collective-permute-start | bytes 208904 | tf_op jit(solution)/shard_map/ppermute | solution.py:635
  21.6 7.8 %collective-permute-start.6 = (bf16[272,128]{1,0:T(8,128)(2,1)S(1)}, bf16[272,128]{1,0:T(8,128)(2,1)S(1)}, u32[]{:S(2)}, u32[]{:S(2)}) collective-permute-start(bf16[272,128]{1,0:T(8,128)(2,1)S(1)} %get-tuple-element.129.refs_0_), channel_id=1, source_target_pairs={{0,2},{1,3},{2,0},{3,1},{4,6},{5,7},{6,4},{7,5},{8,10},{9,11},{10,... | collective-permute-start | bytes 208904 | tf_op jit(solution)/shard_map/ppermute | solution.py:635
  24.2 6.2 %collective-permute-start.7 = (bf16[272,128]{1,0:T(8,128)(2,1)S(1)}, bf16[272,128]{1,0:T(8,128)(2,1)S(1)}, u32[]{:S(2)}, u32[]{:S(2)}) collective-permute-start(bf16[272,128]{1,0:T(8,128)(2,1)S(1)} %get-tuple-element.129.refs_0_), channel_id=1, source_target_pairs={{0,3},{1,2},{2,1},{3,0},{4,7},{5,6},{6,5},{7,4},{8,11},{9,10},{10,... | collective-permute-start | bytes 208904 | tf_op jit(solution)/shard_map/ppermute | solution.py:635
  24.2 7.3 %collective-permute-start.8 = (bf16[272,128]{1,0:T(8,128)(2,1)S(1)}, bf16[272,128]{1,0:T(8,128)(2,1)S(1)}, u32[]{:S(2)}, u32[]{:S(2)}) collective-permute-start(bf16[272,128]{1,0:T(8,128)(2,1)S(1)} %get-tuple-element.129.refs_0_), channel_id=1, source_target_pairs={{0,8},{4,12},{8,0},{12,4},{1,9},{5,13},{9,1},{13,5},{2,10},{6,14},... | collective-permute-start | bytes 208904 | tf_op jit(solution)/shard_map/ppermute | solution.py:635
  25.2 6.3 %collective-permute-start.9 = (bf16[272,128]{1,0:T(8,128)(2,1)S(1)}, bf16[272,128]{1,0:T(8,128)(2,1)S(1)}, u32[]{:S(2)}, u32[]{:S(2)}) collective-permute-start(bf16[272,128]{1,0:T(8,128)(2,1)S(1)} %collective-permute-done.5.refs_1_), channel_id=1, source_target_pairs={{0,8},{4,12},{8,0},{12,4},{1,9},{5,13},{9,1},{13,5},{2,10},{6,14},... | collective-permute-start | bytes 208904 | tf_op jit(solution)/shard_map/ppermute | solution.py:635
  29.4 4.3 %collective-permute-start.10 = (bf16[272,128]{1,0:T(8,128)(2,1)S(1)}, bf16[272,128]{1,0:T(8,128)(2,1)S(1)}, u32[]{:S(2)}, u32[]{:S(2)}) collective-permute-start(bf16[272,128]{1,0:T(8,128)(2,1)S(1)} %collective-permute-done.6.refs_2_), channel_id=1, source_target_pairs={{0,8},{4,12},{8,0},{12,4},{1,9},{5,13},{9,1},{13,5},{2,10},{6,14},... | collective-permute-start | bytes 208904 | tf_op jit(solution)/shard_map/ppermute | solution.py:635
  30.4 4.3 %collective-permute-start.11 = (bf16[272,128]{1,0:T(8,128)(2,1)S(1)}, bf16[272,128]{1,0:T(8,128)(2,1)S(1)}, u32[]{:S(2)}, u32[]{:S(2)}) collective-permute-start(bf16[272,128]{1,0:T(8,128)(2,1)S(1)} %collective-permute-done.7.refs_3_), channel_id=1, source_target_pairs={{0,8},{4,12},{8,0},{12,4},{1,9},{5,13},{9,1},{13,5},{2,10},{6,14},... | collective-permute-start | bytes 208904 | tf_op jit(solution)/shard_map/ppermute | solution.py:635
  31.4 3.7 %collective-permute-start.12 = (bf16[1088,128]{1,0:T(8,128)(2,1)S(1)}, bf16[1088,128]{1,0:T(8,128)(2,1)S(1)}, u32[]{:S(2)}, u32[]{:S(2)}) collective-permute-start(bf16[1088,128]{1,0:T(8,128)(2,1)S(1)} %pad_maximum_fusion), channel_id=1, source_target_pairs={{0,4},{4,0},{8,12},{12,8},{1,5},{5,1},{9,13},{13,9},{2,6},{6,2},{1... | collective-permute-start | bytes 835592 | tf_op jit(solution)/shard_map/ppermute | solution.py:635
  34.7 1.8 %collective-permute-start.13 = (bf16[1088,128]{1,0:T(8,128)(2,1)S(1)}, bf16[1088,128]{1,0:T(8,128)(2,1)S(1)}, u32[]{:S(2)}, u32[]{:S(2)}) collective-permute-start(bf16[1088,128]{1,0:T(8,128)(2,1)S(1)} %pad_maximum_fusion.1), channel_id=1, source_target_pairs={{0,4},{4,0},{8,12},{12,8},{1,5},{5,1},{9,13},{13,9},{2,6},{6,2},{1... | collective-permute-start | bytes 835592 | tf_op jit(solution)/shard_map/ppermute | solution.py:635
  40.2 4.6 %collective-permute-start.15 = (bf16[256,128]{1,0:T(8,128)(2,1)S(1)}, bf16[256,128]{1,0:T(8,128)(2,1)S(1)}, u32[]{:S(2)}, u32[]{:S(2)}) collective-permute-start(bf16[256,128]{1,0:T(8,128)(2,1)S(1)} %shard_map.190.refs_0_), channel_id=1, source_target_pairs={{0,8},{4,12},{8,0},{12,4},{1,9},{5,13},{9,1},{13,5},{2,10},{6,14},... | collective-permute-start | bytes 196616 | tf_op jit(solution)/shard_map/ppermute | solution.py:626
  41.7 3.1 %collective-permute-start.14 = (bf16[256,128]{1,0:T(8,128)(2,1)S(1)}, bf16[256,128]{1,0:T(8,128)(2,1)S(1)}, u32[]{:S(2)}, u32[]{:S(2)}) collective-permute-start(bf16[256,128]{1,0:T(8,128)(2,1)S(1)} %shard_map.190.refs_0_), channel_id=1, source_target_pairs={{0,4},{4,0},{8,12},{12,8},{1,5},{5,1},{9,13},{13,9},{2,6},{6,2},{1... | collective-permute-start | bytes 196616 | tf_op jit(solution)/shard_map/ppermute | solution.py:626
  44.8 1.3 %collective-permute-start.16 = (bf16[256,128]{1,0:T(8,128)(2,1)S(1)}, bf16[256,128]{1,0:T(8,128)(2,1)S(1)}, u32[]{:S(2)}, u32[]{:S(2)}) collective-permute-start(bf16[256,128]{1,0:T(8,128)(2,1)S(1)} %collective-permute-done.15.refs_2_), channel_id=1, source_target_pairs={{0,4},{4,0},{8,12},{12,8},{1,5},{5,1},{9,13},{13,9},{2,6},{6,2},{1... | collective-permute-start | bytes 196616 | tf_op jit(solution)/shard_map/ppermute | solution.py:626
